TPU v7x, 128 devices: a whole 4x4x4 slice. The times are simulated.
128 devices in a mesh: grp: 2 (over x_lo), dp: 64 (over x_hi, z, y, core).
Axes of the slice: x: 4 (x_hi: 2, x_lo: 2; x = x_hi * 2 + x_lo), y: 4, z: 4, core: 2. Of those that a mesh axis runs over, the one named last changes fastest.
Arguments:
- attn_out: bfloat16 [32768, 1408], P(('grp', 'dp'))
- out_grad: bfloat16 [32768, 1408], P(('grp', 'dp'))
- image_counts: int32 [128], replicated, may hold values from 1 to 1, as said below
- column_owner: int32 [64], replicated, may hold values from 0 to 63, each once
- damping: float32 [2], replicated, may hold values from 1 to 4
Outputs:
- factors: float32 [2, 1408, 1408], P(None, 'dp')
- preconditioned: float32 [1408, 1408], P(None, 'dp')
Inputs may be any that keep to these rules, and one draw needn't show every extreme that they name: image_counts[e] counts the real images of the device at place e of the order grp, dp; some device holds 1 images and some device holds 1. `column_owner`: a permutation.
All inputs are finite; a program needn't handle non-finite values.
Results may differ from a plain program's by a relative error of at most 0.007.
The roundings to bfloat16 on the way count: a program that leaves them out, or rounds other values in their place, can miss the bound.
Values may be sent and summed in bfloat16 or wider, within the bound.
No kernel may reach another device: no remote copies, remote signals or barrier semaphores. Data moves between devices by JAX's collectives and lax.ppermute only.
A program may use at most 128 MiB of HBM per device.

v0:
```python
import jax
import jax.numpy as jnp
from jax import lax
from jax.sharding import PartitionSpec as P

TOK = 256


def chol_apply(low, rhs):
    inner = lax.linalg.triangular_solve(low, rhs, left_side=True, lower=True)
    return lax.linalg.triangular_solve(low, inner, left_side=True, lower=True, transpose_a=True)


def outer_sum(left, right):
    return lax.dot_general(
        left, right, (((0,), (0,)), ((), ())), preferred_element_type=jnp.float32
    )


def per_device(attn_out, out_grad, image_counts, column_owner, damping):
    n_dp = lax.axis_size("dp")
    dp_index = lax.axis_index("dp")
    grp_index = lax.axis_index("grp")
    place = grp_index * n_dp + dp_index
    per_dev = attn_out.shape[0]
    width = attn_out.shape[1]
    block = width // n_dp
    count = lax.dynamic_index_in_dim(image_counts, place, 0, keepdims=False)
    keep = (jnp.arange(per_dev) // TOK < count).astype(jnp.bfloat16)[:, None]
    act_kept = attn_out * keep
    grad_kept = out_grad * keep
    part_a = outer_sum(act_kept, attn_out)
    part_g = outer_sum(grad_kept, out_grad)
    part_w = outer_sum(grad_kept, attn_out)
    rows_a, rows_g, rows_w = (
        lax.psum_scatter(part_a, "dp", scatter_dimension=0, tiled=True),
        lax.psum_scatter(part_g, "dp", scatter_dimension=0, tiled=True),
        lax.psum_scatter(part_w, "dp", scatter_dimension=0, tiled=True),
    )
    rows_a, rows_g, rows_w = lax.psum((rows_a, rows_g, rows_w), "grp")
    total = (TOK * jnp.sum(image_counts)).astype(jnp.float32)
    cov_a = rows_a / total
    cov_g = rows_g / total
    grad_rows = rows_w / total
    factors = jnp.stack([cov_a, cov_g])
    row_ids = dp_index * block + jnp.arange(block)
    identity = (row_ids[:, None] == jnp.arange(width)[None, :]).astype(jnp.float32)
    damp_a = (cov_a + damping[0] * identity).astype(jnp.bfloat16)
    damp_g = (cov_g + damping[1] * identity).astype(jnp.bfloat16)
    full_a, full_g = (
        lax.all_gather(damp_a, "dp", axis=0, tiled=True),
        lax.all_gather(damp_g, "dp", axis=0, tiled=True),
    )
    low_a = jnp.linalg.cholesky(full_a.astype(jnp.float32)).astype(jnp.bfloat16)
    low_g = jnp.linalg.cholesky(full_g.astype(jnp.float32)).astype(jnp.bfloat16)
    low_a = lax.optimization_barrier(low_a).astype(jnp.float32)
    low_g = lax.optimization_barrier(low_g).astype(jnp.float32)
    right_done = chol_apply(low_a, grad_rows.T).T
    routed = right_done.reshape(block, n_dp, block)[:, column_owner, :]
    columns = lax.all_to_all(routed, "dp", split_axis=1, concat_axis=0, tiled=True)
    columns = columns.reshape(width, block)
    preconditioned = chol_apply(low_g, columns)
    return (factors, preconditioned)


def solution(mesh):
    placed = (P(("grp", "dp"), None), P(("grp", "dp"), None), P(), P(), P())
    return jax.shard_map(
        per_device,
        mesh=mesh,
        in_specs=placed,
        out_specs=(P(None, "dp", None), P(None, "dp")),
        check_vma=False,
    )
```

profile of v0, /device:TPU:0, one launch (start us, length us, event | category | flops | bytes accessed | tf_op | source)
XLA Modules:
  0.0 1783.7 jit_solution(15354647725589136523)
XLA Ops:
  24.1 247.7 %fusion.314 = (f32[32,1408]{1,0:T(8,128)S(1)}, f32[32,1408]{1,0:T(8,128)S(1)}, f32[32,1408]{1,0:T(8,128)S(1)}) fusion(f32[1408,1408]{1,0:T(8,128)} %fusion.87, f32[1408,1408]{1,0:T(8,128)} %fusion.83, f32[1408,1408]{1,0:T(8,128)} %fusion.85), kind=kCustom, calls=%all-reduce-scatter.3 | all-reduce-scatter fusion | flops 8650753 | bytes 24330752
  280.9 23.2 %collective-permute-start.35 = (f32[32,1408]{1,0:T(8,128)S(1)}, f32[32,1408]{1,0:T(8,128)S(1)}, u32[]{:S(2)}, u32[]{:S(2)}) collective-permute-start(f32[32,1408]{1,0:T(8,128)S(1)} %get-tuple-element.65), channel_id=1, source_target_pairs={{0,16},{1,17},{2,18},{3,19},{4,20},{5,21},{6,22},{7,23},{8,24},{9,... | collective-permute-start | bytes 540680
  321.4 11.7 collective-permute-start.28
  334.4 17.7 collective-permute-start.26
  376.4 10.4 collective-permute-start.17
  494.7 10.3 collective-permute-start.50
  506.5 32.9 %concatenate.141 = f32[662,1408]{1,0:T(8,128)} concatenate(f32[22,1408]{1,0:T(8,128)} %copy-done.37, f32[32,1408]{1,0:T(8,128)S(1)} %collective-permute-done.38, f32[32,1408]{1,0:T(8,128)S(1)} %collective-permute-done.37, f32[32,1408]{1,0:T(8,128)S(1)} %collective-permute-done.36, f32[32,1408]{1,0:T(8,128)S(1)} %collective-permute-done.35, ...), dimensions={0} | concatenate | bytes 7456768
  539.4 35.1 %concatenate.140 = f32[662,1408]{1,0:T(8,128)} concatenate(f32[22,1408]{1,0:T(8,128)} %copy-done.36, f32[32,1408]{1,0:T(8,128)} %copy-done.7, f32[32,1408]{1,0:T(8,128)} %copy-done.8, f32[32,1408]{1,0:T(8,128)} %copy-done.9, f32[32,1408]{1,0:T(8,128)} %copy-done.10, f32[32,1408]{1,0:T(8,128)} %copy-done.13, f32[32,1408]{1,0:T(8,128)} %copy-done.16, f32[32,1408]{1,0:T(8,128)} %copy-done.19, ...), dimensions={0} | concatenate | bytes 7456768
  619.7 32.2 %concatenate.142 = f32[662,1408]{1,0:T(8,128)} concatenate(f32[22,1408]{1,0:T(8,128)S(1)} %copy-done.35, f32[32,1408]{1,0:T(8,128)S(1)} %copy-done.12, f32[32,1408]{1,0:T(8,128)S(1)} %copy-done.15, f32[32,1408]{1,0:T(8,128)S(1)} %copy-done.18, f32[32,1408]{1,0:T(8,128)S(1)} %copy-done.21, f32[32,1408]{1,0:T(8,128)} %collective-permute-done.54, ...), dimensions={0} | concatenate | bytes 7456768
  655.6 32.4 %all-reduce.11.cloned.1.call-done = (f32[22,1408]{1,0:T(8,128)}, f32[22,1408]{1,0:T(8,128)}, f32[22,1408]{1,0:T(8,128)}) async-done(((f32[22,1408]{1,0:T(8,128)}, f32[22,1408]{1,0:T(8,128)}, f32[22,1408]{1,0:T(8,128)}), (f32[22,1408]{1,0:T(8,128)}, f32[22,1408]{1,0:T(8,128)}, f32[22,1408]{1,0:T(8,128)})) %all-reduce.11.cloned.1.call-update) | async-done | bytes 371728 | tf_op jit(solution)/shard_map/psum | solution.py:40
  692.8 72.6 %all-gather.7.cloned.1.call-done = bf16[64,22,1408]{2,1,0:T(8,128)(2,1)} async-done(((bf16[1,22,1408]{2,1,0:T(8,128)(2,1)}), bf16[64,22,1408]{2,1,0:T(8,128)(2,1)}) %all-gather.7.cloned.1.call-update) | async-done | bytes 3964944 | tf_op jit(solution)/shard_map/all_gather | solution.py:51
  790.3 11.7 cholesky.1073
  805.7 9.8 custom-call.90
  820.0 11.9 cholesky.1092
  832.5 9.8 custom-call.91
  846.4 11.7 cholesky.1113
  858.8 9.8 custom-call.92
  873.4 11.7 cholesky.1132
  885.7 9.8 custom-call.93
  900.1 12.1 cholesky.1151
  912.9 9.8 custom-call.94
  927.4 11.7 cholesky.1170
  939.7 9.8 custom-call.95
  954.4 11.7 cholesky.1189
  966.7 9.8 custom-call.96
  981.0 11.9 cholesky.1208
  1007.3 11.7 cholesky.1227
  1033.0 12.1 cholesky.1246
  1058.5 11.7 cholesky.1263
  1091.8 32.3 %while.8 = (s32[]{:T(128)}, f32[1408,1408]{1,0:T(8,128)}, s32[11,2]{0,1:T(2,128)S(1)}, f32[11,128,128]{2,1,0:T(8,128)S(1)}, s32[]{:T(128)}) while((s32[]{:T(128)}, f32[1408,1408]{1,0:T(8,128)}, s32[11,2]{0,1:T(2,128)S(1)}, f32[11,128,128]{2,1,0:T(8,128)S(1)}, s32[]{:T(128)}) %tuple.212), condition=%wide.while_cond.1, body=%wide.while_body.1.sunk | while | flops 2 | bytes 131189 | solution.py:11
  1124.1 108.2 %custom-call.101 = f32[11,128,128]{1,2,0:T(8,128)S(1)} custom-call(f32[11,128,128]{2,1,0:T(8,128)S(1)} %get-tuple-element.34), custom_call_target="InvertDiagBlocksLowerTriangular" | custom-call | tf_op jit(solution)/shard_map/triangular_solve/custom-call.22 | solution.py:11
  1299.8 11.7 cholesky.868
  1329.4 11.9 cholesky.887
  1355.9 11.7 cholesky.908
  1382.8 11.7 cholesky.927
  1395.2 9.8 custom-call.83
  1409.6 12.1 cholesky.946
  1422.3 9.8 custom-call.84
  1436.8 11.7 cholesky.965
  1463.8 11.7 cholesky.984
  1476.2 9.8 custom-call.86
  1490.5 11.9 cholesky.1003
  1503.0 9.8 custom-call.87
  1516.8 11.7 cholesky.1022
  1542.5 12.1 cholesky.1041
  1568.0 11.7 cholesky.1058
  1601.6 31.4 %while.9 = (s32[]{:T(128)}, f32[1408,1408]{1,0:T(8,128)}, s32[11,2]{0,1:T(2,128)S(1)}, f32[11,128,128]{2,1,0:T(8,128)S(1)}, s32[]{:T(128)}) while((s32[]{:T(128)}, f32[1408,1408]{1,0:T(8,128)}, s32[11,2]{0,1:T(2,128)S(1)}, f32[11,128,128]{2,1,0:T(8,128)S(1)}, s32[]{:T(128)}) %tuple.225), condition=%wide.while_cond.1.clone, body=%wide.while_body.1.clone.sunk | while | flops 2 | bytes 131189 | solution.py:11
  1633.0 108.2 %custom-call.103 = f32[11,128,128]{1,2,0:T(8,128)S(1)} custom-call(f32[11,128,128]{2,1,0:T(8,128)S(1)} %get-tuple-element.36), custom_call_target="InvertDiagBlocksLowerTriangular" | custom-call | tf_op jit(solution)/shard_map/triangular_solve/custom-call.22 | solution.py:11
  (627 shorter events, 640.2 us)
Async XLA Ops:
  7.2 680.7 %all-reduce.11.cloned.1.call-start = ((), (), s32[]{:S(2)}) async-start(), calls=%async_computation.3 | async-start | bytes 811008 | tf_op jit(solution)/shard_map/psum | solution.py:40
  271.7 39.6 %collective-permute-start.38 = (f32[32,1408]{1,0:T(8,128)S(1)}, f32[32,1408]{1,0:T(8,128)S(1)}, u32[]{:S(2)}, u32[]{:S(2)}) collective-permute-start(f32[32,1408]{1,0:T(8,128)S(1)} %get-tuple-element.65), channel_id=1, source_target_pairs={{0,19},{1,20},{2,21},{3,22},{4,23},{5,24},{6,25},{7,26},{8,27},{9,... | collective-permute-start | bytes 540680
  273.1 39.6 %collective-permute-start.37 = (f32[32,1408]{1,0:T(8,128)S(1)}, f32[32,1408]{1,0:T(8,128)S(1)}, u32[]{:S(2)}, u32[]{:S(2)}) collective-permute-start(f32[32,1408]{1,0:T(8,128)S(1)} %get-tuple-element.65), channel_id=1, source_target_pairs={{0,18},{1,19},{2,20},{3,21},{4,22},{5,23},{6,24},{7,25},{8,26},{9,... | collective-permute-start | bytes 540680
  277.0 27.1 %collective-permute-start.59 = (f32[22,1408]{1,0:T(8,128)S(1)}, f32[22,1408]{1,0:T(8,128)S(1)}, u32[]{:S(2)}, u32[]{:S(2)}) collective-permute-start(f32[22,1408]{1,0:T(8,128)S(1)} %slice.683), channel_id=1, source_target_pairs={{0,20},{1,21},{2,22},{3,23},{4,24},{5,25},{6,26},{7,27},{8,28},{9,... | collective-permute-start | bytes 371720
  279.4 34.5 %collective-permute-start.36 = (f32[32,1408]{1,0:T(8,128)S(1)}, f32[32,1408]{1,0:T(8,128)S(1)}, u32[]{:S(2)}, u32[]{:S(2)}) collective-permute-start(f32[32,1408]{1,0:T(8,128)S(1)} %get-tuple-element.65), channel_id=1, source_target_pairs={{0,17},{1,18},{2,19},{3,20},{4,21},{5,22},{6,23},{7,24},{8,25},{9,... | collective-permute-start | bytes 540680
  280.9 34.4 %collective-permute-start.35 = (f32[32,1408]{1,0:T(8,128)S(1)}, f32[32,1408]{1,0:T(8,128)S(1)}, u32[]{:S(2)}, u32[]{:S(2)}) collective-permute-start(f32[32,1408]{1,0:T(8,128)S(1)} %get-tuple-element.65), channel_id=1, source_target_pairs={{0,16},{1,17},{2,18},{3,19},{4,20},{5,21},{6,22},{7,23},{8,24},{9,... | collective-permute-start | bytes 540680
  312.6 20.5 %collective-permute-start.32 = (f32[32,1408]{1,0:T(8,128)S(1)}, f32[32,1408]{1,0:T(8,128)S(1)}, u32[]{:S(2)}, u32[]{:S(2)}) collective-permute-start(f32[32,1408]{1,0:T(8,128)S(1)} %get-tuple-element.65), channel_id=1, source_target_pairs={{0,13},{1,14},{2,15},{3,16},{4,17},{5,18},{6,19},{7,20},{8,21},{9,... | collective-permute-start | bytes 540680
  313.9 20.5 %collective-permute-start.31 = (f32[32,1408]{1,0:T(8,128)S(1)}, f32[32,1408]{1,0:T(8,128)S(1)}, u32[]{:S(2)}, u32[]{:S(2)}) collective-permute-start(f32[32,1408]{1,0:T(8,128)S(1)} %get-tuple-element.65), channel_id=1, source_target_pairs={{0,12},{1,13},{2,14},{3,15},{4,16},{5,17},{6,18},{7,19},{8,20},{9,... | collective-permute-start | bytes 540680
  315.3 36.9 %collective-permute-start.30 = (f32[32,1408]{1,0:T(8,128)S(1)}, f32[32,1408]{1,0:T(8,128)S(1)}, u32[]{:S(2)}, u32[]{:S(2)}) collective-permute-start(f32[32,1408]{1,0:T(8,128)S(1)} %get-tuple-element.65), channel_id=1, source_target_pairs={{0,11},{1,12},{2,13},{3,14},{4,15},{5,16},{6,17},{7,18},{8,19},{9,... | collective-permute-start | bytes 540680
  317.8 36.6 %collective-permute-start.29 = (f32[32,1408]{1,0:T(8,128)S(1)}, f32[32,1408]{1,0:T(8,128)S(1)}, u32[]{:S(2)}, u32[]{:S(2)}) collective-permute-start(f32[32,1408]{1,0:T(8,128)S(1)} %get-tuple-element.65), channel_id=1, source_target_pairs={{0,10},{1,11},{2,12},{3,13},{4,14},{5,15},{6,16},{7,17},{8,18},{9,... | collective-permute-start | bytes 540680
  321.4 39.2 %collective-permute-start.28 = (f32[32,1408]{1,0:T(8,128)S(1)}, f32[32,1408]{1,0:T(8,128)S(1)}, u32[]{:S(2)}, u32[]{:S(2)}) collective-permute-start(f32[32,1408]{1,0:T(8,128)S(1)} %get-tuple-element.65), channel_id=1, source_target_pairs={{0,9},{1,10},{2,11},{3,12},{4,13},{5,14},{6,15},{7,16},{8,17},{9,1... | collective-permute-start | bytes 540680
  333.1 32.1 %collective-permute-start.27 = (f32[32,1408]{1,0:T(8,128)S(1)}, f32[32,1408]{1,0:T(8,128)S(1)}, u32[]{:S(2)}, u32[]{:S(2)}) collective-permute-start(f32[32,1408]{1,0:T(8,128)S(1)} %get-tuple-element.65), channel_id=1, source_target_pairs={{0,8},{1,9},{2,10},{3,11},{4,12},{5,13},{6,14},{7,15},{8,16},{9,17... | collective-permute-start | bytes 540680
  334.4 32.1 %collective-permute-start.26 = (f32[32,1408]{1,0:T(8,128)S(1)}, f32[32,1408]{1,0:T(8,128)S(1)}, u32[]{:S(2)}, u32[]{:S(2)}) collective-permute-start(f32[32,1408]{1,0:T(8,128)S(1)} %get-tuple-element.65), channel_id=1, source_target_pairs={{0,7},{1,8},{2,9},{3,10},{4,11},{5,12},{6,13},{7,14},{8,15},{9,16}... | collective-permute-start | bytes 540680
  365.2 21.6 %collective-permute-start.22 = (f32[32,1408]{1,0:T(8,128)S(1)}, f32[32,1408]{1,0:T(8,128)S(1)}, u32[]{:S(2)}, u32[]{:S(2)}) collective-permute-start(f32[32,1408]{1,0:T(8,128)S(1)} %get-tuple-element.65), channel_id=1, source_target_pairs={{0,3},{1,4},{2,5},{3,6},{4,7},{5,8},{6,9},{7,10},{8,11},{9,12},{10... | collective-permute-start | bytes 540680
  366.5 21.6 %collective-permute-start.21 = (f32[32,1408]{1,0:T(8,128)S(1)}, f32[32,1408]{1,0:T(8,128)S(1)}, u32[]{:S(2)}, u32[]{:S(2)}) collective-permute-start(f32[32,1408]{1,0:T(8,128)S(1)} %get-tuple-element.65), channel_id=1, source_target_pairs={{0,2},{1,3},{2,4},{3,5},{4,6},{5,7},{6,8},{7,9},{8,10},{9,11},{10,... | collective-permute-start | bytes 540680
  369.7 21.9 %collective-permute-start.20 = (f32[32,1408]{1,0:T(8,128)S(1)}, f32[32,1408]{1,0:T(8,128)S(1)}, u32[]{:S(2)}, u32[]{:S(2)}) collective-permute-start(f32[32,1408]{1,0:T(8,128)S(1)} %get-tuple-element.65), channel_id=1, source_target_pairs={{0,1},{1,2},{2,3},{3,4},{4,5},{5,6},{6,7},{7,8},{8,9},{9,10},{10,1... | collective-permute-start | bytes 540680
  372.3 21.0 %collective-permute-start.18 = (f32[32,1408]{1,0:T(8,128)S(1)}, f32[32,1408]{1,0:T(8,128)S(1)}, u32[]{:S(2)}, u32[]{:S(2)}) collective-permute-start(f32[32,1408]{1,0:T(8,128)S(1)} %get-tuple-element.66), channel_id=1, source_target_pairs={{0,19},{1,20},{2,21},{3,22},{4,23},{5,24},{6,25},{7,26},{8,27},{9,... | collective-permute-start | bytes 540680
  376.4 20.4 %collective-permute-start.17 = (f32[32,1408]{1,0:T(8,128)S(1)}, f32[32,1408]{1,0:T(8,128)S(1)}, u32[]{:S(2)}, u32[]{:S(2)}) collective-permute-start(f32[32,1408]{1,0:T(8,128)S(1)} %get-tuple-element.66), channel_id=1, source_target_pairs={{0,18},{1,19},{2,20},{3,21},{4,22},{5,23},{6,24},{7,25},{8,26},{9,... | collective-permute-start | bytes 540680
  388.1 18.6 %collective-permute-start.15 = (f32[32,1408]{1,0:T(8,128)S(1)}, f32[32,1408]{1,0:T(8,128)S(1)}, u32[]{:S(2)}, u32[]{:S(2)}) collective-permute-start(f32[32,1408]{1,0:T(8,128)S(1)} %get-tuple-element.66), channel_id=1, source_target_pairs={{0,16},{1,17},{2,18},{3,19},{4,20},{5,21},{6,22},{7,23},{8,24},{9,... | collective-permute-start | bytes 540680
  391.6 23.3 %collective-permute-start.14 = (f32[32,1408]{1,0:T(8,128)S(1)}, f32[32,1408]{1,0:T(8,128)S(1)}, u32[]{:S(2)}, u32[]{:S(2)}) collective-permute-start(f32[32,1408]{1,0:T(8,128)S(1)} %get-tuple-element.66), channel_id=1, source_target_pairs={{0,15},{1,16},{2,17},{3,18},{4,19},{5,20},{6,21},{7,22},{8,23},{9,... | collective-permute-start | bytes 540680
  393.3 25.1 %collective-permute-start.13 = (f32[32,1408]{1,0:T(8,128)S(1)}, f32[32,1408]{1,0:T(8,128)S(1)}, u32[]{:S(2)}, u32[]{:S(2)}) collective-permute-start(f32[32,1408]{1,0:T(8,128)S(1)} %get-tuple-element.66), channel_id=1, source_target_pairs={{0,14},{1,15},{2,16},{3,17},{4,18},{5,19},{6,20},{7,21},{8,22},{9,... | collective-permute-start | bytes 540680
  396.8 27.0 %collective-permute-start.12 = (f32[32,1408]{1,0:T(8,128)S(1)}, f32[32,1408]{1,0:T(8,128)S(1)}, u32[]{:S(2)}, u32[]{:S(2)}) collective-permute-start(f32[32,1408]{1,0:T(8,128)S(1)} %get-tuple-element.66), channel_id=1, source_target_pairs={{0,13},{1,14},{2,15},{3,16},{4,17},{5,18},{6,19},{7,20},{8,21},{9,... | collective-permute-start | bytes 540680
  399.7 32.4 %collective-permute-start.11 = (f32[32,1408]{1,0:T(8,128)S(1)}, f32[32,1408]{1,0:T(8,128)S(1)}, u32[]{:S(2)}, u32[]{:S(2)}) collective-permute-start(f32[32,1408]{1,0:T(8,128)S(1)} %get-tuple-element.66), channel_id=1, source_target_pairs={{0,12},{1,13},{2,14},{3,15},{4,16},{5,17},{6,18},{7,19},{8,20},{9,... | collective-permute-start | bytes 540680
  406.8 27.8 %collective-permute-start.10 = (f32[32,1408]{1,0:T(8,128)S(1)}, f32[32,1408]{1,0:T(8,128)S(1)}, u32[]{:S(2)}, u32[]{:S(2)}) collective-permute-start(f32[32,1408]{1,0:T(8,128)S(1)} %get-tuple-element.66), channel_id=1, source_target_pairs={{0,11},{1,12},{2,13},{3,14},{4,15},{5,16},{6,17},{7,18},{8,19},{9,... | collective-permute-start | bytes 540680
  414.9 25.0 %collective-permute-start.9 = (f32[32,1408]{1,0:T(8,128)S(1)}, f32[32,1408]{1,0:T(8,128)S(1)}, u32[]{:S(2)}, u32[]{:S(2)}) collective-permute-start(f32[32,1408]{1,0:T(8,128)S(1)} %get-tuple-element.66), channel_id=1, source_target_pairs={{0,10},{1,11},{2,12},{3,13},{4,14},{5,15},{6,16},{7,17},{8,18},{9,... | collective-permute-start | bytes 540680
  418.4 22.8 %collective-permute-start.8 = (f32[32,1408]{1,0:T(8,128)S(1)}, f32[32,1408]{1,0:T(8,128)S(1)}, u32[]{:S(2)}, u32[]{:S(2)}) collective-permute-start(f32[32,1408]{1,0:T(8,128)S(1)} %get-tuple-element.66), channel_id=1, source_target_pairs={{0,9},{1,10},{2,11},{3,12},{4,13},{5,14},{6,15},{7,16},{8,17},{9,1... | collective-permute-start | bytes 540680
  423.8 22.8 %collective-permute-start.7 = (f32[32,1408]{1,0:T(8,128)S(1)}, f32[32,1408]{1,0:T(8,128)S(1)}, u32[]{:S(2)}, u32[]{:S(2)}) collective-permute-start(f32[32,1408]{1,0:T(8,128)S(1)} %get-tuple-element.66), channel_id=1, source_target_pairs={{0,8},{1,9},{2,10},{3,11},{4,12},{5,13},{6,14},{7,15},{8,16},{9,17... | collective-permute-start | bytes 540680
  434.6 22.5 %collective-permute-start.5 = (f32[32,1408]{1,0:T(8,128)S(1)}, f32[32,1408]{1,0:T(8,128)S(1)}, u32[]{:S(2)}, u32[]{:S(2)}) collective-permute-start(f32[32,1408]{1,0:T(8,128)S(1)} %get-tuple-element.66), channel_id=1, source_target_pairs={{0,6},{1,7},{2,8},{3,9},{4,10},{5,11},{6,12},{7,13},{8,14},{9,15},... | collective-permute-start | bytes 540680
  439.9 18.5 %collective-permute-start.4 = (f32[32,1408]{1,0:T(8,128)S(1)}, f32[32,1408]{1,0:T(8,128)S(1)}, u32[]{:S(2)}, u32[]{:S(2)}) collective-permute-start(f32[32,1408]{1,0:T(8,128)S(1)} %get-tuple-element.66), channel_id=1, source_target_pairs={{0,5},{1,6},{2,7},{3,8},{4,9},{5,10},{6,11},{7,12},{8,13},{9,14},{... | collective-permute-start | bytes 540680
  441.2 22.0 %collective-permute-start.3 = (f32[32,1408]{1,0:T(8,128)S(1)}, f32[32,1408]{1,0:T(8,128)S(1)}, u32[]{:S(2)}, u32[]{:S(2)}) collective-permute-start(f32[32,1408]{1,0:T(8,128)S(1)} %get-tuple-element.66), channel_id=1, source_target_pairs={{0,4},{1,5},{2,6},{3,7},{4,8},{5,9},{6,10},{7,11},{8,12},{9,13},{1... | collective-permute-start | bytes 540680
  446.6 23.8 %collective-permute-start.2 = (f32[32,1408]{1,0:T(8,128)S(1)}, f32[32,1408]{1,0:T(8,128)S(1)}, u32[]{:S(2)}, u32[]{:S(2)}) collective-permute-start(f32[32,1408]{1,0:T(8,128)S(1)} %get-tuple-element.66), channel_id=1, source_target_pairs={{0,3},{1,4},{2,5},{3,6},{4,7},{5,8},{6,9},{7,10},{8,11},{9,12},{10... | collective-permute-start | bytes 540680
  448.8 27.8 %collective-permute-start.1 = (f32[32,1408]{1,0:T(8,128)S(1)}, f32[32,1408]{1,0:T(8,128)S(1)}, u32[]{:S(2)}, u32[]{:S(2)}) collective-permute-start(f32[32,1408]{1,0:T(8,128)S(1)} %get-tuple-element.66), channel_id=1, source_target_pairs={{0,2},{1,3},{2,4},{3,5},{4,6},{5,7},{6,8},{7,9},{8,10},{9,11},{10,... | collective-permute-start | bytes 540680
  457.0 21.9 %collective-permute-start = (f32[32,1408]{1,0:T(8,128)S(1)}, f32[32,1408]{1,0:T(8,128)S(1)}, u32[]{:S(2)}, u32[]{:S(2)}) collective-permute-start(f32[32,1408]{1,0:T(8,128)S(1)} %get-tuple-element.66), channel_id=1, source_target_pairs={{0,1},{1,2},{2,3},{3,4},{4,5},{5,6},{6,7},{7,8},{8,9},{9,10},{10,1... | collective-permute-start | bytes 540680
  458.4 24.1 %collective-permute-start.58 = (f32[32,1408]{1,0:T(8,128)S(1)}, f32[32,1408]{1,0:T(8,128)S(1)}, u32[]{:S(2)}, u32[]{:S(2)}) collective-permute-start(f32[32,1408]{1,0:T(8,128)S(1)} %get-tuple-element.67), channel_id=1, source_target_pairs={{0,19},{1,20},{2,21},{3,22},{4,23},{5,24},{6,25},{7,26},{8,27},{9,... | collective-permute-start | bytes 540680
  463.2 21.2 %collective-permute-start.57 = (f32[32,1408]{1,0:T(8,128)S(1)}, f32[32,1408]{1,0:T(8,128)S(1)}, u32[]{:S(2)}, u32[]{:S(2)}) collective-permute-start(f32[32,1408]{1,0:T(8,128)S(1)} %get-tuple-element.67), channel_id=1, source_target_pairs={{0,18},{1,19},{2,20},{3,21},{4,22},{5,23},{6,24},{7,25},{8,26},{9,... | collective-permute-start | bytes 540680
  476.6 18.1 %collective-permute-start.55 = (f32[32,1408]{1,0:T(8,128)S(1)}, f32[32,1408]{1,0:T(8,128)S(1)}, u32[]{:S(2)}, u32[]{:S(2)}) collective-permute-start(f32[32,1408]{1,0:T(8,128)S(1)} %get-tuple-element.67), channel_id=1, source_target_pairs={{0,16},{1,17},{2,18},{3,19},{4,20},{5,21},{6,22},{7,23},{8,24},{9,... | collective-permute-start | bytes 540680
  478.9 95.6 %collective-permute-start.54 = (f32[32,1408]{1,0:T(8,128)S(1)}, f32[32,1408]{1,0:T(8,128)}, u32[]{:S(2)}, u32[]{:S(2)}) collective-permute-start(f32[32,1408]{1,0:T(8,128)S(1)} %get-tuple-element.67), channel_id=1, source_target_pairs={{0,15},{1,16},{2,17},{3,18},{4,19},{5,20},{6,21},{7,22},{8,23},{9,... | collective-permute-start | bytes 540680
  482.5 93.4 %collective-permute-start.53 = (f32[32,1408]{1,0:T(8,128)S(1)}, f32[32,1408]{1,0:T(8,128)}, u32[]{:S(2)}, u32[]{:S(2)}) collective-permute-start(f32[32,1408]{1,0:T(8,128)S(1)} %get-tuple-element.67), channel_id=1, source_target_pairs={{0,14},{1,15},{2,16},{3,17},{4,18},{5,19},{6,20},{7,21},{8,22},{9,... | collective-permute-start | bytes 540680
  484.4 99.1 %collective-permute-start.52 = (f32[32,1408]{1,0:T(8,128)S(1)}, f32[32,1408]{1,0:T(8,128)}, u32[]{:S(2)}, u32[]{:S(2)}) collective-permute-start(f32[32,1408]{1,0:T(8,128)S(1)} %get-tuple-element.67), channel_id=1, source_target_pairs={{0,13},{1,14},{2,15},{3,16},{4,17},{5,18},{6,19},{7,20},{8,21},{9,... | collective-permute-start | bytes 540680
  486.4 101.3 %collective-permute-start.51 = (f32[32,1408]{1,0:T(8,128)S(1)}, f32[32,1408]{1,0:T(8,128)}, u32[]{:S(2)}, u32[]{:S(2)}) collective-permute-start(f32[32,1408]{1,0:T(8,128)S(1)} %get-tuple-element.67), channel_id=1, source_target_pairs={{0,12},{1,13},{2,14},{3,15},{4,16},{5,17},{6,18},{7,19},{8,20},{9,... | collective-permute-start | bytes 540680
  494.7 98.3 %collective-permute-start.50 = (f32[32,1408]{1,0:T(8,128)S(1)}, f32[32,1408]{1,0:T(8,128)}, u32[]{:S(2)}, u32[]{:S(2)}) collective-permute-start(f32[32,1408]{1,0:T(8,128)S(1)} %get-tuple-element.67), channel_id=1, source_target_pairs={{0,11},{1,12},{2,13},{3,14},{4,15},{5,16},{6,17},{7,18},{8,19},{9,... | collective-permute-start | bytes 540680
  574.5 23.9 %collective-permute-start.49 = (f32[32,1408]{1,0:T(8,128)S(1)}, f32[32,1408]{1,0:T(8,128)S(1)}, u32[]{:S(2)}, u32[]{:S(2)}) collective-permute-start(f32[32,1408]{1,0:T(8,128)S(1)} %get-tuple-element.67), channel_id=1, source_target_pairs={{0,10},{1,11},{2,12},{3,13},{4,14},{5,15},{6,16},{7,17},{8,18},{9,... | collective-permute-start | bytes 540680
  575.8 25.5 %collective-permute-start.48 = (f32[32,1408]{1,0:T(8,128)S(1)}, f32[32,1408]{1,0:T(8,128)S(1)}, u32[]{:S(2)}, u32[]{:S(2)}) collective-permute-start(f32[32,1408]{1,0:T(8,128)S(1)} %get-tuple-element.67), channel_id=1, source_target_pairs={{0,9},{1,10},{2,11},{3,12},{4,13},{5,14},{6,15},{7,16},{8,17},{9,1... | collective-permute-start | bytes 540680
  583.5 23.5 %collective-permute-start.47 = (f32[32,1408]{1,0:T(8,128)S(1)}, f32[32,1408]{1,0:T(8,128)S(1)}, u32[]{:S(2)}, u32[]{:S(2)}) collective-permute-start(f32[32,1408]{1,0:T(8,128)S(1)} %get-tuple-element.67), channel_id=1, source_target_pairs={{0,8},{1,9},{2,10},{3,11},{4,12},{5,13},{6,14},{7,15},{8,16},{9,17... | collective-permute-start | bytes 540680
  587.7 20.6 %collective-permute-start.46 = (f32[32,1408]{1,0:T(8,128)S(1)}, f32[32,1408]{1,0:T(8,128)S(1)}, u32[]{:S(2)}, u32[]{:S(2)}) collective-permute-start(f32[32,1408]{1,0:T(8,128)S(1)} %get-tuple-element.67), channel_id=1, source_target_pairs={{0,7},{1,8},{2,9},{3,10},{4,11},{5,12},{6,13},{7,14},{8,15},{9,16}... | collective-permute-start | bytes 540680
  653.6 111.9 %all-gather.7.cloned.1.call-start = ((), (), s32[]{:S(2)}) async-start(), calls=%async_computation.2 | async-start | bytes 4392960 | tf_op jit(solution)/shard_map/all_gather | solution.py:51
  690.9 584.0 %all-gather.5.cloned.1.call-start = ((), (), s32[]{:S(2)}) async-start(), calls=%async_computation.1 | async-start | bytes 4392960 | tf_op jit(solution)/shard_map/all_gather | solution.py:52
  1268.0 473.3 %all-to-all-start = ((f32[64,1,484]{2,1,0:T(1,128)}), f32[64,1,484]{2,1,0:T(1,128)S(1)}, u32[]{:S(2)}, u32[]{:S(2)}) async-start(f32[64,1,484]{2,1,0:T(1,128)} %reshape.299), calls=%async_computation | async-start | bytes 262144 | tf_op jit(solution)/shard_map/all_to_all | solution.py:60
  (59 other events, 3557.5 us)
Sparse Core Ops, SparseCore 0:
  653.7 34.1 all-reduce.10
  692.2 73.2 all-gather.6
  769.1 70.6 all-gather.4
where the time goes:
time: 1810 us; the launch traced here: 1780 us
  other arithmetic  732 us (40%)
  starting transfers between devices  276 us (15%)
  blocking collectives  248 us (14%)
  local copies, waits for them, and re-layouts  223 us (12%)
  matrix products  161 us (9%)
  waiting for transfers between devices  110 us (6%)
  between operations  32.7 us (2%)
    unnamed x60, starting transfers between devices  269 us
    unnamed x1, blocking collectives  248 us
    another operation x42, other arithmetic, per_device(): low_g = jnp.linalg.cholesky(full_g.astype(jnp.float32)).astype(jnp.bfloat16)  241 us
    another operation x42, other arithmetic, per_device(): low_a = jnp.linalg.cholesky(full_a.astype(jnp.float32)).astype(jnp.bfloat16)  241 us
    another operation x5, other arithmetic, chol_apply(): lax.linalg.triangular_solve(low, inner, left_side=True, lower=True, trans...  224 us
    unnamed x194, local copies, waits for them, and re-layouts  117 us
    all_gather x1, waiting for transfers between devices, per_device(): lax.all_gather(damp_a, 'dp', axis=0, tiled=True)  72.6 us
    another operation x83, local copies, waits for them, and re-layouts, chol_apply(): lax.linalg.triangular_solve(low, inner, left_side=True, lower=True, trans...  63.4 us
  transfers between devices with their start and end apart: 64, of which 5 were waited for; matrix products, arithmetic and copies ran while one was open for 57% of the time, Pallas kernels for 0%

commit v1 on v0

v1 whole, which is shorter than its diff:
```python
import jax
import jax.numpy as jnp
from jax import lax
from jax.experimental import pallas as pl
from jax.experimental.pallas import tpu as pltpu
from jax.sharding import PartitionSpec as P

TOK = 256
B = 128
HALF = 64
SLAB = 16
ROWS = 24
F32 = jnp.float32
BF16 = jnp.bfloat16
NT = (((1,), (1,)), ((), ()))
NN = (((1,), (0,)), ((), ()))
TN = (((0,), (0,)), ((), ()))
VM = pl.BlockSpec(memory_space=pltpu.VMEM)
SM = pl.BlockSpec(memory_space=pltpu.SMEM)
PARAMS = pltpu.CompilerParams(vmem_limit_bytes=48 * 1024 * 1024)


def dot(a, b, dims=NT):
    return lax.dot_general(a, b, dims, preferred_element_type=F32)


def split(x):
    hi = x.astype(BF16)
    return hi, (x - hi.astype(F32)).astype(BF16)


def row(x, t):
    return jnp.broadcast_to(x[..., t : t + 1, :], x.shape)


def col(x, c):
    return jnp.broadcast_to(x[..., c : c + 1], x.shape)


def rounded(x):
    return x.astype(BF16).astype(F32)


def tri(i, j):
    return i * (i + 1) // 2 + j


def gram_kernel(core_ref, *refs):
    pieces, out_ref, tmp_ref = refs[:-2], refs[-2], refs[-1]
    nb = pieces[0].shape[1] // B
    start = pl.multiple_of(core_ref[0] * HALF, HALF)
    for i in range(nb):
        wide = (i + 1) * B
        acc = None
        for ref in pieces:
            p = dot(ref[:, i * B : wide], ref[:, :wide], TN)
            acc = p if acc is None else acc + p
        tmp_ref[:, :wide] = acc
        for j in range(i + 1):
            t = tri(i, j)
            out_ref[t * HALF : (t + 1) * HALF, :] = tmp_ref[pl.ds(start, HALF), j * B : (j + 1) * B]
    used = tri(nb, 0) * HALF
    out_ref[used:, :] = jnp.zeros((out_ref.shape[0] - used, B), F32)


def gram(core, pieces, slots):
    width = pieces[0].shape[1]
    return pl.pallas_call(
        gram_kernel,
        out_shape=jax.ShapeDtypeStruct((slots * SLAB, B), F32),
        in_specs=[SM] + [VM] * len(pieces),
        out_specs=VM,
        scratch_shapes=[pltpu.VMEM((B, width), F32)],
        compiler_params=PARAMS,
        name="gram",
    )(core, *pieces)


def factor_diag(block):
    a = block.reshape(16, 8, B)
    lane = lax.broadcasted_iota(jnp.int32, (8, B), 1)
    sub = lax.broadcasted_iota(jnp.int32, (8, B), 0)
    x = jnp.stack([(lane == sub + 8 * g).astype(F32) for g in range(16)])
    inv, inv_r = [], []
    for g in range(16):
        here = (lane >= 8 * g) & (lane < 8 * g + 8)
        cg = [col(a[0], 8 * g + t) for t in range(8)]
        v = jnp.where(here, (lane == sub + 8 * g).astype(F32), a[0])
        xg = x[0]
        rest = a[1:]
        xr = x[1:]
        if g < 15:
            cr = [col(rest, 8 * g + t) for t in range(8)]
            rest = jnp.where(here[None], 0.0, rest)
        for t in range(8):
            p = row(cg[t], t)
            r = lax.rsqrt(p)
            lt = jnp.where(sub > t, cg[t] * r, 0.0)
            vn = row(v, t) * r
            v = jnp.where(sub == t, vn, v - lt * vn)
            xn = row(xg, t) / rounded(p * r)
            xg = jnp.where(sub == t, xn, xg - rounded(lt) * xn)
            cs = {s: row(cg[s], t) * r for s in range(t + 1, 8)}
            for s in range(t + 1, 8):
                cg[s] = cg[s] - lt * cs[s]
            if g < 15:
                lr = cr[t] * r[None]
                rest = rest - lr * vn[None]
                xr = xr - rounded(lr) * xn[None]
                for s in range(t + 1, 8):
                    cr[s] = cr[s] - lr * cs[s][None]
        inv.append(jnp.where(lane <= sub + 8 * g, v, 0.0))
        inv_r.append(xg)
        a, x = rest, xr
    return jnp.concatenate(inv, 0), jnp.concatenate(inv_r, 0)


def chol_kernel(core_ref, mine_ref, other_ref, low_ref, inv_ref, lo_ref, s_ref, w_ref):
    n = low_ref.shape[0]
    nb = n // B
    first = core_ref[0] == 0

    def block(i, j):
        t = tri(i, j) * HALF
        mine = mine_ref[t : t + HALF, :].astype(F32)
        other = other_ref[t : t + HALF, :].astype(F32)
        return jnp.concatenate([jnp.where(first, mine, other), jnp.where(first, other, mine)], 0)

    def update(kk):
        r0 = kk * B
        s = jnp.concatenate([block(i, kk) for i in range(kk, nb)], 0)
        if kk:
            wts = jnp.concatenate([low_ref[r0 : r0 + B, :r0], lo_ref[r0 : r0 + B, :r0]], 0)
            pr = dot(low_ref[r0:, :r0], wts)
            s = s - (pr[:, :B] + pr[:, B:] + dot(lo_ref[r0:, :r0], low_ref[r0 : r0 + B, :r0]))
        s_ref[r0:, :] = s

    def panel(kk):
        r0 = kk * B
        r1 = r0 + B
        shi, slo = split(s_ref[r1:, :])
        pr = dot(shi, w_ref[...])
        lp = pr[:, :B] + pr[:, B:] + dot(slo, w_ref[:B, :])
        hi, lo = split(lp)
        low_ref[r1:, r0:r1] = hi
        lo_ref[r1:, r0:r1] = lo

    def step(k, _):
        for kk in range(nb):
            pl.when(k == kk)(lambda kk=kk: update(kk))
        r0 = pl.multiple_of(k * B, B)
        linv, lrinv = factor_diag(s_ref[pl.ds(r0, B), :])
        inv_ref[pl.ds(r0, B), :] = lrinv
        hi, lo = split(linv)
        w_ref[:B, :] = hi
        w_ref[B:, :] = lo
        for kk in range(nb - 1):
            pl.when(k == kk)(lambda kk=kk: panel(kk))
        return 0

    lax.fori_loop(0, nb, step, 0)


def chol(core, mine, other, n):
    return pl.pallas_call(
        chol_kernel,
        out_shape=(jax.ShapeDtypeStruct((n, n), BF16), jax.ShapeDtypeStruct((n, B), F32)),
        in_specs=[SM, VM, VM],
        out_specs=(VM, VM),
        scratch_shapes=[
            pltpu.VMEM((n, n), BF16),
            pltpu.VMEM((n, B), F32),
            pltpu.VMEM((2 * B, B), BF16),
        ],
        compiler_params=PARAMS,
        name="cholesky",
    )(core, mine, other)


def solve_kernel(rhs_ref, low_ref, inv_ref, out_ref):
    n = low_ref.shape[0]
    nb = n // B
    m = rhs_ref.shape[0]

    def stacked(x):
        return jnp.concatenate(split(x), 0)

    def fold(p):
        return p[:m] + p[m:]

    acc = [rhs_ref[:, b * B : (b + 1) * B] for b in range(nb)]
    for b in range(nb):
        r0, r1 = b * B, (b + 1) * B
        w = stacked(inv_ref[r0:r1, :])
        p = fold(dot(stacked(acc[b]), w))
        y = p[:, :B] + p[:, B:]
        acc[b] = y
        ys = stacked(y)
        for c in range(b + 1, nb):
            acc[c] = acc[c] - fold(dot(ys, low_ref[c * B : (c + 1) * B, r0:r1]))
    for b in reversed(range(nb)):
        r0, r1 = b * B, (b + 1) * B
        w = jnp.concatenate(split(inv_ref[r0:r1, :]), 1)
        p = fold(dot(stacked(acc[b]), w, NN))
        z = p[:, :B] + p[:, B:]
        out_ref[:, r0:r1] = z
        zs = stacked(z)
        for c in range(b):
            acc[c] = acc[c] - fold(dot(zs, low_ref[r0:r1, c * B : (c + 1) * B], NN))


def solve(rhs, low, inv):
    return pl.pallas_call(
        solve_kernel,
        out_shape=jax.ShapeDtypeStruct(rhs.shape, F32),
        in_specs=[VM] * 3,
        out_specs=VM,
        compiler_params=PARAMS,
        name="solve",
    )(rhs, low, inv)


def rows_kernel(at_ref, all_ref, out_ref, s_ref):
    m, n = out_ref.shape
    nb = n // B
    for i in range(nb):
        for j in range(i + 1):
            t = tri(i, j) * HALF
            blk = jnp.concatenate([all_ref[0, t : t + HALF, :], all_ref[1, t : t + HALF, :]], 0)
            s_ref[i * B : (i + 1) * B, j * B : (j + 1) * B] = blk
            if i > j:
                s_ref[j * B : (j + 1) * B, i * B : (i + 1) * B] = blk.T
    at = at_ref[0]
    window = s_ref[pl.ds(pl.multiple_of(at // 8 * 8, 8), 32), :]
    shift = at % 8
    out = window[:m]
    for k in range(1, 8):
        out = jnp.where(shift == k, window[k : k + m], out)
    out_ref[...] = out


def rows_of(at, both, n, m):
    return pl.pallas_call(
        rows_kernel,
        out_shape=jax.ShapeDtypeStruct((m, n), F32),
        in_specs=[SM, VM],
        out_specs=VM,
        scratch_shapes=[pltpu.VMEM((n + 8, n), F32)],
        compiler_params=PARAMS,
        name="rows",
    )(at, both)


def per_device(attn_out, out_grad, image_counts, column_owner, damping):
    n_dp = lax.axis_size("dp")
    dp_index = lax.axis_index("dp")
    grp_index = lax.axis_index("grp")
    place = grp_index * n_dp + dp_index
    per_dev, width = attn_out.shape
    block = width // n_dp
    chips = n_dp // 2
    core = dp_index % 2
    chip = dp_index // 2
    nb = width // B
    used = tri(nb, 0) * HALF // SLAB
    per_chip = -(-used // chips)
    same_core = [list(range(c, n_dp, 2)) for c in range(2)]
    swap_core = [(d, d ^ 1) for d in range(n_dp)]
    swap_grp = [(0, 1), (1, 0)]
    core_arr = core.astype(jnp.int32)[None]
    is_a = grp_index == 0

    count = lax.dynamic_index_in_dim(image_counts, place, 0, keepdims=False)
    keep = (jnp.arange(per_dev) // TOK < count).astype(BF16)[:, None]
    act = attn_out * keep
    grad = out_grad * keep
    own = jnp.where(is_a, act, grad)
    other = jnp.where(is_a, grad, act)
    from_grp = lax.ppermute(other, "grp", swap_grp)
    act_c = lax.ppermute(act, "dp", swap_core)
    grad_c = lax.ppermute(grad, "dp", swap_core)
    own_c = jnp.where(is_a, act_c, grad_c)
    from_grp_c = lax.ppermute(from_grp, "dp", swap_core)

    total = (TOK * jnp.sum(image_counts)).astype(F32)
    part = gram(core_arr, [own, own_c, from_grp, from_grp_c], chips * per_chip)
    part = part.reshape(chips, per_chip * SLAB, B)
    got = lax.all_to_all(part, "dp", split_axis=0, concat_axis=0, tiled=True, axis_index_groups=same_core)
    slabs = jnp.sum(got, axis=0) / total

    flat = chip * (per_chip * SLAB) + jnp.arange(per_chip * SLAB)
    t = flat // HALF
    on_diag = jnp.zeros(t.shape, bool)
    for i in range(nb):
        on_diag = on_diag | (t == tri(i, i))
    in_row = core * HALF + flat % HALF
    diag = (on_diag & (flat < used * SLAB))[:, None] & (in_row[:, None] == jnp.arange(B)[None, :])
    damp = jnp.where(is_a, damping[0], damping[1])
    damped = (slabs + damp * diag.astype(F32)).astype(BF16)
    spread = jnp.broadcast_to(damped[None], (chips,) + damped.shape)
    mine = lax.all_to_all(spread, "dp", split_axis=0, concat_axis=0, tiled=True, axis_index_groups=same_core)
    mine = mine.reshape(chips * per_chip * SLAB, B)
    theirs = lax.ppermute(mine, "dp", swap_core)
    low, inv = chol(core_arr, mine, theirs, width)

    every = lax.all_gather(slabs, "dp", axis=0, tiled=False)
    every = every.reshape(chips, 2, per_chip * SLAB, B).transpose(1, 0, 2, 3).reshape(2, -1, B)
    at = (dp_index * block).astype(jnp.int32)[None]
    my_rows = rows_of(at, every, width, ROWS)[:block]
    their_rows = lax.ppermute(my_rows, "grp", swap_grp)
    factors = jnp.stack([jnp.where(is_a, my_rows, their_rows), jnp.where(is_a, their_rows, my_rows)])

    part_w = lax.dot_general(
        jnp.concatenate([grad, grad_c]), jnp.concatenate([act, act_c]), TN, preferred_element_type=F32
    )
    part_w = jnp.pad(part_w, ((0, n_dp * ROWS - width), (0, 0))).reshape(chips, 2, ROWS, width)
    part_w = lax.dynamic_index_in_dim(part_w, core, 1, keepdims=False)
    got_w = lax.all_to_all(part_w, "dp", split_axis=0, concat_axis=0, tiled=True, axis_index_groups=same_core)
    rows_w = jnp.sum(got_w, axis=0)
    rows_w = (rows_w + lax.ppermute(rows_w, "grp", swap_grp)) / total

    right = solve(rows_w, low, inv)
    routed = right.T.reshape(n_dp, block, ROWS)[column_owner]
    routed = lax.ppermute(routed, "grp", [(0, 1)])
    columns = lax.all_to_all(routed, "dp", split_axis=0, concat_axis=0, tiled=True)
    columns = columns.transpose(1, 0, 2).reshape(block, n_dp * ROWS)[:, :width]
    columns = jnp.pad(columns, ((0, ROWS - block), (0, 0)))
    left = solve(columns, low, inv)[:block]
    back = lax.ppermute(left, "grp", [(1, 0)])
    preconditioned = jnp.where(is_a, back, left).T
    return (factors, preconditioned)


def solution(mesh):
    placed = (P(("grp", "dp"), None), P(("grp", "dp"), None), P(), P(), P())
    return jax.shard_map(
        per_device,
        mesh=mesh,
        in_specs=placed,
        out_specs=(P(None, "dp", None), P(None, "dp")),
        check_vma=False,
    )
```

time: 1810 us -> 307 us (0.17); the launches traced: 1780 us -> 306 us
  other arithmetic: 732 us -> 11.2 us
  starting transfers between devices: 276 us -> 29.8 us
  blocking collectives: 248 us -> 21.5 us
  local copies, waits for them, and re-layouts: 223 us -> 18.1 us
  matrix products: 161 us -> 4.01 us
  Pallas kernels: 0 us -> 74.1 us
  waiting for transfers between devices: 110 us -> 131 us
    another operation x90 -> x2, other arithmetic: 706 us -> 0.04 us  [per_device(): jnp.stack([jnp.where(is_a, my_rows, their_rows), jnp.where(is_a, their_ro...]
    unnamed x60 -> x0, starting transfers between devices: 269 us -> none
    unnamed x1 -> x0, blocking collectives: 248 us -> none
    another operation x124 -> x0, matrix products: 147 us -> none  [the longest x20 42.2 us: per_device(): low_g = jnp.linalg.cholesky(full_g.astype(jnp.float32)).astype(jnp.bfloat16)]
    unnamed x194 -> x13, local copies, waits for them, and re-layouts: 117 us -> 5.87 us
    all_to_all x1 -> x3, waiting for transfers between devices: 0.01 us -> 101 us  [the longest x1 58 us: per_device(): lax.all_to_all(part_w, 'dp', split_axis=0, concat_axis=0, tiled=True, axi...]
    pallas_call x0 -> x5, Pallas kernels: none -> 74.1 us  [the longest x1 56.9 us: chol(): pl.pallas_call(chol_kernel, out_shape=(jax.ShapeDtypeStruct((n, n), BF16)...]
    all_gather x2 -> x1, waiting for transfers between devices: 72.6 us -> 0.02 us  [per_device(): every = lax.all_gather(slabs, 'dp', axis=0, tiled=False)]
  transfers between devices with their start and end apart: 64 -> 13, of which waited for: 5 -> 7; matrix products, arithmetic and copies ran while one was open for 57% -> 8% of each run, Pallas kernels for 0% -> 23%
where the time goes in v1:
time: 307 us; the launch traced here: 306 us
  waiting for transfers between devices  131 us (43%)
  Pallas kernels  74.1 us (24%)
  starting transfers between devices  29.8 us (10%)
  blocking collectives  21.5 us (7%)
  local copies, waits for them, and re-layouts  18.1 us (6%)
  between operations  16.3 us (5%)
  other arithmetic  11.2 us (4%)
  matrix products  4.01 us (1%)
    all_to_all x1, waiting for transfers between devices, per_device(): lax.all_to_all(part_w, 'dp', split_axis=0, concat_axis=0, tiled=True, axi...  58 us
    pallas_call x1, Pallas kernels, chol(): pl.pallas_call(chol_kernel, out_shape=(jax.ShapeDtypeStruct((n, n), BF16)...  56.9 us
    all_to_all x1, waiting for transfers between devices, per_device(): lax.all_to_all(part, 'dp', split_axis=0, concat_axis=0, tiled=True, axis_...  30.5 us
    all_to_all x1, blocking collectives, per_device(): lax.all_to_all(routed, 'dp', split_axis=0, concat_axis=0, tiled=True)  21.5 us
    ppermute x1, waiting for transfers between devices, per_device(): from_grp = lax.ppermute(other, 'grp', swap_grp)  15.6 us
    all_to_all x1, waiting for transfers between devices, per_device(): lax.all_to_all(spread, 'dp', split_axis=0, concat_axis=0, tiled=True, axi...  12.8 us
    pallas_call x2, Pallas kernels, solve(): pl.pallas_call(solve_kernel, out_shape=jax.ShapeDtypeStruct(rhs.shape, F3...  11.9 us
    all_to_all x1, starting transfers between devices, per_device(): lax.all_to_all(part, 'dp', split_axis=0, concat_axis=0, tiled=True, axis_...  11.2 us
  transfers between devices with their start and end apart: 13, of which 7 were waited for; matrix products, arithmetic and copies ran while one was open for 8% of the time, Pallas kernels for 23%

profile of v1, /device:TPU:0, one launch (start us, length us, event | category | flops | bytes accessed | tf_op | source)
XLA Modules:
  0.0 306.2 jit_solution(3869479452303409237)
XLA Ops:
  7.2 1.2 dynamic_slice.8
  8.4 0.6 compare_convert_fusion
  9.1 2.5 broadcast_select_fusion
  11.6 1.6 collective-permute-start.2
  13.1 0.5 collective-permute-start.1
  13.6 15.6 %collective-permute-done.2.refs_2_ = bf16[256,1408]{1,0:T(8,128)(2,1)S(1)} collective-permute-done((bf16[256,1408]{1,0:T(8,128)(2,1)S(1)}, bf16[256,1408]{1,0:T(8,128)(2,1)S(1)}, u32[]{:S(2)}, u32[]{:S(2)}) %collective-permute-start.2) | collective-permute-done | bytes 720928 | tf_op jit(solution)/shard_map/ppermute | solution.py:279
  29.3 1.2 broadcast_select_fusion.2.refs_0_
  30.5 1.2 broadcast_select_fusion.1.refs_1_
  31.7 4.2 %gram.1 = f32[4608,128]{1,0:T(8,128)} custom-call(s32[1]{0:T(128)} %bitcast.1.core_ref, bf16[256,1408]{1,0:T(8,128)(2,1)S(1)} %broadcast_select_fusion.2.refs_0_, bf16[256,1408]{1,0:T(8,128)(2,1)S(1)} %broadcast_select_fusion.1.refs_1_, bf16[256,1408]{1,0:T(8,128)(2,1)S(1)} %collective-permute-done.2.refs_2_, ...), custom_call_target="tpu_custom_call" | custom-call | tf_op jit(solution)/shard_map/gram/pallas_call | solution.py:68
  35.9 11.2 %all-to-all-start = ((f32[32,144,128]{2,1,0:T(8,128)}), f32[32,144,128]{2,1,0:T(8,128)S(1)}, u32[]{:S(2)}, u32[]{:S(2)}) async-start(f32[32,144,128]{2,1,0:T(8,128)} %bitcast.3), calls=%async_computation | async-start | bytes 4718592 | tf_op jit(solution)/shard_map/all_to_all | solution.py:288
  47.2 0.6 reduce_sum.28
  48.5 0.6 fusion.11
  50.4 30.5 %all-to-all-done = f32[32,144,128]{2,1,0:T(8,128)S(1)} async-done(((f32[32,144,128]{2,1,0:T(8,128)}), f32[32,144,128]{2,1,0:T(8,128)S(1)}, u32[]{:S(2)}, u32[]{:S(2)}) %all-to-all-start) | async-done | bytes 2359328 | tf_op jit(solution)/shard_map/all_to_all | solution.py:288
  81.0 0.7 add_convert_fusion
  81.7 1.2 broadcast_in_dim.10
  82.9 5.4 %all-to-all-start.2 = ((bf16[32,144,128]{2,1,0:T(8,128)(2,1)}), bf16[32,144,128]{2,1,0:T(8,128)(2,1)S(1)}, u32[]{:S(2)}, u32[]{:S(2)}) async-start(bf16[32,144,128]{2,1,0:T(8,128)(2,1)} %broadcast_in_dim.10), calls=%async_computation.2 | async-start | bytes 2359296 | tf_op jit(solution)/shard_map/all_to_all | solution.py:301
  88.3 4.0 %fusion = f32[1408,1408]{1,0:T(8,128)S(1)} fusion(bf16[256,1408]{1,0:T(8,128)(2,1)} %collective-permute-done.1, bf16[256,1408]{1,0:T(8,128)(2,1)S(1)} %get-tuple-element.17, bf16[256,1408]{1,0:T(8,128)(2,1)} %collective-permute-done, bf16[256,1408]{1,0:T(8,128)(2,1)} %get-tuple-element.18), kind=kOutput, calls=%fused_computation.2 | convolution fusion | flops 2035810304 | bytes 10813440 | tf_op jit(solution)/shard_map/dot_general | solution.py:313
  92.3 0.6 pad.8
  92.8 2.3 dynamic-slice_bitcast_fusion
  95.2 12.8 %all-to-all-done.2 = bf16[32,144,128]{2,1,0:T(8,128)(2,1)S(1)} async-done(((bf16[32,144,128]{2,1,0:T(8,128)(2,1)}), bf16[32,144,128]{2,1,0:T(8,128)(2,1)S(1)}, u32[]{:S(2)}, u32[]{:S(2)}) %all-to-all-start.2) | async-done | bytes 1179680 | tf_op jit(solution)/shard_map/all_to_all | solution.py:301
  108.0 5.3 %all-to-all-start.1 = ((f32[32,24,1408]{2,1,0:T(8,128)}), f32[32,24,1408]{2,1,0:T(8,128)}, u32[]{:S(2)}, u32[]{:S(2)}) async-start(f32[32,24,1408]{2,1,0:T(8,128)} %dynamic-slice_bitcast_fusion), calls=%async_computation.1 | async-start | bytes 8650752 | tf_op jit(solution)/shard_map/all_to_all | solution.py:318
  113.4 58.0 %all-to-all-done.1 = f32[32,24,1408]{2,1,0:T(8,128)} async-done(((f32[32,24,1408]{2,1,0:T(8,128)}), f32[32,24,1408]{2,1,0:T(8,128)}, u32[]{:S(2)}, u32[]{:S(2)}) %all-to-all-start.1) | async-done | bytes 4325408 | tf_op jit(solution)/shard_map/all_to_all | solution.py:318
  171.4 2.4 reduce_sum.29
  174.1 7.4 %collective-permute-done.5 = f32[24,1408]{1,0:T(8,128)S(1)} collective-permute-done((f32[24,1408]{1,0:T(8,128)S(1)}, f32[24,1408]{1,0:T(8,128)S(1)}, u32[]{:S(2)}, u32[]{:S(2)}) %collective-permute-start.5) | collective-permute-done | bytes 135200 | tf_op jit(solution)/shard_map/ppermute | solution.py:320
  181.6 56.9 %cholesky.1 = (bf16[1408,1408]{1,0:T(8,128)(2,1)}, f32[1408,128]{1,0:T(8,128)S(1)}) custom-call(s32[1]{0:T(128)} %bitcast.1.core_ref, bf16[4608,128]{1,0:T(8,128)(2,1)S(1)} %bitcast.28, bf16[4608,128]{1,0:T(8,128)(2,1)S(1)} %collective-permute-done.6.other_ref), custom_call_target="tpu_custom_call" | custom-call | tf_op jit(solution)/shard_map/cholesky/pallas_call | solution.py:165
  238.5 2.1 copy-done
  240.6 5.9 %solve.2 = f32[24,1408]{1,0:T(8,128)S(1)} custom-call(f32[24,1408]{1,0:T(8,128)S(1)} %add_divide_fusion.rhs_ref, bf16[1408,1408]{1,0:T(8,128)(2,1)S(1)} %copy-done, f32[1408,128]{1,0:T(8,128)S(1)} %get-tuple-element.5.inv_ref), custom_call_target="tpu_custom_call" | custom-call | tf_op jit(solution)/shard_map/solve/pallas_call | solution.py:213
  246.5 0.9 reshape.147
  247.4 0.6 copy.18
  248.0 0.6 gather_fusion
  248.9 1.4 collective-permute-start.7
  250.3 3.9 %collective-permute-done.7 = f32[64,22,24]{0,2,1:T(8,128)S(1)} collective-permute-done((f32[64,22,24]{0,2,1:T(8,128)S(1)}, f32[64,22,24]{0,2,1:T(8,128)S(1)}, u32[]{:S(2)}, u32[]{:S(2)}) %collective-permute-start.7) | collective-permute-done | bytes 135200 | tf_op jit(solution)/shard_map/ppermute | solution.py:324
  254.3 0.3 copy.20
  254.6 0.5 reshape.160
  255.1 21.5 %all_to_all.20 = f32[64,1,528]{2,1,0:T(1,128)S(1)} all-to-all(f32[64,1,528]{2,1,0:T(1,128)S(1)} %reshape.160), channel_id=1, replica_groups=mesh['grp'=2,'dp'=64] {'dp'}, dimensions={0} | all-to-all | bytes 270336 | tf_op jit(solution)/shard_map/all_to_all | solution.py:325
  276.6 0.5 broadcast.212
  277.1 1.0 reduce
  278.1 0.3 reshape.161
  278.6 0.4 reshape.148
  279.0 2.1 copy-done.1
  281.1 5.9 %solve.3 = f32[24,1408]{1,0:T(8,128)S(1)} custom-call(f32[24,1408]{1,0:T(8,128)S(1)} %pad.9.rhs_ref, bf16[1408,1408]{1,0:T(8,128)(2,1)S(1)} %copy-done.1, f32[1408,128]{1,0:T(8,128)S(1)} %get-tuple-element.5.inv_ref), custom_call_target="tpu_custom_call" | custom-call | tf_op jit(solution)/shard_map/solve/pallas_call | solution.py:213
  287.1 1.3 collective-permute-start.8
  288.4 2.6 copy.17
  291.0 1.2 rows.1
  292.2 2.7 collective-permute-start.4
  294.9 0.7 select_bitcast_fusion
  295.6 2.9 collective-permute-done.4
  298.6 0.8 copy.22
  (32 shorter events, 1.1 us)
Async XLA Ops:
  11.6 17.7 %collective-permute-start.2 = (bf16[256,1408]{1,0:T(8,128)(2,1)S(1)}, bf16[256,1408]{1,0:T(8,128)(2,1)S(1)}, u32[]{:S(2)}, u32[]{:S(2)}) collective-permute-start(bf16[256,1408]{1,0:T(8,128)(2,1)S(1)} %get-tuple-element.16), channel_id=1, source_target_pairs={{0,64},{64,0},{1,65},{65,1},{2,66},{66,2},{3,67},{67,3},{4,68},{68... | collective-permute-start | bytes 2162696 | tf_op jit(solution)/shard_map/ppermute | solution.py:279
  13.1 17.3 %collective-permute-start = (bf16[256,1408]{1,0:T(8,128)(2,1)}, bf16[256,1408]{1,0:T(8,128)(2,1)}, u32[]{:S(2)}, u32[]{:S(2)}) collective-permute-start(bf16[256,1408]{1,0:T(8,128)(2,1)} %get-tuple-element.18), channel_id=1, source_target_pairs={{0,1},{1,0},{2,3},{3,2},{4,5},{5,4},{6,7},{7,6},{8,9},{9,8},{10,11... | collective-permute-start | bytes 2162696 | tf_op jit(solution)/shard_map/ppermute | solution.py:280
  13.1 17.4 %collective-permute-start.1 = (bf16[256,1408]{1,0:T(8,128)(2,1)S(1)}, bf16[256,1408]{1,0:T(8,128)(2,1)}, u32[]{:S(2)}, u32[]{:S(2)}) collective-permute-start(bf16[256,1408]{1,0:T(8,128)(2,1)S(1)} %get-tuple-element.17), channel_id=1, source_target_pairs={{0,1},{1,0},{2,3},{3,2},{4,5},{5,4},{6,7},{7,6},{8,9},{9,8},{10,11... | collective-permute-start | bytes 2162696 | tf_op jit(solution)/shard_map/ppermute | solution.py:281
  29.3 2.4 collective-permute-start.3
  35.9 11.2 %copy-start.3 = (s32[128]{0:T(128)S(1)}, s32[128]{0:T(128)}, u32[]{:S(2)}) copy-start(s32[128]{0:T(128)} %param.7) | copy-start | bytes 1540
  35.9 12.5 %copy-start.2 = (f32[2]{0:T(128)S(1)}, f32[2]{0:T(128)}, u32[]{:S(2)}) copy-start(f32[2]{0:T(128)} %param.9) | copy-start | bytes 28
  35.9 45.0 %all-to-all-start = ((f32[32,144,128]{2,1,0:T(8,128)}), f32[32,144,128]{2,1,0:T(8,128)S(1)}, u32[]{:S(2)}, u32[]{:S(2)}) async-start(f32[32,144,128]{2,1,0:T(8,128)} %bitcast.3), calls=%async_computation | async-start | bytes 4718592 | tf_op jit(solution)/shard_map/all_to_all | solution.py:288
  47.1 241.3 %all-gather.3.cloned.1.call-start = ((), (), s32[]{:S(2)}) async-start(), calls=%async_computation.4 | async-start | bytes 4792320 | tf_op jit(solution)/shard_map/all_gather | solution.py:306
  82.9 25.1 %all-to-all-start.2 = ((bf16[32,144,128]{2,1,0:T(8,128)(2,1)}), bf16[32,144,128]{2,1,0:T(8,128)(2,1)S(1)}, u32[]{:S(2)}, u32[]{:S(2)}) async-start(bf16[32,144,128]{2,1,0:T(8,128)(2,1)} %broadcast_in_dim.10), calls=%async_computation.2 | async-start | bytes 2359296 | tf_op jit(solution)/shard_map/all_to_all | solution.py:301
  108.0 63.4 %all-to-all-start.1 = ((f32[32,24,1408]{2,1,0:T(8,128)}), f32[32,24,1408]{2,1,0:T(8,128)}, u32[]{:S(2)}, u32[]{:S(2)}) async-start(f32[32,24,1408]{2,1,0:T(8,128)} %dynamic-slice_bitcast_fusion), calls=%async_computation.1 | async-start | bytes 8650752 | tf_op jit(solution)/shard_map/all_to_all | solution.py:318
  113.3 60.8 %copy-start.4 = (s32[64]{0:T(128)S(1)}, s32[64]{0:T(128)}, u32[]{:S(2)}) copy-start(s32[64]{0:T(128)} %param.8) | copy-start | bytes 772
  113.3 68.3 %collective-permute-start.6 = (bf16[4608,128]{1,0:T(8,128)(2,1)S(1)}, bf16[4608,128]{1,0:T(8,128)(2,1)S(1)}, u32[]{:S(2)}, u32[]{:S(2)}) collective-permute-start(bf16[4608,128]{1,0:T(8,128)(2,1)S(1)} %bitcast.27), channel_id=1, source_target_pairs={{0,1},{1,0},{2,3},{3,2},{4,5},{5,4},{6,7},{7,6},{8,9},{9,8},{10,11... | collective-permute-start | bytes 3538952 | tf_op jit(solution)/shard_map/ppermute | solution.py:303
  173.8 7.7 %collective-permute-start.5 = (f32[24,1408]{1,0:T(8,128)S(1)}, f32[24,1408]{1,0:T(8,128)S(1)}, u32[]{:S(2)}, u32[]{:S(2)}) collective-permute-start(f32[24,1408]{1,0:T(8,128)S(1)} %reduce_sum.29), channel_id=1, source_target_pairs={{0,64},{64,0},{1,65},{65,1},{2,66},{66,2},{3,67},{67,3},{4,68},{68... | collective-permute-start | bytes 405512 | tf_op jit(solution)/shard_map/ppermute | solution.py:320
  238.5 2.1 copy-start
  248.9 5.4 %collective-permute-start.7 = (f32[64,22,24]{0,2,1:T(8,128)S(1)}, f32[64,22,24]{0,2,1:T(8,128)S(1)}, u32[]{:S(2)}, u32[]{:S(2)}) collective-permute-start(f32[64,22,24]{0,2,1:T(8,128)S(1)} %copy.19), channel_id=1, source_target_pairs={{0,64},{1,65},{2,66},{3,67},{4,68},{5,69},{6,70},{7,71},{8,72},{9,... | collective-permute-start | bytes 405512 | tf_op jit(solution)/shard_map/ppermute | solution.py:324
  279.0 2.1 copy-start.1
  287.1 7.9 %collective-permute-start.8 = (f32[22,1408]{1,0:T(8,128)S(1)}, f32[22,1408]{1,0:T(8,128)S(1)}, u32[]{:S(2)}, u32[]{:S(2)}) collective-permute-start(f32[22,1408]{1,0:T(8,128)S(1)} %bitcast.30), channel_id=1, source_target_pairs={{64,0},{65,1},{66,2},{67,3},{68,4},{69,5},{70,6},{71,7},{72,8},{73... | collective-permute-start | bytes 371720 | tf_op jit(solution)/shard_map/ppermute | solution.py:329
  292.2 6.3 %collective-permute-start.4 = (f32[22,1408]{1,0:T(8,128)S(1)}, f32[22,1408]{1,0:T(8,128)S(1)}, u32[]{:S(2)}, u32[]{:S(2)}) collective-permute-start(f32[22,1408]{1,0:T(8,128)S(1)} %bitcast.31), channel_id=1, source_target_pairs={{0,64},{64,0},{1,65},{65,1},{2,66},{66,2},{3,67},{67,3},{4,68},{68... | collective-permute-start | bytes 371720 | tf_op jit(solution)/shard_map/ppermute | solution.py:310
Sparse Core Ops, SparseCore 0:
  81.8 116.6 all-gather.2

commit v2 on v1

--- a/solution.py
+++ b/solution.py
@@ -16,8 +16,17 @@
 NN = (((1,), (0,)), ((), ()))
 TN = (((0,), (0,)), ((), ()))
 VM = pl.BlockSpec(memory_space=pltpu.VMEM)
+ANY = pl.BlockSpec(memory_space=pl.ANY)
 SM = pl.BlockSpec(memory_space=pltpu.SMEM)
-PARAMS = pltpu.CompilerParams(vmem_limit_bytes=48 * 1024 * 1024)
+MIB = 1024 * 1024
+
+
+def params(mib):
+    return pltpu.CompilerParams(vmem_limit_bytes=mib * MIB)
+
+
+def cost(micros):
+    return pl.CostEstimate(flops=int(micros * 1.1e9), bytes_accessed=MIB, transcendentals=0)
 
 
 def dot(a, b, dims=NT):
@@ -45,15 +54,15 @@
     return i * (i + 1) // 2 + j
 
 
-def gram_kernel(core_ref, *refs):
+def gram_kernel(core_ref, keep_ref, *refs):
     pieces, out_ref, tmp_ref = refs[:-2], refs[-2], refs[-1]
     nb = pieces[0].shape[1] // B
     start = pl.multiple_of(core_ref[0] * HALF, HALF)
     for i in range(nb):
         wide = (i + 1) * B
         acc = None
-        for ref in pieces:
-            p = dot(ref[:, i * B : wide], ref[:, :wide], TN)
+        for k, ref in enumerate(pieces):
+            p = dot(ref[:, i * B : wide] * keep_ref[k].astype(BF16), ref[:, :wide], TN)
             acc = p if acc is None else acc + p
         tmp_ref[:, :wide] = acc
         for j in range(i + 1):
@@ -63,17 +72,18 @@
     out_ref[used:, :] = jnp.zeros((out_ref.shape[0] - used, B), F32)
 
 
-def gram(core, pieces, slots):
+def gram(core, keeps, pieces, slots):
     width = pieces[0].shape[1]
     return pl.pallas_call(
         gram_kernel,
         out_shape=jax.ShapeDtypeStruct((slots * SLAB, B), F32),
-        in_specs=[SM] + [VM] * len(pieces),
+        in_specs=[SM, SM] + [VM] * len(pieces),
         out_specs=VM,
         scratch_shapes=[pltpu.VMEM((B, width), F32)],
-        compiler_params=PARAMS,
+        compiler_params=params(24),
+        cost_estimate=cost(3),
         name="gram",
-    )(core, *pieces)
+    )(core, keeps, *pieces)
 
 
 def factor_diag(block):
@@ -172,12 +182,13 @@
             pltpu.VMEM((n, B), F32),
             pltpu.VMEM((2 * B, B), BF16),
         ],
-        compiler_params=PARAMS,
+        compiler_params=params(24),
+        cost_estimate=cost(57),
         name="cholesky",
     )(core, mine, other)
 
 
-def solve_kernel(rhs_ref, low_ref, inv_ref, out_ref):
+def solve_kernel(rhs_ref, low_ref, inv_ref, after_ref, out_ref):
     n = low_ref.shape[0]
     nb = n // B
     m = rhs_ref.shape[0]
@@ -209,24 +220,47 @@
             acc[c] = acc[c] - fold(dot(zs, low_ref[r0:r1, c * B : (c + 1) * B], NN))
 
 
-def solve(rhs, low, inv):
+def solve(rhs, low, inv, after):
     return pl.pallas_call(
         solve_kernel,
         out_shape=jax.ShapeDtypeStruct(rhs.shape, F32),
-        in_specs=[VM] * 3,
+        in_specs=[VM] * 3 + [ANY],
         out_specs=VM,
-        compiler_params=PARAMS,
+        compiler_params=params(16),
+        cost_estimate=cost(7),
         name="solve",
-    )(rhs, low, inv)
+    )(rhs, low, inv, after)
+
+
+def sum_kernel(parts_ref, after_ref, out_ref):
+    acc = parts_ref[0]
+    for k in range(1, parts_ref.shape[0]):
+        acc = acc + parts_ref[k]
+    out_ref[...] = acc
+
+
+def sum_parts(parts, after):
+    return pl.pallas_call(
+        sum_kernel,
+        out_shape=jax.ShapeDtypeStruct(parts.shape[1:], F32),
+        in_specs=[VM, ANY],
+        out_specs=VM,
+        compiler_params=params(16),
+        cost_estimate=cost(3),
+        name="sum_parts",
+    )(parts, after)
 
 
 def rows_kernel(at_ref, all_ref, out_ref, s_ref):
     m, n = out_ref.shape
     nb = n // B
+    per = all_ref.shape[1]
     for i in range(nb):
         for j in range(i + 1):
             t = tri(i, j) * HALF
-            blk = jnp.concatenate([all_ref[0, t : t + HALF, :], all_ref[1, t : t + HALF, :]], 0)
+            blk = jnp.concatenate(
+                [all_ref[2 * (f // per) + c, f % per : f % per + SLAB, :]
+                 for c in range(2) for f in range(t, t + HALF, SLAB)], 0)
             s_ref[i * B : (i + 1) * B, j * B : (j + 1) * B] = blk
             if i > j:
                 s_ref[j * B : (j + 1) * B, i * B : (i + 1) * B] = blk.T
@@ -246,7 +280,8 @@
         in_specs=[SM, VM],
         out_specs=VM,
         scratch_shapes=[pltpu.VMEM((n + 8, n), F32)],
-        compiler_params=PARAMS,
+        compiler_params=params(24),
+        cost_estimate=cost(3),
         name="rows",
     )(at, both)
 
@@ -255,7 +290,6 @@
     n_dp = lax.axis_size("dp")
     dp_index = lax.axis_index("dp")
     grp_index = lax.axis_index("grp")
-    place = grp_index * n_dp + dp_index
     per_dev, width = attn_out.shape
     block = width // n_dp
     chips = n_dp // 2
@@ -270,20 +304,41 @@
     core_arr = core.astype(jnp.int32)[None]
     is_a = grp_index == 0
 
-    count = lax.dynamic_index_in_dim(image_counts, place, 0, keepdims=False)
-    keep = (jnp.arange(per_dev) // TOK < count).astype(BF16)[:, None]
-    act = attn_out * keep
-    grad = out_grad * keep
-    own = jnp.where(is_a, act, grad)
-    other = jnp.where(is_a, grad, act)
-    from_grp = lax.ppermute(other, "grp", swap_grp)
-    act_c = lax.ppermute(act, "dp", swap_core)
-    grad_c = lax.ppermute(grad, "dp", swap_core)
+    def keep_of(grp, dp):
+        return (lax.dynamic_index_in_dim(image_counts, grp * n_dp + dp, 0, keepdims=False) > 0).astype(F32)
+
+    flip = n_dp // 2
+    near = [(g * n_dp + d, (1 - g) * n_dp + d) for g in range(2) for d in range(n_dp)]
+    far = [(g * n_dp + d, (1 - g) * n_dp + d ^ flip) for g in range(2) for d in range(n_dp)]
+    both = ("grp", "dp")
+    half = per_dev // 2
+
+    def cross(perm, rows):
+        to_a = lax.ppermute(attn_out[rows], both, [p for p in perm if p[1] < n_dp])
+        to_g = lax.ppermute(out_grad[rows], both, [p for p in perm if p[1] >= n_dp])
+        return jnp.where(is_a, to_a, to_g)
+
+    from_near = cross(near, slice(0, half))
+    from_far = cross(far, slice(half, None))
+    act_c = lax.ppermute(attn_out, "dp", swap_core)
+    grad_c = lax.ppermute(out_grad, "dp", swap_core)
+    own = jnp.where(is_a, attn_out, out_grad)
     own_c = jnp.where(is_a, act_c, grad_c)
-    from_grp_c = lax.ppermute(from_grp, "dp", swap_core)
+    near_c = lax.ppermute(from_near, "dp", swap_core)
+    far_c = lax.ppermute(from_far, "dp", swap_core)
+    over, mate, away = 1 - grp_index, dp_index ^ 1, dp_index ^ flip
+    keeps = jnp.stack([
+        keep_of(grp_index, dp_index),
+        keep_of(grp_index, mate),
+        keep_of(over, dp_index),
+        keep_of(over, away),
+        keep_of(over, mate),
+        keep_of(over, away ^ 1),
+    ])
+    pieces = [own, own_c, from_near, from_far, near_c, far_c]
 
     total = (TOK * jnp.sum(image_counts)).astype(F32)
-    part = gram(core_arr, [own, own_c, from_grp, from_grp_c], chips * per_chip)
+    part = gram(core_arr, keeps, pieces, chips * per_chip)
     part = part.reshape(chips, per_chip * SLAB, B)
     got = lax.all_to_all(part, "dp", split_axis=0, concat_axis=0, tiled=True, axis_index_groups=same_core)
     slabs = jnp.sum(got, axis=0) / total
@@ -303,29 +358,28 @@
     theirs = lax.ppermute(mine, "dp", swap_core)
     low, inv = chol(core_arr, mine, theirs, width)
 
+    slabs, mine = lax.optimization_barrier((slabs, mine))
     every = lax.all_gather(slabs, "dp", axis=0, tiled=False)
-    every = every.reshape(chips, 2, per_chip * SLAB, B).transpose(1, 0, 2, 3).reshape(2, -1, B)
     at = (dp_index * block).astype(jnp.int32)[None]
     my_rows = rows_of(at, every, width, ROWS)[:block]
     their_rows = lax.ppermute(my_rows, "grp", swap_grp)
     factors = jnp.stack([jnp.where(is_a, my_rows, their_rows), jnp.where(is_a, their_rows, my_rows)])
 
-    part_w = lax.dot_general(
-        jnp.concatenate([grad, grad_c]), jnp.concatenate([act, act_c]), TN, preferred_element_type=F32
-    )
+    kept = jnp.concatenate([out_grad * keeps[0].astype(BF16), grad_c * keeps[1].astype(BF16)])
+    part_w = dot(kept, jnp.concatenate([attn_out, act_c]), TN)
     part_w = jnp.pad(part_w, ((0, n_dp * ROWS - width), (0, 0))).reshape(chips, 2, ROWS, width)
     part_w = lax.dynamic_index_in_dim(part_w, core, 1, keepdims=False)
     got_w = lax.all_to_all(part_w, "dp", split_axis=0, concat_axis=0, tiled=True, axis_index_groups=same_core)
-    rows_w = jnp.sum(got_w, axis=0)
+    rows_w = sum_parts(got_w, inv)
     rows_w = (rows_w + lax.ppermute(rows_w, "grp", swap_grp)) / total
 
-    right = solve(rows_w, low, inv)
+    right = solve(rows_w, low, inv, inv)
     routed = right.T.reshape(n_dp, block, ROWS)[column_owner]
     routed = lax.ppermute(routed, "grp", [(0, 1)])
     columns = lax.all_to_all(routed, "dp", split_axis=0, concat_axis=0, tiled=True)
     columns = columns.transpose(1, 0, 2).reshape(block, n_dp * ROWS)[:, :width]
     columns = jnp.pad(columns, ((0, ROWS - block), (0, 0)))
-    left = solve(columns, low, inv)[:block]
+    left = solve(columns, low, inv, my_rows)[:block]
     back = lax.ppermute(left, "grp", [(1, 0)])
     preconditioned = jnp.where(is_a, back, left).T
     return (factors, preconditioned)

time: 307 us -> 276 us (0.90)
  waiting for transfers between devices: 131 us -> 65.1 us
  starting transfers between devices: 29.8 us -> 56.6 us
  blocking collectives: 21.5 us -> 26.9 us
  between operations: 16.3 us -> 20.3 us
  other arithmetic: 11.2 us -> 7.43 us
    all_to_all x1, waiting for transfers between devices: 58 us -> 4.23 us  [per_device(): lax.all_to_all(part_w, 'dp', split_axis=0, concat_axis=0, tiled=True, axi...]
    ppermute x4 -> x8, starting transfers between devices: 2.09 us -> 15.8 us  [the longest x2 12.5 us: cross(): to_g = lax.ppermute(out_grad[rows], both, [p for p in perm if p[1] >= n_dp])]
    ppermute x4 -> x8, waiting for transfers between devices: 15.6 us -> 6.42 us  [the longest x2 5.9 us: cross(): to_g = lax.ppermute(out_grad[rows], both, [p for p in perm if p[1] >= n_dp])]
    ppermute x1, starting transfers between devices: 0.26 us -> 8.12 us  [per_device(): rows_w = (rows_w + lax.ppermute(rows_w, 'grp', swap_grp)) / total]
    all_to_all x1, blocking collectives: 21.5 us -> 26.9 us  [per_device(): lax.all_to_all(spread, 'dp', split_axis=0, concat_axis=0, tiled=True, axi...]
    all_to_all x1, starting transfers between devices: 5.35 us -> 10.6 us  [per_device(): lax.all_to_all(routed, 'dp', split_axis=0, concat_axis=0, tiled=True)]
    ppermute x1, waiting for transfers between devices: 0.01 us -> 5.04 us  [per_device(): back = lax.ppermute(left, 'grp', [(1, 0)])]
    ppermute x1, waiting for transfers between devices: 7.44 us -> 2.98 us  [per_device(): rows_w = (rows_w + lax.ppermute(rows_w, 'grp', swap_grp)) / total]
  transfers between devices with their start and end apart: 13 -> 17, of which waited for: 7 -> 8; matrix products, arithmetic and copies ran while one was open for 8% -> 9% of each run, Pallas kernels for 23% -> 25%
where the time goes in v2:
time: 276 us
  Pallas kernels  76.4 us (28%)
  waiting for transfers between devices  65.1 us (24%)
  starting transfers between devices  56.6 us (21%)
  blocking collectives  26.9 us (10%)
  between operations  20.3 us (7%)
  local copies, waits for them, and re-layouts  18.6 us (7%)
  other arithmetic  7.43 us (3%)
  matrix products  4.21 us (2%)
    pallas_call x1, Pallas kernels, chol(): pl.pallas_call(chol_kernel, out_shape=(jax.ShapeDtypeStruct((n, n), BF16)...  54.9 us
    all_to_all x1, waiting for transfers between devices, per_device(): lax.all_to_all(part, 'dp', split_axis=0, concat_axis=0, tiled=True, axis_...  28.4 us
    all_to_all x1, blocking collectives, per_device(): lax.all_to_all(spread, 'dp', split_axis=0, concat_axis=0, tiled=True, axi...  26.9 us
    ppermute x2, starting transfers between devices, cross(): to_g = lax.ppermute(out_grad[rows], both, [p for p in perm if p[1] >= n_dp])  12.5 us
    pallas_call x2, Pallas kernels, solve(): pl.pallas_call(solve_kernel, out_shape=jax.ShapeDtypeStruct(rhs.shape, F3...  11.9 us
    all_to_all x1, starting transfers between devices, per_device(): lax.all_to_all(routed, 'dp', split_axis=0, concat_axis=0, tiled=True)  10.6 us
    all_to_all x1, waiting for transfers between devices, per_device(): lax.all_to_all(routed, 'dp', split_axis=0, concat_axis=0, tiled=True)  10.3 us
    all_to_all x1, starting transfers between devices, per_device(): lax.all_to_all(part, 'dp', split_axis=0, concat_axis=0, tiled=True, axis_...  9.79 us
  transfers between devices with their start and end apart: 17, of which 8 were waited for; matrix products, arithmetic and copies ran while one was open for 9% of the time, Pallas kernels for 25%

profile of v2, /device:TPU:0, one launch (start us, length us, event | category | flops | bytes accessed | tf_op | source)
XLA Modules:
  0.0 275.6 jit_solution(8418027039300043674)
XLA Ops:
  7.8 1.9 fusion.12
  9.7 1.3 collective-permute-start.2
  11.0 2.0 fusion.11
  13.0 6.0 %collective-permute-start.3 = (bf16[128,1408]{1,0:T(8,128)(2,1)}, bf16[128,1408]{1,0:T(8,128)(2,1)}, u32[]{:S(2)}, u32[]{:S(2)}) collective-permute-start(bf16[128,1408]{1,0:T(8,128)(2,1)} %get-tuple-element.23), channel_id=1, source_target_pairs={{0,64},{1,65},{2,66},{3,67},{4,68},{5,69},{6,70},{7,71},{8,72},{9,... | collective-permute-start | bytes 1081352 | tf_op jit(solution)/shard_map/ppermute | solution.py:318
  19.0 1.3 collective-permute-start.4
  20.3 0.7 fusion.13
  25.0 1.0 broadcast_multiply_fusion.1
  26.1 6.4 %collective-permute-start.5 = (bf16[128,1408]{1,0:T(8,128)(2,1)S(1)}, bf16[128,1408]{1,0:T(8,128)(2,1)S(1)}, u32[]{:S(2)}, u32[]{:S(2)}) collective-permute-start(bf16[128,1408]{1,0:T(8,128)(2,1)S(1)} %copy-done.7), channel_id=1, source_target_pairs={{0,96},{1,97},{2,98},{3,99},{4,100},{5,101},{6,102},{7,103},{8,104... | collective-permute-start | bytes 1081352 | tf_op jit(solution)/shard_map/ppermute | solution.py:318
  32.5 1.0 broadcast_select_fusion.3.refs_2_
  33.7 5.9 %collective-permute-done.5 = bf16[128,1408]{1,0:T(8,128)(2,1)S(1)} collective-permute-done((bf16[128,1408]{1,0:T(8,128)(2,1)S(1)}, bf16[128,1408]{1,0:T(8,128)(2,1)S(1)}, u32[]{:S(2)}, u32[]{:S(2)}) %collective-permute-start.5) | collective-permute-done | bytes 360480 | tf_op jit(solution)/shard_map/ppermute | solution.py:318
  39.6 1.0 broadcast_select_fusion.2.refs_3_
  40.7 1.1 broadcast_multiply_fusion
  41.8 0.5 collective-permute-done.7.refs_5_
  42.3 5.9 %gram.1 = f32[4608,128]{1,0:T(8,128)} custom-call(s32[1]{0:T(128)} %bitcast.1.core_ref, f32[6]{0:T(128)S(1)} %stack.8.keep_ref, bf16[256,1408]{1,0:T(8,128)(2,1)S(1)} %get-tuple-element.19.refs_0_, bf16[256,1408]{1,0:T(8,128)(2,1)S(1)} %get-tuple-element.21.refs_1_, bf16[128,1408]{1,0:T(8,128)(2,1)S(1)} %broadcast_select_fusion.3.refs_2_, ...), custom_call_target="tpu_custom_call" | custom-call | flops 3300000000 | bytes 1048576 | tf_op jit(solution)/shard_map/gram/pallas_call | solution.py:77
  48.2 9.8 %all-to-all-start = ((f32[32,144,128]{2,1,0:T(8,128)}), f32[32,144,128]{2,1,0:T(8,128)S(1)}, u32[]{:S(2)}, u32[]{:S(2)}) async-start(f32[32,144,128]{2,1,0:T(8,128)} %bitcast.2), calls=%async_computation | async-start | bytes 4718592 | tf_op jit(solution)/shard_map/all_to_all | solution.py:343
  58.1 0.6 reduce_sum.19
  59.4 0.6 fusion.14
  61.3 28.4 %all-to-all-done = f32[32,144,128]{2,1,0:T(8,128)S(1)} async-done(((f32[32,144,128]{2,1,0:T(8,128)}), f32[32,144,128]{2,1,0:T(8,128)S(1)}, u32[]{:S(2)}, u32[]{:S(2)}) %all-to-all-start) | async-done | bytes 2359328 | tf_op jit(solution)/shard_map/all_to_all | solution.py:343
  89.9 0.7 add_convert_fusion
  90.7 26.9 %all_to_all.20 = bf16[32,144,128]{2,1,0:T(8,128)(2,1)S(1)} all-to-all(bf16[32,144,128]{2,1,0:T(8,128)(2,1)S(1)} %broadcast_in_dim.20), channel_id=1, replica_groups={{0,2,4,6,8,10,12,14,16,18,20,22,24,26,28,30,32,34,36,38,40,42,44,46,48,..., dimensions={0} | all-to-all | bytes 2359296 | tf_op jit(solution)/shard_map/all_to_all | solution.py:356
  117.7 4.2 %fusion = f32[1408,1408]{1,0:T(8,128)S(1)} fusion(bf16[256,1408]{1,0:T(8,128)(2,1)} %get-tuple-element.20, bf16[256,1408]{1,0:T(8,128)(2,1)} %get-tuple-element.18, bf16[256,1408]{1,0:T(8,128)(2,1)} %copy-done.6, bf16[256,1408]{1,0:T(8,128)(2,1)} %param.5), kind=kOutput, calls=%fused_computation.2 | convolution fusion | flops 2035810304 | bytes 10813440 | tf_op jit(solution)/shard_map/dot_general | solution.py:33
  121.9 0.6 pad.8
  122.4 2.4 dynamic-slice_bitcast_fusion
  124.9 5.0 %all-to-all-start.2 = ((f32[32,24,1408]{2,1,0:T(8,128)}), f32[32,24,1408]{2,1,0:T(8,128)}, u32[]{:S(2)}, u32[]{:S(2)}) async-start(f32[32,24,1408]{2,1,0:T(8,128)} %dynamic-slice_bitcast_fusion), calls=%async_computation.2 | async-start | bytes 8650752 | tf_op jit(solution)/shard_map/all_to_all | solution.py:372
  129.9 54.9 %cholesky.1 = (bf16[1408,1408]{1,0:T(8,128)(2,1)S(1)}, f32[1408,128]{1,0:T(8,128)S(1)}) custom-call(s32[1]{0:T(128)} %bitcast.1.core_ref, bf16[4608,128]{1,0:T(8,128)(2,1)S(1)} %bitcast.27, bf16[4608,128]{1,0:T(8,128)(2,1)S(1)} %collective-permute-done.9.other_ref), custom_call_target="tpu_custom_call" | custom-call | flops 62699999232 | bytes 1048576 | tf_op jit(solution)/shard_map/cholesky/pallas_call | solution.py:175
  184.8 1.9 copy-done.1
  186.7 4.2 %all-to-all-done.2.parts_ref = f32[32,24,1408]{2,1,0:T(8,128)} async-done(((f32[32,24,1408]{2,1,0:T(8,128)}), f32[32,24,1408]{2,1,0:T(8,128)}, u32[]{:S(2)}, u32[]{:S(2)}) %all-to-all-start.2) | async-done | bytes 4325408 | tf_op jit(solution)/shard_map/all_to_all | solution.py:372
  190.9 2.6 sum_parts.1
  193.5 8.1 %collective-permute-start.10 = (f32[24,1408]{1,0:T(8,128)S(1)}, f32[24,1408]{1,0:T(8,128)S(1)}, u32[]{:S(2)}, u32[]{:S(2)}) collective-permute-start(f32[24,1408]{1,0:T(8,128)S(1)} %sum_parts.1), channel_id=1, source_target_pairs={{0,64},{64,0},{1,65},{65,1},{2,66},{66,2},{3,67},{67,3},{4,68},{68... | collective-permute-start | bytes 405512 | tf_op jit(solution)/shard_map/ppermute | solution.py:374
  201.7 3.0 %collective-permute-done.10 = f32[24,1408]{1,0:T(8,128)S(1)} collective-permute-done((f32[24,1408]{1,0:T(8,128)S(1)}, f32[24,1408]{1,0:T(8,128)S(1)}, u32[]{:S(2)}, u32[]{:S(2)}) %collective-permute-start.10) | collective-permute-done | bytes 135200 | tf_op jit(solution)/shard_map/ppermute | solution.py:374
  204.7 5.9 %solve.2 = f32[24,1408]{1,0:T(8,128)S(1)} custom-call(f32[24,1408]{1,0:T(8,128)S(1)} %add_divide_fusion.rhs_ref, bf16[1408,1408]{1,0:T(8,128)(2,1)S(1)} %copy-done.2, f32[1408,128]{1,0:T(8,128)S(1)} %get-tuple-element.6.after_ref.inv_ref, f32[1408,128]{1,0:T(8,128)S(1)} %get-tuple-element.6.after_ref.inv_ref), custom_call_target="tpu_custom_call" | custom-call | flops 7699999744 | bytes 1048576 | tf_op jit(solution)/shard_map/solve/pallas_call | solution.py:224
  210.6 0.9 reshape.142
  211.5 0.6 copy.19
  212.0 0.6 gather_fusion
  212.9 3.9 %collective-permute-start.11 = (f32[64,22,24]{0,2,1:T(8,128)S(1)}, f32[64,22,24]{0,2,1:T(8,128)S(1)}, u32[]{:S(2)}, u32[]{:S(2)}) collective-permute-start(f32[64,22,24]{0,2,1:T(8,128)S(1)} %copy.20), channel_id=1, source_target_pairs={{0,64},{1,65},{2,66},{3,67},{4,68},{5,69},{6,70},{7,71},{8,72},{9,... | collective-permute-start | bytes 405512 | tf_op jit(solution)/shard_map/ppermute | solution.py:378
  216.9 7.7 %collective-permute-done.11 = f32[64,22,24]{0,2,1:T(8,128)S(1)} collective-permute-done((f32[64,22,24]{0,2,1:T(8,128)S(1)}, f32[64,22,24]{0,2,1:T(8,128)S(1)}, u32[]{:S(2)}, u32[]{:S(2)}) %collective-permute-start.11) | collective-permute-done | bytes 135200 | tf_op jit(solution)/shard_map/ppermute | solution.py:378
  224.9 1.2 reshape.154
  226.1 10.6 %all-to-all-start.3 = ((f32[64,1,528]{2,1,0:T(1,128)}), f32[64,1,528]{2,1,0:T(1,128)S(1)}, u32[]{:S(2)}, u32[]{:S(2)}) async-start(f32[64,1,528]{2,1,0:T(1,128)} %reshape.154), calls=%async_computation.3 | async-start | bytes 327680 | tf_op jit(solution)/shard_map/all_to_all | solution.py:379
  236.7 10.3 %all-to-all-done.3 = f32[64,1,528]{2,1,0:T(1,128)S(1)} async-done(((f32[64,1,528]{2,1,0:T(1,128)}), f32[64,1,528]{2,1,0:T(1,128)S(1)}, u32[]{:S(2)}, u32[]{:S(2)}) %all-to-all-start.3) | async-done | bytes 135200 | tf_op jit(solution)/shard_map/all_to_all | solution.py:379
  247.5 1.0 reduce
  249.4 2.3 copy-done
  251.7 1.2 rows.1
  252.9 2.0 collective-permute-start.8
  254.9 5.9 %solve.3 = f32[24,1408]{1,0:T(8,128)S(1)} custom-call(f32[24,1408]{1,0:T(8,128)S(1)} %pad.9.rhs_ref, bf16[1408,1408]{1,0:T(8,128)(2,1)S(1)} %copy-done.3, f32[1408,128]{1,0:T(8,128)S(1)} %get-tuple-element.6.after_ref.inv_ref, f32[22,1408]{1,0:T(8,128)S(1)} %bitcast.29), custom_call_target="tpu_custom_call" | custom-call | flops 7699999744 | bytes 1048576 | tf_op jit(solution)/shard_map/solve/pallas_call | solution.py:224
  260.8 1.3 collective-permute-start.12
  262.2 0.8 copy.23
  263.0 5.0 %collective-permute-done.12 = f32[22,1408]{1,0:T(8,128)S(1)} collective-permute-done((f32[22,1408]{1,0:T(8,128)S(1)}, f32[22,1408]{1,0:T(8,128)S(1)}, u32[]{:S(2)}, u32[]{:S(2)}) %collective-permute-start.12) | collective-permute-done | bytes 123936 | tf_op jit(solution)/shard_map/ppermute | solution.py:383
  268.0 0.7 select_bitcast_fusion
  (54 shorter events, 3.4 us)
Async XLA Ops:
  7.2 17.8 %copy-start.4 = (bf16[256,1408]{1,0:T(8,128)(2,1)S(1)}, bf16[256,1408]{1,0:T(8,128)(2,1)}, u32[]{:S(2)}) copy-start(bf16[256,1408]{1,0:T(8,128)(2,1)} %param.6) | copy-start | bytes 2162692
  7.2 17.8 %copy-start.5 = (bf16[256,1408]{1,0:T(8,128)(2,1)S(1)}, bf16[256,1408]{1,0:T(8,128)(2,1)}, u32[]{:S(2)}) copy-start(bf16[256,1408]{1,0:T(8,128)(2,1)} %param.5) | copy-start | bytes 2162692
  7.2 13.1 %copy-start.8 = (s32[128]{0:T(128)S(1)}, s32[128]{0:T(128)}, u32[]{:S(2)}) copy-start(s32[128]{0:T(128)} %param.7) | copy-start | bytes 1540
  7.2 33.5 %collective-permute-start.1 = (bf16[256,1408]{1,0:T(8,128)(2,1)}, bf16[256,1408]{1,0:T(8,128)(2,1)S(1)}, u32[]{:S(2)}, u32[]{:S(2)}) collective-permute-start(bf16[256,1408]{1,0:T(8,128)(2,1)} %param.6), channel_id=1, source_target_pairs={{0,1},{1,0},{2,3},{3,2},{4,5},{5,4},{6,7},{7,6},{8,9},{9,8},{10,11... | collective-permute-start | bytes 2162696 | tf_op jit(solution)/shard_map/ppermute | solution.py:324
  7.3 33.4 %collective-permute-start = (bf16[256,1408]{1,0:T(8,128)(2,1)}, bf16[256,1408]{1,0:T(8,128)(2,1)S(1)}, u32[]{:S(2)}, u32[]{:S(2)}) collective-permute-start(bf16[256,1408]{1,0:T(8,128)(2,1)} %param.5), channel_id=1, source_target_pairs={{0,1},{1,0},{2,3},{3,2},{4,5},{5,4},{6,7},{7,6},{8,9},{9,8},{10,11... | collective-permute-start | bytes 2162696 | tf_op jit(solution)/shard_map/ppermute | solution.py:323
  9.7 16.4 %collective-permute-start.2 = (bf16[128,1408]{1,0:T(8,128)(2,1)}, bf16[128,1408]{1,0:T(8,128)(2,1)}, u32[]{:S(2)}, u32[]{:S(2)}) collective-permute-start(bf16[128,1408]{1,0:T(8,128)(2,1)} %get-tuple-element.25), channel_id=1, source_target_pairs={{64,0},{65,1},{66,2},{67,3},{68,4},{69,5},{70,6},{71,7},{72,8},{73... | collective-permute-start | bytes 1081352 | tf_op jit(solution)/shard_map/ppermute | solution.py:317
  13.0 19.5 %collective-permute-start.3 = (bf16[128,1408]{1,0:T(8,128)(2,1)}, bf16[128,1408]{1,0:T(8,128)(2,1)}, u32[]{:S(2)}, u32[]{:S(2)}) collective-permute-start(bf16[128,1408]{1,0:T(8,128)(2,1)} %get-tuple-element.23), channel_id=1, source_target_pairs={{0,64},{1,65},{2,66},{3,67},{4,68},{5,69},{6,70},{7,71},{8,72},{9,... | collective-permute-start | bytes 1081352 | tf_op jit(solution)/shard_map/ppermute | solution.py:318
  19.0 14.6 %collective-permute-start.4 = (bf16[128,1408]{1,0:T(8,128)(2,1)S(1)}, bf16[128,1408]{1,0:T(8,128)(2,1)}, u32[]{:S(2)}, u32[]{:S(2)}) collective-permute-start(bf16[128,1408]{1,0:T(8,128)(2,1)S(1)} %get-tuple-element.24), channel_id=1, source_target_pairs={{64,32},{65,33},{66,34},{67,35},{68,36},{69,37},{70,38},{71,39},{7... | collective-permute-start | bytes 1081352 | tf_op jit(solution)/shard_map/ppermute | solution.py:317
  25.0 1.1 copy-start.7
  26.1 13.5 %collective-permute-start.5 = (bf16[128,1408]{1,0:T(8,128)(2,1)S(1)}, bf16[128,1408]{1,0:T(8,128)(2,1)S(1)}, u32[]{:S(2)}, u32[]{:S(2)}) collective-permute-start(bf16[128,1408]{1,0:T(8,128)(2,1)S(1)} %copy-done.7), channel_id=1, source_target_pairs={{0,96},{1,97},{2,98},{3,99},{4,100},{5,101},{6,102},{7,103},{8,104... | collective-permute-start | bytes 1081352 | tf_op jit(solution)/shard_map/ppermute | solution.py:318
  33.6 8.3 %collective-permute-start.6 = (bf16[128,1408]{1,0:T(8,128)(2,1)S(1)}, bf16[128,1408]{1,0:T(8,128)(2,1)S(1)}, u32[]{:S(2)}, u32[]{:S(2)}) collective-permute-start(bf16[128,1408]{1,0:T(8,128)(2,1)S(1)} %broadcast_select_fusion.3.refs_2_), channel_id=1, source_target_pairs={{0,1},{1,0},{2,3},{3,2},{4,5},{5,4},{6,7},{7,6},{8,9},{9,8},{10,11... | collective-permute-start | bytes 1081352 | tf_op jit(solution)/shard_map/ppermute | solution.py:327
  40.6 1.8 collective-permute-start.7
  40.7 7.5 %copy-start.6 = (bf16[256,1408]{1,0:T(8,128)(2,1)}, bf16[256,1408]{1,0:T(8,128)(2,1)S(1)}, u32[]{:S(2)}) copy-start(bf16[256,1408]{1,0:T(8,128)(2,1)S(1)} %collective-permute-done) | copy-start | bytes 2162692
  48.2 11.1 %copy-start.9 = (f32[2]{0:T(128)S(1)}, f32[2]{0:T(128)}, u32[]{:S(2)}) copy-start(f32[2]{0:T(128)} %param.9) | copy-start | bytes 28
  48.2 41.5 %all-to-all-start = ((f32[32,144,128]{2,1,0:T(8,128)}), f32[32,144,128]{2,1,0:T(8,128)S(1)}, u32[]{:S(2)}, u32[]{:S(2)}) async-start(f32[32,144,128]{2,1,0:T(8,128)} %bitcast.2), calls=%async_computation | async-start | bytes 4718592 | tf_op jit(solution)/shard_map/all_to_all | solution.py:343
  58.0 191.4 %all-gather.3.cloned.1.call-start = ((), (), s32[]{:S(2)}) async-start(), calls=%async_computation.4 | async-start | bytes 4792320 | tf_op jit(solution)/shard_map/all_gather | solution.py:362
  117.6 12.3 %collective-permute-start.9 = (bf16[4608,128]{1,0:T(8,128)(2,1)S(1)}, bf16[4608,128]{1,0:T(8,128)(2,1)S(1)}, u32[]{:S(2)}, u32[]{:S(2)}) collective-permute-start(bf16[4608,128]{1,0:T(8,128)(2,1)S(1)} %bitcast.26), channel_id=1, source_target_pairs={{0,1},{1,0},{2,3},{3,2},{4,5},{5,4},{6,7},{7,6},{8,9},{9,8},{10,11... | collective-permute-start | bytes 3538952 | tf_op jit(solution)/shard_map/ppermute | solution.py:358
  124.9 66.1 %all-to-all-start.2 = ((f32[32,24,1408]{2,1,0:T(8,128)}), f32[32,24,1408]{2,1,0:T(8,128)}, u32[]{:S(2)}, u32[]{:S(2)}) async-start(f32[32,24,1408]{2,1,0:T(8,128)} %dynamic-slice_bitcast_fusion), calls=%async_computation.2 | async-start | bytes 8650752 | tf_op jit(solution)/shard_map/all_to_all | solution.py:372
  184.8 1.9 copy-start.1
  190.9 10.7 %copy-start.10 = (s32[64]{0:T(128)S(1)}, s32[64]{0:T(128)}, u32[]{:S(2)}) copy-start(s32[64]{0:T(128)} %param.8) | copy-start | bytes 772
  190.9 13.7 %copy-start.2 = (bf16[1408,1408]{1,0:T(8,128)(2,1)S(1)}, bf16[1408,1408]{1,0:T(8,128)(2,1)}, u32[]{:S(2)}) copy-start(bf16[1408,1408]{1,0:T(8,128)(2,1)} %copy-done.1) | copy-start | bytes 11894788
  193.5 11.1 %collective-permute-start.10 = (f32[24,1408]{1,0:T(8,128)S(1)}, f32[24,1408]{1,0:T(8,128)S(1)}, u32[]{:S(2)}, u32[]{:S(2)}) collective-permute-start(f32[24,1408]{1,0:T(8,128)S(1)} %sum_parts.1), channel_id=1, source_target_pairs={{0,64},{64,0},{1,65},{65,1},{2,66},{66,2},{3,67},{67,3},{4,68},{68... | collective-permute-start | bytes 405512 | tf_op jit(solution)/shard_map/ppermute | solution.py:374
  212.9 11.7 %collective-permute-start.11 = (f32[64,22,24]{0,2,1:T(8,128)S(1)}, f32[64,22,24]{0,2,1:T(8,128)S(1)}, u32[]{:S(2)}, u32[]{:S(2)}) collective-permute-start(f32[64,22,24]{0,2,1:T(8,128)S(1)} %copy.20), channel_id=1, source_target_pairs={{0,64},{1,65},{2,66},{3,67},{4,68},{5,69},{6,70},{7,71},{8,72},{9,... | collective-permute-start | bytes 405512 | tf_op jit(solution)/shard_map/ppermute | solution.py:378
  226.1 20.8 %all-to-all-start.3 = ((f32[64,1,528]{2,1,0:T(1,128)}), f32[64,1,528]{2,1,0:T(1,128)S(1)}, u32[]{:S(2)}, u32[]{:S(2)}) async-start(f32[64,1,528]{2,1,0:T(1,128)} %reshape.154), calls=%async_computation.3 | async-start | bytes 327680 | tf_op jit(solution)/shard_map/all_to_all | solution.py:379
  249.4 2.3 copy-start
  251.7 3.1 %copy-start.3 = (bf16[1408,1408]{1,0:T(8,128)(2,1)S(1)}, bf16[1408,1408]{1,0:T(8,128)(2,1)}, u32[]{:S(2)}) copy-start(bf16[1408,1408]{1,0:T(8,128)(2,1)} %copy-done.1) | copy-start | bytes 11894788
  252.9 9.2 %collective-permute-start.8 = (f32[22,1408]{1,0:T(8,128)S(1)}, f32[22,1408]{1,0:T(8,128)S(1)}, u32[]{:S(2)}, u32[]{:S(2)}) collective-permute-start(f32[22,1408]{1,0:T(8,128)S(1)} %bitcast.28), channel_id=1, source_target_pairs={{0,64},{64,0},{1,65},{65,1},{2,66},{66,2},{3,67},{67,3},{4,68},{68... | collective-permute-start | bytes 371720 | tf_op jit(solution)/shard_map/ppermute | solution.py:365
  260.8 7.2 %collective-permute-start.12 = (f32[22,1408]{1,0:T(8,128)S(1)}, f32[22,1408]{1,0:T(8,128)S(1)}, u32[]{:S(2)}, u32[]{:S(2)}) collective-permute-start(f32[22,1408]{1,0:T(8,128)S(1)} %bitcast.31), channel_id=1, source_target_pairs={{64,0},{65,1},{66,2},{67,3},{68,4},{69,5},{70,6},{71,7},{72,8},{73... | collective-permute-start | bytes 371720 | tf_op jit(solution)/shard_map/ppermute | solution.py:383
Sparse Core Ops, SparseCore 0:
  117.7 119.7 all-gather.2

commit v3 on v2

--- a/solution.py
+++ b/solution.py
@@ -50,19 +50,33 @@
     return x.astype(BF16).astype(F32)
 
 
+def token(x):
+    return x[(0,) * (x.ndim - 2)][:8, :B]
+
+
 def tri(i, j):
     return i * (i + 1) // 2 + j
 
 
+def columns_of(group, cols, keep_ref=None):
+    parts = [ref[:, cols] if keep_ref is None else ref[:, cols] * keep_ref[k].astype(BF16) for k, ref in group]
+    return parts[0] if len(parts) == 1 else jnp.concatenate(parts, 0)
+
+
+def grouped(refs):
+    pairs = list(enumerate(refs))
+    return [pairs[0:1], pairs[1:2], pairs[2:4], pairs[4:6]]
+
+
 def gram_kernel(core_ref, keep_ref, *refs):
-    pieces, out_ref, tmp_ref = refs[:-2], refs[-2], refs[-1]
-    nb = pieces[0].shape[1] // B
+    pieces, out_ref, tmp_ref = grouped(refs[:6]), refs[6], refs[7]
+    nb = refs[0].shape[1] // B
     start = pl.multiple_of(core_ref[0] * HALF, HALF)
     for i in range(nb):
         wide = (i + 1) * B
         acc = None
-        for k, ref in enumerate(pieces):
-            p = dot(ref[:, i * B : wide] * keep_ref[k].astype(BF16), ref[:, :wide], TN)
+        for group in pieces:
+            p = dot(columns_of(group, slice(i * B, wide), keep_ref), columns_of(group, slice(0, wide)), TN)
             acc = p if acc is None else acc + p
         tmp_ref[:, :wide] = acc
         for j in range(i + 1):
@@ -81,9 +95,37 @@
         out_specs=VM,
         scratch_shapes=[pltpu.VMEM((B, width), F32)],
         compiler_params=params(24),
-        cost_estimate=cost(3),
+        cost_estimate=cost(4),
         name="gram",
     )(core, keeps, *pieces)
+
+
+def cross_kernel(core_ref, keep_ref, after_ref, *refs):
+    left, right, out_ref, tmp_ref = grouped(refs[:6]), grouped(refs[6:12]), refs[12], refs[13]
+    n = refs[0].shape[1]
+    for i in range(n // B):
+        acc = None
+        for lg, rg in zip(left, right):
+            p = dot(columns_of(lg, slice(i * B, (i + 1) * B), keep_ref), columns_of(rg, slice(0, n)), TN)
+            acc = p if acc is None else acc + p
+        tmp_ref[i * B : (i + 1) * B, :] = acc
+    tmp_ref[n:, :] = jnp.zeros((tmp_ref.shape[0] - n, n), F32)
+    for q in range(out_ref.shape[0]):
+        out_ref[q] = tmp_ref[pl.ds(pl.multiple_of((2 * q + core_ref[0]) * ROWS, 8), ROWS), :]
+
+
+def cross(core, keeps, after, left, right, chips):
+    width = left[0].shape[1]
+    return pl.pallas_call(
+        cross_kernel,
+        out_shape=jax.ShapeDtypeStruct((chips, ROWS, width), F32),
+        in_specs=[SM, SM, ANY] + [VM] * 12,
+        out_specs=VM,
+        scratch_shapes=[pltpu.VMEM((2 * chips * ROWS, width), F32)],
+        compiler_params=params(32),
+        cost_estimate=cost(8),
+        name="cross",
+    )(core, keeps, after, *left, *right)
 
 
 def factor_diag(block):
@@ -125,20 +167,21 @@
     return jnp.concatenate(inv, 0), jnp.concatenate(inv_r, 0)
 
 
+def block_of(mine_ref, other_ref, first, i, j):
+    t = tri(i, j) * HALF
+    mine = mine_ref[t : t + HALF, :].astype(F32)
+    other = other_ref[t : t + HALF, :].astype(F32)
+    return jnp.concatenate([jnp.where(first, mine, other), jnp.where(first, other, mine)], 0)
+
+
 def chol_kernel(core_ref, mine_ref, other_ref, low_ref, inv_ref, lo_ref, s_ref, w_ref):
     n = low_ref.shape[0]
     nb = n // B
     first = core_ref[0] == 0
 
-    def block(i, j):
-        t = tri(i, j) * HALF
-        mine = mine_ref[t : t + HALF, :].astype(F32)
-        other = other_ref[t : t + HALF, :].astype(F32)
-        return jnp.concatenate([jnp.where(first, mine, other), jnp.where(first, other, mine)], 0)
-
     def update(kk):
         r0 = kk * B
-        s = jnp.concatenate([block(i, kk) for i in range(kk, nb)], 0)
+        s = jnp.concatenate([block_of(mine_ref, other_ref, first, i, kk) for i in range(kk, nb)], 0)
         if kk:
             wts = jnp.concatenate([low_ref[r0 : r0 + B, :r0], lo_ref[r0 : r0 + B, :r0]], 0)
             pr = dot(low_ref[r0:, :r0], wts)
@@ -182,16 +225,17 @@
             pltpu.VMEM((n, B), F32),
             pltpu.VMEM((2 * B, B), BF16),
         ],
-        compiler_params=params(24),
+        compiler_params=params(16),
         cost_estimate=cost(57),
         name="cholesky",
     )(core, mine, other)
 
 
-def solve_kernel(rhs_ref, low_ref, inv_ref, after_ref, out_ref):
+def solve_kernel(total_ref, parts_ref, low_ref, inv_ref, after_ref, out_ref):
     n = low_ref.shape[0]
     nb = n // B
-    m = rhs_ref.shape[0]
+    m = parts_ref.shape[1]
+    total = total_ref[0]
 
     def stacked(x):
         return jnp.concatenate(split(x), 0)
@@ -199,7 +243,14 @@
     def fold(p):
         return p[:m] + p[m:]
 
-    acc = [rhs_ref[:, b * B : (b + 1) * B] for b in range(nb)]
+    def rhs(b):
+        cols = slice(b * B, (b + 1) * B)
+        s = parts_ref[0, :, cols]
+        for k in range(1, parts_ref.shape[0]):
+            s = s + parts_ref[k, :, cols]
+        return s / total
+
+    acc = [rhs(b) for b in range(nb)]
     for b in range(nb):
         r0, r1 = b * B, (b + 1) * B
         w = stacked(inv_ref[r0:r1, :])
@@ -220,16 +271,16 @@
             acc[c] = acc[c] - fold(dot(zs, low_ref[r0:r1, c * B : (c + 1) * B], NN))
 
 
-def solve(rhs, low, inv, after):
+def solve(total, parts, low, inv, after):
     return pl.pallas_call(
         solve_kernel,
-        out_shape=jax.ShapeDtypeStruct(rhs.shape, F32),
-        in_specs=[VM] * 3 + [ANY],
+        out_shape=jax.ShapeDtypeStruct(parts.shape[1:], F32),
+        in_specs=[SM] + [VM] * 3 + [ANY],
         out_specs=VM,
-        compiler_params=params(16),
+        compiler_params=params(14),
         cost_estimate=cost(7),
         name="solve",
-    )(rhs, low, inv, after)
+    )(total, parts, low, inv, after)
 
 
 def sum_kernel(parts_ref, after_ref, out_ref):
@@ -251,16 +302,13 @@
     )(parts, after)
 
 
-def rows_kernel(at_ref, all_ref, out_ref, s_ref):
+def rows_kernel(at_ref, core_ref, mine_ref, other_ref, diag_ref, out_ref, s_ref):
     m, n = out_ref.shape
     nb = n // B
-    per = all_ref.shape[1]
+    first = core_ref[0] == 0
     for i in range(nb):
         for j in range(i + 1):
-            t = tri(i, j) * HALF
-            blk = jnp.concatenate(
-                [all_ref[2 * (f // per) + c, f % per : f % per + SLAB, :]
-                 for c in range(2) for f in range(t, t + HALF, SLAB)], 0)
+            blk = block_of(mine_ref, other_ref, first, i, j)
             s_ref[i * B : (i + 1) * B, j * B : (j + 1) * B] = blk
             if i > j:
                 s_ref[j * B : (j + 1) * B, i * B : (i + 1) * B] = blk.T
@@ -270,20 +318,22 @@
     out = window[:m]
     for k in range(1, 8):
         out = jnp.where(shift == k, window[k : k + m], out)
-    out_ref[...] = out
-
-
-def rows_of(at, both, n, m):
+    ri = lax.broadcasted_iota(jnp.int32, (m, n), 0)
+    ci = lax.broadcasted_iota(jnp.int32, (m, n), 1)
+    out_ref[...] = jnp.where(ci == ri + at, diag_ref[...], out)
+
+
+def rows_of(at, core, mine, other, diag, n, m):
     return pl.pallas_call(
         rows_kernel,
         out_shape=jax.ShapeDtypeStruct((m, n), F32),
-        in_specs=[SM, VM],
+        in_specs=[SM, SM, VM, VM, VM],
         out_specs=VM,
         scratch_shapes=[pltpu.VMEM((n + 8, n), F32)],
-        compiler_params=params(24),
+        compiler_params=params(14),
         cost_estimate=cost(3),
         name="rows",
-    )(at, both)
+    )(at, core, mine, other, diag)
 
 
 def per_device(attn_out, out_grad, image_counts, column_owner, damping):
@@ -313,13 +363,12 @@
     both = ("grp", "dp")
     half = per_dev // 2
 
-    def cross(perm, rows):
-        to_a = lax.ppermute(attn_out[rows], both, [p for p in perm if p[1] < n_dp])
-        to_g = lax.ppermute(out_grad[rows], both, [p for p in perm if p[1] >= n_dp])
-        return jnp.where(is_a, to_a, to_g)
-
-    from_near = cross(near, slice(0, half))
-    from_far = cross(far, slice(half, None))
+    def to_a(perm):
+        return [p for p in perm if p[1] < n_dp]
+
+    other = jnp.where(is_a, out_grad, attn_out)
+    from_near = lax.ppermute(other[:half], both, near)
+    from_far = lax.ppermute(other[half:], both, far)
     act_c = lax.ppermute(attn_out, "dp", swap_core)
     grad_c = lax.ppermute(out_grad, "dp", swap_core)
     own = jnp.where(is_a, attn_out, out_grad)
@@ -339,9 +388,21 @@
 
     total = (TOK * jnp.sum(image_counts)).astype(F32)
     part = gram(core_arr, keeps, pieces, chips * per_chip)
-    part = part.reshape(chips, per_chip * SLAB, B)
-    got = lax.all_to_all(part, "dp", split_axis=0, concat_axis=0, tiled=True, axis_index_groups=same_core)
-    slabs = jnp.sum(got, axis=0) / total
+    got = lax.all_to_all(
+        part.reshape(chips, per_chip * SLAB, B), "dp", split_axis=0, concat_axis=0, tiled=True, axis_index_groups=same_core
+    )
+
+    out_grad_, _ = lax.optimization_barrier((out_grad, from_near))
+    grad_near = lax.ppermute(out_grad_[:half], both, to_a(near))
+    grad_far = lax.ppermute(out_grad_[half:], both, to_a(far))
+    grads = [
+        out_grad, grad_c, grad_near, grad_far,
+        lax.ppermute(grad_near, "dp", swap_core), lax.ppermute(grad_far, "dp", swap_core),
+    ]
+    acts = [attn_out, act_c, from_near, from_far, near_c, far_c]
+    part_w = cross(core_arr, keeps, token(part), grads, acts, chips)
+
+    slabs = sum_parts(got, token(part_w)) / total
 
     flat = chip * (per_chip * SLAB) + jnp.arange(per_chip * SLAB)
     t = flat // HALF
@@ -358,28 +419,30 @@
     theirs = lax.ppermute(mine, "dp", swap_core)
     low, inv = chol(core_arr, mine, theirs, width)
 
-    slabs, mine = lax.optimization_barrier((slabs, mine))
-    every = lax.all_gather(slabs, "dp", axis=0, tiled=False)
+    got_w = lax.all_to_all(part_w, "dp", split_axis=0, concat_axis=0, tiled=True, axis_index_groups=same_core)
+
+    squares = jnp.stack([attn_out, out_grad]).astype(F32)
+    squares = jnp.sum(squares * squares, axis=1) * keeps[0]
+    diags = lax.psum(squares, both) / total
     at = (dp_index * block).astype(jnp.int32)[None]
-    my_rows = rows_of(at, every, width, ROWS)[:block]
+    my_diag = jnp.where(is_a, diags[0], diags[1])[None]
+    my_rows = rows_of(at, core_arr, mine, theirs, my_diag, width, ROWS)[:block]
     their_rows = lax.ppermute(my_rows, "grp", swap_grp)
     factors = jnp.stack([jnp.where(is_a, my_rows, their_rows), jnp.where(is_a, their_rows, my_rows)])
 
-    kept = jnp.concatenate([out_grad * keeps[0].astype(BF16), grad_c * keeps[1].astype(BF16)])
-    part_w = dot(kept, jnp.concatenate([attn_out, act_c]), TN)
-    part_w = jnp.pad(part_w, ((0, n_dp * ROWS - width), (0, 0))).reshape(chips, 2, ROWS, width)
-    part_w = lax.dynamic_index_in_dim(part_w, core, 1, keepdims=False)
-    got_w = lax.all_to_all(part_w, "dp", split_axis=0, concat_axis=0, tiled=True, axis_index_groups=same_core)
-    rows_w = sum_parts(got_w, inv)
-    rows_w = (rows_w + lax.ppermute(rows_w, "grp", swap_grp)) / total
-
-    right = solve(rows_w, low, inv, inv)
-    routed = right.T.reshape(n_dp, block, ROWS)[column_owner]
-    routed = lax.ppermute(routed, "grp", [(0, 1)])
-    columns = lax.all_to_all(routed, "dp", split_axis=0, concat_axis=0, tiled=True)
+    right = solve(total[None], got_w, low, inv, token(inv))
+    order = column_owner.reshape(chips, 2).T.reshape(n_dp)
+    routed = right.T.reshape(n_dp, block, ROWS)[order].reshape(2, chips, block, ROWS)
+    mine_t = lax.dynamic_index_in_dim(routed, core, 0, keepdims=False)
+    other_t = lax.dynamic_index_in_dim(routed, 1 - core, 0, keepdims=False)
+    same = lax.ppermute(mine_t, both, [(d, n_dp + d) for d in range(n_dp)])
+    cross_t = lax.ppermute(other_t, both, [(d, n_dp + (d ^ 1)) for d in range(n_dp)])
+    is_first = core == 0
+    pair = jnp.concatenate([jnp.where(is_first, same, cross_t), jnp.where(is_first, cross_t, same)], axis=2)
+    columns = lax.all_to_all(pair, "dp", split_axis=0, concat_axis=0, tiled=True, axis_index_groups=same_core)
     columns = columns.transpose(1, 0, 2).reshape(block, n_dp * ROWS)[:, :width]
     columns = jnp.pad(columns, ((0, ROWS - block), (0, 0)))
-    left = solve(columns, low, inv, my_rows)[:block]
+    left = solve(jnp.ones((1,), F32), columns[None], low, inv, token(my_rows))[:block]
     back = lax.ppermute(left, "grp", [(1, 0)])
     preconditioned = jnp.where(is_a, back, left).T
     return (factors, preconditioned)

time: 276 us -> 311 us (1.13)
  blocking collectives: 26.9 us -> 71.1 us
  between operations: 20.3 us -> 6.96 us
  local copies, waits for them, and re-layouts: 18.6 us -> 29.4 us
  starting transfers between devices: 56.6 us -> 47.5 us
  Pallas kernels: 76.4 us -> 81.4 us
  matrix products: 4.21 us -> 0 us
  waiting for transfers between devices: 65.1 us -> 68.9 us
    psum x0 -> x1, blocking collectives: none -> 71.1 us  [per_device(): diags = lax.psum(squares, both) / total]
    ppermute x6 -> x8, waiting for transfers between devices: 16.6 us -> 52.5 us  [the longest x1 32.4 us: per_device(): grad_near = lax.ppermute(out_grad_[:half], both, to_a(near))]
    all_to_all x2 -> x3, waiting for transfers between devices: 38.7 us -> 10.1 us  [the longest x1 10.1 us: per_device(): lax.all_to_all(pair, 'dp', split_axis=0, concat_axis=0, tiled=True, axis_...]
    all_to_all x1 -> x0, blocking collectives: 26.9 us -> none  [per_device(): lax.all_to_all(spread, 'dp', split_axis=0, concat_axis=0, tiled=True, axi...]
    ppermute x6 -> x8, starting transfers between devices: 27.1 us -> 13.2 us  [the longest x1 5.65 us: per_device(): same = lax.ppermute(mine_t, both, [(d, n_dp + d) for d in range(n_dp)])]
    unnamed x25 -> x41, local copies, waits for them, and re-layouts: 6.52 us -> 18.2 us
    pallas_call x2 -> x3, Pallas kernels: 11.9 us -> 20.5 us  [the longest x2 14.1 us: solve(): pl.pallas_call(solve_kernel, out_shape=jax.ShapeDtypeStruct(parts.shape[1...]
    all_to_all x2 -> x3, starting transfers between devices: 20.4 us -> 26.7 us  [the longest x1 9.54 us: per_device(): lax.all_to_all(part.reshape(chips, per_chip * SLAB, B), 'dp', split_axis=...]
  transfers between devices with their start and end apart: 17 -> 19, of which waited for: 8 -> 9; matrix products, arithmetic and copies ran while one was open for 9% -> 3% of each run, Pallas kernels for 25% -> 20%
where the time goes in v3:
time: 311 us; the launch traced here: 310 us
  Pallas kernels  81.4 us (26%)
  blocking collectives  71.1 us (23%)
  waiting for transfers between devices  68.9 us (22%)
  starting transfers between devices  47.5 us (15%)
  local copies, waits for them, and re-layouts  29.4 us (9%)
  between operations  6.96 us (2%)
  other arithmetic  4.61 us (1%)
    psum x1, blocking collectives, per_device(): diags = lax.psum(squares, both) / total  71.1 us
    pallas_call x1, Pallas kernels, chol(): pl.pallas_call(chol_kernel, out_shape=(jax.ShapeDtypeStruct((n, n), BF16)...  55.1 us
    ppermute x1, waiting for transfers between devices, per_device(): grad_near = lax.ppermute(out_grad_[:half], both, to_a(near))  32.4 us
    unnamed x41, local copies, waits for them, and re-layouts  18.2 us
    pallas_call x2, Pallas kernels, solve(): pl.pallas_call(solve_kernel, out_shape=jax.ShapeDtypeStruct(parts.shape[1...  14.1 us
    all_to_all x1, waiting for transfers between devices, per_device(): lax.all_to_all(pair, 'dp', split_axis=0, concat_axis=0, tiled=True, axis_...  10.1 us
    all_to_all x1, starting transfers between devices, per_device(): lax.all_to_all(part.reshape(chips, per_chip * SLAB, B), 'dp', split_axis=...  9.54 us
    all_to_all x1, starting transfers between devices, per_device(): lax.all_to_all(spread, 'dp', split_axis=0, concat_axis=0, tiled=True, axi...  9.33 us
  transfers between devices with their start and end apart: 19, of which 9 were waited for; matrix products, arithmetic and copies ran while one was open for 3% of the time, Pallas kernels for 20%

profile of v3, /device:TPU:0, one launch (start us, length us, event | category | flops | bytes accessed | tf_op | source)
XLA Modules:
  0.0 310.0 jit_solution(8906116699122778615)
XLA Ops:
  1.2 1.5 broadcast_select_fusion
  3.5 1.6 collective-permute-start.2
  5.1 2.1 collective-permute-start.3
  11.7 2.2 collective-permute-done.2.refs_2_.refs_8_
  13.9 2.7 collective-permute-done.3.refs_3_.refs_9_
  16.7 1.5 collective-permute-done.5.refs_5_.refs_11_
  18.3 3.3 %gram.1 = f32[4608,128]{1,0:T(8,128)S(1)} custom-call(s32[1]{0:T(128)} %bitcast.1.core_ref, f32[6]{0:T(128)S(1)} %stack.27.keep_ref, bf16[256,1408]{1,0:T(8,128)(2,1)S(1)} %get-tuple-element.15.refs_0_, bf16[256,1408]{1,0:T(8,128)(2,1)S(1)} %broadcast_select_fusion.1.refs_1_, bf16[128,1408]{1,0:T(8,128)(2,1)S(1)} %collective-permute-done.2.refs_2_.refs_8_, ...), custom_call_target="tpu_custom_call" | custom-call | flops 4400000000 | bytes 1048576 | tf_op jit(solution)/shard_map/gram/pallas_call | solution.py:91
  21.6 1.5 copy-done.3
  23.1 9.5 %all-to-all-start = ((f32[32,144,128]{2,1,0:T(8,128)}), f32[32,144,128]{2,1,0:T(8,128)}, u32[]{:S(2)}, u32[]{:S(2)}) async-start(f32[32,144,128]{2,1,0:T(8,128)} %bitcast.36), calls=%async_computation | async-start | bytes 4718592 | tf_op jit(solution)/shard_map/all_to_all | solution.py:391
  32.7 1.3 collective-permute-start.6
  34.0 1.3 collective-permute-start.7
  35.3 32.4 %collective-permute-done.6.refs_2_ = bf16[128,1408]{1,0:T(8,128)(2,1)} collective-permute-done((bf16[128,1408]{1,0:T(8,128)(2,1)S(1)}, bf16[128,1408]{1,0:T(8,128)(2,1)}, u32[]{:S(2)}, u32[]{:S(2)}) %collective-permute-start.6) | collective-permute-done | bytes 360480 | tf_op jit(solution)/shard_map/ppermute | solution.py:396
  67.8 1.7 collective-permute-done.7.refs_3_
  73.5 1.0 copy-done.8
  74.5 1.0 copy-done.10
  75.5 1.0 copy-done.12
  76.4 6.3 %cross.1 = f32[32,24,1408]{2,1,0:T(8,128)S(1)} custom-call(s32[1]{0:T(128)} %bitcast.1.core_ref, f32[6]{0:T(128)S(1)} %stack.27.keep_ref, f32[8,128]{1,0:T(8,128)S(1)} %slice.69.after_ref, bf16[256,1408]{1,0:T(8,128)(2,1)S(1)} %copy-done, bf16[256,1408]{1,0:T(8,128)(2,1)S(1)} %collective-permute-done.1.refs_1_, ...), custom_call_target="tpu_custom_call" | custom-call | flops 8800000000 | bytes 1048576 | tf_op jit(solution)/shard_map/cross/pallas_call | solution.py:119
  82.8 2.0 copy-done.1
  84.8 1.8 sum_parts.1
  86.7 1.2 broadcast_in_dim.12
  87.9 9.3 %all-to-all-start.1 = ((bf16[32,144,128]{2,1,0:T(8,128)(2,1)}), bf16[32,144,128]{2,1,0:T(8,128)(2,1)S(1)}, u32[]{:S(2)}, u32[]{:S(2)}) async-start(bf16[32,144,128]{2,1,0:T(8,128)(2,1)} %broadcast_in_dim.12), calls=%async_computation.1 | async-start | bytes 2359296 | tf_op jit(solution)/shard_map/all_to_all | solution.py:417
  97.9 71.1 %psum.7 = f32[2,1408]{1,0:T(2,128)S(1)} all-reduce(f32[2,1408]{1,0:T(2,128)S(1)} %broadcast_multiply_fusion), channel_id=1, replica_groups=mesh['grp'=2,'dp'=64] {'grp','dp'}, use_global_device_ids=true, to_apply=%region_2.3 | all-reduce | flops 2816 | bytes 22528 | tf_op jit(solution)/shard_map/psum | solution.py:426
  169.1 5.6 %all-to-all-start.2 = ((f32[32,24,1408]{2,1,0:T(8,128)}), f32[32,24,1408]{2,1,0:T(8,128)}, u32[]{:S(2)}, u32[]{:S(2)}) async-start(f32[32,24,1408]{2,1,0:T(8,128)} %copy-done.1), calls=%async_computation.2 | async-start | bytes 8650752 | tf_op jit(solution)/shard_map/all_to_all | solution.py:422
  174.7 1.0 copy-done.4
  175.7 1.3 copy-done.5
  177.0 55.1 %cholesky.1 = (bf16[1408,1408]{1,0:T(8,128)(2,1)S(1)}, f32[1408,128]{1,0:T(8,128)S(1)}) custom-call(s32[1]{0:T(128)} %bitcast.1.core_ref, bf16[4608,128]{1,0:T(8,128)(2,1)S(1)} %bitcast.38, bf16[4608,128]{1,0:T(8,128)(2,1)S(1)} %copy-done.5), custom_call_target="tpu_custom_call" | custom-call | flops 62699999232 | bytes 1048576 | tf_op jit(solution)/shard_map/cholesky/pallas_call | solution.py:218
  232.1 1.9 copy-done.13
  234.0 2.1 copy-done.14
  236.2 8.2 %solve.2 = f32[24,1408]{1,0:T(8,128)S(1)} custom-call(f32[1]{0:T(128)} %bitcast.12.total_ref, f32[32,24,1408]{2,1,0:T(8,128)} %all-to-all-done.2.parts_ref, bf16[1408,1408]{1,0:T(8,128)(2,1)S(1)} %copy-done.14, f32[1408,128]{1,0:T(8,128)S(1)} %get-tuple-element.7.inv_ref, f32[8,128]{1,0:T(8,128)S(1)} %slice.61.after_ref), custom_call_target="tpu_custom_call" | custom-call | flops 7699999744 | bytes 1048576 | tf_op jit(solution)/shard_map/solve/pallas_call | solution.py:275
  244.4 1.8 reshape.136
  246.1 1.6 copy.17
  247.8 1.5 gather_fusion
  249.3 1.2 dynamic-slice_bitcast_fusion.1
  250.4 5.6 %collective-permute-start.12 = (f32[32,22,24]{2,1,0:T(8,128)S(1)}, f32[32,22,24]{2,1,0:T(8,128)S(1)}, u32[]{:S(2)}, u32[]{:S(2)}) collective-permute-start(f32[32,22,24]{2,1,0:T(8,128)S(1)} %get-tuple-element.18), channel_id=1, source_target_pairs={{0,64},{1,65},{2,66},{3,67},{4,68},{5,69},{6,70},{7,71},{8,72},{9,... | collective-permute-start | bytes 202760 | tf_op jit(solution)/shard_map/ppermute | solution.py:438
  256.1 1.3 collective-permute-start.13
  257.4 1.3 copy-done.6
  258.7 0.8 rows.1
  259.6 6.0 %collective-permute-done.12 = f32[32,22,24]{2,1,0:T(8,128)S(1)} collective-permute-done((f32[32,22,24]{2,1,0:T(8,128)S(1)}, f32[32,22,24]{2,1,0:T(8,128)S(1)}, u32[]{:S(2)}, u32[]{:S(2)}) %collective-permute-start.12) | collective-permute-done | bytes 67616 | tf_op jit(solution)/shard_map/ppermute | solution.py:438
  265.6 7.5 %collective-permute-done.13 = f32[32,22,24]{2,1,0:T(8,128)S(1)} collective-permute-done((f32[32,22,24]{2,1,0:T(8,128)S(1)}, f32[32,22,24]{2,1,0:T(8,128)S(1)}, u32[]{:S(2)}, u32[]{:S(2)}) %collective-permute-start.13) | collective-permute-done | bytes 67616 | tf_op jit(solution)/shard_map/ppermute | solution.py:439
  273.3 1.0 reshape.149
  274.4 7.8 %all-to-all-start.3 = ((f32[32,1,1056]{2,1,0:T(1,128)}), f32[32,1,1056]{2,1,0:T(1,128)S(1)}, u32[]{:S(2)}, u32[]{:S(2)}) async-start(f32[32,1,1056]{2,1,0:T(1,128)} %reshape.149), calls=%async_computation.3 | async-start | bytes 294912 | tf_op jit(solution)/shard_map/all_to_all | solution.py:442
  282.2 10.1 %all-to-all-done.3 = f32[32,1,1056]{2,1,0:T(1,128)S(1)} async-done(((f32[32,1,1056]{2,1,0:T(1,128)}), f32[32,1,1056]{2,1,0:T(1,128)S(1)}, u32[]{:S(2)}, u32[]{:S(2)}) %all-to-all-start.3) | async-done | bytes 135200 | tf_op jit(solution)/shard_map/all_to_all | solution.py:442
  292.8 1.0 reduce
  294.3 2.1 copy-done.15
  296.4 5.9 %solve.3 = f32[24,1408]{1,0:T(8,128)S(1)} custom-call(f32[1]{0:T(128)} %constant.126.clone.1.total_ref, f32[1,24,1408]{2,1,0:T(8,128)S(1)} %pad_bitcast_fusion.parts_ref, bf16[1408,1408]{1,0:T(8,128)(2,1)S(1)} %copy-done.15, f32[1408,128]{1,0:T(8,128)S(1)} %get-tuple-element.7.inv_ref, f32[8,128]{1,0:T(8,128)S(1)} %slice.76.after_ref), custom_call_target="tpu_custom_call" | custom-call | flops 7699999744 | bytes 1048576 | tf_op jit(solution)/shard_map/solve/pallas_call | solution.py:275
  302.4 1.3 collective-permute-start.14
  303.7 0.8 copy.19
  304.5 4.8 %collective-permute-done.14 = f32[22,1408]{1,0:T(8,128)S(1)} collective-permute-done((f32[22,1408]{1,0:T(8,128)S(1)}, f32[22,1408]{1,0:T(8,128)S(1)}, u32[]{:S(2)}, u32[]{:S(2)}) %collective-permute-start.14) | collective-permute-done | bytes 123936 | tf_op jit(solution)/shard_map/ppermute | solution.py:446
  (80 shorter events, 7.1 us)
Async XLA Ops:
  0.6 6.5 %copy-start.16 = (s32[128]{0:T(128)S(1)}, s32[128]{0:T(128)}, u32[]{:S(2)}) copy-start(s32[128]{0:T(128)} %param.7) | copy-start | bytes 1540
  0.6 16.0 %collective-permute-start = (bf16[256,1408]{1,0:T(8,128)(2,1)}, bf16[256,1408]{1,0:T(8,128)(2,1)S(1)}, u32[]{:S(2)}, u32[]{:S(2)}) collective-permute-start(bf16[256,1408]{1,0:T(8,128)(2,1)} %refs_6_.1), channel_id=1, source_target_pairs={{0,1},{1,0},{2,3},{3,2},{4,5},{5,4},{6,7},{7,6},{8,9},{9,8},{10,11... | collective-permute-start | bytes 2162696 | tf_op jit(solution)/shard_map/ppermute | solution.py:372
  0.7 15.9 %collective-permute-start.1 = (bf16[256,1408]{1,0:T(8,128)(2,1)}, bf16[256,1408]{1,0:T(8,128)(2,1)S(1)}, u32[]{:S(2)}, u32[]{:S(2)}) collective-permute-start(bf16[256,1408]{1,0:T(8,128)(2,1)} %refs_0_.1), channel_id=1, source_target_pairs={{0,1},{1,0},{2,3},{3,2},{4,5},{5,4},{6,7},{7,6},{8,9},{9,8},{10,11... | collective-permute-start | bytes 2162696 | tf_op jit(solution)/shard_map/ppermute | solution.py:373
  3.5 10.4 %collective-permute-start.2 = (bf16[128,1408]{1,0:T(8,128)(2,1)S(1)}, bf16[128,1408]{1,0:T(8,128)(2,1)S(1)}, u32[]{:S(2)}, u32[]{:S(2)}) collective-permute-start(bf16[128,1408]{1,0:T(8,128)(2,1)S(1)} %get-tuple-element.23), channel_id=1, source_target_pairs={{0,64},{1,65},{2,66},{3,67},{4,68},{5,69},{6,70},{7,71},{8,72},{9,... | collective-permute-start | bytes 1081352 | tf_op jit(solution)/shard_map/ppermute | solution.py:370
  5.1 11.6 %collective-permute-start.3 = (bf16[128,1408]{1,0:T(8,128)(2,1)}, bf16[128,1408]{1,0:T(8,128)(2,1)S(1)}, u32[]{:S(2)}, u32[]{:S(2)}) collective-permute-start(bf16[128,1408]{1,0:T(8,128)(2,1)} %get-tuple-element.22), channel_id=1, source_target_pairs={{0,96},{1,97},{2,98},{3,99},{4,100},{5,101},{6,102},{7,103},{8,104... | collective-permute-start | bytes 1081352 | tf_op jit(solution)/shard_map/ppermute | solution.py:371
  13.9 2.8 collective-permute-start.4
  16.6 5.0 %copy-start.7 = (bf16[128,1408]{1,0:T(8,128)(2,1)}, bf16[128,1408]{1,0:T(8,128)(2,1)S(1)}, u32[]{:S(2)}) copy-start(bf16[128,1408]{1,0:T(8,128)(2,1)S(1)} %collective-permute-done.3.refs_3_.refs_9_) | copy-start | bytes 1081348
  16.6 1.7 collective-permute-start.5
  16.7 4.9 %copy-start.9 = (bf16[128,1408]{1,0:T(8,128)(2,1)}, bf16[128,1408]{1,0:T(8,128)(2,1)S(1)}, u32[]{:S(2)}) copy-start(bf16[128,1408]{1,0:T(8,128)(2,1)S(1)} %collective-permute-done.4.refs_4_.refs_10_) | copy-start | bytes 1081348
  18.3 3.3 %copy-start.11 = (bf16[128,1408]{1,0:T(8,128)(2,1)}, bf16[128,1408]{1,0:T(8,128)(2,1)S(1)}, u32[]{:S(2)}) copy-start(bf16[128,1408]{1,0:T(8,128)(2,1)S(1)} %collective-permute-done.5.refs_5_.refs_11_) | copy-start | bytes 1081348
  21.6 1.5 copy-start.3
  23.1 9.6 %copy-start = (bf16[256,1408]{1,0:T(8,128)(2,1)S(1)}, bf16[256,1408]{1,0:T(8,128)(2,1)}, u32[]{:S(2)}) copy-start(bf16[256,1408]{1,0:T(8,128)(2,1)} %refs_0_.1) | copy-start | bytes 2162692
  23.1 47.7 %copy-start.17 = (f32[2]{0:T(128)S(1)}, f32[2]{0:T(128)}, u32[]{:S(2)}) copy-start(f32[2]{0:T(128)} %param.9) | copy-start | bytes 28
  23.1 50.4 %copy-start.2 = (bf16[256,1408]{1,0:T(8,128)(2,1)S(1)}, bf16[256,1408]{1,0:T(8,128)(2,1)}, u32[]{:S(2)}) copy-start(bf16[256,1408]{1,0:T(8,128)(2,1)} %refs_6_.1) | copy-start | bytes 2162692
  23.1 61.7 %all-to-all-start = ((f32[32,144,128]{2,1,0:T(8,128)}), f32[32,144,128]{2,1,0:T(8,128)}, u32[]{:S(2)}, u32[]{:S(2)}) async-start(f32[32,144,128]{2,1,0:T(8,128)} %bitcast.36), calls=%async_computation | async-start | bytes 4718592 | tf_op jit(solution)/shard_map/all_to_all | solution.py:391
  32.7 35.0 %collective-permute-start.6 = (bf16[128,1408]{1,0:T(8,128)(2,1)S(1)}, bf16[128,1408]{1,0:T(8,128)(2,1)}, u32[]{:S(2)}, u32[]{:S(2)}) collective-permute-start(bf16[128,1408]{1,0:T(8,128)(2,1)S(1)} %get-tuple-element.21), channel_id=1, source_target_pairs={{64,0},{65,1},{66,2},{67,3},{68,4},{69,5},{70,6},{71,7},{72,8},{73... | collective-permute-start | bytes 1081352 | tf_op jit(solution)/shard_map/ppermute | solution.py:396
  34.0 35.4 %collective-permute-start.7 = (bf16[128,1408]{1,0:T(8,128)(2,1)S(1)}, bf16[128,1408]{1,0:T(8,128)(2,1)}, u32[]{:S(2)}, u32[]{:S(2)}) collective-permute-start(bf16[128,1408]{1,0:T(8,128)(2,1)S(1)} %get-tuple-element.20), channel_id=1, source_target_pairs={{64,32},{65,33},{66,34},{67,35},{68,36},{69,37},{70,38},{71,39},{7... | collective-permute-start | bytes 1081352 | tf_op jit(solution)/shard_map/ppermute | solution.py:397
  67.8 5.7 %collective-permute-start.8 = (bf16[128,1408]{1,0:T(8,128)(2,1)}, bf16[128,1408]{1,0:T(8,128)(2,1)}, u32[]{:S(2)}, u32[]{:S(2)}) collective-permute-start(bf16[128,1408]{1,0:T(8,128)(2,1)} %collective-permute-done.6.refs_2_), channel_id=1, source_target_pairs={{0,1},{1,0},{2,3},{3,2},{4,5},{5,4},{6,7},{7,6},{8,9},{9,8},{10,11... | collective-permute-start | bytes 1081352 | tf_op jit(solution)/shard_map/ppermute | solution.py:400
  69.5 4.0 %collective-permute-start.9 = (bf16[128,1408]{1,0:T(8,128)(2,1)}, bf16[128,1408]{1,0:T(8,128)(2,1)}, u32[]{:S(2)}, u32[]{:S(2)}) collective-permute-start(bf16[128,1408]{1,0:T(8,128)(2,1)} %collective-permute-done.7.refs_3_), channel_id=1, source_target_pairs={{0,1},{1,0},{2,3},{3,2},{4,5},{5,4},{6,7},{7,6},{8,9},{9,8},{10,11... | collective-permute-start | bytes 1081352 | tf_op jit(solution)/shard_map/ppermute | solution.py:400
  73.5 1.0 copy-start.8
  74.5 1.0 copy-start.10
  75.5 1.0 copy-start.12
  82.8 2.0 copy-start.1
  86.6 10.7 %copy-start.18 = (s32[64]{0:T(128)S(1)}, s32[64]{0:T(128)}, u32[]{:S(2)}) copy-start(s32[64]{0:T(128)} %param.8) | copy-start | bytes 772
  87.9 81.1 %all-to-all-start.1 = ((bf16[32,144,128]{2,1,0:T(8,128)(2,1)}), bf16[32,144,128]{2,1,0:T(8,128)(2,1)S(1)}, u32[]{:S(2)}, u32[]{:S(2)}) async-start(bf16[32,144,128]{2,1,0:T(8,128)(2,1)} %broadcast_in_dim.12), calls=%async_computation.1 | async-start | bytes 2359296 | tf_op jit(solution)/shard_map/all_to_all | solution.py:417
  169.0 5.7 %collective-permute-start.10 = (bf16[4608,128]{1,0:T(8,128)(2,1)S(1)}, bf16[4608,128]{1,0:T(8,128)(2,1)S(1)}, u32[]{:S(2)}, u32[]{:S(2)}) collective-permute-start(bf16[4608,128]{1,0:T(8,128)(2,1)S(1)} %bitcast.37), channel_id=1, source_target_pairs={{0,1},{1,0},{2,3},{3,2},{4,5},{5,4},{6,7},{7,6},{8,9},{9,8},{10,11... | collective-permute-start | bytes 3538952 | tf_op jit(solution)/shard_map/ppermute | solution.py:419
  169.1 65.0 %all-to-all-start.2 = ((f32[32,24,1408]{2,1,0:T(8,128)}), f32[32,24,1408]{2,1,0:T(8,128)}, u32[]{:S(2)}, u32[]{:S(2)}) async-start(f32[32,24,1408]{2,1,0:T(8,128)} %copy-done.1), calls=%async_computation.2 | async-start | bytes 8650752 | tf_op jit(solution)/shard_map/all_to_all | solution.py:422
  174.7 1.0 copy-start.4
  175.7 1.3 copy-start.5
  232.1 1.9 copy-start.13
  234.0 2.1 copy-start.14
  250.4 15.2 %collective-permute-start.12 = (f32[32,22,24]{2,1,0:T(8,128)S(1)}, f32[32,22,24]{2,1,0:T(8,128)S(1)}, u32[]{:S(2)}, u32[]{:S(2)}) collective-permute-start(f32[32,22,24]{2,1,0:T(8,128)S(1)} %get-tuple-element.18), channel_id=1, source_target_pairs={{0,64},{1,65},{2,66},{3,67},{4,68},{5,69},{6,70},{7,71},{8,72},{9,... | collective-permute-start | bytes 202760 | tf_op jit(solution)/shard_map/ppermute | solution.py:438
  256.1 17.0 %collective-permute-start.13 = (f32[32,22,24]{2,1,0:T(8,128)S(1)}, f32[32,22,24]{2,1,0:T(8,128)S(1)}, u32[]{:S(2)}, u32[]{:S(2)}) collective-permute-start(f32[32,22,24]{2,1,0:T(8,128)S(1)} %get-tuple-element.19), channel_id=1, source_target_pairs={{0,65},{1,64},{2,67},{3,66},{4,69},{5,68},{6,71},{7,70},{8,73},{9,... | collective-permute-start | bytes 202760 | tf_op jit(solution)/shard_map/ppermute | solution.py:439
  257.4 1.3 copy-start.6
  259.5 22.7 %collective-permute-start.11 = (f32[22,1408]{1,0:T(8,128)S(1)}, f32[22,1408]{1,0:T(8,128)S(1)}, u32[]{:S(2)}, u32[]{:S(2)}) collective-permute-start(f32[22,1408]{1,0:T(8,128)S(1)} %bitcast.40), channel_id=1, source_target_pairs={{0,64},{64,0},{1,65},{65,1},{2,66},{66,2},{3,67},{67,3},{4,68},{68... | collective-permute-start | bytes 371720 | tf_op jit(solution)/shard_map/ppermute | solution.py:430
  274.4 17.9 %all-to-all-start.3 = ((f32[32,1,1056]{2,1,0:T(1,128)}), f32[32,1,1056]{2,1,0:T(1,128)S(1)}, u32[]{:S(2)}, u32[]{:S(2)}) async-start(f32[32,1,1056]{2,1,0:T(1,128)} %reshape.149), calls=%async_computation.3 | async-start | bytes 294912 | tf_op jit(solution)/shard_map/all_to_all | solution.py:442
  294.3 2.1 copy-start.15
  302.4 6.9 %collective-permute-start.14 = (f32[22,1408]{1,0:T(8,128)S(1)}, f32[22,1408]{1,0:T(8,128)S(1)}, u32[]{:S(2)}, u32[]{:S(2)}) collective-permute-start(f32[22,1408]{1,0:T(8,128)S(1)} %bitcast.42), channel_id=1, source_target_pairs={{64,0},{65,1},{66,2},{67,3},{68,4},{69,5},{70,6},{71,7},{72,8},{73... | collective-permute-start | bytes 371720 | tf_op jit(solution)/shard_map/ppermute | solution.py:446

commit v4 on v3

--- a/solution.py
+++ b/solution.py
@@ -1,3 +1,5 @@
+import functools
+
 import jax
 import jax.numpy as jnp
 from jax import lax
@@ -18,6 +20,7 @@
 VM = pl.BlockSpec(memory_space=pltpu.VMEM)
 ANY = pl.BlockSpec(memory_space=pl.ANY)
 SM = pl.BlockSpec(memory_space=pltpu.SMEM)
+TOKEN = jax.ShapeDtypeStruct((8, B), F32)
 MIB = 1024 * 1024
 
 
@@ -50,33 +53,32 @@
     return x.astype(BF16).astype(F32)
 
 
-def token(x):
-    return x[(0,) * (x.ndim - 2)][:8, :B]
-
-
 def tri(i, j):
     return i * (i + 1) // 2 + j
 
 
-def columns_of(group, cols, keep_ref=None):
-    parts = [ref[:, cols] if keep_ref is None else ref[:, cols] * keep_ref[k].astype(BF16) for k, ref in group]
+def pieces_of(refs):
+    own, mate, near, far, near_mate, far_mate = refs
+    return [[(0, own)], [(1, mate)], [(2, near), (3, far)], [(4, near_mate), (5, far_mate)]]
+
+
+def columns_of(group, which, cols, keep_ref=None):
+    parts = [
+        ref[which, :, cols] if keep_ref is None else ref[which, :, cols] * keep_ref[k].astype(BF16) for k, ref in group
+    ]
     return parts[0] if len(parts) == 1 else jnp.concatenate(parts, 0)
 
 
-def grouped(refs):
-    pairs = list(enumerate(refs))
-    return [pairs[0:1], pairs[1:2], pairs[2:4], pairs[4:6]]
-
-
 def gram_kernel(core_ref, keep_ref, *refs):
-    pieces, out_ref, tmp_ref = grouped(refs[:6]), refs[6], refs[7]
-    nb = refs[0].shape[1] // B
+    pieces, (out_ref, token_ref, tmp_ref) = pieces_of(refs[:6]), refs[6:]
+    token_ref[...] = jnp.zeros_like(token_ref)
+    nb = refs[0].shape[2] // B
     start = pl.multiple_of(core_ref[0] * HALF, HALF)
     for i in range(nb):
         wide = (i + 1) * B
         acc = None
         for group in pieces:
-            p = dot(columns_of(group, slice(i * B, wide), keep_ref), columns_of(group, slice(0, wide)), TN)
+            p = dot(columns_of(group, 0, slice(i * B, wide), keep_ref), columns_of(group, 0, slice(0, wide)), TN)
             acc = p if acc is None else acc + p
         tmp_ref[:, :wide] = acc
         for j in range(i + 1):
@@ -87,63 +89,67 @@
 
 
 def gram(core, keeps, pieces, slots):
-    width = pieces[0].shape[1]
+    width = pieces[0].shape[2]
     return pl.pallas_call(
         gram_kernel,
-        out_shape=jax.ShapeDtypeStruct((slots * SLAB, B), F32),
-        in_specs=[SM, SM] + [VM] * len(pieces),
-        out_specs=VM,
+        out_shape=(jax.ShapeDtypeStruct((slots * SLAB, B), F32), TOKEN),
+        in_specs=[SM, SM] + [VM] * 6,
+        out_specs=(VM, VM),
         scratch_shapes=[pltpu.VMEM((B, width), F32)],
-        compiler_params=params(24),
+        compiler_params=params(12),
         cost_estimate=cost(4),
         name="gram",
     )(core, keeps, *pieces)
 
 
-def cross_kernel(core_ref, keep_ref, after_ref, *refs):
-    left, right, out_ref, tmp_ref = grouped(refs[:6]), grouped(refs[6:12]), refs[12], refs[13]
-    n = refs[0].shape[1]
+def cross_kernel(core_ref, grp_ref, keep_ref, after_ref, *refs):
+    pieces, (out_ref, token_ref, tmp_ref) = pieces_of(refs[:6]), refs[6:]
+    token_ref[...] = jnp.zeros_like(token_ref)
+    n = refs[0].shape[2]
+    wide = out_ref.shape[2]
+    grp = grp_ref[0]
+    cols = pl.ds(pl.multiple_of(grp * (n - wide), B), wide)
     for i in range(n // B):
         acc = None
-        for lg, rg in zip(left, right):
-            p = dot(columns_of(lg, slice(i * B, (i + 1) * B), keep_ref), columns_of(rg, slice(0, n)), TN)
+        for group in pieces:
+            p = dot(columns_of(group, 1 - grp, slice(i * B, (i + 1) * B), keep_ref), columns_of(group, grp, cols), TN)
             acc = p if acc is None else acc + p
         tmp_ref[i * B : (i + 1) * B, :] = acc
-    tmp_ref[n:, :] = jnp.zeros((tmp_ref.shape[0] - n, n), F32)
+    tmp_ref[n:, :] = jnp.zeros((tmp_ref.shape[0] - n, wide), F32)
     for q in range(out_ref.shape[0]):
         out_ref[q] = tmp_ref[pl.ds(pl.multiple_of((2 * q + core_ref[0]) * ROWS, 8), ROWS), :]
 
 
-def cross(core, keeps, after, left, right, chips):
-    width = left[0].shape[1]
+def cross(core, grp, keeps, after, pieces, chips, wide):
     return pl.pallas_call(
         cross_kernel,
-        out_shape=jax.ShapeDtypeStruct((chips, ROWS, width), F32),
-        in_specs=[SM, SM, ANY] + [VM] * 12,
-        out_specs=VM,
-        scratch_shapes=[pltpu.VMEM((2 * chips * ROWS, width), F32)],
-        compiler_params=params(32),
-        cost_estimate=cost(8),
+        out_shape=(jax.ShapeDtypeStruct((chips, ROWS, wide), F32), TOKEN),
+        in_specs=[SM, SM, SM, ANY] + [VM] * 6,
+        out_specs=(VM, VM),
+        scratch_shapes=[pltpu.VMEM((2 * chips * ROWS, wide), F32)],
+        compiler_params=params(14),
+        cost_estimate=cost(7),
         name="cross",
-    )(core, keeps, after, *left, *right)
+    )(core, grp, keeps, after, *pieces)
 
 
 def factor_diag(block):
-    a = block.reshape(16, 8, B)
+    a = [block[8 * i : 8 * i + 8, :] for i in range(16)]
     lane = lax.broadcasted_iota(jnp.int32, (8, B), 1)
     sub = lax.broadcasted_iota(jnp.int32, (8, B), 0)
-    x = jnp.stack([(lane == sub + 8 * g).astype(F32) for g in range(16)])
+    x = [(lane == sub + 8 * g).astype(F32) for g in range(16)]
     inv, inv_r = [], []
+    cg = [col(a[0], t) for t in range(8)]
     for g in range(16):
         here = (lane >= 8 * g) & (lane < 8 * g + 8)
-        cg = [col(a[0], 8 * g + t) for t in range(8)]
-        v = jnp.where(here, (lane == sub + 8 * g).astype(F32), a[0])
-        xg = x[0]
-        rest = a[1:]
-        xr = x[1:]
+        v = jnp.where(here, (lane == sub + 8 * g).astype(F32), a[g])
+        xg = x[g]
         if g < 15:
-            cr = [col(rest, 8 * g + t) for t in range(8)]
-            rest = jnp.where(here[None], 0.0, rest)
+            near = a[g + 1]
+            cr = [col(near, 8 * g + t) for t in range(8)]
+            nxt = [col(near, 8 * g + 8 + t) for t in range(8)]
+            near, xr = jnp.where(here, 0.0, near), x[g + 1]
+        rs, vs, xs, css = [], [], [], []
         for t in range(8):
             p = row(cg[t], t)
             r = lax.rsqrt(p)
@@ -155,15 +161,33 @@
             cs = {s: row(cg[s], t) * r for s in range(t + 1, 8)}
             for s in range(t + 1, 8):
                 cg[s] = cg[s] - lt * cs[s]
+            rs.append(r)
+            vs.append(vn)
+            xs.append(xn)
+            css.append(cs)
             if g < 15:
-                lr = cr[t] * r[None]
-                rest = rest - lr * vn[None]
-                xr = xr - rounded(lr) * xn[None]
+                lr = cr[t] * r
+                for s in range(8):
+                    nxt[s] = nxt[s] - lr * row(lr, s)
+                near = near - lr * vn
+                xr = xr - rounded(lr) * xn
                 for s in range(t + 1, 8):
-                    cr[s] = cr[s] - lr * cs[s][None]
+                    cr[s] = cr[s] - lr * cs[s]
         inv.append(jnp.where(lane <= sub + 8 * g, v, 0.0))
         inv_r.append(xg)
-        a, x = rest, xr
+        if g < 15:
+            a[g + 1], x[g + 1] = near, xr
+            cg = nxt
+        for i in range(g + 2, 16):
+            c = [col(a[i], 8 * g + t) for t in range(8)]
+            ai, xi = jnp.where(here, 0.0, a[i]), x[i]
+            for t in range(8):
+                l = c[t] * rs[t]
+                ai = ai - l * vs[t]
+                xi = xi - rounded(l) * xs[t]
+                for s in range(t + 1, 8):
+                    c[s] = c[s] - l * css[t][s]
+            a[i], x[i] = ai, xi
     return jnp.concatenate(inv, 0), jnp.concatenate(inv_r, 0)
 
 
@@ -225,30 +249,20 @@
             pltpu.VMEM((n, B), F32),
             pltpu.VMEM((2 * B, B), BF16),
         ],
-        compiler_params=params(16),
+        compiler_params=params(14),
         cost_estimate=cost(57),
         name="cholesky",
     )(core, mine, other)
 
 
-def solve_kernel(total_ref, parts_ref, low_ref, inv_ref, after_ref, out_ref):
-    n = low_ref.shape[0]
-    nb = n // B
-    m = parts_ref.shape[1]
-    total = total_ref[0]
+def solve_into(rhs, m, low_ref, inv_ref, out_ref):
+    nb = low_ref.shape[0] // B
 
     def stacked(x):
         return jnp.concatenate(split(x), 0)
 
     def fold(p):
         return p[:m] + p[m:]
-
-    def rhs(b):
-        cols = slice(b * B, (b + 1) * B)
-        s = parts_ref[0, :, cols]
-        for k in range(1, parts_ref.shape[0]):
-            s = s + parts_ref[k, :, cols]
-        return s / total
 
     acc = [rhs(b) for b in range(nb)]
     for b in range(nb):
@@ -271,16 +285,57 @@
             acc[c] = acc[c] - fold(dot(zs, low_ref[r0:r1, c * B : (c + 1) * B], NN))
 
 
-def solve(total, parts, low, inv, after):
+def solve_kernel(rhs_ref, low_ref, inv_ref, after_ref, out_ref):
+    solve_into(lambda b: rhs_ref[:, b * B : (b + 1) * B], rhs_ref.shape[0], low_ref, inv_ref, out_ref)
+
+
+def solve(rhs, low, inv, after):
     return pl.pallas_call(
         solve_kernel,
-        out_shape=jax.ShapeDtypeStruct(parts.shape[1:], F32),
-        in_specs=[SM] + [VM] * 3 + [ANY],
+        out_shape=jax.ShapeDtypeStruct(rhs.shape, F32),
+        in_specs=[VM] * 3 + [ANY],
         out_specs=VM,
-        compiler_params=params(14),
+        compiler_params=params(8),
         cost_estimate=cost(7),
         name="solve",
-    )(total, parts, low, inv, after)
+    )(rhs, low, inv, after)
+
+
+def route_kernel(block, owner_ref, first_ref, last_ref, low_ref, inv_ref, out_ref, t_ref, r_ref):
+    n = low_ref.shape[0]
+    m, wide = first_ref.shape
+
+    def rhs(b):
+        at = b * B
+        return first_ref[:, at : at + B] if at < wide else last_ref[:, at - (n - wide) : at - (n - wide) + B]
+
+    solve_into(rhs, m, low_ref, inv_ref, t_ref)
+    t_ref[:, n:] = jnp.zeros((m, t_ref.shape[1] - n), F32)
+    lane = lax.broadcasted_iota(jnp.int32, (m, 2 * B), 1)
+    for h in range(2):
+        for q in range(owner_ref.shape[1]):
+            to, off = block * q // B * B, block * q % B
+            src = owner_ref[h, q] * block
+            win = t_ref[:, pl.ds(pl.multiple_of(src // B * B, B), 2 * B)]
+            win = pltpu.roll(win, (off + 2 * B - src % B) % (2 * B), 1)
+            old = r_ref[h, :, to : to + 2 * B]
+            r_ref[h, :, to : to + 2 * B] = jnp.where((lane >= off) & (lane < off + block), win, old)
+        out_ref[h] = r_ref[h, :, : out_ref.shape[2]]
+
+
+def solve_and_route(owner, first, last, low, inv, block):
+    m, n = first.shape[0], low.shape[0]
+    wide = -(-owner.shape[1] * block // B) * B
+    return pl.pallas_call(
+        functools.partial(route_kernel, block),
+        out_shape=jax.ShapeDtypeStruct((2, m, wide), F32),
+        in_specs=[SM] + [VM] * 4,
+        out_specs=VM,
+        scratch_shapes=[pltpu.VMEM((m, n + B), F32), pltpu.VMEM((2, m, wide + B), F32)],
+        compiler_params=params(8),
+        cost_estimate=cost(9),
+        name="solve_and_route",
+    )(owner, first, last, low, inv)
 
 
 def sum_kernel(parts_ref, after_ref, out_ref):
@@ -296,7 +351,7 @@
         out_shape=jax.ShapeDtypeStruct(parts.shape[1:], F32),
         in_specs=[VM, ANY],
         out_specs=VM,
-        compiler_params=params(16),
+        compiler_params=params(8),
         cost_estimate=cost(3),
         name="sum_parts",
     )(parts, after)
@@ -330,7 +385,7 @@
         in_specs=[SM, SM, VM, VM, VM],
         out_specs=VM,
         scratch_shapes=[pltpu.VMEM((n + 8, n), F32)],
-        compiler_params=params(14),
+        compiler_params=params(12),
         cost_estimate=cost(3),
         name="rows",
     )(at, core, mine, other, diag)
@@ -363,18 +418,11 @@
     both = ("grp", "dp")
     half = per_dev // 2
 
-    def to_a(perm):
-        return [p for p in perm if p[1] < n_dp]
-
-    other = jnp.where(is_a, out_grad, attn_out)
-    from_near = lax.ppermute(other[:half], both, near)
-    from_far = lax.ppermute(other[half:], both, far)
-    act_c = lax.ppermute(attn_out, "dp", swap_core)
-    grad_c = lax.ppermute(out_grad, "dp", swap_core)
-    own = jnp.where(is_a, attn_out, out_grad)
-    own_c = jnp.where(is_a, act_c, grad_c)
-    near_c = lax.ppermute(from_near, "dp", swap_core)
-    far_c = lax.ppermute(from_far, "dp", swap_core)
+    own = jnp.stack([jnp.where(is_a, attn_out, out_grad), jnp.where(is_a, out_grad, attn_out)])
+    from_near = lax.ppermute(own[::-1, :half], both, near)
+    from_far = lax.ppermute(own[::-1, half:], both, far)
+    pieces = [own, lax.ppermute(own, "dp", swap_core), from_near, from_far]
+    pieces += [lax.ppermute(from_near, "dp", swap_core), lax.ppermute(from_far, "dp", swap_core)]
     over, mate, away = 1 - grp_index, dp_index ^ 1, dp_index ^ flip
     keeps = jnp.stack([
         keep_of(grp_index, dp_index),
@@ -384,25 +432,16 @@
         keep_of(over, mate),
         keep_of(over, away ^ 1),
     ])
-    pieces = [own, own_c, from_near, from_far, near_c, far_c]
-
     total = (TOK * jnp.sum(image_counts)).astype(F32)
-    part = gram(core_arr, keeps, pieces, chips * per_chip)
+    part, gram_done = gram(core_arr, keeps, pieces, chips * per_chip)
     got = lax.all_to_all(
         part.reshape(chips, per_chip * SLAB, B), "dp", split_axis=0, concat_axis=0, tiled=True, axis_index_groups=same_core
     )
 
-    out_grad_, _ = lax.optimization_barrier((out_grad, from_near))
-    grad_near = lax.ppermute(out_grad_[:half], both, to_a(near))
-    grad_far = lax.ppermute(out_grad_[half:], both, to_a(far))
-    grads = [
-        out_grad, grad_c, grad_near, grad_far,
-        lax.ppermute(grad_near, "dp", swap_core), lax.ppermute(grad_far, "dp", swap_core),
-    ]
-    acts = [attn_out, act_c, from_near, from_far, near_c, far_c]
-    part_w = cross(core_arr, keeps, token(part), grads, acts, chips)
-
-    slabs = sum_parts(got, token(part_w)) / total
+    wide = (nb + 2) // 2 * B
+    part_w, cross_done = cross(core_arr, grp_index.astype(jnp.int32)[None], keeps, gram_done, pieces, chips, wide)
+
+    slabs = sum_parts(got, cross_done) / total
 
     flat = chip * (per_chip * SLAB) + jnp.arange(per_chip * SLAB)
     t = flat // HALF
@@ -421,28 +460,30 @@
 
     got_w = lax.all_to_all(part_w, "dp", split_axis=0, concat_axis=0, tiled=True, axis_index_groups=same_core)
 
-    squares = jnp.stack([attn_out, out_grad]).astype(F32)
-    squares = jnp.sum(squares * squares, axis=1) * keeps[0]
-    diags = lax.psum(squares, both) / total
+    pad = 256 - per_chip * SLAB
+    diags = jnp.pad(jnp.sum(slabs * diag.astype(F32), axis=1), (0, pad)).reshape(2, B)
+    diags = lax.all_gather(diags, "dp", axis=0, tiled=False).reshape(chips, 2, 256)[:, :, : per_chip * SLAB]
+    diags = diags.transpose(1, 0, 2).reshape(2, -1)
+    my_diag = jnp.concatenate([diags[c, tri(i, i) * HALF : tri(i, i) * HALF + HALF] for i in range(nb) for c in range(2)])[None]
     at = (dp_index * block).astype(jnp.int32)[None]
-    my_diag = jnp.where(is_a, diags[0], diags[1])[None]
     my_rows = rows_of(at, core_arr, mine, theirs, my_diag, width, ROWS)[:block]
     their_rows = lax.ppermute(my_rows, "grp", swap_grp)
     factors = jnp.stack([jnp.where(is_a, my_rows, their_rows), jnp.where(is_a, their_rows, my_rows)])
 
-    right = solve(total[None], got_w, low, inv, token(inv))
-    order = column_owner.reshape(chips, 2).T.reshape(n_dp)
-    routed = right.T.reshape(n_dp, block, ROWS)[order].reshape(2, chips, block, ROWS)
-    mine_t = lax.dynamic_index_in_dim(routed, core, 0, keepdims=False)
-    other_t = lax.dynamic_index_in_dim(routed, 1 - core, 0, keepdims=False)
-    same = lax.ppermute(mine_t, both, [(d, n_dp + d) for d in range(n_dp)])
-    cross_t = lax.ppermute(other_t, both, [(d, n_dp + (d ^ 1)) for d in range(n_dp)])
+    order = column_owner.reshape(chips, 2)
+    order = jnp.stack([jnp.where(core == 0, order[:, 0], order[:, 1]), jnp.where(core == 0, order[:, 1], order[:, 0])])
+    my_w = sum_parts(got_w, inv) / total
+    last_w = lax.ppermute(my_w, "grp", [(1, 0)])
+    routed = solve_and_route(order, my_w, last_w, low, inv, block)
+    same = lax.ppermute(routed[0], both, [(d, n_dp + d) for d in range(n_dp)])
+    cross_t = lax.ppermute(routed[1], both, [(d, n_dp + (d ^ 1)) for d in range(n_dp)])
     is_first = core == 0
-    pair = jnp.concatenate([jnp.where(is_first, same, cross_t), jnp.where(is_first, cross_t, same)], axis=2)
+    pair = jnp.concatenate([jnp.where(is_first, same, cross_t), jnp.where(is_first, cross_t, same)])
+    pair = pair[:, : chips * block].reshape(2 * ROWS, chips, block).transpose(1, 2, 0)
     columns = lax.all_to_all(pair, "dp", split_axis=0, concat_axis=0, tiled=True, axis_index_groups=same_core)
     columns = columns.transpose(1, 0, 2).reshape(block, n_dp * ROWS)[:, :width]
     columns = jnp.pad(columns, ((0, ROWS - block), (0, 0)))
-    left = solve(jnp.ones((1,), F32), columns[None], low, inv, token(my_rows))[:block]
+    left = solve(columns, low, inv, my_rows)[:block]
     back = lax.ppermute(left, "grp", [(1, 0)])
     preconditioned = jnp.where(is_a, back, left).T
     return (factors, preconditioned)

time: 311 us -> 343 us (1.10)
  blocking collectives: 71.1 us -> 147 us
  starting transfers between devices: 47.5 us -> 26.8 us
  waiting for transfers between devices: 68.9 us -> 56.8 us
  Pallas kernels: 81.4 us -> 72.1 us
    all_gather x0 -> x1, blocking collectives: none -> 122 us  [per_device(): lax.all_gather(diags, 'dp', axis=0, tiled=False).reshape(chips, 2, 256)]
    psum x1 -> x0, blocking collectives: 71.1 us -> none  [per_device(): diags = lax.psum(squares, both) / total]
    ppermute x12 -> x8, waiting for transfers between devices: 54.1 us -> 20 us  [the longest x1 13.2 us: per_device(): from_near = lax.ppermute(own[::-1, :half], both, near)]
    all_to_all x0 -> x1, blocking collectives: none -> 25.8 us  [per_device(): lax.all_to_all(spread, 'dp', split_axis=0, concat_axis=0, tiled=True, axi...]
    all_to_all x1, waiting for transfers between devices: 0.01 us -> 21.9 us  [per_device(): lax.all_to_all(part.reshape(chips, per_chip * SLAB, B), 'dp', split_axis=...]
    all_to_all x1 -> x0, starting transfers between devices: 9.33 us -> none  [per_device(): lax.all_to_all(spread, 'dp', split_axis=0, concat_axis=0, tiled=True, axi...]
    pallas_call x1, Pallas kernels: 55.1 us -> 45.8 us  [chol(): pl.pallas_call(chol_kernel, out_shape=(jax.ShapeDtypeStruct((n, n), BF16)...]
    ppermute x12 -> x8, starting transfers between devices: 13.8 us -> 8.02 us  [the longest x1 2.1 us: per_device(): from_far = lax.ppermute(own[::-1, half:], both, far)]
  transfers between devices with their start and end apart: 19 -> 14, of which waited for: 9 -> 7; matrix products, arithmetic and copies ran while one was open for 3% -> 4% of each run, Pallas kernels for 20% -> 16%
where the time goes in v4:
time: 343 us; the launch traced here: 342 us
  blocking collectives  147 us (43%)
  Pallas kernels  72.1 us (21%)
  waiting for transfers between devices  56.8 us (17%)
  local copies, waits for them, and re-layouts  27.7 us (8%)
  starting transfers between devices  26.8 us (8%)
  between operations  6.77 us (2%)
  other arithmetic  4.6 us (1%)
    all_gather x1, blocking collectives, per_device(): lax.all_gather(diags, 'dp', axis=0, tiled=False).reshape(chips, 2, 256)  122 us
    pallas_call x1, Pallas kernels, chol(): pl.pallas_call(chol_kernel, out_shape=(jax.ShapeDtypeStruct((n, n), BF16)...  45.8 us
    all_to_all x1, blocking collectives, per_device(): lax.all_to_all(spread, 'dp', split_axis=0, concat_axis=0, tiled=True, axi...  25.8 us
    all_to_all x1, waiting for transfers between devices, per_device(): lax.all_to_all(part.reshape(chips, per_chip * SLAB, B), 'dp', split_axis=...  21.9 us
    unnamed x33, local copies, waits for them, and re-layouts  15.5 us
    ppermute x1, waiting for transfers between devices, per_device(): from_near = lax.ppermute(own[::-1, :half], both, near)  13.2 us
    all_to_all x1, waiting for transfers between devices, per_device(): lax.all_to_all(pair, 'dp', split_axis=0, concat_axis=0, tiled=True, axis_...  9.64 us
    all_to_all x1, starting transfers between devices, per_device(): lax.all_to_all(part.reshape(chips, per_chip * SLAB, B), 'dp', split_axis=...  9.42 us
  transfers between devices with their start and end apart: 14, of which 7 were waited for; matrix products, arithmetic and copies ran while one was open for 4% of the time, Pallas kernels for 16%

profile of v4, /device:TPU:0, one launch (start us, length us, event | category | flops | bytes accessed | tf_op | source)
XLA Modules:
  0.0 342.1 jit_solution(14745714893142826485)
XLA Ops:
  0.6 1.5 select_bitcast_fusion.1
  2.3 0.9 rev.6
  3.2 1.6 collective-permute-start.1
  4.8 0.9 rev.7
  5.7 2.1 collective-permute-start.2
  8.0 13.2 %collective-permute-done.1.refs_2_ = bf16[2,128,1408]{2,1,0:T(8,128)(2,1)} collective-permute-done((bf16[2,128,1408]{2,1,0:T(8,128)(2,1)}, bf16[2,128,1408]{2,1,0:T(8,128)(2,1)}, u32[]{:S(2)}, u32[]{:S(2)}) %collective-permute-start.1) | collective-permute-done | bytes 720928 | tf_op jit(solution)/shard_map/ppermute | solution.py:422
  21.2 3.6 %collective-permute-done.2.refs_3_ = bf16[2,128,1408]{2,1,0:T(8,128)(2,1)} collective-permute-done((bf16[2,128,1408]{2,1,0:T(8,128)(2,1)}, bf16[2,128,1408]{2,1,0:T(8,128)(2,1)}, u32[]{:S(2)}, u32[]{:S(2)}) %collective-permute-start.2) | collective-permute-done | bytes 720928 | tf_op jit(solution)/shard_map/ppermute | solution.py:423
  24.8 0.7 fusion.5
  29.4 5.1 %gram.1 = (f32[4608,128]{1,0:T(8,128)S(1)}, f32[8,128]{1,0:T(8,128)S(1)}) custom-call(s32[1]{0:T(128)} %bitcast.1.core_ref, f32[6]{0:T(128)S(1)} %stack.35.keep_ref, bf16[2,256,1408]{2,1,0:T(8,128)(2,1)S(1)} %pad_maximum_fusion.refs_0_, bf16[2,256,1408]{2,1,0:T(8,128)(2,1)S(1)} %collective-permute-done.refs_1_, ...), custom_call_target="tpu_custom_call" | custom-call | flops 4400000000 | bytes 1048576 | tf_op jit(solution)/shard_map/gram/pallas_call | solution.py:93
  34.5 1.4 copy-done
  35.9 9.4 %all-to-all-start = ((f32[32,144,128]{2,1,0:T(8,128)}), f32[32,144,128]{2,1,0:T(8,128)S(1)}, u32[]{:S(2)}, u32[]{:S(2)}) async-start(f32[32,144,128]{2,1,0:T(8,128)} %bitcast.77), calls=%async_computation | async-start | bytes 4718592 | tf_op jit(solution)/shard_map/all_to_all | solution.py:437
  45.3 0.6 reduce_sum.18
  48.6 1.4 copy-done.2
  50.0 1.4 copy-done.4
  51.3 5.8 %cross.1 = (f32[32,24,768]{2,1,0:T(8,128)}, f32[8,128]{1,0:T(8,128)S(1)}) custom-call(s32[1]{0:T(128)} %bitcast.1.core_ref, s32[1]{0:T(128)} %bitcast.5.grp_ref, f32[6]{0:T(128)S(1)} %stack.35.keep_ref, f32[8,128]{1,0:T(8,128)S(1)} %get-tuple-element.9.after_ref, bf16[2,256,1408]{2,1,0:T(8,128)(2,1)S(1)} %copy-done.2, bf16[2,256,1408]{2,1,0:T(8,128)(2,1)S(1)} %copy-done.4, ...), custom_call_target="tpu_custom_call" | custom-call | flops 7699999744 | bytes 1048576 | tf_op jit(solution)/shard_map/cross/pallas_call | solution.py:124
  57.1 21.9 %all-to-all-done.parts_ref = f32[32,144,128]{2,1,0:T(8,128)S(1)} async-done(((f32[32,144,128]{2,1,0:T(8,128)}), f32[32,144,128]{2,1,0:T(8,128)S(1)}, u32[]{:S(2)}, u32[]{:S(2)}) %all-to-all-start) | async-done | bytes 2359328 | tf_op jit(solution)/shard_map/all_to_all | solution.py:437
  79.6 25.8 %all_to_all.20 = bf16[32,144,128]{2,1,0:T(8,128)(2,1)S(1)} all-to-all(bf16[32,144,128]{2,1,0:T(8,128)(2,1)S(1)} %broadcast_in_dim.24), channel_id=1, replica_groups={{0,2,4,6,8,10,12,14,16,18,20,22,24,26,28,30,32,34,36,38,40,42,44,46,48,..., dimensions={0} | all-to-all | bytes 2359296 | tf_op jit(solution)/shard_map/all_to_all | solution.py:456
  105.7 4.1 %all-to-all-start.2 = ((f32[32,24,768]{2,1,0:T(8,128)}), f32[32,24,768]{2,1,0:T(8,128)S(1)}, u32[]{:S(2)}, u32[]{:S(2)}) async-start(f32[32,24,768]{2,1,0:T(8,128)} %get-tuple-element.11), calls=%async_computation.2 | async-start | bytes 4718592 | tf_op jit(solution)/shard_map/all_to_all | solution.py:461
  109.8 121.6 %all_gather.3 = f32[64,2,128]{2,1,0:T(2,128)} all-gather(f32[1,2,128]{2,1,0:T(2,128)S(1)} %pad_bitcast_fusion), channel_id=1, replica_groups=mesh['grp'=2,'dp'=64] {'dp'}, dimensions={0}, use_global_device_ids=true | all-gather | bytes 66560 | tf_op jit(solution)/shard_map/all_gather | solution.py:465
  231.4 1.5 reshape.146
  232.9 0.8 slice_bitcast_fusion.2
  233.8 0.6 copy.16
  234.4 1.6 reshape.147
  236.0 1.6 slice_bitcast_fusion.3
  237.5 45.8 %cholesky.1 = (bf16[1408,1408]{1,0:T(8,128)(2,1)S(1)}, f32[1408,128]{1,0:T(8,128)S(1)}) custom-call(s32[1]{0:T(128)} %bitcast.1.core_ref, bf16[4608,128]{1,0:T(8,128)(2,1)S(1)} %bitcast.79, bf16[4608,128]{1,0:T(8,128)(2,1)} %collective-permute-done.5.other_ref), custom_call_target="tpu_custom_call" | custom-call | flops 62699999232 | bytes 1048576 | tf_op jit(solution)/shard_map/cholesky/pallas_call | solution.py:242
  283.3 0.9 copy-done.5
  284.3 1.9 copy-done.9
  286.2 1.1 copy-done.6
  287.4 1.5 collective-permute-start.7
  288.9 0.8 slice_bitcast_fusion.22
  289.7 0.8 concatenate.6
  290.5 3.3 collective-permute-done.7.last_ref
  293.8 1.1 copy-done.7
  294.9 2.1 copy-done.10
  297.0 7.2 %solve_and_route.1 = f32[2,24,768]{2,1,0:T(8,128)S(1)} custom-call(s32[2,32]{1,0:T(2,128)S(1)} %pad_add_fusion.owner_ref, f32[24,768]{1,0:T(8,128)S(1)} %broadcast_divide_fusion.first_ref, f32[24,768]{1,0:T(8,128)S(1)} %collective-permute-done.7.last_ref, bf16[1408,1408]{1,0:T(8,128)(2,1)S(1)} %copy-done.10, f32[1408,128]{1,0:T(8,128)S(1)} %copy-done.7), custom_call_target="tpu_custom_call" | custom-call | flops 9900000256 | bytes 1048576 | tf_op jit(solution)/shard_map/solve_and_route/pallas_call | solution.py:329
  304.2 1.5 collective-permute-start.8
  305.7 1.3 collective-permute-start.9
  307.0 2.1 rows.1
  309.5 1.0 reshape.153
  310.5 3.9 %all-to-all-start.3 = ((f32[32,1,1056]{2,1,0:T(1,128)}), f32[32,1,1056]{2,1,0:T(1,128)S(1)}, u32[]{:S(2)}, u32[]{:S(2)}) async-start(f32[32,1,1056]{2,1,0:T(1,128)} %reshape.153), calls=%async_computation.3 | async-start | bytes 294912 | tf_op jit(solution)/shard_map/all_to_all | solution.py:483
  314.8 9.6 %all-to-all-done.3 = f32[32,1,1056]{2,1,0:T(1,128)S(1)} async-done(((f32[32,1,1056]{2,1,0:T(1,128)}), f32[32,1,1056]{2,1,0:T(1,128)S(1)}, u32[]{:S(2)}, u32[]{:S(2)}) %all-to-all-start.3) | async-done | bytes 135200 | tf_op jit(solution)/shard_map/all_to_all | solution.py:483
  325.0 1.0 reduce.4
  326.5 2.1 copy-done.11
  328.6 5.9 %solve.1 = f32[24,1408]{1,0:T(8,128)S(1)} custom-call(f32[24,1408]{1,0:T(8,128)S(1)} %pad.9.rhs_ref, bf16[1408,1408]{1,0:T(8,128)(2,1)S(1)} %copy-done.11, f32[1408,128]{1,0:T(8,128)S(1)} %copy-done.8, f32[22,1408]{1,0:T(8,128)S(1)} %bitcast.82), custom_call_target="tpu_custom_call" | custom-call | flops 7699999744 | bytes 1048576 | tf_op jit(solution)/shard_map/solve/pallas_call | solution.py:293
  334.5 1.3 collective-permute-start.10
  335.9 0.8 copy.19
  336.7 4.8 %collective-permute-done.10 = f32[22,1408]{1,0:T(8,128)S(1)} collective-permute-done((f32[22,1408]{1,0:T(8,128)S(1)}, f32[22,1408]{1,0:T(8,128)S(1)}, u32[]{:S(2)}, u32[]{:S(2)}) %collective-permute-start.10) | collective-permute-done | bytes 123936 | tf_op jit(solution)/shard_map/ppermute | solution.py:487
  341.5 0.7 select_bitcast_fusion.2
  (64 shorter events, 3.9 us)
Async XLA Ops:
  3.2 18.0 %collective-permute-start.1 = (bf16[2,128,1408]{2,1,0:T(8,128)(2,1)}, bf16[2,128,1408]{2,1,0:T(8,128)(2,1)}, u32[]{:S(2)}, u32[]{:S(2)}) collective-permute-start(bf16[2,128,1408]{2,1,0:T(8,128)(2,1)} %rev.6), channel_id=1, source_target_pairs={{0,64},{1,65},{2,66},{3,67},{4,68},{5,69},{6,70},{7,71},{8,72},{9,... | collective-permute-start | bytes 2162696 | tf_op jit(solution)/shard_map/ppermute | solution.py:422
  5.7 19.1 %copy-start.12 = (s32[128]{0:T(128)S(1)}, s32[128]{0:T(128)}, u32[]{:S(2)}) copy-start(s32[128]{0:T(128)} %param.7) | copy-start | bytes 1540
  5.7 19.1 %collective-permute-start.2 = (bf16[2,128,1408]{2,1,0:T(8,128)(2,1)}, bf16[2,128,1408]{2,1,0:T(8,128)(2,1)}, u32[]{:S(2)}, u32[]{:S(2)}) collective-permute-start(bf16[2,128,1408]{2,1,0:T(8,128)(2,1)} %rev.7), channel_id=1, source_target_pairs={{0,96},{1,97},{2,98},{3,99},{4,100},{5,101},{6,102},{7,103},{8,104... | collective-permute-start | bytes 2162696 | tf_op jit(solution)/shard_map/ppermute | solution.py:423
  7.9 26.5 %copy-start.1 = (bf16[2,256,1408]{2,1,0:T(8,128)(2,1)}, bf16[2,256,1408]{2,1,0:T(8,128)(2,1)S(1)}, u32[]{:S(2)}) copy-start(bf16[2,256,1408]{2,1,0:T(8,128)(2,1)S(1)} %pad_maximum_fusion.refs_0_) | copy-start | bytes 4325380
  8.0 21.4 %collective-permute-start = (bf16[2,256,1408]{2,1,0:T(8,128)(2,1)S(1)}, bf16[2,256,1408]{2,1,0:T(8,128)(2,1)S(1)}, u32[]{:S(2)}, u32[]{:S(2)}) collective-permute-start(bf16[2,256,1408]{2,1,0:T(8,128)(2,1)S(1)} %pad_maximum_fusion.refs_0_), channel_id=1, source_target_pairs={{0,1},{1,0},{2,3},{3,2},{4,5},{5,4},{6,7},{7,6},{8,9},{9,8},{10,11... | collective-permute-start | bytes 4325384 | tf_op jit(solution)/shard_map/ppermute | solution.py:424
  21.2 8.1 %collective-permute-start.3 = (bf16[2,128,1408]{2,1,0:T(8,128)(2,1)}, bf16[2,128,1408]{2,1,0:T(8,128)(2,1)}, u32[]{:S(2)}, u32[]{:S(2)}) collective-permute-start(bf16[2,128,1408]{2,1,0:T(8,128)(2,1)} %collective-permute-done.1.refs_2_), channel_id=1, source_target_pairs={{0,1},{1,0},{2,3},{3,2},{4,5},{5,4},{6,7},{7,6},{8,9},{9,8},{10,11... | collective-permute-start | bytes 2162696 | tf_op jit(solution)/shard_map/ppermute | solution.py:425
  24.8 4.5 %collective-permute-start.4 = (bf16[2,128,1408]{2,1,0:T(8,128)(2,1)}, bf16[2,128,1408]{2,1,0:T(8,128)(2,1)}, u32[]{:S(2)}, u32[]{:S(2)}) collective-permute-start(bf16[2,128,1408]{2,1,0:T(8,128)(2,1)} %collective-permute-done.2.refs_3_), channel_id=1, source_target_pairs={{0,1},{1,0},{2,3},{3,2},{4,5},{5,4},{6,7},{7,6},{8,9},{9,8},{10,11... | collective-permute-start | bytes 2162696 | tf_op jit(solution)/shard_map/ppermute | solution.py:425
  29.4 5.1 %copy-start.3 = (bf16[2,256,1408]{2,1,0:T(8,128)(2,1)}, bf16[2,256,1408]{2,1,0:T(8,128)(2,1)S(1)}, u32[]{:S(2)}) copy-start(bf16[2,256,1408]{2,1,0:T(8,128)(2,1)S(1)} %collective-permute-done.refs_1_) | copy-start | bytes 4325380
  34.4 1.4 copy-start
  35.9 10.7 %copy-start.13 = (f32[2]{0:T(128)S(1)}, f32[2]{0:T(128)}, u32[]{:S(2)}) copy-start(f32[2]{0:T(128)} %param.9) | copy-start | bytes 28
  35.9 43.2 %all-to-all-start = ((f32[32,144,128]{2,1,0:T(8,128)}), f32[32,144,128]{2,1,0:T(8,128)S(1)}, u32[]{:S(2)}, u32[]{:S(2)}) async-start(f32[32,144,128]{2,1,0:T(8,128)} %bitcast.77), calls=%async_computation | async-start | bytes 4718592 | tf_op jit(solution)/shard_map/all_to_all | solution.py:437
  48.6 1.4 copy-start.2
  50.0 1.4 copy-start.4
  79.6 25.8 %copy-start.14 = (s32[64]{0:T(128)S(1)}, s32[64]{0:T(128)}, u32[]{:S(2)}) copy-start(s32[64]{0:T(128)} %param.8) | copy-start | bytes 772
  105.4 132.1 %collective-permute-start.5 = (bf16[4608,128]{1,0:T(8,128)(2,1)S(1)}, bf16[4608,128]{1,0:T(8,128)(2,1)}, u32[]{:S(2)}, u32[]{:S(2)}) collective-permute-start(bf16[4608,128]{1,0:T(8,128)(2,1)S(1)} %bitcast.78), channel_id=1, source_target_pairs={{0,1},{1,0},{2,3},{3,2},{4,5},{5,4},{6,7},{7,6},{8,9},{9,8},{10,11... | collective-permute-start | bytes 3538952 | tf_op jit(solution)/shard_map/ppermute | solution.py:458
  105.7 180.4 %all-to-all-start.2 = ((f32[32,24,768]{2,1,0:T(8,128)}), f32[32,24,768]{2,1,0:T(8,128)S(1)}, u32[]{:S(2)}, u32[]{:S(2)}) async-start(f32[32,24,768]{2,1,0:T(8,128)} %get-tuple-element.11), calls=%async_computation.2 | async-start | bytes 4718592 | tf_op jit(solution)/shard_map/all_to_all | solution.py:461
  283.3 0.9 copy-start.5
  284.3 1.9 copy-start.9
  286.2 1.1 copy-start.6
  287.4 6.4 %collective-permute-start.7 = (f32[24,768]{1,0:T(8,128)S(1)}, f32[24,768]{1,0:T(8,128)S(1)}, u32[]{:S(2)}, u32[]{:S(2)}) collective-permute-start(f32[24,768]{1,0:T(8,128)S(1)} %broadcast_divide_fusion.first_ref), channel_id=1, source_target_pairs={{64,0},{65,1},{66,2},{67,3},{68,4},{69,5},{70,6},{71,7},{72,8},{73... | collective-permute-start | bytes 221192 | tf_op jit(solution)/shard_map/ppermute | solution.py:476
  293.8 1.1 copy-start.7
  294.9 2.1 copy-start.10
  304.2 5.0 %collective-permute-start.8 = (f32[24,768]{1,0:T(8,128)S(1)}, f32[24,768]{1,0:T(8,128)S(1)}, u32[]{:S(2)}, u32[]{:S(2)}) collective-permute-start(f32[24,768]{1,0:T(8,128)S(1)} %get-tuple-element.32), channel_id=1, source_target_pairs={{0,64},{1,65},{2,66},{3,67},{4,68},{5,69},{6,70},{7,71},{8,72},{9,... | collective-permute-start | bytes 221192 | tf_op jit(solution)/shard_map/ppermute | solution.py:478
  305.7 3.5 %collective-permute-start.9 = (f32[24,768]{1,0:T(8,128)S(1)}, f32[24,768]{1,0:T(8,128)S(1)}, u32[]{:S(2)}, u32[]{:S(2)}) collective-permute-start(f32[24,768]{1,0:T(8,128)S(1)} %get-tuple-element.33), channel_id=1, source_target_pairs={{0,65},{1,64},{2,67},{3,66},{4,69},{5,68},{6,71},{7,70},{8,73},{9,... | collective-permute-start | bytes 221192 | tf_op jit(solution)/shard_map/ppermute | solution.py:479
  309.1 5.7 %collective-permute-start.6 = (f32[22,1408]{1,0:T(8,128)S(1)}, f32[22,1408]{1,0:T(8,128)S(1)}, u32[]{:S(2)}, u32[]{:S(2)}) collective-permute-start(f32[22,1408]{1,0:T(8,128)S(1)} %bitcast.81), channel_id=1, source_target_pairs={{0,64},{64,0},{1,65},{65,1},{2,66},{66,2},{3,67},{67,3},{4,68},{68... | collective-permute-start | bytes 371720 | tf_op jit(solution)/shard_map/ppermute | solution.py:470
  310.5 14.0 %all-to-all-start.3 = ((f32[32,1,1056]{2,1,0:T(1,128)}), f32[32,1,1056]{2,1,0:T(1,128)S(1)}, u32[]{:S(2)}, u32[]{:S(2)}) async-start(f32[32,1,1056]{2,1,0:T(1,128)} %reshape.153), calls=%async_computation.3 | async-start | bytes 294912 | tf_op jit(solution)/shard_map/all_to_all | solution.py:483
  314.8 11.7 %copy-start.8 = (f32[1408,128]{1,0:T(8,128)S(1)}, f32[1408,128]{1,0:T(8,128)}, u32[]{:S(2)}) copy-start(f32[1408,128]{1,0:T(8,128)} %copy-done.5) | copy-start | bytes 2162692
  326.5 2.1 copy-start.11
  334.5 6.9 %collective-permute-start.10 = (f32[22,1408]{1,0:T(8,128)S(1)}, f32[22,1408]{1,0:T(8,128)S(1)}, u32[]{:S(2)}, u32[]{:S(2)}) collective-permute-start(f32[22,1408]{1,0:T(8,128)S(1)} %bitcast.83), channel_id=1, source_target_pairs={{64,0},{65,1},{66,2},{67,3},{68,4},{69,5},{70,6},{71,7},{72,8},{73... | collective-permute-start | bytes 371720 | tf_op jit(solution)/shard_map/ppermute | solution.py:487

commit v5 on v4

--- a/solution.py
+++ b/solution.py
@@ -19,6 +19,7 @@
 TN = (((0,), (0,)), ((), ()))
 VM = pl.BlockSpec(memory_space=pltpu.VMEM)
 ANY = pl.BlockSpec(memory_space=pl.ANY)
+HBM = pl.BlockSpec(memory_space=pltpu.HBM)
 SM = pl.BlockSpec(memory_space=pltpu.SMEM)
 TOKEN = jax.ShapeDtypeStruct((8, B), F32)
 MIB = 1024 * 1024
@@ -62,75 +63,91 @@
     return [[(0, own)], [(1, mate)], [(2, near), (3, far)], [(4, near_mate), (5, far_mate)]]
 
 
-def columns_of(group, which, cols, keep_ref=None):
-    parts = [
-        ref[which, :, cols] if keep_ref is None else ref[which, :, cols] * keep_ref[k].astype(BF16) for k, ref in group
-    ]
+def columns_of(group, cols, keep_ref=None):
+    parts = [ref[:, cols] if keep_ref is None else ref[:, cols] * keep_ref[k].astype(BF16) for k, ref in group]
     return parts[0] if len(parts) == 1 else jnp.concatenate(parts, 0)
 
 
 def gram_kernel(core_ref, keep_ref, *refs):
-    pieces, (out_ref, token_ref, tmp_ref) = pieces_of(refs[:6]), refs[6:]
-    token_ref[...] = jnp.zeros_like(token_ref)
-    nb = refs[0].shape[2] // B
+    pieces, (hbm_ref, squares_ref, out_ref, tmp_ref, sem) = pieces_of(refs[:6]), refs[6:]
+    nb = refs[0].shape[1] // B
     start = pl.multiple_of(core_ref[0] * HALF, HALF)
+    on = lax.broadcasted_iota(jnp.int32, (B, B), 0) == lax.broadcasted_iota(jnp.int32, (B, B), 1)
+    copies = []
+
+    def send(lo, hi):
+        copies.append(pltpu.make_async_copy(out_ref.at[lo:hi], hbm_ref.at[lo:hi], sem.at[len(copies)]))
+        copies[-1].start()
+
+    used = tri(nb, 0) * HALF
+    out_ref[used:, :] = jnp.zeros((out_ref.shape[0] - used, B), F32)
+    send(used, out_ref.shape[0])
     for i in range(nb):
         wide = (i + 1) * B
         acc = None
         for group in pieces:
-            p = dot(columns_of(group, 0, slice(i * B, wide), keep_ref), columns_of(group, 0, slice(0, wide)), TN)
+            p = dot(columns_of(group, slice(i * B, wide), keep_ref), columns_of(group, slice(0, wide)), TN)
             acc = p if acc is None else acc + p
         tmp_ref[:, :wide] = acc
+        diag = jnp.sum(jnp.where(on, acc[:, i * B :], 0.0), axis=0, keepdims=True)
+        squares_ref[:, i * B : wide] = jnp.broadcast_to(diag, (8, B))
         for j in range(i + 1):
             t = tri(i, j)
             out_ref[t * HALF : (t + 1) * HALF, :] = tmp_ref[pl.ds(start, HALF), j * B : (j + 1) * B]
-    used = tri(nb, 0) * HALF
-    out_ref[used:, :] = jnp.zeros((out_ref.shape[0] - used, B), F32)
+        send(tri(i, 0) * HALF, tri(i + 1, 0) * HALF)
+    for copy in copies:
+        copy.wait()
 
 
 def gram(core, keeps, pieces, slots):
-    width = pieces[0].shape[2]
+    width = pieces[0].shape[1]
     return pl.pallas_call(
         gram_kernel,
-        out_shape=(jax.ShapeDtypeStruct((slots * SLAB, B), F32), TOKEN),
+        out_shape=(jax.ShapeDtypeStruct((slots * SLAB, B), F32), jax.ShapeDtypeStruct((8, width), F32)),
         in_specs=[SM, SM] + [VM] * 6,
-        out_specs=(VM, VM),
-        scratch_shapes=[pltpu.VMEM((B, width), F32)],
-        compiler_params=params(12),
+        out_specs=(HBM, VM),
+        scratch_shapes=[
+            pltpu.VMEM((slots * SLAB, B), F32),
+            pltpu.VMEM((B, width), F32),
+            pltpu.SemaphoreType.DMA((width // B + 1,)),
+        ],
+        compiler_params=params(56),
         cost_estimate=cost(4),
         name="gram",
     )(core, keeps, *pieces)
 
 
 def cross_kernel(core_ref, grp_ref, keep_ref, after_ref, *refs):
-    pieces, (out_ref, token_ref, tmp_ref) = pieces_of(refs[:6]), refs[6:]
-    token_ref[...] = jnp.zeros_like(token_ref)
-    n = refs[0].shape[2]
+    mine, other, (out_ref, tmp_ref) = pieces_of(refs[:6]), pieces_of(refs[6:12]), refs[12:]
+    n = refs[0].shape[1]
     wide = out_ref.shape[2]
-    grp = grp_ref[0]
-    cols = pl.ds(pl.multiple_of(grp * (n - wide), B), wide)
-    for i in range(n // B):
-        acc = None
-        for group in pieces:
-            p = dot(columns_of(group, 1 - grp, slice(i * B, (i + 1) * B), keep_ref), columns_of(group, grp, cols), TN)
-            acc = p if acc is None else acc + p
-        tmp_ref[i * B : (i + 1) * B, :] = acc
+
+    def run(left, right, first):
+        for i in range(n // B):
+            acc = None
+            for lg, rg in zip(left, right):
+                p = dot(columns_of(lg, slice(i * B, (i + 1) * B), keep_ref), columns_of(rg, slice(first, first + wide)), TN)
+                acc = p if acc is None else acc + p
+            tmp_ref[i * B : (i + 1) * B, :] = acc
+
+    pl.when(grp_ref[0] == 0)(lambda: run(other, mine, 0))
+    pl.when(grp_ref[0] == 1)(lambda: run(mine, other, n - wide))
     tmp_ref[n:, :] = jnp.zeros((tmp_ref.shape[0] - n, wide), F32)
     for q in range(out_ref.shape[0]):
         out_ref[q] = tmp_ref[pl.ds(pl.multiple_of((2 * q + core_ref[0]) * ROWS, 8), ROWS), :]
 
 
-def cross(core, grp, keeps, after, pieces, chips, wide):
+def cross(core, grp, keeps, after, mine, other, chips, wide):
     return pl.pallas_call(
         cross_kernel,
-        out_shape=(jax.ShapeDtypeStruct((chips, ROWS, wide), F32), TOKEN),
-        in_specs=[SM, SM, SM, ANY] + [VM] * 6,
-        out_specs=(VM, VM),
+        out_shape=jax.ShapeDtypeStruct((chips, ROWS, wide), F32),
+        in_specs=[SM, SM, SM, ANY] + [VM] * 12,
+        out_specs=VM,
         scratch_shapes=[pltpu.VMEM((2 * chips * ROWS, wide), F32)],
-        compiler_params=params(14),
-        cost_estimate=cost(7),
+        compiler_params=params(56),
+        cost_estimate=cost(30),
         name="cross",
-    )(core, grp, keeps, after, *pieces)
+    )(core, grp, keeps, after, *mine, *other)
 
 
 def factor_diag(block):
@@ -198,7 +215,8 @@
     return jnp.concatenate([jnp.where(first, mine, other), jnp.where(first, other, mine)], 0)
 
 
-def chol_kernel(core_ref, mine_ref, other_ref, low_ref, inv_ref, lo_ref, s_ref, w_ref):
+def chol_kernel(core_ref, mine_ref, other_ref, low_hbm, inv_hbm, done_ref, low_ref, inv_ref, lo_ref, s_ref, w_ref, sem):
+    done_ref[...] = jnp.zeros_like(done_ref)
     n = low_ref.shape[0]
     nb = n // B
     first = core_ref[0] == 0
@@ -226,8 +244,11 @@
         for kk in range(nb):
             pl.when(k == kk)(lambda kk=kk: update(kk))
         r0 = pl.multiple_of(k * B, B)
+        rows = pl.ds(r0, B)
+        pltpu.make_async_copy(low_ref.at[rows], low_hbm.at[rows], sem.at[0, k]).start()
         linv, lrinv = factor_diag(s_ref[pl.ds(r0, B), :])
-        inv_ref[pl.ds(r0, B), :] = lrinv
+        inv_ref[rows, :] = lrinv
+        pltpu.make_async_copy(inv_ref.at[rows], inv_hbm.at[rows], sem.at[1, k]).start()
         hi, lo = split(linv)
         w_ref[:B, :] = hi
         w_ref[B:, :] = lo
@@ -236,27 +257,40 @@
         return 0
 
     lax.fori_loop(0, nb, step, 0)
+    for k in range(nb):
+        rows = slice(k * B, (k + 1) * B)
+        pltpu.make_async_copy(low_ref.at[rows], low_hbm.at[rows], sem.at[0, k]).wait()
+        pltpu.make_async_copy(inv_ref.at[rows], inv_hbm.at[rows], sem.at[1, k]).wait()
 
 
 def chol(core, mine, other, n):
     return pl.pallas_call(
         chol_kernel,
-        out_shape=(jax.ShapeDtypeStruct((n, n), BF16), jax.ShapeDtypeStruct((n, B), F32)),
+        out_shape=(jax.ShapeDtypeStruct((n, n), BF16), jax.ShapeDtypeStruct((n, B), F32), TOKEN),
         in_specs=[SM, VM, VM],
-        out_specs=(VM, VM),
+        out_specs=(HBM, HBM, VM),
         scratch_shapes=[
             pltpu.VMEM((n, n), BF16),
             pltpu.VMEM((n, B), F32),
+            pltpu.VMEM((n, n), BF16),
+            pltpu.VMEM((n, B), F32),
             pltpu.VMEM((2 * B, B), BF16),
+            pltpu.SemaphoreType.DMA((2, n // B)),
         ],
-        compiler_params=params(14),
+        compiler_params=params(56),
         cost_estimate=cost(57),
         name="cholesky",
     )(core, mine, other)
 
 
-def solve_into(rhs, m, low_ref, inv_ref, out_ref):
+def solve_into(rhs, m, low_hbm, inv_hbm, out_ref, low_ref, inv_ref, sem):
     nb = low_ref.shape[0] // B
+    copies = [pltpu.make_async_copy(inv_hbm, inv_ref, sem.at[0])]
+    for b in range(1, nb):
+        part = (slice(b * B, (b + 1) * B), slice(0, b * B))
+        copies.append(pltpu.make_async_copy(low_hbm.at[part], low_ref.at[part], sem.at[b]))
+    for copy in copies:
+        copy.start()
 
     def stacked(x):
         return jnp.concatenate(split(x), 0)
@@ -264,16 +298,19 @@
     def fold(p):
         return p[:m] + p[m:]
 
-    acc = [rhs(b) for b in range(nb)]
+    acc, ys = [], []
     for b in range(nb):
         r0, r1 = b * B, (b + 1) * B
-        w = stacked(inv_ref[r0:r1, :])
-        p = fold(dot(stacked(acc[b]), w))
+        copies[b].wait()
+        s = rhs(b)
+        if b > 1:
+            s = s - fold(dot(jnp.concatenate(ys[:-1], 1), low_ref[r0:r1, : r0 - B]))
+        if b:
+            s = s - fold(dot(ys[-1], low_ref[r0:r1, r0 - B : r0]))
+        p = fold(dot(stacked(s), stacked(inv_ref[r0:r1, :])))
         y = p[:, :B] + p[:, B:]
-        acc[b] = y
-        ys = stacked(y)
-        for c in range(b + 1, nb):
-            acc[c] = acc[c] - fold(dot(ys, low_ref[c * B : (c + 1) * B, r0:r1]))
+        acc.append(y)
+        ys.append(stacked(y))
     for b in reversed(range(nb)):
         r0, r1 = b * B, (b + 1) * B
         w = jnp.concatenate(split(inv_ref[r0:r1, :]), 1)
@@ -285,23 +322,28 @@
             acc[c] = acc[c] - fold(dot(zs, low_ref[r0:r1, c * B : (c + 1) * B], NN))
 
 
-def solve_kernel(rhs_ref, low_ref, inv_ref, after_ref, out_ref):
-    solve_into(lambda b: rhs_ref[:, b * B : (b + 1) * B], rhs_ref.shape[0], low_ref, inv_ref, out_ref)
+def solve_scratch(n):
+    return [pltpu.VMEM((n, n), BF16), pltpu.VMEM((n, B), F32), pltpu.SemaphoreType.DMA((n // B,))]
+
+
+def solve_kernel(rhs_ref, low_ref, inv_ref, after_ref, out_ref, *scratch):
+    solve_into(lambda b: rhs_ref[:, b * B : (b + 1) * B], rhs_ref.shape[0], low_ref, inv_ref, out_ref, *scratch)
 
 
 def solve(rhs, low, inv, after):
     return pl.pallas_call(
         solve_kernel,
         out_shape=jax.ShapeDtypeStruct(rhs.shape, F32),
-        in_specs=[VM] * 3 + [ANY],
+        in_specs=[VM, HBM, HBM, ANY],
         out_specs=VM,
-        compiler_params=params(8),
+        scratch_shapes=solve_scratch(low.shape[0]),
+        compiler_params=params(56),
         cost_estimate=cost(7),
         name="solve",
     )(rhs, low, inv, after)
 
 
-def route_kernel(block, owner_ref, first_ref, last_ref, low_ref, inv_ref, out_ref, t_ref, r_ref):
+def route_kernel(block, owner_ref, first_ref, last_ref, low_ref, inv_ref, out_ref, t_ref, r_ref, *scratch):
     n = low_ref.shape[0]
     m, wide = first_ref.shape
 
@@ -309,7 +351,7 @@
         at = b * B
         return first_ref[:, at : at + B] if at < wide else last_ref[:, at - (n - wide) : at - (n - wide) + B]
 
-    solve_into(rhs, m, low_ref, inv_ref, t_ref)
+    solve_into(rhs, m, low_ref, inv_ref, t_ref, *scratch)
     t_ref[:, n:] = jnp.zeros((m, t_ref.shape[1] - n), F32)
     lane = lax.broadcasted_iota(jnp.int32, (m, 2 * B), 1)
     for h in range(2):
@@ -329,35 +371,36 @@
     return pl.pallas_call(
         functools.partial(route_kernel, block),
         out_shape=jax.ShapeDtypeStruct((2, m, wide), F32),
-        in_specs=[SM] + [VM] * 4,
+        in_specs=[SM, VM, VM, HBM, HBM],
         out_specs=VM,
-        scratch_shapes=[pltpu.VMEM((m, n + B), F32), pltpu.VMEM((2, m, wide + B), F32)],
-        compiler_params=params(8),
+        scratch_shapes=[pltpu.VMEM((m, n + B), F32), pltpu.VMEM((2, m, wide + B), F32)] + solve_scratch(n),
+        compiler_params=params(56),
         cost_estimate=cost(9),
         name="solve_and_route",
     )(owner, first, last, low, inv)
 
 
-def sum_kernel(parts_ref, after_ref, out_ref):
+def sum_kernel(parts_ref, *refs):
+    out_ref = refs[-1]
     acc = parts_ref[0]
     for k in range(1, parts_ref.shape[0]):
         acc = acc + parts_ref[k]
     out_ref[...] = acc
 
 
-def sum_parts(parts, after):
+def sum_parts(parts, *after):
     return pl.pallas_call(
         sum_kernel,
         out_shape=jax.ShapeDtypeStruct(parts.shape[1:], F32),
-        in_specs=[VM, ANY],
+        in_specs=[VM] + [ANY] * len(after),
         out_specs=VM,
-        compiler_params=params(8),
+        compiler_params=params(24),
         cost_estimate=cost(3),
         name="sum_parts",
-    )(parts, after)
-
-
-def rows_kernel(at_ref, core_ref, mine_ref, other_ref, diag_ref, out_ref, s_ref):
+    )(parts, *after)
+
+
+def rows_kernel(at_ref, core_ref, mine_ref, other_ref, out_ref, s_ref):
     m, n = out_ref.shape
     nb = n // B
     first = core_ref[0] == 0
@@ -373,22 +416,20 @@
     out = window[:m]
     for k in range(1, 8):
         out = jnp.where(shift == k, window[k : k + m], out)
-    ri = lax.broadcasted_iota(jnp.int32, (m, n), 0)
-    ci = lax.broadcasted_iota(jnp.int32, (m, n), 1)
-    out_ref[...] = jnp.where(ci == ri + at, diag_ref[...], out)
-
-
-def rows_of(at, core, mine, other, diag, n, m):
+    out_ref[...] = out
+
+
+def rows_of(at, core, mine, other, n, m):
     return pl.pallas_call(
         rows_kernel,
         out_shape=jax.ShapeDtypeStruct((m, n), F32),
-        in_specs=[SM, SM, VM, VM, VM],
+        in_specs=[SM, SM, VM, VM],
         out_specs=VM,
         scratch_shapes=[pltpu.VMEM((n + 8, n), F32)],
-        compiler_params=params(12),
+        compiler_params=params(40),
         cost_estimate=cost(3),
         name="rows",
-    )(at, core, mine, other, diag)
+    )(at, core, mine, other)
 
 
 def per_device(attn_out, out_grad, image_counts, column_owner, damping):
@@ -418,11 +459,17 @@
     both = ("grp", "dp")
     half = per_dev // 2
 
-    own = jnp.stack([jnp.where(is_a, attn_out, out_grad), jnp.where(is_a, out_grad, attn_out)])
-    from_near = lax.ppermute(own[::-1, :half], both, near)
-    from_far = lax.ppermute(own[::-1, half:], both, far)
-    pieces = [own, lax.ppermute(own, "dp", swap_core), from_near, from_far]
-    pieces += [lax.ppermute(from_near, "dp", swap_core), lax.ppermute(from_far, "dp", swap_core)]
+    first = jnp.where(is_a, attn_out, out_grad)
+    second = jnp.where(is_a, out_grad, attn_out)
+
+    def around(own, sent):
+        mate = lax.ppermute(own, "dp", swap_core)
+        from_near = lax.ppermute(sent[:half], both, near)
+        from_far = lax.ppermute(sent[half:], both, far)
+        near_mate = lax.ppermute(from_near, "dp", swap_core)
+        return [own, mate, from_near, from_far, near_mate, lax.ppermute(from_far, "dp", swap_core)]
+
+    mine_rows = around(first, second)
     over, mate, away = 1 - grp_index, dp_index ^ 1, dp_index ^ flip
     keeps = jnp.stack([
         keep_of(grp_index, dp_index),
@@ -433,15 +480,12 @@
         keep_of(over, away ^ 1),
     ])
     total = (TOK * jnp.sum(image_counts)).astype(F32)
-    part, gram_done = gram(core_arr, keeps, pieces, chips * per_chip)
+    part, squares = gram(core_arr, keeps, mine_rows, chips * per_chip)
     got = lax.all_to_all(
         part.reshape(chips, per_chip * SLAB, B), "dp", split_axis=0, concat_axis=0, tiled=True, axis_index_groups=same_core
     )
-
-    wide = (nb + 2) // 2 * B
-    part_w, cross_done = cross(core_arr, grp_index.astype(jnp.int32)[None], keeps, gram_done, pieces, chips, wide)
-
-    slabs = sum_parts(got, cross_done) / total
+    other_rows = around(second, first)
+    slabs = sum_parts(got, *[rows[:SLAB, :B] for rows in other_rows[1:]]) / total
 
     flat = chip * (per_chip * SLAB) + jnp.arange(per_chip * SLAB)
     t = flat // HALF
@@ -455,24 +499,20 @@
     spread = jnp.broadcast_to(damped[None], (chips,) + damped.shape)
     mine = lax.all_to_all(spread, "dp", split_axis=0, concat_axis=0, tiled=True, axis_index_groups=same_core)
     mine = mine.reshape(chips * per_chip * SLAB, B)
+    wide = (nb + 2) // 2 * B
+    part_w = cross(core_arr, grp_index.astype(jnp.int32)[None], keeps, damped[:SLAB], mine_rows, other_rows, chips, wide)
+    mine, part_w = lax.optimization_barrier((mine, part_w))
     theirs = lax.ppermute(mine, "dp", swap_core)
-    low, inv = chol(core_arr, mine, theirs, width)
+    low, inv, chol_done = chol(core_arr, mine, theirs, width)
 
     got_w = lax.all_to_all(part_w, "dp", split_axis=0, concat_axis=0, tiled=True, axis_index_groups=same_core)
 
-    pad = 256 - per_chip * SLAB
-    diags = jnp.pad(jnp.sum(slabs * diag.astype(F32), axis=1), (0, pad)).reshape(2, B)
-    diags = lax.all_gather(diags, "dp", axis=0, tiled=False).reshape(chips, 2, 256)[:, :, : per_chip * SLAB]
-    diags = diags.transpose(1, 0, 2).reshape(2, -1)
-    my_diag = jnp.concatenate([diags[c, tri(i, i) * HALF : tri(i, i) * HALF + HALF] for i in range(nb) for c in range(2)])[None]
     at = (dp_index * block).astype(jnp.int32)[None]
-    my_rows = rows_of(at, core_arr, mine, theirs, my_diag, width, ROWS)[:block]
-    their_rows = lax.ppermute(my_rows, "grp", swap_grp)
-    factors = jnp.stack([jnp.where(is_a, my_rows, their_rows), jnp.where(is_a, their_rows, my_rows)])
+    my_rows = rows_of(at, core_arr, mine, theirs, width, ROWS)
 
     order = column_owner.reshape(chips, 2)
     order = jnp.stack([jnp.where(core == 0, order[:, 0], order[:, 1]), jnp.where(core == 0, order[:, 1], order[:, 0])])
-    my_w = sum_parts(got_w, inv) / total
+    my_w = sum_parts(got_w, chol_done) / total
     last_w = lax.ppermute(my_w, "grp", [(1, 0)])
     routed = solve_and_route(order, my_w, last_w, low, inv, block)
     same = lax.ppermute(routed[0], both, [(d, n_dp + d) for d in range(n_dp)])
@@ -480,10 +520,17 @@
     is_first = core == 0
     pair = jnp.concatenate([jnp.where(is_first, same, cross_t), jnp.where(is_first, cross_t, same)])
     pair = pair[:, : chips * block].reshape(2 * ROWS, chips, block).transpose(1, 2, 0)
+    squares = lax.dynamic_index_in_dim(squares[0].reshape(chips, 2, block), core, 1, keepdims=False)
+    pair = jnp.concatenate([pair, squares[:, :, None]], axis=2)
     columns = lax.all_to_all(pair, "dp", split_axis=0, concat_axis=0, tiled=True, axis_index_groups=same_core)
-    columns = columns.transpose(1, 0, 2).reshape(block, n_dp * ROWS)[:, :width]
+    squares = jnp.sum(columns[:, :, 2 * ROWS], axis=0) / total
+    columns = columns[:, :, : 2 * ROWS].transpose(1, 0, 2).reshape(block, n_dp * ROWS)[:, :width]
     columns = jnp.pad(columns, ((0, ROWS - block), (0, 0)))
     left = solve(columns, low, inv, my_rows)[:block]
+    here = (dp_index * block + jnp.arange(block))[:, None] == jnp.arange(width)[None, :]
+    my_rows = jnp.where(here, squares[:, None], my_rows[:block])
+    their_rows = lax.ppermute(my_rows, "grp", swap_grp)
+    factors = jnp.stack([jnp.where(is_a, my_rows, their_rows), jnp.where(is_a, their_rows, my_rows)])
     back = lax.ppermute(left, "grp", [(1, 0)])
     preconditioned = jnp.where(is_a, back, left).T
     return (factors, preconditioned)

time: 343 us -> 235 us (0.69)
  blocking collectives: 147 us -> 0 us
  starting transfers between devices: 26.8 us -> 49.4 us
  waiting for transfers between devices: 56.8 us -> 71.4 us
  local copies, waits for them, and re-layouts: 27.7 us -> 15.7 us
  Pallas kernels: 72.1 us -> 82.7 us
    all_gather x1 -> x0, blocking collectives: 122 us -> none  [per_device(): lax.all_gather(diags, 'dp', axis=0, tiled=False).reshape(chips, 2, 256)]
    all_to_all x1 -> x0, blocking collectives: 25.8 us -> none  [per_device(): lax.all_to_all(spread, 'dp', split_axis=0, concat_axis=0, tiled=True, axi...]
    ppermute x5 -> x10, waiting for transfers between devices: 16.8 us -> 41.6 us  [the longest x2 37.6 us: around(): from_near = lax.ppermute(sent[:half], both, near)]
    all_to_all x1, waiting for transfers between devices: 21.9 us -> 0.01 us  [per_device(): lax.all_to_all(part.reshape(chips, per_chip * SLAB, B), 'dp', split_axis=...]
    all_to_all x0 -> x1, waiting for transfers between devices: none -> 12.4 us  [per_device(): lax.all_to_all(spread, 'dp', split_axis=0, concat_axis=0, tiled=True, axi...]
    unnamed x33 -> x35, local copies, waits for them, and re-layouts: 15.5 us -> 4.38 us
    all_to_all x0 -> x1, starting transfers between devices: none -> 9.71 us  [per_device(): lax.all_to_all(spread, 'dp', split_axis=0, concat_axis=0, tiled=True, axi...]
    all_to_all x1, starting transfers between devices: 3.86 us -> 9.82 us  [per_device(): lax.all_to_all(pair, 'dp', split_axis=0, concat_axis=0, tiled=True, axis_...]
  transfers between devices with their start and end apart: 14 -> 20, of which waited for: 7 -> 10; matrix products, arithmetic and copies ran while one was open for 4% -> 5% of each run, Pallas kernels for 16% -> 28%
where the time goes in v5:
time: 235 us; the launch traced here: 234 us
  Pallas kernels  82.7 us (35%)
  waiting for transfers between devices  71.4 us (30%)
  starting transfers between devices  49.4 us (21%)
  local copies, waits for them, and re-layouts  15.7 us (7%)
  other arithmetic  7.79 us (3%)
  between operations  6.93 us (3%)
    pallas_call x1, Pallas kernels, chol(): pl.pallas_call(chol_kernel, out_shape=(jax.ShapeDtypeStruct((n, n), BF16)...  47.6 us
    ppermute x2, waiting for transfers between devices, around(): from_near = lax.ppermute(sent[:half], both, near)  37.6 us
    all_to_all x1, waiting for transfers between devices, per_device(): lax.all_to_all(spread, 'dp', split_axis=0, concat_axis=0, tiled=True, axi...  12.4 us
    pallas_call x1, Pallas kernels, solve_and_route(): pl.pallas_call(functools.partial(route_kernel, block), out_shape=jax.Shap...  10.3 us
    all_to_all x1, starting transfers between devices, per_device(): lax.all_to_all(pair, 'dp', split_axis=0, concat_axis=0, tiled=True, axis_...  9.82 us
    all_to_all x1, starting transfers between devices, per_device(): lax.all_to_all(spread, 'dp', split_axis=0, concat_axis=0, tiled=True, axi...  9.71 us
    pallas_call x1, Pallas kernels, solve(): pl.pallas_call(solve_kernel, out_shape=jax.ShapeDtypeStruct(rhs.shape, F3...  9.57 us
    all_to_all x1, starting transfers between devices, per_device(): lax.all_to_all(part.reshape(chips, per_chip * SLAB, B), 'dp', split_axis=...  9.3 us
  transfers between devices with their start and end apart: 20, of which 10 were waited for; matrix products, arithmetic and copies ran while one was open for 5% of the time, Pallas kernels for 28%

profile of v5, /device:TPU:0, one launch (start us, length us, event | category | flops | bytes accessed | tf_op | source)
XLA Modules:
  0.0 233.9 jit_solution(15578498820591092777)
XLA Ops:
  0.6 1.5 broadcast_select_fusion
  2.3 1.7 collective-permute-start.1
  3.9 2.1 collective-permute-start.2
  6.0 7.1 %collective-permute-done.1.refs_2_ = bf16[128,1408]{1,0:T(8,128)(2,1)S(1)} collective-permute-done((bf16[128,1408]{1,0:T(8,128)(2,1)S(1)}, bf16[128,1408]{1,0:T(8,128)(2,1)S(1)}, u32[]{:S(2)}, u32[]{:S(2)}) %collective-permute-start.1) | collective-permute-done | bytes 360480 | tf_op jit(solution)/shard_map/ppermute | solution.py:467
  13.2 2.5 %collective-permute-done.2.refs_3_ = bf16[128,1408]{1,0:T(8,128)(2,1)S(1)} collective-permute-done((bf16[128,1408]{1,0:T(8,128)(2,1)S(1)}, bf16[128,1408]{1,0:T(8,128)(2,1)S(1)}, u32[]{:S(2)}, u32[]{:S(2)}) %collective-permute-start.2) | collective-permute-done | bytes 360480 | tf_op jit(solution)/shard_map/ppermute | solution.py:468
  15.7 0.7 fusion.6
  21.0 0.8 copy-done.11
  22.0 6.0 %gram.1 = (f32[4608,128]{1,0:T(8,128)}, f32[8,1408]{1,0:T(8,128)}) custom-call(s32[1]{0:T(128)} %bitcast.core_ref, f32[6]{0:T(128)} %stack.27.keep_ref, bf16[256,1408]{1,0:T(8,128)(2,1)} %copy-done.5, bf16[256,1408]{1,0:T(8,128)(2,1)} %copy-done.11, bf16[128,1408]{1,0:T(8,128)(2,1)} %copy-done.12, bf16[128,1408]{1,0:T(8,128)(2,1)} %copy-done.13, ...), custom_call_target="tpu_custom_call" | custom-call | flops 4400000000 | bytes 1048576 | tf_op jit(solution)/shard_map/gram/pallas_call | solution.py:104
  28.0 9.3 %all-to-all-start = ((f32[32,144,128]{2,1,0:T(8,128)}), f32[32,144,128]{2,1,0:T(8,128)S(1)}, u32[]{:S(2)}, u32[]{:S(2)}) async-start(f32[32,144,128]{2,1,0:T(8,128)} %bitcast.29), calls=%async_computation | async-start | bytes 4718592 | tf_op jit(solution)/shard_map/all_to_all | solution.py:484
  37.6 1.1 fusion.3
  38.7 1.5 collective-permute-start.6
  40.3 2.4 %collective-permute-start.7 = (bf16[128,1408]{1,0:T(8,128)(2,1)S(1)}, bf16[128,1408]{1,0:T(8,128)(2,1)}, u32[]{:S(2)}, u32[]{:S(2)}) collective-permute-start(bf16[128,1408]{1,0:T(8,128)(2,1)S(1)} %get-tuple-element.24), channel_id=1, source_target_pairs={{0,96},{1,97},{2,98},{3,99},{4,100},{5,101},{6,102},{7,103},{8,104... | collective-permute-start | bytes 1081352 | tf_op jit(solution)/shard_map/ppermute | solution.py:468
  42.6 30.5 %collective-permute-done.6.refs_8_ = bf16[128,1408]{1,0:T(8,128)(2,1)S(1)} collective-permute-done((bf16[128,1408]{1,0:T(8,128)(2,1)S(1)}, bf16[128,1408]{1,0:T(8,128)(2,1)S(1)}, u32[]{:S(2)}, u32[]{:S(2)}) %collective-permute-start.6) | collective-permute-done | bytes 360480 | tf_op jit(solution)/shard_map/ppermute | solution.py:467
  73.1 1.4 collective-permute-done.7.refs_9_
  74.6 0.6 reduce_sum.18
  77.8 0.7 slice.102.refs_2_
  78.5 0.7 slice.98.refs_0_
  79.2 0.7 slice.103.refs_3_
  79.9 0.7 slice.104.refs_4_
  81.4 1.3 broadcast_in_dim.16
  82.7 9.7 %all-to-all-start.1 = ((bf16[32,144,128]{2,1,0:T(8,128)(2,1)}), bf16[32,144,128]{2,1,0:T(8,128)(2,1)S(1)}, u32[]{:S(2)}, u32[]{:S(2)}) async-start(bf16[32,144,128]{2,1,0:T(8,128)(2,1)} %broadcast_in_dim.16), calls=%async_computation.1 | async-start | bytes 2359296 | tf_op jit(solution)/shard_map/all_to_all | solution.py:500
  92.4 6.9 %cross.1 = f32[32,24,768]{2,1,0:T(8,128)} custom-call(s32[1]{0:T(128)} %bitcast.core_ref, s32[1]{0:T(128)} %bitcast.5.grp_ref, f32[6]{0:T(128)} %stack.27.keep_ref, bf16[16,128]{1,0:T(8,128)(2,1)} %slice.105.after_ref, bf16[256,1408]{1,0:T(8,128)(2,1)} %copy-done.5, bf16[256,1408]{1,0:T(8,128)(2,1)} %copy-done.11, bf16[128,1408]{1,0:T(8,128)(2,1)} %copy-done.12, ...), custom_call_target="tpu_custom_call" | custom-call | flops 32999999488 | bytes 1048576 | tf_op jit(solution)/shard_map/cross/pallas_call | solution.py:141
  99.3 12.4 %all-to-all-done.1 = bf16[32,144,128]{2,1,0:T(8,128)(2,1)S(1)} async-done(((bf16[32,144,128]{2,1,0:T(8,128)(2,1)}), bf16[32,144,128]{2,1,0:T(8,128)(2,1)S(1)}, u32[]{:S(2)}, u32[]{:S(2)}) %all-to-all-start.1) | async-done | bytes 1179680 | tf_op jit(solution)/shard_map/all_to_all | solution.py:500
  111.9 0.7 pad_add_fusion.owner_ref
  112.6 5.4 %all-to-all-start.2 = ((f32[32,24,768]{2,1,0:T(8,128)}), f32[32,24,768]{2,1,0:T(8,128)S(1)}, u32[]{:S(2)}, u32[]{:S(2)}) async-start(f32[32,24,768]{2,1,0:T(8,128)} %cross.1), calls=%async_computation.2 | async-start | bytes 4718592 | tf_op jit(solution)/shard_map/all_to_all | solution.py:508
  118.0 47.6 %cholesky.1 = (bf16[1408,1408]{1,0:T(8,128)(2,1)}, f32[1408,128]{1,0:T(8,128)}, f32[8,128]{1,0:T(8,128)}) custom-call(s32[1]{0:T(128)} %bitcast.core_ref, bf16[4608,128]{1,0:T(8,128)(2,1)} %bitcast.27, bf16[4608,128]{1,0:T(8,128)(2,1)} %collective-permute-done.10.other_ref), custom_call_target="tpu_custom_call" | custom-call | flops 62699999232 | bytes 1048576 | tf_op jit(solution)/shard_map/cholesky/pallas_call | solution.py:267
  165.7 0.7 copy-done.3
  166.5 1.5 collective-permute-start.11
  168.0 0.8 slice_reduce_fusion.1
  169.0 3.8 %collective-permute-done.11.last_ref = f32[24,768]{1,0:T(8,128)S(1)} collective-permute-done((f32[24,768]{1,0:T(8,128)S(1)}, f32[24,768]{1,0:T(8,128)S(1)}, u32[]{:S(2)}, u32[]{:S(2)}) %collective-permute-start.11) | collective-permute-done | bytes 73760 | tf_op jit(solution)/shard_map/ppermute | solution.py:516
  173.4 10.3 %solve_and_route.1 = f32[2,24,768]{2,1,0:T(8,128)} custom-call(s32[2,32]{1,0:T(2,128)} %pad_add_fusion.owner_ref, f32[24,768]{1,0:T(8,128)} %copy-done.6, f32[24,768]{1,0:T(8,128)} %copy-done.15, bf16[1408,1408]{1,0:T(8,128)(2,1)} %get-tuple-element.13.low_ref, f32[1408,128]{1,0:T(8,128)} %get-tuple-element.14.inv_ref), custom_call_target="tpu_custom_call" | custom-call | flops 9900000256 | bytes 1048576 | tf_op jit(solution)/shard_map/solve_and_route/pallas_call | solution.py:371
  183.6 1.0 slice_bitcast_fusion.2
  184.7 1.6 collective-permute-start.12
  186.2 1.3 collective-permute-start.13
  188.2 1.5 collective-permute-done.13
  190.1 1.0 reshape.154
  191.1 9.8 %all-to-all-start.3 = ((f32[32,1,1078]{2,1,0:T(1,128)}), f32[32,1,1078]{2,1,0:T(1,128)S(1)}, u32[]{:S(2)}, u32[]{:S(2)}) async-start(f32[32,1,1078]{2,1,0:T(1,128)} %reshape.154), calls=%async_computation.3 | async-start | bytes 294912 | tf_op jit(solution)/shard_map/all_to_all | solution.py:525
  200.9 2.1 rows.1.after_ref
  203.0 8.0 %all-to-all-done.3 = f32[32,1,1078]{2,1,0:T(1,128)S(1)} async-done(((f32[32,1,1078]{2,1,0:T(1,128)}), f32[32,1,1078]{2,1,0:T(1,128)S(1)}, u32[]{:S(2)}, u32[]{:S(2)}) %all-to-all-start.3) | async-done | bytes 138016 | tf_op jit(solution)/shard_map/all_to_all | solution.py:525
  211.5 1.0 reduce.7
  213.1 1.5 collective-permute-start.14
  215.0 0.7 pad.4.rhs_ref
  215.6 9.6 %solve.1 = f32[24,1408]{1,0:T(8,128)} custom-call(f32[24,1408]{1,0:T(8,128)} %pad.4.rhs_ref, bf16[1408,1408]{1,0:T(8,128)(2,1)} %get-tuple-element.13.low_ref, f32[1408,128]{1,0:T(8,128)} %get-tuple-element.14.inv_ref, f32[24,1408]{1,0:T(8,128)} %copy-done.2), custom_call_target="tpu_custom_call" | custom-call | flops 7699999744 | bytes 1048576 | tf_op jit(solution)/shard_map/solve/pallas_call | solution.py:334
  225.2 1.3 collective-permute-start.15
  226.5 1.0 select_bitcast_fusion.2
  227.6 0.8 copy.14
  228.4 3.9 %collective-permute-done.15 = f32[22,1408]{1,0:T(8,128)S(1)} collective-permute-done((f32[22,1408]{1,0:T(8,128)}, f32[22,1408]{1,0:T(8,128)S(1)}, u32[]{:S(2)}, u32[]{:S(2)}) %collective-permute-start.15) | collective-permute-done | bytes 123936 | tf_op jit(solution)/shard_map/ppermute | solution.py:534
  232.3 1.6 select_bitcast_fusion
  (81 shorter events, 6.4 us)
Async XLA Ops:
  0.6 15.1 %copy-start.7 = (s32[128]{0:T(128)S(1)}, s32[128]{0:T(128)}, u32[]{:S(2)}) copy-start(s32[128]{0:T(128)} %param.7) | copy-start | bytes 1540
  2.1 18.8 %copy-start.5 = (bf16[256,1408]{1,0:T(8,128)(2,1)}, bf16[256,1408]{1,0:T(8,128)(2,1)S(1)}, u32[]{:S(2)}) copy-start(bf16[256,1408]{1,0:T(8,128)(2,1)S(1)} %get-tuple-element.23.refs_0_) | copy-start | bytes 2162692
  2.1 35.2 %copy-start.4 = (bf16[256,1408]{1,0:T(8,128)(2,1)}, bf16[256,1408]{1,0:T(8,128)(2,1)S(1)}, u32[]{:S(2)}) copy-start(bf16[256,1408]{1,0:T(8,128)(2,1)S(1)} %get-tuple-element.22.refs_6_) | copy-start | bytes 2162692
  2.1 18.8 %collective-permute-start = (bf16[256,1408]{1,0:T(8,128)(2,1)S(1)}, bf16[256,1408]{1,0:T(8,128)(2,1)S(1)}, u32[]{:S(2)}, u32[]{:S(2)}) collective-permute-start(bf16[256,1408]{1,0:T(8,128)(2,1)S(1)} %get-tuple-element.23.refs_0_), channel_id=1, source_target_pairs={{0,1},{1,0},{2,3},{3,2},{4,5},{5,4},{6,7},{7,6},{8,9},{9,8},{10,11... | collective-permute-start | bytes 2162696 | tf_op jit(solution)/shard_map/ppermute | solution.py:466
  2.3 10.9 %collective-permute-start.1 = (bf16[128,1408]{1,0:T(8,128)(2,1)S(1)}, bf16[128,1408]{1,0:T(8,128)(2,1)S(1)}, u32[]{:S(2)}, u32[]{:S(2)}) collective-permute-start(bf16[128,1408]{1,0:T(8,128)(2,1)S(1)} %get-tuple-element.27), channel_id=1, source_target_pairs={{0,64},{1,65},{2,66},{3,67},{4,68},{5,69},{6,70},{7,71},{8,72},{9,... | collective-permute-start | bytes 1081352 | tf_op jit(solution)/shard_map/ppermute | solution.py:467
  3.9 11.7 %collective-permute-start.2 = (bf16[128,1408]{1,0:T(8,128)(2,1)S(1)}, bf16[128,1408]{1,0:T(8,128)(2,1)S(1)}, u32[]{:S(2)}, u32[]{:S(2)}) collective-permute-start(bf16[128,1408]{1,0:T(8,128)(2,1)S(1)} %get-tuple-element.26), channel_id=1, source_target_pairs={{0,96},{1,97},{2,98},{3,99},{4,100},{5,101},{6,102},{7,103},{8,104... | collective-permute-start | bytes 1081352 | tf_op jit(solution)/shard_map/ppermute | solution.py:468
  13.2 7.8 %copy-start.12 = (bf16[128,1408]{1,0:T(8,128)(2,1)}, bf16[128,1408]{1,0:T(8,128)(2,1)S(1)}, u32[]{:S(2)}) copy-start(bf16[128,1408]{1,0:T(8,128)(2,1)S(1)} %collective-permute-done.1.refs_2_) | copy-start | bytes 1081348
  13.2 7.7 %collective-permute-start.3 = (bf16[128,1408]{1,0:T(8,128)(2,1)S(1)}, bf16[128,1408]{1,0:T(8,128)(2,1)S(1)}, u32[]{:S(2)}, u32[]{:S(2)}) collective-permute-start(bf16[128,1408]{1,0:T(8,128)(2,1)S(1)} %collective-permute-done.1.refs_2_), channel_id=1, source_target_pairs={{0,1},{1,0},{2,3},{3,2},{4,5},{5,4},{6,7},{7,6},{8,9},{9,8},{10,11... | collective-permute-start | bytes 1081352 | tf_op jit(solution)/shard_map/ppermute | solution.py:469
  15.7 5.3 %copy-start.13 = (bf16[128,1408]{1,0:T(8,128)(2,1)}, bf16[128,1408]{1,0:T(8,128)(2,1)S(1)}, u32[]{:S(2)}) copy-start(bf16[128,1408]{1,0:T(8,128)(2,1)S(1)} %collective-permute-done.2.refs_3_) | copy-start | bytes 1081348
  15.7 5.3 %collective-permute-start.4 = (bf16[128,1408]{1,0:T(8,128)(2,1)S(1)}, bf16[128,1408]{1,0:T(8,128)(2,1)}, u32[]{:S(2)}, u32[]{:S(2)}) collective-permute-start(bf16[128,1408]{1,0:T(8,128)(2,1)S(1)} %collective-permute-done.2.refs_3_), channel_id=1, source_target_pairs={{0,1},{1,0},{2,3},{3,2},{4,5},{5,4},{6,7},{7,6},{8,9},{9,8},{10,11... | collective-permute-start | bytes 1081352 | tf_op jit(solution)/shard_map/ppermute | solution.py:470
  20.9 0.9 copy-start.11
  20.9 1.0 copy-start.14
  28.0 47.9 %copy-start.8 = (f32[2]{0:T(128)S(1)}, f32[2]{0:T(128)}, u32[]{:S(2)}) copy-start(f32[2]{0:T(128)} %param.9) | copy-start | bytes 28
  28.0 52.5 %all-to-all-start = ((f32[32,144,128]{2,1,0:T(8,128)}), f32[32,144,128]{2,1,0:T(8,128)S(1)}, u32[]{:S(2)}, u32[]{:S(2)}) async-start(f32[32,144,128]{2,1,0:T(8,128)} %bitcast.29), calls=%async_computation | async-start | bytes 4718592 | tf_op jit(solution)/shard_map/all_to_all | solution.py:484
  37.3 41.2 %collective-permute-start.5 = (bf16[256,1408]{1,0:T(8,128)(2,1)S(1)}, bf16[256,1408]{1,0:T(8,128)(2,1)}, u32[]{:S(2)}, u32[]{:S(2)}) collective-permute-start(bf16[256,1408]{1,0:T(8,128)(2,1)S(1)} %get-tuple-element.22.refs_6_), channel_id=1, source_target_pairs={{0,1},{1,0},{2,3},{3,2},{4,5},{5,4},{6,7},{7,6},{8,9},{9,8},{10,11... | collective-permute-start | bytes 2162696 | tf_op jit(solution)/shard_map/ppermute | solution.py:466
  38.7 34.4 %collective-permute-start.6 = (bf16[128,1408]{1,0:T(8,128)(2,1)S(1)}, bf16[128,1408]{1,0:T(8,128)(2,1)S(1)}, u32[]{:S(2)}, u32[]{:S(2)}) collective-permute-start(bf16[128,1408]{1,0:T(8,128)(2,1)S(1)} %get-tuple-element.25), channel_id=1, source_target_pairs={{0,64},{1,65},{2,66},{3,67},{4,68},{5,69},{6,70},{7,71},{8,72},{9,... | collective-permute-start | bytes 1081352 | tf_op jit(solution)/shard_map/ppermute | solution.py:467
  40.3 34.3 %collective-permute-start.7 = (bf16[128,1408]{1,0:T(8,128)(2,1)S(1)}, bf16[128,1408]{1,0:T(8,128)(2,1)}, u32[]{:S(2)}, u32[]{:S(2)}) collective-permute-start(bf16[128,1408]{1,0:T(8,128)(2,1)S(1)} %get-tuple-element.24), channel_id=1, source_target_pairs={{0,96},{1,97},{2,98},{3,99},{4,100},{5,101},{6,102},{7,103},{8,104... | collective-permute-start | bytes 1081352 | tf_op jit(solution)/shard_map/ppermute | solution.py:468
  73.1 7.5 %copy-start.10 = (bf16[128,1408]{1,0:T(8,128)(2,1)}, bf16[128,1408]{1,0:T(8,128)(2,1)S(1)}, u32[]{:S(2)}) copy-start(bf16[128,1408]{1,0:T(8,128)(2,1)S(1)} %collective-permute-done.6.refs_8_) | copy-start | bytes 1081348
  73.1 6.1 %collective-permute-start.8 = (bf16[128,1408]{1,0:T(8,128)(2,1)S(1)}, bf16[128,1408]{1,0:T(8,128)(2,1)}, u32[]{:S(2)}, u32[]{:S(2)}) collective-permute-start(bf16[128,1408]{1,0:T(8,128)(2,1)S(1)} %collective-permute-done.6.refs_8_), channel_id=1, source_target_pairs={{0,1},{1,0},{2,3},{3,2},{4,5},{5,4},{6,7},{7,6},{8,9},{9,8},{10,11... | collective-permute-start | bytes 1081352 | tf_op jit(solution)/shard_map/ppermute | solution.py:469
  74.6 5.3 %collective-permute-start.9 = (bf16[128,1408]{1,0:T(8,128)(2,1)}, bf16[128,1408]{1,0:T(8,128)(2,1)}, u32[]{:S(2)}, u32[]{:S(2)}) collective-permute-start(bf16[128,1408]{1,0:T(8,128)(2,1)} %collective-permute-done.7.refs_9_), channel_id=1, source_target_pairs={{0,1},{1,0},{2,3},{3,2},{4,5},{5,4},{6,7},{7,6},{8,9},{9,8},{10,11... | collective-permute-start | bytes 1081352 | tf_op jit(solution)/shard_map/ppermute | solution.py:470
  82.7 29.0 %all-to-all-start.1 = ((bf16[32,144,128]{2,1,0:T(8,128)(2,1)}), bf16[32,144,128]{2,1,0:T(8,128)(2,1)S(1)}, u32[]{:S(2)}, u32[]{:S(2)}) async-start(bf16[32,144,128]{2,1,0:T(8,128)(2,1)} %broadcast_in_dim.16), calls=%async_computation.1 | async-start | bytes 2359296 | tf_op jit(solution)/shard_map/all_to_all | solution.py:500
  92.4 19.3 %copy-start.9 = (s32[64]{0:T(128)S(1)}, s32[64]{0:T(128)}, u32[]{:S(2)}) copy-start(s32[64]{0:T(128)} %param.8) | copy-start | bytes 772
  111.6 1.0 copy-start
  111.6 6.4 %collective-permute-start.10 = (bf16[4608,128]{1,0:T(8,128)(2,1)S(1)}, bf16[4608,128]{1,0:T(8,128)(2,1)}, u32[]{:S(2)}, u32[]{:S(2)}) collective-permute-start(bf16[4608,128]{1,0:T(8,128)(2,1)S(1)} %bitcast.26), channel_id=1, source_target_pairs={{0,1},{1,0},{2,3},{3,2},{4,5},{5,4},{6,7},{7,6},{8,9},{9,8},{10,11... | collective-permute-start | bytes 3538952 | tf_op jit(solution)/shard_map/ppermute | solution.py:505
  112.6 53.0 %all-to-all-start.2 = ((f32[32,24,768]{2,1,0:T(8,128)}), f32[32,24,768]{2,1,0:T(8,128)S(1)}, u32[]{:S(2)}, u32[]{:S(2)}) async-start(f32[32,24,768]{2,1,0:T(8,128)} %cross.1), calls=%async_computation.2 | async-start | bytes 4718592 | tf_op jit(solution)/shard_map/all_to_all | solution.py:508
  165.6 0.7 copy-start.3
  166.5 6.3 %copy-start.6 = (f32[24,768]{1,0:T(8,128)}, f32[24,768]{1,0:T(8,128)S(1)}, u32[]{:S(2)}) copy-start(f32[24,768]{1,0:T(8,128)S(1)} %broadcast_divide_fusion.first_ref) | copy-start | bytes 221188
  166.5 6.2 %collective-permute-start.11 = (f32[24,768]{1,0:T(8,128)S(1)}, f32[24,768]{1,0:T(8,128)S(1)}, u32[]{:S(2)}, u32[]{:S(2)}) collective-permute-start(f32[24,768]{1,0:T(8,128)S(1)} %broadcast_divide_fusion.first_ref), channel_id=1, source_target_pairs={{64,0},{65,1},{66,2},{67,3},{68,4},{69,5},{70,6},{71,7},{72,8},{73... | collective-permute-start | bytes 221192 | tf_op jit(solution)/shard_map/ppermute | solution.py:516
  172.7 0.6 copy-start.15
  183.6 17.3 %copy-start.1 = (bf16[32,144,128]{2,1,0:T(8,128)(2,1)S(1)}, bf16[32,144,128]{2,1,0:T(8,128)(2,1)}, u32[]{:S(2)}) copy-start(bf16[32,144,128]{2,1,0:T(8,128)(2,1)} %copy-done) | copy-start | bytes 3538948
  184.7 3.5 %collective-permute-start.12 = (f32[24,768]{1,0:T(8,128)S(1)}, f32[24,768]{1,0:T(8,128)S(1)}, u32[]{:S(2)}, u32[]{:S(2)}) collective-permute-start(f32[24,768]{1,0:T(8,128)S(1)} %get-tuple-element.32), channel_id=1, source_target_pairs={{0,64},{1,65},{2,66},{3,67},{4,68},{5,69},{6,70},{7,71},{8,72},{9,... | collective-permute-start | bytes 221192 | tf_op jit(solution)/shard_map/ppermute | solution.py:518
  186.2 3.4 %collective-permute-start.13 = (f32[24,768]{1,0:T(8,128)S(1)}, f32[24,768]{1,0:T(8,128)S(1)}, u32[]{:S(2)}, u32[]{:S(2)}) collective-permute-start(f32[24,768]{1,0:T(8,128)S(1)} %get-tuple-element.33), channel_id=1, source_target_pairs={{0,65},{1,64},{2,67},{3,66},{4,69},{5,68},{6,71},{7,70},{8,73},{9,... | collective-permute-start | bytes 221192 | tf_op jit(solution)/shard_map/ppermute | solution.py:519
  191.1 19.9 %all-to-all-start.3 = ((f32[32,1,1078]{2,1,0:T(1,128)}), f32[32,1,1078]{2,1,0:T(1,128)S(1)}, u32[]{:S(2)}, u32[]{:S(2)}) async-start(f32[32,1,1078]{2,1,0:T(1,128)} %reshape.154), calls=%async_computation.3 | async-start | bytes 294912 | tf_op jit(solution)/shard_map/all_to_all | solution.py:525
  203.0 12.6 %copy-start.2 = (f32[24,1408]{1,0:T(8,128)}, f32[24,1408]{1,0:T(8,128)S(1)}, u32[]{:S(2)}) copy-start(f32[24,1408]{1,0:T(8,128)S(1)} %rows.1.after_ref) | copy-start | bytes 405508
  213.1 13.4 %collective-permute-start.14 = (f32[22,1408]{1,0:T(8,128)S(1)}, f32[22,1408]{1,0:T(8,128)S(1)}, u32[]{:S(2)}, u32[]{:S(2)}) collective-permute-start(f32[22,1408]{1,0:T(8,128)S(1)} %slice_select_fusion), channel_id=1, source_target_pairs={{0,64},{64,0},{1,65},{65,1},{2,66},{66,2},{3,67},{67,3},{4,68},{68... | collective-permute-start | bytes 371720 | tf_op jit(solution)/shard_map/ppermute | solution.py:532
  225.2 7.1 %collective-permute-start.15 = (f32[22,1408]{1,0:T(8,128)}, f32[22,1408]{1,0:T(8,128)S(1)}, u32[]{:S(2)}, u32[]{:S(2)}) collective-permute-start(f32[22,1408]{1,0:T(8,128)} %bitcast.31), channel_id=1, source_target_pairs={{64,0},{65,1},{66,2},{67,3},{68,4},{69,5},{70,6},{71,7},{72,8},{73... | collective-permute-start | bytes 371720 | tf_op jit(solution)/shard_map/ppermute | solution.py:534

commit v6 on v5

--- a/solution.py
+++ b/solution.py
@@ -12,6 +12,7 @@
 HALF = 64
 SLAB = 16
 ROWS = 24
+WIDE = 14336
 F32 = jnp.float32
 BF16 = jnp.bfloat16
 NT = (((1,), (1,)), ((), ()))
@@ -111,43 +112,35 @@
             pltpu.VMEM((B, width), F32),
             pltpu.SemaphoreType.DMA((width // B + 1,)),
         ],
-        compiler_params=params(56),
+        compiler_params=params(24),
         cost_estimate=cost(4),
         name="gram",
     )(core, keeps, *pieces)
 
 
-def cross_kernel(core_ref, grp_ref, keep_ref, after_ref, *refs):
-    mine, other, (out_ref, tmp_ref) = pieces_of(refs[:6]), pieces_of(refs[6:12]), refs[12:]
-    n = refs[0].shape[1]
-    wide = out_ref.shape[2]
-
-    def run(left, right, first):
-        for i in range(n // B):
-            acc = None
-            for lg, rg in zip(left, right):
-                p = dot(columns_of(lg, slice(i * B, (i + 1) * B), keep_ref), columns_of(rg, slice(first, first + wide)), TN)
-                acc = p if acc is None else acc + p
-            tmp_ref[i * B : (i + 1) * B, :] = acc
-
-    pl.when(grp_ref[0] == 0)(lambda: run(other, mine, 0))
-    pl.when(grp_ref[0] == 1)(lambda: run(mine, other, n - wide))
-    tmp_ref[n:, :] = jnp.zeros((tmp_ref.shape[0] - n, wide), F32)
+def cross_kernel(core_ref, keep_ref, after_ref, grad_ref, grad_mate_ref, act_ref, act_mate_ref, out_ref, tmp_ref):
+    n = act_ref.shape[1]
+    for i in range(n // B):
+        cols = slice(i * B, (i + 1) * B)
+        own = dot(grad_ref[:, cols] * keep_ref[0].astype(BF16), act_ref[...], TN)
+        tmp_ref[cols, :] = own + dot(grad_mate_ref[:, cols] * keep_ref[1].astype(BF16), act_mate_ref[...], TN)
+    tmp_ref[n:, :] = jnp.zeros((tmp_ref.shape[0] - n, n), F32)
     for q in range(out_ref.shape[0]):
         out_ref[q] = tmp_ref[pl.ds(pl.multiple_of((2 * q + core_ref[0]) * ROWS, 8), ROWS), :]
 
 
-def cross(core, grp, keeps, after, mine, other, chips, wide):
+def cross(core, keeps, after, grads, acts, chips):
+    width = acts[0].shape[1]
     return pl.pallas_call(
         cross_kernel,
-        out_shape=jax.ShapeDtypeStruct((chips, ROWS, wide), F32),
-        in_specs=[SM, SM, SM, ANY] + [VM] * 12,
+        out_shape=jax.ShapeDtypeStruct((chips, ROWS, width), F32),
+        in_specs=[SM, SM, ANY] + [VM] * 4,
         out_specs=VM,
-        scratch_shapes=[pltpu.VMEM((2 * chips * ROWS, wide), F32)],
-        compiler_params=params(56),
+        scratch_shapes=[pltpu.VMEM((2 * chips * ROWS, width), F32)],
+        compiler_params=params(32),
         cost_estimate=cost(30),
         name="cross",
-    )(core, grp, keeps, after, *mine, *other)
+    )(core, keeps, after, *grads, *acts)
 
 
 def factor_diag(block):
@@ -245,7 +238,7 @@
             pl.when(k == kk)(lambda kk=kk: update(kk))
         r0 = pl.multiple_of(k * B, B)
         rows = pl.ds(r0, B)
-        pltpu.make_async_copy(low_ref.at[rows], low_hbm.at[rows], sem.at[0, k]).start()
+        pltpu.make_async_copy(low_ref.at[rows], low_hbm.at[rows, :n], sem.at[0, k]).start()
         linv, lrinv = factor_diag(s_ref[pl.ds(r0, B), :])
         inv_ref[rows, :] = lrinv
         pltpu.make_async_copy(inv_ref.at[rows], inv_hbm.at[rows], sem.at[1, k]).start()
@@ -259,14 +252,14 @@
     lax.fori_loop(0, nb, step, 0)
     for k in range(nb):
         rows = slice(k * B, (k + 1) * B)
-        pltpu.make_async_copy(low_ref.at[rows], low_hbm.at[rows], sem.at[0, k]).wait()
+        pltpu.make_async_copy(low_ref.at[rows], low_hbm.at[rows, :n], sem.at[0, k]).wait()
         pltpu.make_async_copy(inv_ref.at[rows], inv_hbm.at[rows], sem.at[1, k]).wait()
 
 
 def chol(core, mine, other, n):
     return pl.pallas_call(
         chol_kernel,
-        out_shape=(jax.ShapeDtypeStruct((n, n), BF16), jax.ShapeDtypeStruct((n, B), F32), TOKEN),
+        out_shape=(jax.ShapeDtypeStruct((n, WIDE), BF16), jax.ShapeDtypeStruct((n, B), F32), TOKEN),
         in_specs=[SM, VM, VM],
         out_specs=(HBM, HBM, VM),
         scratch_shapes=[
@@ -277,7 +270,7 @@
             pltpu.VMEM((2 * B, B), BF16),
             pltpu.SemaphoreType.DMA((2, n // B)),
         ],
-        compiler_params=params(56),
+        compiler_params=params(28),
         cost_estimate=cost(57),
         name="cholesky",
     )(core, mine, other)
@@ -285,9 +278,9 @@
 
 def solve_into(rhs, m, low_hbm, inv_hbm, out_ref, low_ref, inv_ref, sem):
     nb = low_ref.shape[0] // B
-    copies = [pltpu.make_async_copy(inv_hbm, inv_ref, sem.at[0])]
-    for b in range(1, nb):
-        part = (slice(b * B, (b + 1) * B), slice(0, b * B))
+    copies = [pltpu.make_async_copy(inv_hbm, inv_ref, sem.at[nb - 1])]
+    for b in range(nb - 1):
+        part = (slice((b + 1) * B, nb * B), slice(b * B, (b + 1) * B))
         copies.append(pltpu.make_async_copy(low_hbm.at[part], low_ref.at[part], sem.at[b]))
     for copy in copies:
         copy.start()
@@ -298,19 +291,18 @@
     def fold(p):
         return p[:m] + p[m:]
 
-    acc, ys = [], []
+    acc = [rhs(b) for b in range(nb)]
+    copies[0].wait()
     for b in range(nb):
         r0, r1 = b * B, (b + 1) * B
-        copies[b].wait()
-        s = rhs(b)
-        if b > 1:
-            s = s - fold(dot(jnp.concatenate(ys[:-1], 1), low_ref[r0:r1, : r0 - B]))
-        if b:
-            s = s - fold(dot(ys[-1], low_ref[r0:r1, r0 - B : r0]))
-        p = fold(dot(stacked(s), stacked(inv_ref[r0:r1, :])))
+        p = fold(dot(stacked(acc[b]), stacked(inv_ref[r0:r1, :])))
         y = p[:, :B] + p[:, B:]
-        acc.append(y)
-        ys.append(stacked(y))
+        acc[b] = y
+        ys = stacked(y)
+        if b < nb - 1:
+            copies[b + 1].wait()
+        for c in range(b + 1, nb):
+            acc[c] = acc[c] - fold(dot(ys, low_ref[c * B : (c + 1) * B, r0:r1]))
     for b in reversed(range(nb)):
         r0, r1 = b * B, (b + 1) * B
         w = jnp.concatenate(split(inv_ref[r0:r1, :]), 1)
@@ -337,47 +329,49 @@
         in_specs=[VM, HBM, HBM, ANY],
         out_specs=VM,
         scratch_shapes=solve_scratch(low.shape[0]),
-        compiler_params=params(56),
+        compiler_params=params(16),
         cost_estimate=cost(7),
         name="solve",
     )(rhs, low, inv, after)
 
 
-def route_kernel(block, owner_ref, first_ref, last_ref, low_ref, inv_ref, out_ref, t_ref, r_ref, *scratch):
+def route_kernel(block, owner_ref, total_ref, one_ref, two_ref, low_ref, inv_ref, same_ref, cross_ref, t_ref, r_ref, *scratch):
     n = low_ref.shape[0]
-    m, wide = first_ref.shape
+    m = one_ref.shape[0]
+    total = total_ref[0]
 
     def rhs(b):
-        at = b * B
-        return first_ref[:, at : at + B] if at < wide else last_ref[:, at - (n - wide) : at - (n - wide) + B]
+        cols = slice(b * B, (b + 1) * B)
+        return (one_ref[:, cols] + two_ref[:, cols]) / total
 
     solve_into(rhs, m, low_ref, inv_ref, t_ref, *scratch)
     t_ref[:, n:] = jnp.zeros((m, t_ref.shape[1] - n), F32)
     lane = lax.broadcasted_iota(jnp.int32, (m, 2 * B), 1)
-    for h in range(2):
+    for h, out_ref in enumerate((same_ref, cross_ref)):
         for q in range(owner_ref.shape[1]):
             to, off = block * q // B * B, block * q % B
             src = owner_ref[h, q] * block
             win = t_ref[:, pl.ds(pl.multiple_of(src // B * B, B), 2 * B)]
             win = pltpu.roll(win, (off + 2 * B - src % B) % (2 * B), 1)
-            old = r_ref[h, :, to : to + 2 * B]
-            r_ref[h, :, to : to + 2 * B] = jnp.where((lane >= off) & (lane < off + block), win, old)
-        out_ref[h] = r_ref[h, :, : out_ref.shape[2]]
-
-
-def solve_and_route(owner, first, last, low, inv, block):
-    m, n = first.shape[0], low.shape[0]
+            old = r_ref[:, to : to + 2 * B]
+            r_ref[:, to : to + 2 * B] = jnp.where((lane >= off) & (lane < off + block), win, old)
+        out_ref[...] = r_ref[:, : out_ref.shape[1]]
+
+
+def solve_and_route(owner, total, one, two, low, inv, block):
+    m, n = one.shape
     wide = -(-owner.shape[1] * block // B) * B
+    out = jax.ShapeDtypeStruct((m, wide), F32)
     return pl.pallas_call(
         functools.partial(route_kernel, block),
-        out_shape=jax.ShapeDtypeStruct((2, m, wide), F32),
-        in_specs=[SM, VM, VM, HBM, HBM],
-        out_specs=VM,
-        scratch_shapes=[pltpu.VMEM((m, n + B), F32), pltpu.VMEM((2, m, wide + B), F32)] + solve_scratch(n),
-        compiler_params=params(56),
+        out_shape=(out, out),
+        in_specs=[SM, SM, VM, VM, HBM, HBM],
+        out_specs=(VM, VM),
+        scratch_shapes=[pltpu.VMEM((m, n + B), F32), pltpu.VMEM((m, wide + B), F32)] + solve_scratch(n),
+        compiler_params=params(16),
         cost_estimate=cost(9),
         name="solve_and_route",
-    )(owner, first, last, low, inv)
+    )(owner, total, one, two, low, inv)
 
 
 def sum_kernel(parts_ref, *refs):
@@ -394,7 +388,7 @@
         out_shape=jax.ShapeDtypeStruct(parts.shape[1:], F32),
         in_specs=[VM] + [ANY] * len(after),
         out_specs=VM,
-        compiler_params=params(24),
+        compiler_params=params(16),
         cost_estimate=cost(3),
         name="sum_parts",
     )(parts, *after)
@@ -426,7 +420,7 @@
         in_specs=[SM, SM, VM, VM],
         out_specs=VM,
         scratch_shapes=[pltpu.VMEM((n + 8, n), F32)],
-        compiler_params=params(40),
+        compiler_params=params(16),
         cost_estimate=cost(3),
         name="rows",
     )(at, core, mine, other)
@@ -459,17 +453,15 @@
     both = ("grp", "dp")
     half = per_dev // 2
 
-    first = jnp.where(is_a, attn_out, out_grad)
-    second = jnp.where(is_a, out_grad, attn_out)
-
-    def around(own, sent):
-        mate = lax.ppermute(own, "dp", swap_core)
-        from_near = lax.ppermute(sent[:half], both, near)
-        from_far = lax.ppermute(sent[half:], both, far)
-        near_mate = lax.ppermute(from_near, "dp", swap_core)
-        return [own, mate, from_near, from_far, near_mate, lax.ppermute(from_far, "dp", swap_core)]
-
-    mine_rows = around(first, second)
+    sent = jnp.where(is_a, out_grad, attn_out)
+    from_near = lax.ppermute(sent[:half], both, near)
+    from_far = lax.ppermute(sent[half:], both, far)
+    act_mate = lax.ppermute(attn_out, "dp", swap_core)
+    grad_mate = lax.ppermute(out_grad, "dp", swap_core)
+    mine_rows = [
+        jnp.where(is_a, attn_out, out_grad), jnp.where(is_a, act_mate, grad_mate), from_near, from_far,
+        lax.ppermute(from_near, "dp", swap_core), lax.ppermute(from_far, "dp", swap_core),
+    ]
     over, mate, away = 1 - grp_index, dp_index ^ 1, dp_index ^ flip
     keeps = jnp.stack([
         keep_of(grp_index, dp_index),
@@ -484,8 +476,7 @@
     got = lax.all_to_all(
         part.reshape(chips, per_chip * SLAB, B), "dp", split_axis=0, concat_axis=0, tiled=True, axis_index_groups=same_core
     )
-    other_rows = around(second, first)
-    slabs = sum_parts(got, *[rows[:SLAB, :B] for rows in other_rows[1:]]) / total
+    slabs = sum_parts(got) / total
 
     flat = chip * (per_chip * SLAB) + jnp.arange(per_chip * SLAB)
     t = flat // HALF
@@ -499,8 +490,7 @@
     spread = jnp.broadcast_to(damped[None], (chips,) + damped.shape)
     mine = lax.all_to_all(spread, "dp", split_axis=0, concat_axis=0, tiled=True, axis_index_groups=same_core)
     mine = mine.reshape(chips * per_chip * SLAB, B)
-    wide = (nb + 2) // 2 * B
-    part_w = cross(core_arr, grp_index.astype(jnp.int32)[None], keeps, damped[:SLAB], mine_rows, other_rows, chips, wide)
+    part_w = cross(core_arr, keeps, damped[:SLAB], [out_grad, grad_mate], [attn_out, act_mate], chips)
     mine, part_w = lax.optimization_barrier((mine, part_w))
     theirs = lax.ppermute(mine, "dp", swap_core)
     low, inv, chol_done = chol(core_arr, mine, theirs, width)
@@ -512,11 +502,11 @@
 
     order = column_owner.reshape(chips, 2)
     order = jnp.stack([jnp.where(core == 0, order[:, 0], order[:, 1]), jnp.where(core == 0, order[:, 1], order[:, 0])])
-    my_w = sum_parts(got_w, chol_done) / total
-    last_w = lax.ppermute(my_w, "grp", [(1, 0)])
-    routed = solve_and_route(order, my_w, last_w, low, inv, block)
-    same = lax.ppermute(routed[0], both, [(d, n_dp + d) for d in range(n_dp)])
-    cross_t = lax.ppermute(routed[1], both, [(d, n_dp + (d ^ 1)) for d in range(n_dp)])
+    my_w = sum_parts(got_w, chol_done)
+    their_w = lax.ppermute(my_w, "grp", [(1, 0)])
+    same, cross_t = solve_and_route(order, total[None], my_w, their_w, low, inv, block)
+    same = lax.ppermute(same, both, [(d, n_dp + d) for d in range(n_dp)])
+    cross_t = lax.ppermute(cross_t, both, [(d, n_dp + (d ^ 1)) for d in range(n_dp)])
     is_first = core == 0
     pair = jnp.concatenate([jnp.where(is_first, same, cross_t), jnp.where(is_first, cross_t, same)])
     pair = pair[:, : chips * block].reshape(2 * ROWS, chips, block).transpose(1, 2, 0)

time: 235 us -> 222 us (0.945)
  waiting for transfers between devices: 71.4 us -> 80.4 us
  Pallas kernels: 82.7 us -> 75.4 us
  starting transfers between devices: 49.4 us -> 42.4 us
  local copies, waits for them, and re-layouts: 15.7 us -> 11.3 us
  other arithmetic: 7.79 us -> 4.88 us
    ppermute x13 -> x9, waiting for transfers between devices: 47.1 us -> 16.6 us  [the longest x1 8.6 us: per_device(): their_w = lax.ppermute(my_w, 'grp', [(1, 0)])]
    all_to_all x1, waiting for transfers between devices: 0.01 us -> 28.4 us  [per_device(): lax.all_to_all(part.reshape(chips, per_chip * SLAB, B), 'dp', split_axis=...]
    all_to_all x1, waiting for transfers between devices: 0.01 us -> 11.2 us  [per_device(): lax.all_to_all(part_w, 'dp', split_axis=0, concat_axis=0, tiled=True, axi...]
    ppermute x13 -> x9, starting transfers between devices: 12.4 us -> 8.55 us  [the longest x1 2.1 us: per_device(): from_far = lax.ppermute(sent[half:], both, far)]
    pallas_call x1, Pallas kernels: 6.88 us -> 3.27 us  [cross(): pl.pallas_call(cross_kernel, out_shape=jax.ShapeDtypeStruct((chips, ROWS,...]
    slice x7 -> x1, local copies, waits for them, and re-layouts: 3.92 us -> 0.79 us  [per_device(): from_far = lax.ppermute(sent[half:], both, far)]
    all_to_all x1, starting transfers between devices: 9.71 us -> 6.74 us  [per_device(): lax.all_to_all(spread, 'dp', split_axis=0, concat_axis=0, tiled=True, axi...]
    unnamed x35 -> x19, local copies, waits for them, and re-layouts: 4.38 us -> 6.27 us
  transfers between devices with their start and end apart: 20 -> 16, of which waited for: 10 -> 11; matrix products, arithmetic and copies ran while one was open for 5% -> 3% of each run, Pallas kernels for 28% -> 27%
where the time goes in v6:
time: 222 us; the launch traced here: 221 us
  waiting for transfers between devices  80.4 us (36%)
  Pallas kernels  75.4 us (34%)
  starting transfers between devices  42.4 us (19%)
  local copies, waits for them, and re-layouts  11.3 us (5%)
  between operations  6.81 us (3%)
  other arithmetic  4.88 us (2%)
    pallas_call x1, Pallas kernels, chol(): pl.pallas_call(chol_kernel, out_shape=(jax.ShapeDtypeStruct((n, WIDE), BF...  46.9 us
    all_to_all x1, waiting for transfers between devices, per_device(): lax.all_to_all(part.reshape(chips, per_chip * SLAB, B), 'dp', split_axis=...  28.4 us
    all_to_all x1, waiting for transfers between devices, per_device(): lax.all_to_all(spread, 'dp', split_axis=0, concat_axis=0, tiled=True, axi...  11.5 us
    all_to_all x1, waiting for transfers between devices, per_device(): lax.all_to_all(part_w, 'dp', split_axis=0, concat_axis=0, tiled=True, axi...  11.2 us
    all_to_all x1, starting transfers between devices, per_device(): lax.all_to_all(part.reshape(chips, per_chip * SLAB, B), 'dp', split_axis=...  9.3 us
    all_to_all x1, starting transfers between devices, per_device(): lax.all_to_all(pair, 'dp', split_axis=0, concat_axis=0, tiled=True, axis_...  9.29 us
    pallas_call x1, Pallas kernels, solve_and_route(): pl.pallas_call(functools.partial(route_kernel, block), out_shape=(out, ou...  8.79 us
    ppermute x1, waiting for transfers between devices, per_device(): their_w = lax.ppermute(my_w, 'grp', [(1, 0)])  8.6 us
  transfers between devices with their start and end apart: 16, of which 11 were waited for; matrix products, arithmetic and copies ran while one was open for 3% of the time, Pallas kernels for 27%

profile of v6, /device:TPU:0, one launch (start us, length us, event | category | flops | bytes accessed | tf_op | source)
XLA Modules:
  0.0 221.1 jit_solution(7295256341372421397)
XLA Ops:
  0.7 0.5 collective-permute-start.1
  1.2 1.5 broadcast_select_fusion
  2.7 0.8 fusion.3
  3.5 1.6 collective-permute-start.2
  5.1 2.1 collective-permute-start.3
  7.2 0.7 fusion.5
  11.7 2.4 %collective-permute-done.2.refs_2_ = bf16[128,1408]{1,0:T(8,128)(2,1)S(1)} collective-permute-done((bf16[128,1408]{1,0:T(8,128)(2,1)}, bf16[128,1408]{1,0:T(8,128)(2,1)S(1)}, u32[]{:S(2)}, u32[]{:S(2)}) %collective-permute-start.2) | collective-permute-done | bytes 360480 | tf_op jit(solution)/shard_map/ppermute | solution.py:457
  14.1 2.3 %collective-permute-done.3.refs_3_ = bf16[128,1408]{1,0:T(8,128)(2,1)S(1)} collective-permute-done((bf16[128,1408]{1,0:T(8,128)(2,1)S(1)}, bf16[128,1408]{1,0:T(8,128)(2,1)S(1)}, u32[]{:S(2)}, u32[]{:S(2)}) %collective-permute-start.3) | collective-permute-done | bytes 360480 | tf_op jit(solution)/shard_map/ppermute | solution.py:458
  16.5 1.6 collective-permute-done.5.refs_5_
  18.1 4.2 %gram.1 = (f32[4608,128]{1,0:T(8,128)}, f32[8,1408]{1,0:T(8,128)S(1)}) custom-call(s32[1]{0:T(128)} %bitcast.1.core_ref, f32[6]{0:T(128)S(1)} %stack.27.keep_ref, bf16[256,1408]{1,0:T(8,128)(2,1)S(1)} %get-tuple-element.27.refs_0_, bf16[256,1408]{1,0:T(8,128)(2,1)S(1)} %broadcast_select_fusion.1.refs_1_, ...), custom_call_target="tpu_custom_call" | custom-call | flops 4400000000 | bytes 1048576 | tf_op jit(solution)/shard_map/gram/pallas_call | solution.py:105
  22.3 9.3 %all-to-all-start = ((f32[32,144,128]{2,1,0:T(8,128)}), f32[32,144,128]{2,1,0:T(8,128)S(1)}, u32[]{:S(2)}, u32[]{:S(2)}) async-start(f32[32,144,128]{2,1,0:T(8,128)} %bitcast.2), calls=%async_computation | async-start | bytes 4718592 | tf_op jit(solution)/shard_map/all_to_all | solution.py:476
  31.6 0.6 reduce_sum.18
  32.9 0.6 fusion.4
  34.9 28.4 %all-to-all-done.parts_ref = f32[32,144,128]{2,1,0:T(8,128)S(1)} async-done(((f32[32,144,128]{2,1,0:T(8,128)}), f32[32,144,128]{2,1,0:T(8,128)S(1)}, u32[]{:S(2)}, u32[]{:S(2)}) %all-to-all-start) | async-done | bytes 2359328 | tf_op jit(solution)/shard_map/all_to_all | solution.py:476
  63.6 1.2 broadcast_in_dim.34
  64.8 6.7 %all-to-all-start.1 = ((bf16[32,144,128]{2,1,0:T(8,128)(2,1)}), bf16[32,144,128]{2,1,0:T(8,128)(2,1)S(1)}, u32[]{:S(2)}, u32[]{:S(2)}) async-start(bf16[32,144,128]{2,1,0:T(8,128)(2,1)} %broadcast_in_dim.34), calls=%async_computation.1 | async-start | bytes 2359296 | tf_op jit(solution)/shard_map/all_to_all | solution.py:491
  71.5 1.1 copy-done.3
  72.6 1.1 copy-done.4
  73.7 3.3 %cross.1 = f32[32,24,1408]{2,1,0:T(8,128)S(1)} custom-call(s32[1]{0:T(128)} %bitcast.1.core_ref, f32[6]{0:T(128)S(1)} %stack.27.keep_ref, bf16[16,128]{1,0:T(8,128)(2,1)S(1)} %slice.62.after_ref, bf16[256,1408]{1,0:T(8,128)(2,1)S(1)} %copy-done.3, bf16[256,1408]{1,0:T(8,128)(2,1)S(1)} %copy-done.2, bf16[256,1408]{1,0:T(8,128)(2,1)S(1)} %copy-done.4, ...), custom_call_target="tpu_custom_call" | custom-call | flops 32999999488 | bytes 1048576 | tf_op jit(solution)/shard_map/cross/pallas_call | solution.py:134
  77.0 2.0 copy-done
  79.0 11.5 %all-to-all-done.1 = bf16[32,144,128]{2,1,0:T(8,128)(2,1)S(1)} async-done(((bf16[32,144,128]{2,1,0:T(8,128)(2,1)}), bf16[32,144,128]{2,1,0:T(8,128)(2,1)S(1)}, u32[]{:S(2)}, u32[]{:S(2)}) %all-to-all-start.1) | async-done | bytes 1179680 | tf_op jit(solution)/shard_map/all_to_all | solution.py:491
  90.9 5.7 %all-to-all-start.2 = ((f32[32,24,1408]{2,1,0:T(8,128)}), f32[32,24,1408]{2,1,0:T(8,128)}, u32[]{:S(2)}, u32[]{:S(2)}) async-start(f32[32,24,1408]{2,1,0:T(8,128)} %copy-done), calls=%async_computation.2 | async-start | bytes 8650752 | tf_op jit(solution)/shard_map/all_to_all | solution.py:498
  96.6 46.9 %cholesky.1 = (bf16[1408,14336]{1,0:T(8,128)(2,1)}, f32[1408,128]{1,0:T(8,128)S(1)}, f32[8,128]{1,0:T(8,128)S(1)}) custom-call(s32[1]{0:T(128)} %bitcast.1.core_ref, bf16[4608,128]{1,0:T(8,128)(2,1)S(1)} %bitcast.23, bf16[4608,128]{1,0:T(8,128)(2,1)} %collective-permute-done.6.other_ref), custom_call_target="tpu_custom_call" | custom-call | flops 62699999232 | bytes 1048576 | tf_op jit(solution)/shard_map/cholesky/pallas_call | solution.py:260
  143.5 11.2 %all-to-all-done.2.parts_ref = f32[32,24,1408]{2,1,0:T(8,128)} async-done(((f32[32,24,1408]{2,1,0:T(8,128)}), f32[32,24,1408]{2,1,0:T(8,128)}, u32[]{:S(2)}, u32[]{:S(2)}) %all-to-all-start.2) | async-done | bytes 4325408 | tf_op jit(solution)/shard_map/all_to_all | solution.py:498
  154.7 2.4 %sum_parts.3.one_ref = f32[24,1408]{1,0:T(8,128)S(1)} custom-call(f32[32,24,1408]{2,1,0:T(8,128)} %all-to-all-done.2.parts_ref, f32[8,128]{1,0:T(8,128)S(1)} %get-tuple-element.14.refs_0_), custom_call_target="tpu_custom_call" | custom-call | flops 3300000000 | bytes 1048576 | tf_op jit(solution)/shard_map/sum_parts/pallas_call | solution.py:386
  157.1 1.5 collective-permute-start.7
  158.9 8.6 %collective-permute-done.7.two_ref = f32[24,1408]{1,0:T(8,128)S(1)} collective-permute-done((f32[24,1408]{1,0:T(8,128)S(1)}, f32[24,1408]{1,0:T(8,128)S(1)}, u32[]{:S(2)}, u32[]{:S(2)}) %collective-permute-start.7) | collective-permute-done | bytes 135200 | tf_op jit(solution)/shard_map/ppermute | solution.py:506
  167.5 8.8 %solve_and_route.1 = (f32[24,768]{1,0:T(8,128)S(1)}, f32[24,768]{1,0:T(8,128)S(1)}) custom-call(s32[2,32]{1,0:T(2,128)S(1)} %pad_add_fusion.owner_ref, f32[1]{0:T(128)} %bitcast.total_ref, f32[24,1408]{1,0:T(8,128)S(1)} %sum_parts.3.one_ref, f32[24,1408]{1,0:T(8,128)S(1)} %collective-permute-done.7.two_ref, bf16[1408,14336]{1,0:T(8,128)(2,1)} %get-tuple-element.15.low_ref, ...), custom_call_target="tpu_custom_call" | custom-call | flops 9900000256 | bytes 1048576 | tf_op jit(solution)/shard_map/solve_and_route/pallas_call | solution.py:365
  176.3 1.5 collective-permute-start.8
  177.8 1.3 collective-permute-start.9
  179.1 0.3 copy.12
  179.4 0.3 collective-permute-done.8
  179.7 1.5 collective-permute-done.9
  181.6 1.0 reshape.154
  182.6 9.3 %all-to-all-start.3 = ((f32[32,1,1078]{2,1,0:T(1,128)}), f32[32,1,1078]{2,1,0:T(1,128)S(1)}, u32[]{:S(2)}, u32[]{:S(2)}) async-start(f32[32,1,1078]{2,1,0:T(1,128)} %reshape.154), calls=%async_computation.3 | async-start | bytes 294912 | tf_op jit(solution)/shard_map/all_to_all | solution.py:515
  191.9 2.1 rows.1.after_ref
  194.0 8.0 %all-to-all-done.3 = f32[32,1,1078]{2,1,0:T(1,128)S(1)} async-done(((f32[32,1,1078]{2,1,0:T(1,128)}), f32[32,1,1078]{2,1,0:T(1,128)S(1)}, u32[]{:S(2)}, u32[]{:S(2)}) %all-to-all-start.3) | async-done | bytes 138016 | tf_op jit(solution)/shard_map/all_to_all | solution.py:515
  202.0 0.5 broadcast.169
  202.5 1.0 reduce.7
  203.5 0.2 reshape.155
  203.7 0.3 slice_reduce_fusion
  204.1 1.5 collective-permute-start.10
  205.7 0.2 reshape.150
  206.0 7.6 %solve.1 = f32[24,1408]{1,0:T(8,128)S(1)} custom-call(f32[24,1408]{1,0:T(8,128)S(1)} %pad.4.rhs_ref, bf16[1408,14336]{1,0:T(8,128)(2,1)} %get-tuple-element.15.low_ref, f32[1408,128]{1,0:T(8,128)S(1)} %get-tuple-element.16.inv_ref, f32[24,1408]{1,0:T(8,128)S(1)} %rows.1.after_ref), custom_call_target="tpu_custom_call" | custom-call | flops 7699999744 | bytes 1048576 | tf_op jit(solution)/shard_map/solve/pallas_call | solution.py:326
  213.5 1.3 collective-permute-start.11
  215.0 0.8 copy.14
  215.8 4.6 %collective-permute-done.11 = f32[22,1408]{1,0:T(8,128)S(1)} collective-permute-done((f32[22,1408]{1,0:T(8,128)S(1)}, f32[22,1408]{1,0:T(8,128)S(1)}, u32[]{:S(2)}, u32[]{:S(2)}) %collective-permute-start.11) | collective-permute-done | bytes 123936 | tf_op jit(solution)/shard_map/ppermute | solution.py:524
  220.4 0.7 select_bitcast_fusion
  (50 shorter events, 1.8 us)
Async XLA Ops:
  0.6 6.5 %copy-start.5 = (s32[128]{0:T(128)S(1)}, s32[128]{0:T(128)}, u32[]{:S(2)}) copy-start(s32[128]{0:T(128)} %param.7) | copy-start | bytes 1540
  0.6 15.8 %collective-permute-start = (bf16[256,1408]{1,0:T(8,128)(2,1)}, bf16[256,1408]{1,0:T(8,128)(2,1)S(1)}, u32[]{:S(2)}, u32[]{:S(2)}) collective-permute-start(bf16[256,1408]{1,0:T(8,128)(2,1)} %act_ref.1), channel_id=1, source_target_pairs={{0,1},{1,0},{2,3},{3,2},{4,5},{5,4},{6,7},{7,6},{8,9},{9,8},{10,11... | collective-permute-start | bytes 2162696 | tf_op jit(solution)/shard_map/ppermute | solution.py:459
  0.7 15.7 %collective-permute-start.1 = (bf16[256,1408]{1,0:T(8,128)(2,1)}, bf16[256,1408]{1,0:T(8,128)(2,1)S(1)}, u32[]{:S(2)}, u32[]{:S(2)}) collective-permute-start(bf16[256,1408]{1,0:T(8,128)(2,1)} %grad_ref.1), channel_id=1, source_target_pairs={{0,1},{1,0},{2,3},{3,2},{4,5},{5,4},{6,7},{7,6},{8,9},{9,8},{10,11... | collective-permute-start | bytes 2162696 | tf_op jit(solution)/shard_map/ppermute | solution.py:460
  3.5 10.6 %collective-permute-start.2 = (bf16[128,1408]{1,0:T(8,128)(2,1)}, bf16[128,1408]{1,0:T(8,128)(2,1)S(1)}, u32[]{:S(2)}, u32[]{:S(2)}) collective-permute-start(bf16[128,1408]{1,0:T(8,128)(2,1)} %get-tuple-element.29), channel_id=1, source_target_pairs={{0,64},{1,65},{2,66},{3,67},{4,68},{5,69},{6,70},{7,71},{8,72},{9,... | collective-permute-start | bytes 1081352 | tf_op jit(solution)/shard_map/ppermute | solution.py:457
  5.1 11.3 %collective-permute-start.3 = (bf16[128,1408]{1,0:T(8,128)(2,1)S(1)}, bf16[128,1408]{1,0:T(8,128)(2,1)S(1)}, u32[]{:S(2)}, u32[]{:S(2)}) collective-permute-start(bf16[128,1408]{1,0:T(8,128)(2,1)S(1)} %get-tuple-element.28), channel_id=1, source_target_pairs={{0,96},{1,97},{2,98},{3,99},{4,100},{5,101},{6,102},{7,103},{8,104... | collective-permute-start | bytes 1081352 | tf_op jit(solution)/shard_map/ppermute | solution.py:458
  14.1 2.4 %collective-permute-start.4 = (bf16[128,1408]{1,0:T(8,128)(2,1)S(1)}, bf16[128,1408]{1,0:T(8,128)(2,1)S(1)}, u32[]{:S(2)}, u32[]{:S(2)}) collective-permute-start(bf16[128,1408]{1,0:T(8,128)(2,1)S(1)} %collective-permute-done.2.refs_2_), channel_id=1, source_target_pairs={{0,1},{1,0},{2,3},{3,2},{4,5},{5,4},{6,7},{7,6},{8,9},{9,8},{10,11... | collective-permute-start | bytes 1081352 | tf_op jit(solution)/shard_map/ppermute | solution.py:463
  16.4 1.7 collective-permute-start.5
  16.4 5.9 %copy-start.1 = (bf16[256,1408]{1,0:T(8,128)(2,1)}, bf16[256,1408]{1,0:T(8,128)(2,1)S(1)}, u32[]{:S(2)}) copy-start(bf16[256,1408]{1,0:T(8,128)(2,1)S(1)} %collective-permute-done.1.grad_mate_ref) | copy-start | bytes 2162692
  22.3 10.6 %copy-start.6 = (f32[2]{0:T(128)S(1)}, f32[2]{0:T(128)}, u32[]{:S(2)}) copy-start(f32[2]{0:T(128)} %param.9) | copy-start | bytes 28
  22.3 41.0 %all-to-all-start = ((f32[32,144,128]{2,1,0:T(8,128)}), f32[32,144,128]{2,1,0:T(8,128)S(1)}, u32[]{:S(2)}, u32[]{:S(2)}) async-start(f32[32,144,128]{2,1,0:T(8,128)} %bitcast.2), calls=%async_computation | async-start | bytes 4718592 | tf_op jit(solution)/shard_map/all_to_all | solution.py:476
  63.4 8.1 %copy-start.2 = (bf16[256,1408]{1,0:T(8,128)(2,1)S(1)}, bf16[256,1408]{1,0:T(8,128)(2,1)}, u32[]{:S(2)}) copy-start(bf16[256,1408]{1,0:T(8,128)(2,1)} %copy-done.1) | copy-start | bytes 2162692
  64.8 25.8 %all-to-all-start.1 = ((bf16[32,144,128]{2,1,0:T(8,128)(2,1)}), bf16[32,144,128]{2,1,0:T(8,128)(2,1)S(1)}, u32[]{:S(2)}, u32[]{:S(2)}) async-start(bf16[32,144,128]{2,1,0:T(8,128)(2,1)} %broadcast_in_dim.34), calls=%async_computation.1 | async-start | bytes 2359296 | tf_op jit(solution)/shard_map/all_to_all | solution.py:491
  71.5 1.1 copy-start.3
  72.6 1.1 copy-start.4
  73.7 16.8 %copy-start.7 = (s32[64]{0:T(128)S(1)}, s32[64]{0:T(128)}, u32[]{:S(2)}) copy-start(s32[64]{0:T(128)} %param.8) | copy-start | bytes 772
  77.0 2.0 copy-start
  90.6 6.1 %collective-permute-start.6 = (bf16[4608,128]{1,0:T(8,128)(2,1)S(1)}, bf16[4608,128]{1,0:T(8,128)(2,1)}, u32[]{:S(2)}, u32[]{:S(2)}) collective-permute-start(bf16[4608,128]{1,0:T(8,128)(2,1)S(1)} %bitcast.22), channel_id=1, source_target_pairs={{0,1},{1,0},{2,3},{3,2},{4,5},{5,4},{6,7},{7,6},{8,9},{9,8},{10,11... | collective-permute-start | bytes 3538952 | tf_op jit(solution)/shard_map/ppermute | solution.py:495
  90.9 63.8 %all-to-all-start.2 = ((f32[32,24,1408]{2,1,0:T(8,128)}), f32[32,24,1408]{2,1,0:T(8,128)}, u32[]{:S(2)}, u32[]{:S(2)}) async-start(f32[32,24,1408]{2,1,0:T(8,128)} %copy-done), calls=%async_computation.2 | async-start | bytes 8650752 | tf_op jit(solution)/shard_map/all_to_all | solution.py:498
  157.1 10.3 %collective-permute-start.7 = (f32[24,1408]{1,0:T(8,128)S(1)}, f32[24,1408]{1,0:T(8,128)S(1)}, u32[]{:S(2)}, u32[]{:S(2)}) collective-permute-start(f32[24,1408]{1,0:T(8,128)S(1)} %sum_parts.3.one_ref), channel_id=1, source_target_pairs={{64,0},{65,1},{66,2},{67,3},{68,4},{69,5},{70,6},{71,7},{72,8},{73... | collective-permute-start | bytes 405512 | tf_op jit(solution)/shard_map/ppermute | solution.py:506
  176.3 3.5 %collective-permute-start.8 = (f32[24,768]{1,0:T(8,128)S(1)}, f32[24,768]{1,0:T(8,128)S(1)}, u32[]{:S(2)}, u32[]{:S(2)}) collective-permute-start(f32[24,768]{1,0:T(8,128)S(1)} %get-tuple-element.17), channel_id=1, source_target_pairs={{0,64},{1,65},{2,66},{3,67},{4,68},{5,69},{6,70},{7,71},{8,72},{9,... | collective-permute-start | bytes 221192 | tf_op jit(solution)/shard_map/ppermute | solution.py:508
  177.8 3.4 %collective-permute-start.9 = (f32[24,768]{1,0:T(8,128)S(1)}, f32[24,768]{1,0:T(8,128)S(1)}, u32[]{:S(2)}, u32[]{:S(2)}) collective-permute-start(f32[24,768]{1,0:T(8,128)S(1)} %get-tuple-element.18), channel_id=1, source_target_pairs={{0,65},{1,64},{2,67},{3,66},{4,69},{5,68},{6,71},{7,70},{8,73},{9,... | collective-permute-start | bytes 221192 | tf_op jit(solution)/shard_map/ppermute | solution.py:509
  182.6 19.4 %all-to-all-start.3 = ((f32[32,1,1078]{2,1,0:T(1,128)}), f32[32,1,1078]{2,1,0:T(1,128)S(1)}, u32[]{:S(2)}, u32[]{:S(2)}) async-start(f32[32,1,1078]{2,1,0:T(1,128)} %reshape.154), calls=%async_computation.3 | async-start | bytes 294912 | tf_op jit(solution)/shard_map/all_to_all | solution.py:515
  204.1 10.7 %collective-permute-start.10 = (f32[22,1408]{1,0:T(8,128)S(1)}, f32[22,1408]{1,0:T(8,128)S(1)}, u32[]{:S(2)}, u32[]{:S(2)}) collective-permute-start(f32[22,1408]{1,0:T(8,128)S(1)} %slice_select_fusion), channel_id=1, source_target_pairs={{0,64},{64,0},{1,65},{65,1},{2,66},{66,2},{3,67},{67,3},{4,68},{68... | collective-permute-start | bytes 371720 | tf_op jit(solution)/shard_map/ppermute | solution.py:522
  213.5 6.9 %collective-permute-start.11 = (f32[22,1408]{1,0:T(8,128)S(1)}, f32[22,1408]{1,0:T(8,128)S(1)}, u32[]{:S(2)}, u32[]{:S(2)}) collective-permute-start(f32[22,1408]{1,0:T(8,128)S(1)} %bitcast.25), channel_id=1, source_target_pairs={{64,0},{65,1},{66,2},{67,3},{68,4},{69,5},{70,6},{71,7},{72,8},{73... | collective-permute-start | bytes 371720 | tf_op jit(solution)/shard_map/ppermute | solution.py:524

commit v7 on v6

--- a/solution.py
+++ b/solution.py
@@ -13,6 +13,7 @@
 SLAB = 16
 ROWS = 24
 WIDE = 14336
+STEP = 512
 F32 = jnp.float32
 BF16 = jnp.bfloat16
 NT = (((1,), (1,)), ((), ()))
@@ -208,7 +209,27 @@
     return jnp.concatenate([jnp.where(first, mine, other), jnp.where(first, other, mine)], 0)
 
 
-def chol_kernel(core_ref, mine_ref, other_ref, low_hbm, inv_hbm, done_ref, low_ref, inv_ref, lo_ref, s_ref, w_ref, sem):
+def join_inverses(low_ref, inv_ref, iv_ref):
+    n = low_ref.shape[0]
+    iv_ref[...] = jnp.zeros_like(iv_ref)
+    for b in range(n // B):
+        at = b * B % STEP
+        iv_ref[b * B : (b + 1) * B, at : at + B] = inv_ref[b * B : (b + 1) * B, :]
+    size = B
+    while size < STEP:
+        for r0 in range(0, n - size, 2 * size):
+            r1 = r0 + size
+            r2 = min(r1 + size, n)
+            at = r0 % STEP
+            left = jnp.concatenate(split(iv_ref[r0:r1, at : at + size]), 1)
+            p = dot(low_ref[r1:r2, r0:r1], left, NN)
+            phi, plo = split(p[:, :size] + p[:, size:])
+            bhi, blo = split(iv_ref[r1:r2, at + size : at + size + r2 - r1])
+            iv_ref[r1:r2, at : at + size] = -(dot(bhi, phi, NN) + dot(bhi, plo, NN) + dot(blo, phi, NN))
+        size *= 2
+
+
+def chol_kernel(core_ref, mine_ref, other_ref, low_hbm, done_ref, low_ref, inv_ref, lo_ref, s_ref, w_ref, iv_ref, hl_ref, sem):
     done_ref[...] = jnp.zeros_like(done_ref)
     n = low_ref.shape[0]
     nb = n // B
@@ -238,10 +259,9 @@
             pl.when(k == kk)(lambda kk=kk: update(kk))
         r0 = pl.multiple_of(k * B, B)
         rows = pl.ds(r0, B)
-        pltpu.make_async_copy(low_ref.at[rows], low_hbm.at[rows, :n], sem.at[0, k]).start()
+        pltpu.make_async_copy(low_ref.at[rows], low_hbm.at[rows, :n], sem.at[k]).start()
         linv, lrinv = factor_diag(s_ref[pl.ds(r0, B), :])
         inv_ref[rows, :] = lrinv
-        pltpu.make_async_copy(inv_ref.at[rows], inv_hbm.at[rows], sem.at[1, k]).start()
         hi, lo = split(linv)
         w_ref[:B, :] = hi
         w_ref[B:, :] = lo
@@ -250,25 +270,35 @@
         return 0
 
     lax.fori_loop(0, nb, step, 0)
-    for k in range(nb):
-        rows = slice(k * B, (k + 1) * B)
-        pltpu.make_async_copy(low_ref.at[rows], low_hbm.at[rows, :n], sem.at[0, k]).wait()
-        pltpu.make_async_copy(inv_ref.at[rows], inv_hbm.at[rows], sem.at[1, k]).wait()
+    join_inverses(low_ref, inv_ref, iv_ref)
+    hi, lo = split(iv_ref[...])
+    hl_ref[:, :STEP] = hi
+    hl_ref[:, STEP:] = lo
+    copies = [
+        pltpu.make_async_copy(low_ref.at[k * B : (k + 1) * B], low_hbm.at[k * B : (k + 1) * B, :n], sem.at[k])
+        for k in range(nb)
+    ]
+    copies.append(pltpu.make_async_copy(hl_ref, low_hbm.at[:, n : n + 2 * STEP], sem.at[nb]))
+    copies[-1].start()
+    for copy in copies:
+        copy.wait()
 
 
 def chol(core, mine, other, n):
     return pl.pallas_call(
         chol_kernel,
-        out_shape=(jax.ShapeDtypeStruct((n, WIDE), BF16), jax.ShapeDtypeStruct((n, B), F32), TOKEN),
+        out_shape=(jax.ShapeDtypeStruct((n, WIDE), BF16), TOKEN),
         in_specs=[SM, VM, VM],
-        out_specs=(HBM, HBM, VM),
+        out_specs=(HBM, VM),
         scratch_shapes=[
             pltpu.VMEM((n, n), BF16),
             pltpu.VMEM((n, B), F32),
             pltpu.VMEM((n, n), BF16),
             pltpu.VMEM((n, B), F32),
             pltpu.VMEM((2 * B, B), BF16),
-            pltpu.SemaphoreType.DMA((2, n // B)),
+            pltpu.VMEM((n, STEP), F32),
+            pltpu.VMEM((n, 2 * STEP), BF16),
+            pltpu.SemaphoreType.DMA((n // B + 1,)),
         ],
         compiler_params=params(28),
         cost_estimate=cost(57),
@@ -276,12 +306,15 @@
     )(core, mine, other)
 
 
-def solve_into(rhs, m, low_hbm, inv_hbm, out_ref, low_ref, inv_ref, sem):
-    nb = low_ref.shape[0] // B
-    copies = [pltpu.make_async_copy(inv_hbm, inv_ref, sem.at[nb - 1])]
-    for b in range(nb - 1):
-        part = (slice((b + 1) * B, nb * B), slice(b * B, (b + 1) * B))
-        copies.append(pltpu.make_async_copy(low_hbm.at[part], low_ref.at[part], sem.at[b]))
+def solve_into(rhs, m, n, low_hbm, out_ref, low_ref, hl_ref, sem):
+    starts = list(range(0, n, STEP))
+    loads = []
+    for r0 in starts:
+        rows = slice(r0, min(r0 + STEP, n))
+        if r0:
+            loads.append((low_hbm.at[rows, :r0], low_ref.at[rows, :r0]))
+        loads.append((low_hbm.at[rows, n : n + 2 * STEP], hl_ref.at[rows]))
+    copies = [pltpu.make_async_copy(src, dst, sem.at[k]) for k, (src, dst) in enumerate(loads)]
     for copy in copies:
         copy.start()
 
@@ -291,60 +324,59 @@
     def fold(p):
         return p[:m] + p[m:]
 
-    acc = [rhs(b) for b in range(nb)]
-    copies[0].wait()
-    for b in range(nb):
-        r0, r1 = b * B, (b + 1) * B
-        p = fold(dot(stacked(acc[b]), stacked(inv_ref[r0:r1, :])))
-        y = p[:, :B] + p[:, B:]
-        acc[b] = y
-        ys = stacked(y)
-        if b < nb - 1:
-            copies[b + 1].wait()
-        for c in range(b + 1, nb):
-            acc[c] = acc[c] - fold(dot(ys, low_ref[c * B : (c + 1) * B, r0:r1]))
-    for b in reversed(range(nb)):
-        r0, r1 = b * B, (b + 1) * B
-        w = jnp.concatenate(split(inv_ref[r0:r1, :]), 1)
-        p = fold(dot(stacked(acc[b]), w, NN))
-        z = p[:, :B] + p[:, B:]
-        out_ref[:, r0:r1] = z
+    def inverted(x, rows, dims):
+        w = rows.stop - rows.start
+        xs = stacked(x)
+        return fold(dot(xs, hl_ref[rows, :w], dims) + dot(xs, hl_ref[rows, STEP : STEP + w], dims))
+
+    parts = [slice(r0, min(r0 + STEP, n)) for r0 in starts]
+    acc = []
+    for rows in parts:
+        s = rhs(rows)
+        for done, y in zip(parts, acc):
+            if done is parts[0]:
+                copies.pop(0).wait()
+            s = s - fold(dot(stacked(y), low_ref[rows, done]))
+        copies.pop(0).wait()
+        acc.append(inverted(s, rows, NT))
+    for k in reversed(range(len(parts))):
+        z = inverted(acc[k], parts[k], NN)
+        out_ref[:, parts[k]] = z
         zs = stacked(z)
-        for c in range(b):
-            acc[c] = acc[c] - fold(dot(zs, low_ref[r0:r1, c * B : (c + 1) * B], NN))
+        for c in range(k):
+            acc[c] = acc[c] - fold(dot(zs, low_ref[parts[k], parts[c]], NN))
 
 
 def solve_scratch(n):
-    return [pltpu.VMEM((n, n), BF16), pltpu.VMEM((n, B), F32), pltpu.SemaphoreType.DMA((n // B,))]
-
-
-def solve_kernel(rhs_ref, low_ref, inv_ref, after_ref, out_ref, *scratch):
-    solve_into(lambda b: rhs_ref[:, b * B : (b + 1) * B], rhs_ref.shape[0], low_ref, inv_ref, out_ref, *scratch)
-
-
-def solve(rhs, low, inv, after):
+    return [pltpu.VMEM((n, n), BF16), pltpu.VMEM((n, 2 * STEP), BF16), pltpu.SemaphoreType.DMA((2 * -(-n // STEP) - 1,))]
+
+
+def solve_kernel(rhs_ref, low_ref, after_ref, out_ref, *scratch):
+    m, n = rhs_ref.shape
+    solve_into(lambda cols: rhs_ref[:, cols], m, n, low_ref, out_ref, *scratch)
+
+
+def solve(rhs, low, after):
     return pl.pallas_call(
         solve_kernel,
         out_shape=jax.ShapeDtypeStruct(rhs.shape, F32),
-        in_specs=[VM, HBM, HBM, ANY],
+        in_specs=[VM, HBM, ANY],
         out_specs=VM,
-        scratch_shapes=solve_scratch(low.shape[0]),
+        scratch_shapes=solve_scratch(rhs.shape[1]),
         compiler_params=params(16),
         cost_estimate=cost(7),
         name="solve",
-    )(rhs, low, inv, after)
-
-
-def route_kernel(block, owner_ref, total_ref, one_ref, two_ref, low_ref, inv_ref, same_ref, cross_ref, t_ref, r_ref, *scratch):
-    n = low_ref.shape[0]
-    m = one_ref.shape[0]
+    )(rhs, low, after)
+
+
+def route_kernel(block, owner_ref, total_ref, one_ref, two_ref, low_ref, same_ref, cross_ref, t_ref, r_ref, *scratch):
+    m, n = one_ref.shape
     total = total_ref[0]
 
-    def rhs(b):
-        cols = slice(b * B, (b + 1) * B)
+    def rhs(cols):
         return (one_ref[:, cols] + two_ref[:, cols]) / total
 
-    solve_into(rhs, m, low_ref, inv_ref, t_ref, *scratch)
+    solve_into(rhs, m, n, low_ref, t_ref, *scratch)
     t_ref[:, n:] = jnp.zeros((m, t_ref.shape[1] - n), F32)
     lane = lax.broadcasted_iota(jnp.int32, (m, 2 * B), 1)
     for h, out_ref in enumerate((same_ref, cross_ref)):
@@ -358,20 +390,20 @@
         out_ref[...] = r_ref[:, : out_ref.shape[1]]
 
 
-def solve_and_route(owner, total, one, two, low, inv, block):
+def solve_and_route(owner, total, one, two, low, block):
     m, n = one.shape
     wide = -(-owner.shape[1] * block // B) * B
     out = jax.ShapeDtypeStruct((m, wide), F32)
     return pl.pallas_call(
         functools.partial(route_kernel, block),
         out_shape=(out, out),
-        in_specs=[SM, SM, VM, VM, HBM, HBM],
+        in_specs=[SM, SM, VM, VM, HBM],
         out_specs=(VM, VM),
         scratch_shapes=[pltpu.VMEM((m, n + B), F32), pltpu.VMEM((m, wide + B), F32)] + solve_scratch(n),
         compiler_params=params(16),
         cost_estimate=cost(9),
         name="solve_and_route",
-    )(owner, total, one, two, low, inv)
+    )(owner, total, one, two, low)
 
 
 def sum_kernel(parts_ref, *refs):
@@ -380,6 +412,33 @@
     for k in range(1, parts_ref.shape[0]):
         acc = acc + parts_ref[k]
     out_ref[...] = acc
+
+
+def damp_kernel(scale_ref, parts_ref, diag_ref, out_ref, done_ref, sum_ref, sem):
+    acc = parts_ref[0]
+    for k in range(1, parts_ref.shape[0]):
+        acc = acc + parts_ref[k]
+    sum_ref[...] = (acc / scale_ref[0] + scale_ref[1] * diag_ref[...]).astype(BF16)
+    copies = [pltpu.make_async_copy(sum_ref, out_ref.at[k], sem.at[k]) for k in range(out_ref.shape[0])]
+    for copy in copies:
+        copy.start()
+    done_ref[...] = jnp.zeros_like(done_ref)
+    for copy in copies:
+        copy.wait()
+
+
+def damp_and_spread(scale, parts, diag):
+    chips = parts.shape[0]
+    return pl.pallas_call(
+        damp_kernel,
+        out_shape=(jax.ShapeDtypeStruct(parts.shape, BF16), TOKEN),
+        in_specs=[SM, VM, VM],
+        out_specs=(HBM, VM),
+        scratch_shapes=[pltpu.VMEM(parts.shape[1:], BF16), pltpu.SemaphoreType.DMA((chips,))],
+        compiler_params=params(16),
+        cost_estimate=cost(3),
+        name="damp_and_spread",
+    )(scale, parts, diag)
 
 
 def sum_parts(parts, *after):
@@ -476,8 +535,6 @@
     got = lax.all_to_all(
         part.reshape(chips, per_chip * SLAB, B), "dp", split_axis=0, concat_axis=0, tiled=True, axis_index_groups=same_core
     )
-    slabs = sum_parts(got) / total
-
     flat = chip * (per_chip * SLAB) + jnp.arange(per_chip * SLAB)
     t = flat // HALF
     on_diag = jnp.zeros(t.shape, bool)
@@ -486,14 +543,13 @@
     in_row = core * HALF + flat % HALF
     diag = (on_diag & (flat < used * SLAB))[:, None] & (in_row[:, None] == jnp.arange(B)[None, :])
     damp = jnp.where(is_a, damping[0], damping[1])
-    damped = (slabs + damp * diag.astype(F32)).astype(BF16)
-    spread = jnp.broadcast_to(damped[None], (chips,) + damped.shape)
+    spread, damp_done = damp_and_spread(jnp.stack([total, damp]), got, diag.astype(F32))
     mine = lax.all_to_all(spread, "dp", split_axis=0, concat_axis=0, tiled=True, axis_index_groups=same_core)
     mine = mine.reshape(chips * per_chip * SLAB, B)
-    part_w = cross(core_arr, keeps, damped[:SLAB], [out_grad, grad_mate], [attn_out, act_mate], chips)
+    part_w = cross(core_arr, keeps, damp_done, [out_grad, grad_mate], [attn_out, act_mate], chips)
     mine, part_w = lax.optimization_barrier((mine, part_w))
     theirs = lax.ppermute(mine, "dp", swap_core)
-    low, inv, chol_done = chol(core_arr, mine, theirs, width)
+    low, chol_done = chol(core_arr, mine, theirs, width)
 
     got_w = lax.all_to_all(part_w, "dp", split_axis=0, concat_axis=0, tiled=True, axis_index_groups=same_core)
 
@@ -504,7 +560,7 @@
     order = jnp.stack([jnp.where(core == 0, order[:, 0], order[:, 1]), jnp.where(core == 0, order[:, 1], order[:, 0])])
     my_w = sum_parts(got_w, chol_done)
     their_w = lax.ppermute(my_w, "grp", [(1, 0)])
-    same, cross_t = solve_and_route(order, total[None], my_w, their_w, low, inv, block)
+    same, cross_t = solve_and_route(order, total[None], my_w, their_w, low, block)
     same = lax.ppermute(same, both, [(d, n_dp + d) for d in range(n_dp)])
     cross_t = lax.ppermute(cross_t, both, [(d, n_dp + (d ^ 1)) for d in range(n_dp)])
     is_first = core == 0
@@ -516,7 +572,7 @@
     squares = jnp.sum(columns[:, :, 2 * ROWS], axis=0) / total
     columns = columns[:, :, : 2 * ROWS].transpose(1, 0, 2).reshape(block, n_dp * ROWS)[:, :width]
     columns = jnp.pad(columns, ((0, ROWS - block), (0, 0)))
-    left = solve(columns, low, inv, my_rows)[:block]
+    left = solve(columns, low, my_rows)[:block]
     here = (dp_index * block + jnp.arange(block))[:, None] == jnp.arange(width)[None, :]
     my_rows = jnp.where(here, squares[:, None], my_rows[:block])
     their_rows = lax.ppermute(my_rows, "grp", swap_grp)

time: 222 us -> 220 us (level)
  Pallas kernels: 75.4 us -> 70 us
    pallas_call x1, Pallas kernels: 7.57 us -> 4.24 us  [solve(): pl.pallas_call(solve_kernel, out_shape=jax.ShapeDtypeStruct(rhs.shape, F3...]
    pallas_call x1, Pallas kernels: 8.79 us -> 5.46 us  [solve_and_route(): pl.pallas_call(functools.partial(route_kernel, block), out_shape=(out, ou...]
  transfers between devices with their start and end apart: 16 -> 16, of which waited for: 11 -> 11; matrix products, arithmetic and copies ran while one was open for 3% -> 3% of each run, Pallas kernels for 27% -> 26%
where the time goes in v7:
time: 220 us; the launch traced here: 219 us
  waiting for transfers between devices  81 us (37%)
  Pallas kernels  70 us (32%)
  starting transfers between devices  42.5 us (19%)
  local copies, waits for them, and re-layouts  11.9 us (5%)
  between operations  6.81 us (3%)
  other arithmetic  6.69 us (3%)
    pallas_call x1, Pallas kernels, chol(): pl.pallas_call(chol_kernel, out_shape=(jax.ShapeDtypeStruct((n, WIDE), BF...  47.6 us
    all_to_all x1, waiting for transfers between devices, per_device(): lax.all_to_all(part.reshape(chips, per_chip * SLAB, B), 'dp', split_axis=...  28.3 us
    all_to_all x1, waiting for transfers between devices, per_device(): lax.all_to_all(spread, 'dp', split_axis=0, concat_axis=0, tiled=True, axi...  11.5 us
    all_to_all x1, waiting for transfers between devices, per_device(): lax.all_to_all(part_w, 'dp', split_axis=0, concat_axis=0, tiled=True, axi...  10.5 us
    all_to_all x1, waiting for transfers between devices, per_device(): lax.all_to_all(pair, 'dp', split_axis=0, concat_axis=0, tiled=True, axis_...  9.31 us
    all_to_all x1, starting transfers between devices, per_device(): lax.all_to_all(part.reshape(chips, per_chip * SLAB, B), 'dp', split_axis=...  9.3 us
    all_to_all x1, starting transfers between devices, per_device(): lax.all_to_all(pair, 'dp', split_axis=0, concat_axis=0, tiled=True, axis_...  9.3 us
    ppermute x1, waiting for transfers between devices, per_device(): their_w = lax.ppermute(my_w, 'grp', [(1, 0)])  8.59 us
  transfers between devices with their start and end apart: 16, of which 11 were waited for; matrix products, arithmetic and copies ran while one was open for 3% of the time, Pallas kernels for 26%

profile of v7, /device:TPU:0, one launch (start us, length us, event | category | flops | bytes accessed | tf_op | source)
XLA Modules:
  0.0 219.0 jit_solution(7944460491009247052)
XLA Ops:
  0.7 0.5 collective-permute-start.1
  1.2 1.5 broadcast_select_fusion
  2.7 0.9 fusion.4
  3.6 1.6 collective-permute-start.2
  5.2 2.1 collective-permute-start.3
  7.3 0.7 fusion.5
  11.9 2.3 %collective-permute-done.2.refs_2_ = bf16[128,1408]{1,0:T(8,128)(2,1)S(1)} collective-permute-done((bf16[128,1408]{1,0:T(8,128)(2,1)}, bf16[128,1408]{1,0:T(8,128)(2,1)S(1)}, u32[]{:S(2)}, u32[]{:S(2)}) %collective-permute-start.2) | collective-permute-done | bytes 360480 | tf_op jit(solution)/shard_map/ppermute | solution.py:516
  14.3 2.5 %collective-permute-done.3.refs_3_ = bf16[128,1408]{1,0:T(8,128)(2,1)S(1)} collective-permute-done((bf16[128,1408]{1,0:T(8,128)(2,1)}, bf16[128,1408]{1,0:T(8,128)(2,1)S(1)}, u32[]{:S(2)}, u32[]{:S(2)}) %collective-permute-start.3) | collective-permute-done | bytes 360480 | tf_op jit(solution)/shard_map/ppermute | solution.py:517
  16.9 1.6 collective-permute-done.5.refs_5_
  18.4 4.2 %gram.1 = (f32[4608,128]{1,0:T(8,128)}, f32[8,1408]{1,0:T(8,128)S(1)}) custom-call(s32[1]{0:T(128)} %bitcast.4.core_ref, f32[6]{0:T(128)S(1)} %stack.36.keep_ref, bf16[256,1408]{1,0:T(8,128)(2,1)S(1)} %get-tuple-element.29.refs_0_, bf16[256,1408]{1,0:T(8,128)(2,1)S(1)} %broadcast_select_fusion.1.refs_1_, ...), custom_call_target="tpu_custom_call" | custom-call | flops 4400000000 | bytes 1048576 | tf_op jit(solution)/shard_map/gram/pallas_call | solution.py:106
  22.7 9.3 %all-to-all-start = ((f32[32,144,128]{2,1,0:T(8,128)}), f32[32,144,128]{2,1,0:T(8,128)S(1)}, u32[]{:S(2)}, u32[]{:S(2)}) async-start(f32[32,144,128]{2,1,0:T(8,128)} %bitcast.5), calls=%async_computation | async-start | bytes 4718592 | tf_op jit(solution)/shard_map/all_to_all | solution.py:535
  32.0 0.6 reduce_sum.18
  33.3 0.6 fusion.6
  35.4 28.3 %all-to-all-done.parts_ref = f32[32,144,128]{2,1,0:T(8,128)S(1)} async-done(((f32[32,144,128]{2,1,0:T(8,128)}), f32[32,144,128]{2,1,0:T(8,128)S(1)}, u32[]{:S(2)}, u32[]{:S(2)}) %all-to-all-start) | async-done | bytes 2359328 | tf_op jit(solution)/shard_map/all_to_all | solution.py:535
  63.7 2.0 damp_and_spread.1
  65.7 6.9 %all-to-all-start.1 = ((bf16[32,144,128]{2,1,0:T(8,128)(2,1)}), bf16[32,144,128]{2,1,0:T(8,128)(2,1)S(1)}, u32[]{:S(2)}, u32[]{:S(2)}) async-start(bf16[32,144,128]{2,1,0:T(8,128)(2,1)} %get-tuple-element.13), calls=%async_computation.1 | async-start | bytes 2359296 | tf_op jit(solution)/shard_map/all_to_all | solution.py:547
  72.6 1.1 copy-done.3
  73.7 1.1 copy-done.4
  74.8 3.3 %cross.1 = f32[32,24,1408]{2,1,0:T(8,128)S(1)} custom-call(s32[1]{0:T(128)} %bitcast.4.core_ref, f32[6]{0:T(128)S(1)} %stack.36.keep_ref, f32[8,128]{1,0:T(8,128)S(1)} %get-tuple-element.14.after_ref, bf16[256,1408]{1,0:T(8,128)(2,1)S(1)} %copy-done.3, bf16[256,1408]{1,0:T(8,128)(2,1)S(1)} %copy-done.2, bf16[256,1408]{1,0:T(8,128)(2,1)S(1)} %copy-done.4, ...), custom_call_target="tpu_custom_call" | custom-call | flops 32999999488 | bytes 1048576 | tf_op jit(solution)/shard_map/cross/pallas_call | solution.py:135
  78.1 2.0 copy-done
  80.1 11.5 %all-to-all-done.1 = bf16[32,144,128]{2,1,0:T(8,128)(2,1)S(1)} async-done(((bf16[32,144,128]{2,1,0:T(8,128)(2,1)}), bf16[32,144,128]{2,1,0:T(8,128)(2,1)S(1)}, u32[]{:S(2)}, u32[]{:S(2)}) %all-to-all-start.1) | async-done | bytes 1179680 | tf_op jit(solution)/shard_map/all_to_all | solution.py:547
  91.9 5.7 %all-to-all-start.2 = ((f32[32,24,1408]{2,1,0:T(8,128)}), f32[32,24,1408]{2,1,0:T(8,128)}, u32[]{:S(2)}, u32[]{:S(2)}) async-start(f32[32,24,1408]{2,1,0:T(8,128)} %copy-done), calls=%async_computation.2 | async-start | bytes 8650752 | tf_op jit(solution)/shard_map/all_to_all | solution.py:554
  97.7 47.6 %cholesky.1 = (bf16[1408,14336]{1,0:T(8,128)(2,1)}, f32[8,128]{1,0:T(8,128)S(1)}) custom-call(s32[1]{0:T(128)} %bitcast.4.core_ref, bf16[4608,128]{1,0:T(8,128)(2,1)S(1)} %bitcast.24, bf16[4608,128]{1,0:T(8,128)(2,1)S(1)} %collective-permute-done.6.other_ref), custom_call_target="tpu_custom_call" | custom-call | flops 62699999232 | bytes 1048576 | tf_op jit(solution)/shard_map/cholesky/pallas_call | solution.py:288
  145.3 10.5 %all-to-all-done.2.parts_ref = f32[32,24,1408]{2,1,0:T(8,128)} async-done(((f32[32,24,1408]{2,1,0:T(8,128)}), f32[32,24,1408]{2,1,0:T(8,128)}, u32[]{:S(2)}, u32[]{:S(2)}) %all-to-all-start.2) | async-done | bytes 4325408 | tf_op jit(solution)/shard_map/all_to_all | solution.py:554
  155.8 2.4 %sum_parts.1.one_ref = f32[24,1408]{1,0:T(8,128)S(1)} custom-call(f32[32,24,1408]{2,1,0:T(8,128)} %all-to-all-done.2.parts_ref, f32[8,128]{1,0:T(8,128)S(1)} %get-tuple-element.17.refs_0_), custom_call_target="tpu_custom_call" | custom-call | flops 3300000000 | bytes 1048576 | tf_op jit(solution)/shard_map/sum_parts/pallas_call | solution.py:445
  158.2 1.5 collective-permute-start.7
  159.9 8.6 %collective-permute-done.7.two_ref = f32[24,1408]{1,0:T(8,128)S(1)} collective-permute-done((f32[24,1408]{1,0:T(8,128)S(1)}, f32[24,1408]{1,0:T(8,128)S(1)}, u32[]{:S(2)}, u32[]{:S(2)}) %collective-permute-start.7) | collective-permute-done | bytes 135200 | tf_op jit(solution)/shard_map/ppermute | solution.py:562
  168.5 5.5 %solve_and_route.1 = (f32[24,768]{1,0:T(8,128)S(1)}, f32[24,768]{1,0:T(8,128)S(1)}) custom-call(s32[2,32]{1,0:T(2,128)S(1)} %pad_add_fusion.owner_ref, f32[1]{0:T(128)} %bitcast.total_ref, f32[24,1408]{1,0:T(8,128)S(1)} %sum_parts.1.one_ref, f32[24,1408]{1,0:T(8,128)S(1)} %collective-permute-done.7.two_ref, bf16[1408,14336]{1,0:T(8,128)(2,1)} %get-tuple-element.18.low_ref), custom_call_target="tpu_custom_call" | custom-call | flops 9900000256 | bytes 1048576 | tf_op jit(solution)/shard_map/solve_and_route/pallas_call | solution.py:397
  174.0 1.5 collective-permute-start.8
  175.5 1.3 collective-permute-start.9
  176.8 0.3 copy.12
  177.1 0.3 collective-permute-done.8
  177.4 1.5 collective-permute-done.9
  179.1 0.8 reshape.148
  179.9 1.9 pad_maximum_fusion
  181.8 2.0 reshape.153
  183.8 9.3 %all-to-all-start.3 = ((f32[32,1,1078]{2,1,0:T(1,128)}), f32[32,1,1078]{2,1,0:T(1,128)S(1)}, u32[]{:S(2)}, u32[]{:S(2)}) async-start(f32[32,1,1078]{2,1,0:T(1,128)} %reshape.153), calls=%async_computation.3 | async-start | bytes 294912 | tf_op jit(solution)/shard_map/all_to_all | solution.py:571
  193.1 0.8 rows.1.after_ref
  193.9 9.3 %all-to-all-done.3 = f32[32,1,1078]{2,1,0:T(1,128)S(1)} async-done(((f32[32,1,1078]{2,1,0:T(1,128)}), f32[32,1,1078]{2,1,0:T(1,128)S(1)}, u32[]{:S(2)}, u32[]{:S(2)}) %all-to-all-start.3) | async-done | bytes 138016 | tf_op jit(solution)/shard_map/all_to_all | solution.py:571
  203.2 0.5 broadcast.163
  203.7 1.0 reduce.7
  204.9 0.3 slice_reduce_fusion
  205.3 1.5 collective-permute-start.10
  207.1 4.2 %solve.1 = f32[24,1408]{1,0:T(8,128)S(1)} custom-call(f32[24,1408]{1,0:T(8,128)S(1)} %pad.4.rhs_ref, bf16[1408,14336]{1,0:T(8,128)(2,1)} %get-tuple-element.18.low_ref, f32[24,1408]{1,0:T(8,128)S(1)} %rows.1.after_ref), custom_call_target="tpu_custom_call" | custom-call | flops 7699999744 | bytes 1048576 | tf_op jit(solution)/shard_map/solve/pallas_call | solution.py:360
  211.4 1.3 collective-permute-start.11
  212.8 0.8 copy.14
  213.7 4.6 %collective-permute-done.11 = f32[22,1408]{1,0:T(8,128)S(1)} collective-permute-done((f32[22,1408]{1,0:T(8,128)S(1)}, f32[22,1408]{1,0:T(8,128)S(1)}, u32[]{:S(2)}, u32[]{:S(2)}) %collective-permute-start.11) | collective-permute-done | bytes 123936 | tf_op jit(solution)/shard_map/ppermute | solution.py:580
  218.3 0.7 select_bitcast_fusion
  (49 shorter events, 2.0 us)
Async XLA Ops:
  0.6 6.7 %copy-start.5 = (s32[128]{0:T(128)S(1)}, s32[128]{0:T(128)}, u32[]{:S(2)}) copy-start(s32[128]{0:T(128)} %param.7) | copy-start | bytes 1540
  0.6 16.1 %collective-permute-start = (bf16[256,1408]{1,0:T(8,128)(2,1)}, bf16[256,1408]{1,0:T(8,128)(2,1)S(1)}, u32[]{:S(2)}, u32[]{:S(2)}) collective-permute-start(bf16[256,1408]{1,0:T(8,128)(2,1)} %act_ref.1), channel_id=1, source_target_pairs={{0,1},{1,0},{2,3},{3,2},{4,5},{5,4},{6,7},{7,6},{8,9},{9,8},{10,11... | collective-permute-start | bytes 2162696 | tf_op jit(solution)/shard_map/ppermute | solution.py:518
  0.7 16.0 %collective-permute-start.1 = (bf16[256,1408]{1,0:T(8,128)(2,1)}, bf16[256,1408]{1,0:T(8,128)(2,1)S(1)}, u32[]{:S(2)}, u32[]{:S(2)}) collective-permute-start(bf16[256,1408]{1,0:T(8,128)(2,1)} %grad_ref.1), channel_id=1, source_target_pairs={{0,1},{1,0},{2,3},{3,2},{4,5},{5,4},{6,7},{7,6},{8,9},{9,8},{10,11... | collective-permute-start | bytes 2162696 | tf_op jit(solution)/shard_map/ppermute | solution.py:519
  3.6 10.6 %collective-permute-start.2 = (bf16[128,1408]{1,0:T(8,128)(2,1)}, bf16[128,1408]{1,0:T(8,128)(2,1)S(1)}, u32[]{:S(2)}, u32[]{:S(2)}) collective-permute-start(bf16[128,1408]{1,0:T(8,128)(2,1)} %get-tuple-element.31), channel_id=1, source_target_pairs={{0,64},{1,65},{2,66},{3,67},{4,68},{5,69},{6,70},{7,71},{8,72},{9,... | collective-permute-start | bytes 1081352 | tf_op jit(solution)/shard_map/ppermute | solution.py:516
  5.2 11.6 %collective-permute-start.3 = (bf16[128,1408]{1,0:T(8,128)(2,1)}, bf16[128,1408]{1,0:T(8,128)(2,1)S(1)}, u32[]{:S(2)}, u32[]{:S(2)}) collective-permute-start(bf16[128,1408]{1,0:T(8,128)(2,1)} %get-tuple-element.30), channel_id=1, source_target_pairs={{0,96},{1,97},{2,98},{3,99},{4,100},{5,101},{6,102},{7,103},{8,104... | collective-permute-start | bytes 1081352 | tf_op jit(solution)/shard_map/ppermute | solution.py:517
  14.2 2.6 %collective-permute-start.4 = (bf16[128,1408]{1,0:T(8,128)(2,1)S(1)}, bf16[128,1408]{1,0:T(8,128)(2,1)S(1)}, u32[]{:S(2)}, u32[]{:S(2)}) collective-permute-start(bf16[128,1408]{1,0:T(8,128)(2,1)S(1)} %collective-permute-done.2.refs_2_), channel_id=1, source_target_pairs={{0,1},{1,0},{2,3},{3,2},{4,5},{5,4},{6,7},{7,6},{8,9},{9,8},{10,11... | collective-permute-start | bytes 1081352 | tf_op jit(solution)/shard_map/ppermute | solution.py:522
  16.8 1.7 collective-permute-start.5
  16.8 5.9 %copy-start.1 = (bf16[256,1408]{1,0:T(8,128)(2,1)}, bf16[256,1408]{1,0:T(8,128)(2,1)S(1)}, u32[]{:S(2)}) copy-start(bf16[256,1408]{1,0:T(8,128)(2,1)S(1)} %collective-permute-done.1.grad_mate_ref) | copy-start | bytes 2162692
  22.7 10.6 %copy-start.6 = (f32[2]{0:T(128)S(1)}, f32[2]{0:T(128)}, u32[]{:S(2)}) copy-start(f32[2]{0:T(128)} %param.9) | copy-start | bytes 28
  22.7 41.0 %all-to-all-start = ((f32[32,144,128]{2,1,0:T(8,128)}), f32[32,144,128]{2,1,0:T(8,128)S(1)}, u32[]{:S(2)}, u32[]{:S(2)}) async-start(f32[32,144,128]{2,1,0:T(8,128)} %bitcast.5), calls=%async_computation | async-start | bytes 4718592 | tf_op jit(solution)/shard_map/all_to_all | solution.py:535
  65.7 6.9 %copy-start.2 = (bf16[256,1408]{1,0:T(8,128)(2,1)S(1)}, bf16[256,1408]{1,0:T(8,128)(2,1)}, u32[]{:S(2)}) copy-start(bf16[256,1408]{1,0:T(8,128)(2,1)} %copy-done.1) | copy-start | bytes 2162692
  65.7 25.9 %all-to-all-start.1 = ((bf16[32,144,128]{2,1,0:T(8,128)(2,1)}), bf16[32,144,128]{2,1,0:T(8,128)(2,1)S(1)}, u32[]{:S(2)}, u32[]{:S(2)}) async-start(bf16[32,144,128]{2,1,0:T(8,128)(2,1)} %get-tuple-element.13), calls=%async_computation.1 | async-start | bytes 2359296 | tf_op jit(solution)/shard_map/all_to_all | solution.py:547
  72.6 1.1 copy-start.3
  73.7 1.1 copy-start.4
  74.8 16.8 %copy-start.7 = (s32[64]{0:T(128)S(1)}, s32[64]{0:T(128)}, u32[]{:S(2)}) copy-start(s32[64]{0:T(128)} %param.8) | copy-start | bytes 772
  78.1 2.0 copy-start
  91.6 6.1 %collective-permute-start.6 = (bf16[4608,128]{1,0:T(8,128)(2,1)S(1)}, bf16[4608,128]{1,0:T(8,128)(2,1)S(1)}, u32[]{:S(2)}, u32[]{:S(2)}) collective-permute-start(bf16[4608,128]{1,0:T(8,128)(2,1)S(1)} %bitcast.23), channel_id=1, source_target_pairs={{0,1},{1,0},{2,3},{3,2},{4,5},{5,4},{6,7},{7,6},{8,9},{9,8},{10,11... | collective-permute-start | bytes 3538952 | tf_op jit(solution)/shard_map/ppermute | solution.py:551
  91.9 63.8 %all-to-all-start.2 = ((f32[32,24,1408]{2,1,0:T(8,128)}), f32[32,24,1408]{2,1,0:T(8,128)}, u32[]{:S(2)}, u32[]{:S(2)}) async-start(f32[32,24,1408]{2,1,0:T(8,128)} %copy-done), calls=%async_computation.2 | async-start | bytes 8650752 | tf_op jit(solution)/shard_map/all_to_all | solution.py:554
  158.2 10.3 %collective-permute-start.7 = (f32[24,1408]{1,0:T(8,128)S(1)}, f32[24,1408]{1,0:T(8,128)S(1)}, u32[]{:S(2)}, u32[]{:S(2)}) collective-permute-start(f32[24,1408]{1,0:T(8,128)S(1)} %sum_parts.1.one_ref), channel_id=1, source_target_pairs={{64,0},{65,1},{66,2},{67,3},{68,4},{69,5},{70,6},{71,7},{72,8},{73... | collective-permute-start | bytes 405512 | tf_op jit(solution)/shard_map/ppermute | solution.py:562
  174.0 3.5 %collective-permute-start.8 = (f32[24,768]{1,0:T(8,128)S(1)}, f32[24,768]{1,0:T(8,128)S(1)}, u32[]{:S(2)}, u32[]{:S(2)}) collective-permute-start(f32[24,768]{1,0:T(8,128)S(1)} %get-tuple-element.19), channel_id=1, source_target_pairs={{0,64},{1,65},{2,66},{3,67},{4,68},{5,69},{6,70},{7,71},{8,72},{9,... | collective-permute-start | bytes 221192 | tf_op jit(solution)/shard_map/ppermute | solution.py:564
  175.5 3.4 %collective-permute-start.9 = (f32[24,768]{1,0:T(8,128)S(1)}, f32[24,768]{1,0:T(8,128)S(1)}, u32[]{:S(2)}, u32[]{:S(2)}) collective-permute-start(f32[24,768]{1,0:T(8,128)S(1)} %get-tuple-element.20), channel_id=1, source_target_pairs={{0,65},{1,64},{2,67},{3,66},{4,69},{5,68},{6,71},{7,70},{8,73},{9,... | collective-permute-start | bytes 221192 | tf_op jit(solution)/shard_map/ppermute | solution.py:565
  183.8 19.4 %all-to-all-start.3 = ((f32[32,1,1078]{2,1,0:T(1,128)}), f32[32,1,1078]{2,1,0:T(1,128)S(1)}, u32[]{:S(2)}, u32[]{:S(2)}) async-start(f32[32,1,1078]{2,1,0:T(1,128)} %reshape.153), calls=%async_computation.3 | async-start | bytes 294912 | tf_op jit(solution)/shard_map/all_to_all | solution.py:571
  205.3 7.4 %collective-permute-start.10 = (f32[22,1408]{1,0:T(8,128)S(1)}, f32[22,1408]{1,0:T(8,128)S(1)}, u32[]{:S(2)}, u32[]{:S(2)}) collective-permute-start(f32[22,1408]{1,0:T(8,128)S(1)} %slice_select_fusion), channel_id=1, source_target_pairs={{0,64},{64,0},{1,65},{65,1},{2,66},{66,2},{3,67},{67,3},{4,68},{68... | collective-permute-start | bytes 371720 | tf_op jit(solution)/shard_map/ppermute | solution.py:578
  211.4 6.9 %collective-permute-start.11 = (f32[22,1408]{1,0:T(8,128)S(1)}, f32[22,1408]{1,0:T(8,128)S(1)}, u32[]{:S(2)}, u32[]{:S(2)}) collective-permute-start(f32[22,1408]{1,0:T(8,128)S(1)} %bitcast.26), channel_id=1, source_target_pairs={{64,0},{65,1},{66,2},{67,3},{68,4},{69,5},{70,6},{71,7},{72,8},{73... | collective-permute-start | bytes 371720 | tf_op jit(solution)/shard_map/ppermute | solution.py:580

commit v8 on v7

--- a/solution.py
+++ b/solution.py
@@ -113,35 +113,43 @@
             pltpu.VMEM((B, width), F32),
             pltpu.SemaphoreType.DMA((width // B + 1,)),
         ],
-        compiler_params=params(24),
+        compiler_params=params(40),
         cost_estimate=cost(4),
         name="gram",
     )(core, keeps, *pieces)
 
 
-def cross_kernel(core_ref, keep_ref, after_ref, grad_ref, grad_mate_ref, act_ref, act_mate_ref, out_ref, tmp_ref):
-    n = act_ref.shape[1]
-    for i in range(n // B):
-        cols = slice(i * B, (i + 1) * B)
-        own = dot(grad_ref[:, cols] * keep_ref[0].astype(BF16), act_ref[...], TN)
-        tmp_ref[cols, :] = own + dot(grad_mate_ref[:, cols] * keep_ref[1].astype(BF16), act_mate_ref[...], TN)
-    tmp_ref[n:, :] = jnp.zeros((tmp_ref.shape[0] - n, n), F32)
+def cross_kernel(core_ref, grp_ref, keep_ref, after_ref, *refs):
+    mine, other, (out_ref, tmp_ref) = pieces_of(refs[:6]), pieces_of(refs[6:12]), refs[12:]
+    n = refs[0].shape[1]
+    wide = out_ref.shape[2]
+
+    def run(left, right, first):
+        for i in range(n // B):
+            acc = None
+            for lg, rg in zip(left, right):
+                p = dot(columns_of(lg, slice(i * B, (i + 1) * B), keep_ref), columns_of(rg, slice(first, first + wide)), TN)
+                acc = p if acc is None else acc + p
+            tmp_ref[i * B : (i + 1) * B, :] = acc
+
+    pl.when(grp_ref[0] == 0)(lambda: run(other, mine, 0))
+    pl.when(grp_ref[0] == 1)(lambda: run(mine, other, n - wide))
+    tmp_ref[n:, :] = jnp.zeros((tmp_ref.shape[0] - n, wide), F32)
     for q in range(out_ref.shape[0]):
         out_ref[q] = tmp_ref[pl.ds(pl.multiple_of((2 * q + core_ref[0]) * ROWS, 8), ROWS), :]
 
 
-def cross(core, keeps, after, grads, acts, chips):
-    width = acts[0].shape[1]
+def cross(core, grp, keeps, after, mine, other, chips, wide):
     return pl.pallas_call(
         cross_kernel,
-        out_shape=jax.ShapeDtypeStruct((chips, ROWS, width), F32),
-        in_specs=[SM, SM, ANY] + [VM] * 4,
+        out_shape=jax.ShapeDtypeStruct((chips, ROWS, wide), F32),
+        in_specs=[SM, SM, SM, ANY] + [VM] * 12,
         out_specs=VM,
-        scratch_shapes=[pltpu.VMEM((2 * chips * ROWS, width), F32)],
-        compiler_params=params(32),
+        scratch_shapes=[pltpu.VMEM((2 * chips * ROWS, wide), F32)],
+        compiler_params=params(40),
         cost_estimate=cost(30),
         name="cross",
-    )(core, keeps, after, *grads, *acts)
+    )(core, grp, keeps, after, *mine, *other)
 
 
 def factor_diag(block):
@@ -370,11 +378,12 @@
 
 
 def route_kernel(block, owner_ref, total_ref, one_ref, two_ref, low_ref, same_ref, cross_ref, t_ref, r_ref, *scratch):
-    m, n = one_ref.shape
-    total = total_ref[0]
+    m, wide = one_ref.shape
+    n = t_ref.shape[1] - B
+    right = jnp.concatenate([one_ref[...], two_ref[:, 2 * wide - n :]], 1) / total_ref[0]
 
     def rhs(cols):
-        return (one_ref[:, cols] + two_ref[:, cols]) / total
+        return right[:, cols]
 
     solve_into(rhs, m, n, low_ref, t_ref, *scratch)
     t_ref[:, n:] = jnp.zeros((m, t_ref.shape[1] - n), F32)
@@ -390,8 +399,8 @@
         out_ref[...] = r_ref[:, : out_ref.shape[1]]
 
 
-def solve_and_route(owner, total, one, two, low, block):
-    m, n = one.shape
+def solve_and_route(owner, total, one, two, low, n, block):
+    m = one.shape[0]
     wide = -(-owner.shape[1] * block // B) * B
     out = jax.ShapeDtypeStruct((m, wide), F32)
     return pl.pallas_call(
@@ -435,7 +444,7 @@
         in_specs=[SM, VM, VM],
         out_specs=(HBM, VM),
         scratch_shapes=[pltpu.VMEM(parts.shape[1:], BF16), pltpu.SemaphoreType.DMA((chips,))],
-        compiler_params=params(16),
+        compiler_params=params(60),
         cost_estimate=cost(3),
         name="damp_and_spread",
     )(scale, parts, diag)
@@ -512,15 +521,18 @@
     both = ("grp", "dp")
     half = per_dev // 2
 
-    sent = jnp.where(is_a, out_grad, attn_out)
-    from_near = lax.ppermute(sent[:half], both, near)
-    from_far = lax.ppermute(sent[half:], both, far)
-    act_mate = lax.ppermute(attn_out, "dp", swap_core)
-    grad_mate = lax.ppermute(out_grad, "dp", swap_core)
-    mine_rows = [
-        jnp.where(is_a, attn_out, out_grad), jnp.where(is_a, act_mate, grad_mate), from_near, from_far,
-        lax.ppermute(from_near, "dp", swap_core), lax.ppermute(from_far, "dp", swap_core),
-    ]
+    def swap(rows):
+        return lax.ppermute(rows[:half], both, near), lax.ppermute(rows[half:], both, far)
+
+    def to_mate(rows):
+        return lax.ppermute(rows, "dp", swap_core)
+
+    first = jnp.where(is_a, attn_out, out_grad)
+    second = jnp.where(is_a, out_grad, attn_out)
+    from_near, from_far = swap(second)
+    mine_rows = [first, to_mate(first), from_near, from_far, to_mate(from_near), to_mate(from_far)]
+    first_later, _, _ = lax.optimization_barrier((first, from_near, from_far))
+    next_near, next_far = swap(first_later)
     over, mate, away = 1 - grp_index, dp_index ^ 1, dp_index ^ flip
     keeps = jnp.stack([
         keep_of(grp_index, dp_index),
@@ -532,6 +544,8 @@
     ])
     total = (TOK * jnp.sum(image_counts)).astype(F32)
     part, squares = gram(core_arr, keeps, mine_rows, chips * per_chip)
+    part, next_near, next_far = lax.optimization_barrier((part, next_near, next_far))
+    other_rows = [second, to_mate(second), next_near, next_far, to_mate(next_near), to_mate(next_far)]
     got = lax.all_to_all(
         part.reshape(chips, per_chip * SLAB, B), "dp", split_axis=0, concat_axis=0, tiled=True, axis_index_groups=same_core
     )
@@ -546,7 +560,8 @@
     spread, damp_done = damp_and_spread(jnp.stack([total, damp]), got, diag.astype(F32))
     mine = lax.all_to_all(spread, "dp", split_axis=0, concat_axis=0, tiled=True, axis_index_groups=same_core)
     mine = mine.reshape(chips * per_chip * SLAB, B)
-    part_w = cross(core_arr, keeps, damp_done, [out_grad, grad_mate], [attn_out, act_mate], chips)
+    wide = (nb + 2) // 2 * B
+    part_w = cross(core_arr, grp_index.astype(jnp.int32)[None], keeps, damp_done, mine_rows, other_rows, chips, wide)
     mine, part_w = lax.optimization_barrier((mine, part_w))
     theirs = lax.ppermute(mine, "dp", swap_core)
     low, chol_done = chol(core_arr, mine, theirs, width)
@@ -560,7 +575,7 @@
     order = jnp.stack([jnp.where(core == 0, order[:, 0], order[:, 1]), jnp.where(core == 0, order[:, 1], order[:, 0])])
     my_w = sum_parts(got_w, chol_done)
     their_w = lax.ppermute(my_w, "grp", [(1, 0)])
-    same, cross_t = solve_and_route(order, total[None], my_w, their_w, low, block)
+    same, cross_t = solve_and_route(order, total[None], my_w, their_w, low, width, block)
     same = lax.ppermute(same, both, [(d, n_dp + d) for d in range(n_dp)])
     cross_t = lax.ppermute(cross_t, both, [(d, n_dp + (d ^ 1)) for d in range(n_dp)])
     is_first = core == 0

time: 220 us -> 211 us (0.959)
  waiting for transfers between devices: 81 us -> 58.5 us
  Pallas kernels: 70 us -> 79.5 us
  starting transfers between devices: 42.5 us -> 46.1 us
    all_to_all x1, waiting for transfers between devices: 10.5 us -> 0.01 us  [per_device(): lax.all_to_all(part_w, 'dp', split_axis=0, concat_axis=0, tiled=True, axi...]
    pallas_call x1, Pallas kernels: 4.2 us -> 8.88 us  [gram(): pl.pallas_call(gram_kernel, out_shape=(jax.ShapeDtypeStruct((slots * SLAB...]
    ppermute x1, waiting for transfers between devices: 8.59 us -> 4.53 us  [per_device(): their_w = lax.ppermute(my_w, 'grp', [(1, 0)])]
    ppermute x6 -> x10, starting transfers between devices: 4.26 us -> 7.04 us  [the longest x2 4.27 us: swap(): lax.ppermute(rows[half:], both, far)]
    all_to_all x1, waiting for transfers between devices: 28.3 us -> 25.9 us  [per_device(): lax.all_to_all(part.reshape(chips, per_chip * SLAB, B), 'dp', split_axis=...]
    all_to_all x1, waiting for transfers between devices: 11.5 us -> 9.27 us  [per_device(): lax.all_to_all(spread, 'dp', split_axis=0, concat_axis=0, tiled=True, axi...]
    ppermute x6 -> x10, waiting for transfers between devices: 6.41 us -> 4.35 us  [the longest x2 2.46 us: swap(): lax.ppermute(rows[half:], both, far)]
    unnamed x19 -> x31, local copies, waits for them, and re-layouts: 7.26 us -> 8.85 us
  transfers between devices with their start and end apart: 16 -> 20, of which waited for: 11 -> 9; matrix products, arithmetic and copies ran while one was open for 3% -> 3% of each run, Pallas kernels for 26% -> 34%
where the time goes in v8:
time: 211 us; the launch traced here: 210 us
  Pallas kernels  79.5 us (38%)
  waiting for transfers between devices  58.5 us (28%)
  starting transfers between devices  46.1 us (22%)
  local copies, waits for them, and re-layouts  12.7 us (6%)
  between operations  6.94 us (3%)
  other arithmetic  6.08 us (3%)
    pallas_call x1, Pallas kernels, chol(): pl.pallas_call(chol_kernel, out_shape=(jax.ShapeDtypeStruct((n, WIDE), BF...  49 us
    all_to_all x1, waiting for transfers between devices, per_device(): lax.all_to_all(part.reshape(chips, per_chip * SLAB, B), 'dp', split_axis=...  25.9 us
    all_to_all x1, starting transfers between devices, per_device(): lax.all_to_all(part.reshape(chips, per_chip * SLAB, B), 'dp', split_axis=...  9.93 us
    all_to_all x1, starting transfers between devices, per_device(): lax.all_to_all(pair, 'dp', split_axis=0, concat_axis=0, tiled=True, axis_...  9.55 us
    all_to_all x1, waiting for transfers between devices, per_device(): lax.all_to_all(spread, 'dp', split_axis=0, concat_axis=0, tiled=True, axi...  9.27 us
    pallas_call x1, Pallas kernels, gram(): pl.pallas_call(gram_kernel, out_shape=(jax.ShapeDtypeStruct((slots * SLAB...  8.88 us
    unnamed x31, local copies, waits for them, and re-layouts  8.85 us
    all_to_all x1, waiting for transfers between devices, per_device(): lax.all_to_all(pair, 'dp', split_axis=0, concat_axis=0, tiled=True, axis_...  8.01 us
  transfers between devices with their start and end apart: 20, of which 9 were waited for; matrix products, arithmetic and copies ran while one was open for 3% of the time, Pallas kernels for 34%

profile of v8, /device:TPU:0, one launch (start us, length us, event | category | flops | bytes accessed | tf_op | source)
XLA Modules:
  0.0 209.9 jit_solution(7143290093227697757)
XLA Ops:
  0.6 1.5 broadcast_select_fusion
  2.1 0.8 fusion.5
  2.9 1.6 collective-permute-start.1
  4.5 2.1 collective-permute-start.2
  6.6 0.7 fusion.6
  11.2 1.9 collective-permute-done.1.refs_2_
  13.1 2.5 %collective-permute-done.2.refs_3_ = bf16[128,1408]{1,0:T(8,128)(2,1)S(1)} collective-permute-done((bf16[128,1408]{1,0:T(8,128)(2,1)S(1)}, bf16[128,1408]{1,0:T(8,128)(2,1)S(1)}, u32[]{:S(2)}, u32[]{:S(2)}) %collective-permute-start.2) | collective-permute-done | bytes 360480 | tf_op jit(solution)/shard_map/ppermute | solution.py:525
  15.6 0.5 collective-permute-start.4
  16.2 2.2 %collective-permute-start.6 = (bf16[128,1408]{1,0:T(8,128)(2,1)S(1)}, bf16[128,1408]{1,0:T(8,128)(2,1)}, u32[]{:S(2)}, u32[]{:S(2)}) collective-permute-start(bf16[128,1408]{1,0:T(8,128)(2,1)S(1)} %get-tuple-element.38), channel_id=1, source_target_pairs={{0,96},{1,97},{2,98},{3,99},{4,100},{5,101},{6,102},{7,103},{8,104... | collective-permute-start | bytes 1081352 | tf_op jit(solution)/shard_map/ppermute | solution.py:525
  18.4 8.9 %gram.1 = (f32[4608,128]{1,0:T(8,128)S(1)}, f32[8,1408]{1,0:T(8,128)S(1)}) custom-call(s32[1]{0:T(128)} %bitcast.4.core_ref, f32[6]{0:T(128)S(1)} %stack.36.keep_ref, bf16[256,1408]{1,0:T(8,128)(2,1)S(1)} %get-tuple-element.17.refs_0_, bf16[256,1408]{1,0:T(8,128)(2,1)S(1)} %collective-permute-done.refs_1_, ...), custom_call_target="tpu_custom_call" | custom-call | flops 4400000000 | bytes 1048576 | tf_op jit(solution)/shard_map/gram/pallas_call | solution.py:106
  27.4 1.4 copy-done
  28.8 9.9 %all-to-all-start = ((f32[32,144,128]{2,1,0:T(8,128)}), f32[32,144,128]{2,1,0:T(8,128)}, u32[]{:S(2)}, u32[]{:S(2)}) async-start(f32[32,144,128]{2,1,0:T(8,128)} %bitcast.24), calls=%async_computation | async-start | bytes 4718592 | tf_op jit(solution)/shard_map/all_to_all | solution.py:549
  38.9 0.6 reduce_sum.18
  40.2 0.6 fusion.7
  42.1 0.7 fusion.1.diag_ref
  42.8 0.5 collective-permute-start.8
  43.4 0.7 pad_maximum_fusion.3.scale_ref
  44.0 25.9 %all-to-all-done.parts_ref = f32[32,144,128]{2,1,0:T(8,128)} async-done(((f32[32,144,128]{2,1,0:T(8,128)}), f32[32,144,128]{2,1,0:T(8,128)}, u32[]{:S(2)}, u32[]{:S(2)}) %all-to-all-start) | async-done | bytes 2359328 | tf_op jit(solution)/shard_map/all_to_all | solution.py:549
  70.0 3.7 %damp_and_spread.1 = (bf16[32,144,128]{2,1,0:T(8,128)(2,1)}, f32[8,128]{1,0:T(8,128)}) custom-call(f32[2]{0:T(128)} %pad_maximum_fusion.3.scale_ref, f32[32,144,128]{2,1,0:T(8,128)} %all-to-all-done.parts_ref, f32[144,128]{1,0:T(8,128)} %fusion.1.diag_ref), custom_call_target="tpu_custom_call" | custom-call | flops 3300000000 | bytes 1048576 | tf_op jit(solution)/shard_map/damp_and_spread/pallas_call | solution.py:441
  73.7 6.7 %all-to-all-start.1 = ((bf16[32,144,128]{2,1,0:T(8,128)(2,1)}), bf16[32,144,128]{2,1,0:T(8,128)(2,1)S(1)}, u32[]{:S(2)}, u32[]{:S(2)}) async-start(bf16[32,144,128]{2,1,0:T(8,128)(2,1)} %get-tuple-element.19), calls=%async_computation.1 | async-start | bytes 2359296 | tf_op jit(solution)/shard_map/all_to_all | solution.py:561
  80.4 1.0 copy-done.3
  81.4 1.0 copy-done.5
  82.4 1.0 copy-done.7
  83.4 1.0 copy-done.9
  84.4 4.4 %cross.1 = f32[32,24,768]{2,1,0:T(8,128)S(1)} custom-call(s32[1]{0:T(128)} %bitcast.4.core_ref, s32[1]{0:T(128)} %bitcast.7.grp_ref, f32[6]{0:T(128)S(1)} %stack.36.keep_ref, f32[8,128]{1,0:T(8,128)S(1)} %copy-done.10, bf16[256,1408]{1,0:T(8,128)(2,1)S(1)} %get-tuple-element.17.refs_0_, bf16[256,1408]{1,0:T(8,128)(2,1)S(1)} %collective-permute-done.refs_1_, ...), custom_call_target="tpu_custom_call" | custom-call | flops 32999999488 | bytes 1048576 | tf_op jit(solution)/shard_map/cross/pallas_call | solution.py:143
  88.8 1.4 copy-done.1
  90.2 9.3 %all-to-all-done.1 = bf16[32,144,128]{2,1,0:T(8,128)(2,1)S(1)} async-done(((bf16[32,144,128]{2,1,0:T(8,128)(2,1)}), bf16[32,144,128]{2,1,0:T(8,128)(2,1)S(1)}, u32[]{:S(2)}, u32[]{:S(2)}) %all-to-all-start.1) | async-done | bytes 1179680 | tf_op jit(solution)/shard_map/all_to_all | solution.py:561
  99.8 5.7 %all-to-all-start.2 = ((f32[32,24,768]{2,1,0:T(8,128)}), f32[32,24,768]{2,1,0:T(8,128)}, u32[]{:S(2)}, u32[]{:S(2)}) async-start(f32[32,24,768]{2,1,0:T(8,128)} %copy-done.1), calls=%async_computation.2 | async-start | bytes 4718592 | tf_op jit(solution)/shard_map/all_to_all | solution.py:569
  105.5 49.0 %cholesky.1 = (bf16[1408,14336]{1,0:T(8,128)(2,1)}, f32[8,128]{1,0:T(8,128)S(1)}) custom-call(s32[1]{0:T(128)} %bitcast.4.core_ref, bf16[4608,128]{1,0:T(8,128)(2,1)S(1)} %bitcast.26, bf16[4608,128]{1,0:T(8,128)(2,1)} %collective-permute-done.10.other_ref), custom_call_target="tpu_custom_call" | custom-call | flops 62699999232 | bytes 1048576 | tf_op jit(solution)/shard_map/cholesky/pallas_call | solution.py:296
  154.5 1.8 sum_parts.1.one_ref
  156.3 1.6 collective-permute-start.11
  158.1 4.5 %collective-permute-done.11.two_ref = f32[24,768]{1,0:T(8,128)S(1)} collective-permute-done((f32[24,768]{1,0:T(8,128)S(1)}, f32[24,768]{1,0:T(8,128)S(1)}, u32[]{:S(2)}, u32[]{:S(2)}) %collective-permute-start.11) | collective-permute-done | bytes 73760 | tf_op jit(solution)/shard_map/ppermute | solution.py:577
  162.6 5.5 %solve_and_route.1 = (f32[24,768]{1,0:T(8,128)S(1)}, f32[24,768]{1,0:T(8,128)S(1)}) custom-call(s32[2,32]{1,0:T(2,128)S(1)} %pad_add_fusion.owner_ref, f32[1]{0:T(128)} %bitcast.total_ref, f32[24,768]{1,0:T(8,128)S(1)} %sum_parts.1.one_ref, f32[24,768]{1,0:T(8,128)S(1)} %collective-permute-done.11.two_ref, bf16[1408,14336]{1,0:T(8,128)(2,1)} %get-tuple-element.26.low_ref), custom_call_target="tpu_custom_call" | custom-call | flops 9900000256 | bytes 1048576 | tf_op jit(solution)/shard_map/solve_and_route/pallas_call | solution.py:406
  168.0 1.5 collective-permute-start.12
  169.6 1.3 collective-permute-start.13
  171.5 1.5 collective-permute-done.13
  173.4 1.0 reshape.153
  174.4 9.5 %all-to-all-start.3 = ((f32[32,1,1078]{2,1,0:T(1,128)}), f32[32,1,1078]{2,1,0:T(1,128)S(1)}, u32[]{:S(2)}, u32[]{:S(2)}) async-start(f32[32,1,1078]{2,1,0:T(1,128)} %reshape.153), calls=%async_computation.3 | async-start | bytes 294912 | tf_op jit(solution)/shard_map/all_to_all | solution.py:586
  184.0 2.1 rows.1.after_ref
  186.1 8.0 %all-to-all-done.3 = f32[32,1,1078]{2,1,0:T(1,128)S(1)} async-done(((f32[32,1,1078]{2,1,0:T(1,128)}), f32[32,1,1078]{2,1,0:T(1,128)S(1)}, u32[]{:S(2)}, u32[]{:S(2)}) %all-to-all-start.3) | async-done | bytes 138016 | tf_op jit(solution)/shard_map/all_to_all | solution.py:586
  194.1 0.5 broadcast.163
  194.6 1.0 reduce.7
  196.2 1.5 collective-permute-start.14
  198.0 4.2 %solve.1 = f32[24,1408]{1,0:T(8,128)S(1)} custom-call(f32[24,1408]{1,0:T(8,128)S(1)} %pad.4.rhs_ref, bf16[1408,14336]{1,0:T(8,128)(2,1)} %get-tuple-element.26.low_ref, f32[24,1408]{1,0:T(8,128)S(1)} %rows.1.after_ref), custom_call_target="tpu_custom_call" | custom-call | flops 7699999744 | bytes 1048576 | tf_op jit(solution)/shard_map/solve/pallas_call | solution.py:368
  202.3 1.3 collective-permute-start.15
  203.7 0.8 copy.14
  204.5 4.6 %collective-permute-done.15 = f32[22,1408]{1,0:T(8,128)S(1)} collective-permute-done((f32[22,1408]{1,0:T(8,128)S(1)}, f32[22,1408]{1,0:T(8,128)S(1)}, u32[]{:S(2)}, u32[]{:S(2)}) %collective-permute-start.15) | collective-permute-done | bytes 123936 | tf_op jit(solution)/shard_map/ppermute | solution.py:595
  209.2 0.7 select_bitcast_fusion
  (69 shorter events, 3.0 us)
Async XLA Ops:
  0.6 6.0 %copy-start.11 = (s32[128]{0:T(128)S(1)}, s32[128]{0:T(128)}, u32[]{:S(2)}) copy-start(s32[128]{0:T(128)} %param.7) | copy-start | bytes 1540
  2.9 10.2 %collective-permute-start.1 = (bf16[128,1408]{1,0:T(8,128)(2,1)}, bf16[128,1408]{1,0:T(8,128)(2,1)S(1)}, u32[]{:S(2)}, u32[]{:S(2)}) collective-permute-start(bf16[128,1408]{1,0:T(8,128)(2,1)} %get-tuple-element.41), channel_id=1, source_target_pairs={{0,64},{1,65},{2,66},{3,67},{4,68},{5,69},{6,70},{7,71},{8,72},{9,... | collective-permute-start | bytes 1081352 | tf_op jit(solution)/shard_map/ppermute | solution.py:525
  4.5 11.1 %collective-permute-start.2 = (bf16[128,1408]{1,0:T(8,128)(2,1)S(1)}, bf16[128,1408]{1,0:T(8,128)(2,1)S(1)}, u32[]{:S(2)}, u32[]{:S(2)}) collective-permute-start(bf16[128,1408]{1,0:T(8,128)(2,1)S(1)} %get-tuple-element.40), channel_id=1, source_target_pairs={{0,96},{1,97},{2,98},{3,99},{4,100},{5,101},{6,102},{7,103},{8,104... | collective-permute-start | bytes 1081352 | tf_op jit(solution)/shard_map/ppermute | solution.py:525
  6.6 11.8 %collective-permute-start = (bf16[256,1408]{1,0:T(8,128)(2,1)S(1)}, bf16[256,1408]{1,0:T(8,128)(2,1)S(1)}, u32[]{:S(2)}, u32[]{:S(2)}) collective-permute-start(bf16[256,1408]{1,0:T(8,128)(2,1)S(1)} %get-tuple-element.17.refs_0_), channel_id=1, source_target_pairs={{0,1},{1,0},{2,3},{3,2},{4,5},{5,4},{6,7},{7,6},{8,9},{9,8},{10,11... | collective-permute-start | bytes 2162696 | tf_op jit(solution)/shard_map/ppermute | solution.py:528
  13.1 14.2 %copy-start.2 = (bf16[128,1408]{1,0:T(8,128)(2,1)}, bf16[128,1408]{1,0:T(8,128)(2,1)S(1)}, u32[]{:S(2)}) copy-start(bf16[128,1408]{1,0:T(8,128)(2,1)S(1)} %collective-permute-done.1.refs_2_) | copy-start | bytes 1081348
  15.6 11.8 %copy-start.4 = (bf16[128,1408]{1,0:T(8,128)(2,1)}, bf16[128,1408]{1,0:T(8,128)(2,1)S(1)}, u32[]{:S(2)}) copy-start(bf16[128,1408]{1,0:T(8,128)(2,1)S(1)} %collective-permute-done.2.refs_3_) | copy-start | bytes 1081348
  15.6 2.8 %collective-permute-start.3 = (bf16[128,1408]{1,0:T(8,128)(2,1)S(1)}, bf16[128,1408]{1,0:T(8,128)(2,1)S(1)}, u32[]{:S(2)}, u32[]{:S(2)}) collective-permute-start(bf16[128,1408]{1,0:T(8,128)(2,1)S(1)} %collective-permute-done.1.refs_2_), channel_id=1, source_target_pairs={{0,1},{1,0},{2,3},{3,2},{4,5},{5,4},{6,7},{7,6},{8,9},{9,8},{10,11... | collective-permute-start | bytes 1081352 | tf_op jit(solution)/shard_map/ppermute | solution.py:528
  15.6 2.8 %collective-permute-start.4 = (bf16[128,1408]{1,0:T(8,128)(2,1)S(1)}, bf16[128,1408]{1,0:T(8,128)(2,1)S(1)}, u32[]{:S(2)}, u32[]{:S(2)}) collective-permute-start(bf16[128,1408]{1,0:T(8,128)(2,1)S(1)} %collective-permute-done.2.refs_3_), channel_id=1, source_target_pairs={{0,1},{1,0},{2,3},{3,2},{4,5},{5,4},{6,7},{7,6},{8,9},{9,8},{10,11... | collective-permute-start | bytes 1081352 | tf_op jit(solution)/shard_map/ppermute | solution.py:528
  16.1 12.7 %collective-permute-start.5 = (bf16[128,1408]{1,0:T(8,128)(2,1)S(1)}, bf16[128,1408]{1,0:T(8,128)(2,1)}, u32[]{:S(2)}, u32[]{:S(2)}) collective-permute-start(bf16[128,1408]{1,0:T(8,128)(2,1)S(1)} %get-tuple-element.39), channel_id=1, source_target_pairs={{0,64},{1,65},{2,66},{3,67},{4,68},{5,69},{6,70},{7,71},{8,72},{9,... | collective-permute-start | bytes 1081352 | tf_op jit(solution)/shard_map/ppermute | solution.py:525
  16.2 12.6 %collective-permute-start.6 = (bf16[128,1408]{1,0:T(8,128)(2,1)S(1)}, bf16[128,1408]{1,0:T(8,128)(2,1)}, u32[]{:S(2)}, u32[]{:S(2)}) collective-permute-start(bf16[128,1408]{1,0:T(8,128)(2,1)S(1)} %get-tuple-element.38), channel_id=1, source_target_pairs={{0,96},{1,97},{2,98},{3,99},{4,100},{5,101},{6,102},{7,103},{8,104... | collective-permute-start | bytes 1081352 | tf_op jit(solution)/shard_map/ppermute | solution.py:525
  18.4 8.9 %copy-start.6 = (bf16[128,1408]{1,0:T(8,128)(2,1)}, bf16[128,1408]{1,0:T(8,128)(2,1)S(1)}, u32[]{:S(2)}) copy-start(bf16[128,1408]{1,0:T(8,128)(2,1)S(1)} %collective-permute-done.3.refs_4_) | copy-start | bytes 1081348
  18.4 8.9 %copy-start.8 = (bf16[128,1408]{1,0:T(8,128)(2,1)}, bf16[128,1408]{1,0:T(8,128)(2,1)S(1)}, u32[]{:S(2)}) copy-start(bf16[128,1408]{1,0:T(8,128)(2,1)S(1)} %collective-permute-done.4.refs_5_) | copy-start | bytes 1081348
  27.4 1.4 copy-start
  28.8 11.3 %copy-start.12 = (f32[2]{0:T(128)S(1)}, f32[2]{0:T(128)}, u32[]{:S(2)}) copy-start(f32[2]{0:T(128)} %param.9) | copy-start | bytes 28
  28.8 41.1 %all-to-all-start = ((f32[32,144,128]{2,1,0:T(8,128)}), f32[32,144,128]{2,1,0:T(8,128)}, u32[]{:S(2)}, u32[]{:S(2)}) async-start(f32[32,144,128]{2,1,0:T(8,128)} %bitcast.24), calls=%async_computation | async-start | bytes 4718592 | tf_op jit(solution)/shard_map/all_to_all | solution.py:549
  38.8 41.6 %collective-permute-start.7 = (bf16[256,1408]{1,0:T(8,128)(2,1)S(1)}, bf16[256,1408]{1,0:T(8,128)(2,1)}, u32[]{:S(2)}, u32[]{:S(2)}) collective-permute-start(bf16[256,1408]{1,0:T(8,128)(2,1)S(1)} %get-tuple-element.36.refs_6_), channel_id=1, source_target_pairs={{0,1},{1,0},{2,3},{3,2},{4,5},{5,4},{6,7},{7,6},{8,9},{9,8},{10,11... | collective-permute-start | bytes 2162696 | tf_op jit(solution)/shard_map/ppermute | solution.py:528
  42.8 37.5 %collective-permute-start.8 = (bf16[128,1408]{1,0:T(8,128)(2,1)}, bf16[128,1408]{1,0:T(8,128)(2,1)}, u32[]{:S(2)}, u32[]{:S(2)}) collective-permute-start(bf16[128,1408]{1,0:T(8,128)(2,1)} %collective-permute-done.5.refs_8_), channel_id=1, source_target_pairs={{0,1},{1,0},{2,3},{3,2},{4,5},{5,4},{6,7},{7,6},{8,9},{9,8},{10,11... | collective-permute-start | bytes 1081352 | tf_op jit(solution)/shard_map/ppermute | solution.py:528
  43.3 37.0 %collective-permute-start.9 = (bf16[128,1408]{1,0:T(8,128)(2,1)}, bf16[128,1408]{1,0:T(8,128)(2,1)}, u32[]{:S(2)}, u32[]{:S(2)}) collective-permute-start(bf16[128,1408]{1,0:T(8,128)(2,1)} %collective-permute-done.6.refs_9_), channel_id=1, source_target_pairs={{0,1},{1,0},{2,3},{3,2},{4,5},{5,4},{6,7},{7,6},{8,9},{9,8},{10,11... | collective-permute-start | bytes 1081352 | tf_op jit(solution)/shard_map/ppermute | solution.py:528
  73.7 6.7 %copy-start.10 = (f32[8,128]{1,0:T(8,128)S(1)}, f32[8,128]{1,0:T(8,128)}, u32[]{:S(2)}) copy-start(f32[8,128]{1,0:T(8,128)} %get-tuple-element.20.after_ref) | copy-start | bytes 12292
  73.7 25.8 %all-to-all-start.1 = ((bf16[32,144,128]{2,1,0:T(8,128)(2,1)}), bf16[32,144,128]{2,1,0:T(8,128)(2,1)S(1)}, u32[]{:S(2)}, u32[]{:S(2)}) async-start(bf16[32,144,128]{2,1,0:T(8,128)(2,1)} %get-tuple-element.19), calls=%async_computation.1 | async-start | bytes 2359296 | tf_op jit(solution)/shard_map/all_to_all | solution.py:561
  80.4 1.0 copy-start.3
  81.4 1.0 copy-start.5
  82.4 1.0 copy-start.7
  83.4 1.0 copy-start.9
  84.3 15.1 %copy-start.13 = (s32[64]{0:T(128)S(1)}, s32[64]{0:T(128)}, u32[]{:S(2)}) copy-start(s32[64]{0:T(128)} %param.8) | copy-start | bytes 772
  88.7 1.4 copy-start.1
  99.5 6.1 %collective-permute-start.10 = (bf16[4608,128]{1,0:T(8,128)(2,1)S(1)}, bf16[4608,128]{1,0:T(8,128)(2,1)}, u32[]{:S(2)}, u32[]{:S(2)}) collective-permute-start(bf16[4608,128]{1,0:T(8,128)(2,1)S(1)} %bitcast.25), channel_id=1, source_target_pairs={{0,1},{1,0},{2,3},{3,2},{4,5},{5,4},{6,7},{7,6},{8,9},{9,8},{10,11... | collective-permute-start | bytes 3538952 | tf_op jit(solution)/shard_map/ppermute | solution.py:566
  99.8 54.7 %all-to-all-start.2 = ((f32[32,24,768]{2,1,0:T(8,128)}), f32[32,24,768]{2,1,0:T(8,128)}, u32[]{:S(2)}, u32[]{:S(2)}) async-start(f32[32,24,768]{2,1,0:T(8,128)} %copy-done.1), calls=%async_computation.2 | async-start | bytes 4718592 | tf_op jit(solution)/shard_map/all_to_all | solution.py:569
  156.3 6.3 %collective-permute-start.11 = (f32[24,768]{1,0:T(8,128)S(1)}, f32[24,768]{1,0:T(8,128)S(1)}, u32[]{:S(2)}, u32[]{:S(2)}) collective-permute-start(f32[24,768]{1,0:T(8,128)S(1)} %sum_parts.1.one_ref), channel_id=1, source_target_pairs={{64,0},{65,1},{66,2},{67,3},{68,4},{69,5},{70,6},{71,7},{72,8},{73... | collective-permute-start | bytes 221192 | tf_op jit(solution)/shard_map/ppermute | solution.py:577
  168.0 3.5 %collective-permute-start.12 = (f32[24,768]{1,0:T(8,128)S(1)}, f32[24,768]{1,0:T(8,128)S(1)}, u32[]{:S(2)}, u32[]{:S(2)}) collective-permute-start(f32[24,768]{1,0:T(8,128)S(1)} %get-tuple-element.27), channel_id=1, source_target_pairs={{0,64},{1,65},{2,66},{3,67},{4,68},{5,69},{6,70},{7,71},{8,72},{9,... | collective-permute-start | bytes 221192 | tf_op jit(solution)/shard_map/ppermute | solution.py:579
  169.6 3.4 %collective-permute-start.13 = (f32[24,768]{1,0:T(8,128)S(1)}, f32[24,768]{1,0:T(8,128)S(1)}, u32[]{:S(2)}, u32[]{:S(2)}) collective-permute-start(f32[24,768]{1,0:T(8,128)S(1)} %get-tuple-element.28), channel_id=1, source_target_pairs={{0,65},{1,64},{2,67},{3,66},{4,69},{5,68},{6,71},{7,70},{8,73},{9,... | collective-permute-start | bytes 221192 | tf_op jit(solution)/shard_map/ppermute | solution.py:580
  174.4 19.7 %all-to-all-start.3 = ((f32[32,1,1078]{2,1,0:T(1,128)}), f32[32,1,1078]{2,1,0:T(1,128)S(1)}, u32[]{:S(2)}, u32[]{:S(2)}) async-start(f32[32,1,1078]{2,1,0:T(1,128)} %reshape.153), calls=%async_computation.3 | async-start | bytes 294912 | tf_op jit(solution)/shard_map/all_to_all | solution.py:586
  196.2 7.4 %collective-permute-start.14 = (f32[22,1408]{1,0:T(8,128)S(1)}, f32[22,1408]{1,0:T(8,128)S(1)}, u32[]{:S(2)}, u32[]{:S(2)}) collective-permute-start(f32[22,1408]{1,0:T(8,128)S(1)} %slice_select_fusion), channel_id=1, source_target_pairs={{0,64},{64,0},{1,65},{65,1},{2,66},{66,2},{3,67},{67,3},{4,68},{68... | collective-permute-start | bytes 371720 | tf_op jit(solution)/shard_map/ppermute | solution.py:593
  202.3 6.9 %collective-permute-start.15 = (f32[22,1408]{1,0:T(8,128)S(1)}, f32[22,1408]{1,0:T(8,128)S(1)}, u32[]{:S(2)}, u32[]{:S(2)}) collective-permute-start(f32[22,1408]{1,0:T(8,128)S(1)} %bitcast.28), channel_id=1, source_target_pairs={{64,0},{65,1},{66,2},{67,3},{68,4},{69,5},{70,6},{71,7},{72,8},{73... | collective-permute-start | bytes 371720 | tf_op jit(solution)/shard_map/ppermute | solution.py:595

commit v9 on v8

--- a/solution.py
+++ b/solution.py
@@ -14,6 +14,7 @@
 ROWS = 24
 WIDE = 14336
 STEP = 512
+REST = 4096
 F32 = jnp.float32
 BF16 = jnp.bfloat16
 NT = (((1,), (1,)), ((), ()))
@@ -71,19 +72,12 @@
 
 
 def gram_kernel(core_ref, keep_ref, *refs):
-    pieces, (hbm_ref, squares_ref, out_ref, tmp_ref, sem) = pieces_of(refs[:6]), refs[6:]
+    pieces, (out_ref, squares_ref, tmp_ref) = pieces_of(refs[:6]), refs[6:]
     nb = refs[0].shape[1] // B
     start = pl.multiple_of(core_ref[0] * HALF, HALF)
     on = lax.broadcasted_iota(jnp.int32, (B, B), 0) == lax.broadcasted_iota(jnp.int32, (B, B), 1)
-    copies = []
-
-    def send(lo, hi):
-        copies.append(pltpu.make_async_copy(out_ref.at[lo:hi], hbm_ref.at[lo:hi], sem.at[len(copies)]))
-        copies[-1].start()
-
     used = tri(nb, 0) * HALF
     out_ref[used:, :] = jnp.zeros((out_ref.shape[0] - used, B), F32)
-    send(used, out_ref.shape[0])
     for i in range(nb):
         wide = (i + 1) * B
         acc = None
@@ -96,9 +90,6 @@
         for j in range(i + 1):
             t = tri(i, j)
             out_ref[t * HALF : (t + 1) * HALF, :] = tmp_ref[pl.ds(start, HALF), j * B : (j + 1) * B]
-        send(tri(i, 0) * HALF, tri(i + 1, 0) * HALF)
-    for copy in copies:
-        copy.wait()
 
 
 def gram(core, keeps, pieces, slots):
@@ -107,12 +98,8 @@
         gram_kernel,
         out_shape=(jax.ShapeDtypeStruct((slots * SLAB, B), F32), jax.ShapeDtypeStruct((8, width), F32)),
         in_specs=[SM, SM] + [VM] * 6,
-        out_specs=(HBM, VM),
-        scratch_shapes=[
-            pltpu.VMEM((slots * SLAB, B), F32),
-            pltpu.VMEM((B, width), F32),
-            pltpu.SemaphoreType.DMA((width // B + 1,)),
-        ],
+        out_specs=(VM, VM),
+        scratch_shapes=[pltpu.VMEM((B, width), F32)],
         compiler_params=params(40),
         cost_estimate=cost(4),
         name="gram",
@@ -217,101 +204,215 @@
     return jnp.concatenate([jnp.where(first, mine, other), jnp.where(first, other, mine)], 0)
 
 
-def join_inverses(low_ref, inv_ref, iv_ref):
-    n = low_ref.shape[0]
+def join_inverses(low_of, inv_ref, iv_ref, first, last):
     iv_ref[...] = jnp.zeros_like(iv_ref)
-    for b in range(n // B):
-        at = b * B % STEP
-        iv_ref[b * B : (b + 1) * B, at : at + B] = inv_ref[b * B : (b + 1) * B, :]
+    for b in range(first, last, B):
+        at = b % STEP
+        iv_ref[b - first : b - first + B, at : at + B] = inv_ref[b - first : b - first + B, :]
     size = B
     while size < STEP:
-        for r0 in range(0, n - size, 2 * size):
+        for r0 in range(first, last - size, 2 * size):
             r1 = r0 + size
-            r2 = min(r1 + size, n)
+            r2 = min(r1 + size, last)
             at = r0 % STEP
-            left = jnp.concatenate(split(iv_ref[r0:r1, at : at + size]), 1)
-            p = dot(low_ref[r1:r2, r0:r1], left, NN)
+            i0, i1, i2 = r0 - first, r1 - first, r2 - first
+            left = jnp.concatenate(split(iv_ref[i0:i1, at : at + size]), 1)
+            p = dot(low_of(slice(r1, r2), slice(r0, r1)), left, NN)
             phi, plo = split(p[:, :size] + p[:, size:])
-            bhi, blo = split(iv_ref[r1:r2, at + size : at + size + r2 - r1])
-            iv_ref[r1:r2, at : at + size] = -(dot(bhi, phi, NN) + dot(bhi, plo, NN) + dot(blo, phi, NN))
+            bhi, blo = split(iv_ref[i1:i2, at + size : at + size + r2 - r1])
+            iv_ref[i1:i2, at : at + size] = -(dot(bhi, phi, NN) + dot(bhi, plo, NN) + dot(blo, phi, NN))
         size *= 2
 
 
-def chol_kernel(core_ref, mine_ref, other_ref, low_hbm, done_ref, low_ref, inv_ref, lo_ref, s_ref, w_ref, iv_ref, hl_ref, sem):
-    done_ref[...] = jnp.zeros_like(done_ref)
-    n = low_ref.shape[0]
-    nb = n // B
-    first = core_ref[0] == 0
-
+def keep_blocks(mine_ref, other_ref, low_hbm, sem, back):
+    n = low_hbm.shape[0]
+    copies = []
+    for half, ref in enumerate((mine_ref, other_ref)):
+        total = ref.shape[0]
+        for p in range(-(-total // n)):
+            rows = min(n, total - p * n)
+            at = n + 2 * STEP + (4 * half + p) * B
+            here, there = ref.at[p * n : p * n + rows], low_hbm.at[:rows, at : at + B]
+            k = len(copies)
+            copies.append(pltpu.make_async_copy(*((there, here) if back else (here, there)), sem.at[k]))
+    for copy in copies:
+        copy.start()
+    return copies
+
+
+def halves_of(x):
+    return jnp.concatenate(split(x), 1)
+
+
+def block_of(mine_ref, other_ref, first, i, j):
+    t = tri(i, j) * HALF
+    mine = mine_ref[t : t + HALF, :].astype(F32)
+    other = other_ref[t : t + HALF, :].astype(F32)
+    return jnp.concatenate([jnp.where(first, mine, other), jnp.where(first, other, mine)], 0)
+
+
+def factor_steps(first, last, nb, base, block, low_ref, lo_ref, inv_ref, s_ref, w_ref, each):
     def update(kk):
         r0 = kk * B
-        s = jnp.concatenate([block_of(mine_ref, other_ref, first, i, kk) for i in range(kk, nb)], 0)
+        at = r0 - base
+        s = jnp.concatenate([block(i, kk) for i in range(kk, nb)], 0)
         if kk:
-            wts = jnp.concatenate([low_ref[r0 : r0 + B, :r0], lo_ref[r0 : r0 + B, :r0]], 0)
-            pr = dot(low_ref[r0:, :r0], wts)
-            s = s - (pr[:, :B] + pr[:, B:] + dot(lo_ref[r0:, :r0], low_ref[r0 : r0 + B, :r0]))
-        s_ref[r0:, :] = s
+            wts = jnp.concatenate([low_ref[at : at + B, :r0], lo_ref[at : at + B, :r0]], 0)
+            pr = dot(low_ref[at:, :r0], wts)
+            s = s - (pr[:, :B] + pr[:, B:] + dot(lo_ref[at:, :r0], low_ref[at : at + B, :r0]))
+        s_ref[at:, :] = s
 
     def panel(kk):
         r0 = kk * B
         r1 = r0 + B
-        shi, slo = split(s_ref[r1:, :])
+        at = r1 - base
+        shi, slo = split(s_ref[at:, :])
         pr = dot(shi, w_ref[...])
         lp = pr[:, :B] + pr[:, B:] + dot(slo, w_ref[:B, :])
         hi, lo = split(lp)
-        low_ref[r1:, r0:r1] = hi
-        lo_ref[r1:, r0:r1] = lo
+        low_ref[at:, r0:r1] = hi
+        lo_ref[at:, r0:r1] = lo
 
     def step(k, _):
-        for kk in range(nb):
+        for kk in range(first, last):
             pl.when(k == kk)(lambda kk=kk: update(kk))
-        r0 = pl.multiple_of(k * B, B)
-        rows = pl.ds(r0, B)
-        pltpu.make_async_copy(low_ref.at[rows], low_hbm.at[rows, :n], sem.at[k]).start()
-        linv, lrinv = factor_diag(s_ref[pl.ds(r0, B), :])
+        rows = pl.ds(pl.multiple_of(k * B - base, B), B)
+        each(k, rows)
+        linv, lrinv = factor_diag(s_ref[rows, :])
         inv_ref[rows, :] = lrinv
         hi, lo = split(linv)
         w_ref[:B, :] = hi
         w_ref[B:, :] = lo
-        for kk in range(nb - 1):
+        for kk in range(first, min(last, nb - 1)):
             pl.when(k == kk)(lambda kk=kk: panel(kk))
         return 0
 
-    lax.fori_loop(0, nb, step, 0)
-    join_inverses(low_ref, inv_ref, iv_ref)
-    hi, lo = split(iv_ref[...])
-    hl_ref[:, :STEP] = hi
-    hl_ref[:, STEP:] = lo
+    lax.fori_loop(first, last, step, 0)
+
+
+def chol_kernel(
+    cut, core_ref, mine_ref, other_ref, low_hbm, tail_s_ref, tail_inv_ref, done_ref,
+    low_ref, lo_ref, inv_ref, s_ref, w_ref, iv_ref, hl_ref, sem, keep_sem,
+):
+    done_ref[...] = jnp.zeros_like(done_ref)
+    kept = keep_blocks(mine_ref, other_ref, low_hbm, keep_sem, False)
+    n = low_ref.shape[0]
+    nb = n // B
+    first = core_ref[0] == 0
+    whole = cut * B // STEP * STEP
+
+    def row_copy(k, rows):
+        return pltpu.make_async_copy(low_ref.at[rows], low_hbm.at[rows, :n], sem.at[k])
+
+    factor_steps(
+        0, cut, nb, 0, functools.partial(block_of, mine_ref, other_ref, first), low_ref, lo_ref, inv_ref, s_ref, w_ref,
+        lambda k, rows: row_copy(k, rows).start(),
+    )
+    join_inverses(lambda rows, cols: low_ref[rows, cols], inv_ref, iv_ref, 0, whole)
+    hl_ref[...] = halves_of(iv_ref[...])
+    last = pltpu.make_async_copy(hl_ref, low_hbm.at[:whole, n : n + 2 * STEP], sem.at[cut])
+    last.start()
+    rest = [
+        pltpu.make_async_copy(low_ref.at[cut * B :], low_hbm.at[cut * B : n, :n], keep_sem.at[8]),
+        pltpu.make_async_copy(lo_ref.at[cut * B :], low_hbm.at[cut * B : n, REST : REST + n], keep_sem.at[9]),
+    ]
+    for copy in rest:
+        copy.start()
+    tail_inv_ref[...] = inv_ref[whole : cut * B, :]
+    for i in range(cut, nb):
+        for j in range(cut, i + 1):
+            at = (slice((i - cut) * B, (i - cut + 1) * B), slice((j - cut) * B, (j - cut + 1) * B))
+            tail_s_ref[at] = block_of(mine_ref, other_ref, first, i, j)
+    for k in range(cut):
+        row_copy(k, slice(k * B, (k + 1) * B)).wait()
+    for copy in [last, *rest, *kept]:
+        copy.wait()
+
+
+def chol_tail_kernel(
+    cut, n, tail_s_ref, tail_inv_ref, in_hbm, low_hbm,
+    low_ref, lo_ref, inv_ref, s_ref, w_ref, iv_ref, hl_ref, sem,
+):
+    whole = cut * B // STEP * STEP
+    skip = cut * B - whole
+    loads = [
+        pltpu.make_async_copy(in_hbm.at[whole:n, :n], low_ref, sem.at[0]),
+        pltpu.make_async_copy(in_hbm.at[cut * B : n, REST : REST + n], lo_ref.at[skip:], sem.at[1]),
+    ]
+    for copy in loads:
+        copy.start()
+    for copy in loads:
+        copy.wait()
+    inv_ref[:skip, :] = tail_inv_ref[...]
+
+    def block(i, j):
+        return tail_s_ref[(i - cut) * B : (i - cut + 1) * B, (j - cut) * B : (j - cut + 1) * B]
+
+    factor_steps(cut, n // B, n // B, whole, block, low_ref, lo_ref, inv_ref, s_ref, w_ref, lambda k, rows: None)
+    join_inverses(lambda rows, cols: low_ref[rows.start - whole : rows.stop - whole, cols], inv_ref, iv_ref, whole, n)
+    hl_ref[...] = halves_of(iv_ref[...])
     copies = [
-        pltpu.make_async_copy(low_ref.at[k * B : (k + 1) * B], low_hbm.at[k * B : (k + 1) * B, :n], sem.at[k])
-        for k in range(nb)
+        pltpu.make_async_copy(low_ref, low_hbm.at[whole:n, :n], sem.at[0]),
+        pltpu.make_async_copy(hl_ref, low_hbm.at[whole:n, n : n + 2 * STEP], sem.at[1]),
     ]
-    copies.append(pltpu.make_async_copy(hl_ref, low_hbm.at[:, n : n + 2 * STEP], sem.at[nb]))
-    copies[-1].start()
+    for copy in copies:
+        copy.start()
     for copy in copies:
         copy.wait()
 
 
-def chol(core, mine, other, n):
-    return pl.pallas_call(
-        chol_kernel,
-        out_shape=(jax.ShapeDtypeStruct((n, WIDE), BF16), TOKEN),
+def chol(core, mine, other, n, cut):
+    whole = cut * B // STEP * STEP
+    left = n - cut * B
+    return pl.pallas_call(
+        functools.partial(chol_kernel, cut),
+        out_shape=(
+            jax.ShapeDtypeStruct((n, WIDE), BF16),
+            jax.ShapeDtypeStruct((left, left), F32),
+            jax.ShapeDtypeStruct((cut * B - whole, B), F32),
+            TOKEN,
+        ),
         in_specs=[SM, VM, VM],
-        out_specs=(HBM, VM),
+        out_specs=(HBM, VM, VM, VM),
         scratch_shapes=[
             pltpu.VMEM((n, n), BF16),
-            pltpu.VMEM((n, B), F32),
             pltpu.VMEM((n, n), BF16),
             pltpu.VMEM((n, B), F32),
+            pltpu.VMEM((n, B), F32),
             pltpu.VMEM((2 * B, B), BF16),
-            pltpu.VMEM((n, STEP), F32),
-            pltpu.VMEM((n, 2 * STEP), BF16),
-            pltpu.SemaphoreType.DMA((n // B + 1,)),
+            pltpu.VMEM((whole, STEP), F32),
+            pltpu.VMEM((whole, 2 * STEP), BF16),
+            pltpu.SemaphoreType.DMA((cut + 1,)),
+            pltpu.SemaphoreType.DMA((10,)),
         ],
         compiler_params=params(28),
-        cost_estimate=cost(57),
+        cost_estimate=cost(39),
         name="cholesky",
     )(core, mine, other)
+
+
+def chol_tail(tail, low, n, cut):
+    rows = n - cut * B // STEP * STEP
+    return pl.pallas_call(
+        functools.partial(chol_tail_kernel, cut, n),
+        out_shape=jax.ShapeDtypeStruct(low.shape, BF16),
+        in_specs=[VM, VM, HBM],
+        out_specs=HBM,
+        input_output_aliases={2: 0},
+        scratch_shapes=[
+            pltpu.VMEM((rows, n), BF16),
+            pltpu.VMEM((rows, n), BF16),
+            pltpu.VMEM((rows, B), F32),
+            pltpu.VMEM((rows, B), F32),
+            pltpu.VMEM((2 * B, B), BF16),
+            pltpu.VMEM((rows, STEP), F32),
+            pltpu.VMEM((rows, 2 * STEP), BF16),
+            pltpu.SemaphoreType.DMA((2,)),
+        ],
+        compiler_params=params(28),
+        cost_estimate=cost(9),
+        name="cholesky_tail",
+    )(*tail, low)
 
 
 def solve_into(rhs, m, n, low_hbm, out_ref, low_ref, hl_ref, sem):
@@ -462,7 +563,9 @@
     )(parts, *after)
 
 
-def rows_kernel(at_ref, core_ref, mine_ref, other_ref, out_ref, s_ref):
+def rows_kernel(at_ref, core_ref, low_hbm, out_ref, s_ref, mine_ref, other_ref, sem):
+    for copy in keep_blocks(mine_ref, other_ref, low_hbm, sem, True):
+        copy.wait()
     m, n = out_ref.shape
     nb = n // B
     first = core_ref[0] == 0
@@ -481,17 +584,22 @@
     out_ref[...] = out
 
 
-def rows_of(at, core, mine, other, n, m):
+def rows_of(at, core, low, n, m, rows):
     return pl.pallas_call(
         rows_kernel,
         out_shape=jax.ShapeDtypeStruct((m, n), F32),
-        in_specs=[SM, SM, VM, VM],
+        in_specs=[SM, SM, HBM],
         out_specs=VM,
-        scratch_shapes=[pltpu.VMEM((n + 8, n), F32)],
-        compiler_params=params(16),
+        scratch_shapes=[
+            pltpu.VMEM((n + 8, n), F32),
+            pltpu.VMEM((rows, B), BF16),
+            pltpu.VMEM((rows, B), BF16),
+            pltpu.SemaphoreType.DMA((8,)),
+        ],
+        compiler_params=params(20),
         cost_estimate=cost(3),
         name="rows",
-    )(at, core, mine, other)
+    )(at, core, low)
 
 
 def per_device(attn_out, out_grad, image_counts, column_owner, damping):
@@ -564,17 +672,19 @@
     part_w = cross(core_arr, grp_index.astype(jnp.int32)[None], keeps, damp_done, mine_rows, other_rows, chips, wide)
     mine, part_w = lax.optimization_barrier((mine, part_w))
     theirs = lax.ppermute(mine, "dp", swap_core)
-    low, chol_done = chol(core_arr, mine, theirs, width)
+    cut = nb - 2
+    low, *tail, chol_done = chol(core_arr, mine, theirs, width, cut)
 
     got_w = lax.all_to_all(part_w, "dp", split_axis=0, concat_axis=0, tiled=True, axis_index_groups=same_core)
 
     at = (dp_index * block).astype(jnp.int32)[None]
-    my_rows = rows_of(at, core_arr, mine, theirs, width, ROWS)
 
     order = column_owner.reshape(chips, 2)
     order = jnp.stack([jnp.where(core == 0, order[:, 0], order[:, 1]), jnp.where(core == 0, order[:, 1], order[:, 0])])
     my_w = sum_parts(got_w, chol_done)
     their_w = lax.ppermute(my_w, "grp", [(1, 0)])
+    low = chol_tail(tail, low, width, cut)
+    my_rows = rows_of(at, core_arr, low, width, ROWS, mine.shape[0])
     same, cross_t = solve_and_route(order, total[None], my_w, their_w, low, width, block)
     same = lax.ppermute(same, both, [(d, n_dp + d) for d in range(n_dp)])
     cross_t = lax.ppermute(cross_t, both, [(d, n_dp + (d ^ 1)) for d in range(n_dp)])

time: 211 us -> 212 us (level)
  Pallas kernels: 79.5 us -> 76.5 us
  local copies, waits for them, and re-layouts: 12.7 us -> 15 us
    ppermute x2, waiting for transfers between devices: 2.46 us -> 8.63 us  [swap(): lax.ppermute(rows[half:], both, far)]
    pallas_call x1, Pallas kernels: 8.88 us -> 3.39 us  [gram(): pl.pallas_call(gram_kernel, out_shape=(jax.ShapeDtypeStruct((slots * SLAB...]
    ppermute x1, waiting for transfers between devices: 4.53 us -> 0.01 us  [per_device(): their_w = lax.ppermute(my_w, 'grp', [(1, 0)])]
    ppermute x1, starting transfers between devices: 1.53 us -> 4.55 us  [per_device(): same = lax.ppermute(same, both, [(d, n_dp + d) for d in range(n_dp)])]
    unnamed x31 -> x35, local copies, waits for them, and re-layouts: 8.85 us -> 11.1 us
    pallas_call x1 -> x2, Pallas kernels: 49 us -> 51 us  [the longest x1 40.3 us: chol(): pl.pallas_call(functools.partial(chol_kernel, cut), out_shape=(jax.ShapeD...]
  transfers between devices with their start and end apart: 20 -> 20, of which waited for: 9 -> 10; matrix products, arithmetic and copies ran while one was open for 3% -> 2% of each run, Pallas kernels for 34% -> 33%
where the time goes in v9:
time: 212 us; the launch traced here: 211 us
  Pallas kernels  76.5 us (36%)
  waiting for transfers between devices  59.4 us (28%)
  starting transfers between devices  47.1 us (22%)
  local copies, waits for them, and re-layouts  15 us (7%)
  between operations  7 us (3%)
  other arithmetic  6.03 us (3%)
    pallas_call x1, Pallas kernels, chol(): pl.pallas_call(functools.partial(chol_kernel, cut), out_shape=(jax.ShapeD...  40.3 us
    all_to_all x1, waiting for transfers between devices, per_device(): lax.all_to_all(part.reshape(chips, per_chip * SLAB, B), 'dp', split_axis=...  25.8 us
    unnamed x35, local copies, waits for them, and re-layouts  11.1 us
    pallas_call x1, Pallas kernels, chol_tail(): pl.pallas_call(functools.partial(chol_tail_kernel, cut, n), out_shape=jax...  10.6 us
    all_to_all x1, starting transfers between devices, per_device(): lax.all_to_all(pair, 'dp', split_axis=0, concat_axis=0, tiled=True, axis_...  9.76 us
    all_to_all x1, waiting for transfers between devices, per_device(): lax.all_to_all(spread, 'dp', split_axis=0, concat_axis=0, tiled=True, axi...  9.28 us
    all_to_all x1, starting transfers between devices, per_device(): lax.all_to_all(part.reshape(chips, per_chip * SLAB, B), 'dp', split_axis=...  9.1 us
    ppermute x2, waiting for transfers between devices, swap(): lax.ppermute(rows[half:], both, far)  8.63 us
  transfers between devices with their start and end apart: 20, of which 10 were waited for; matrix products, arithmetic and copies ran while one was open for 2% of the time, Pallas kernels for 33%

profile of v9, /device:TPU:0, one launch (start us, length us, event | category | flops | bytes accessed | tf_op | source)
XLA Modules:
  0.0 210.9 jit_solution(8270833435590368450)
XLA Ops:
  0.6 1.5 broadcast_select_fusion
  2.1 0.8 fusion.5
  2.9 2.8 %collective-permute-start.2 = (bf16[128,1408]{1,0:T(8,128)(2,1)}, bf16[128,1408]{1,0:T(8,128)(2,1)S(1)}, u32[]{:S(2)}, u32[]{:S(2)}) collective-permute-start(bf16[128,1408]{1,0:T(8,128)(2,1)} %get-tuple-element.44), channel_id=1, source_target_pairs={{0,96},{1,97},{2,98},{3,99},{4,100},{5,101},{6,102},{7,103},{8,104... | collective-permute-start | bytes 1081352 | tf_op jit(solution)/shard_map/ppermute | solution.py:633
  6.0 0.7 fusion.6
  10.7 3.7 %collective-permute-done.2.refs_3_ = bf16[128,1408]{1,0:T(8,128)(2,1)S(1)} collective-permute-done((bf16[128,1408]{1,0:T(8,128)(2,1)}, bf16[128,1408]{1,0:T(8,128)(2,1)S(1)}, u32[]{:S(2)}, u32[]{:S(2)}) %collective-permute-start.2) | collective-permute-done | bytes 360480 | tf_op jit(solution)/shard_map/ppermute | solution.py:633
  14.4 1.3 collective-permute-done.1.refs_2_
  16.2 1.9 collective-permute-start.6
  18.1 3.4 %gram.1 = (f32[4608,128]{1,0:T(8,128)S(1)}, f32[8,1408]{1,0:T(8,128)S(1)}) custom-call(s32[1]{0:T(128)} %bitcast.4.core_ref, f32[6]{0:T(128)S(1)} %stack.36.keep_ref, bf16[256,1408]{1,0:T(8,128)(2,1)S(1)} %get-tuple-element.19.refs_0_, bf16[256,1408]{1,0:T(8,128)(2,1)S(1)} %collective-permute-done.refs_1_, ...), custom_call_target="tpu_custom_call" | custom-call | flops 4400000000 | bytes 1048576 | tf_op jit(solution)/shard_map/gram/pallas_call | solution.py:97
  21.5 1.4 copy-done
  23.0 4.9 %collective-permute-done.6.refs_9_ = bf16[128,1408]{1,0:T(8,128)(2,1)} collective-permute-done((bf16[128,1408]{1,0:T(8,128)(2,1)S(1)}, bf16[128,1408]{1,0:T(8,128)(2,1)}, u32[]{:S(2)}, u32[]{:S(2)}) %collective-permute-start.6) | collective-permute-done | bytes 360480 | tf_op jit(solution)/shard_map/ppermute | solution.py:633
  28.3 9.1 %all-to-all-start = ((f32[32,144,128]{2,1,0:T(8,128)}), f32[32,144,128]{2,1,0:T(8,128)}, u32[]{:S(2)}, u32[]{:S(2)}) async-start(f32[32,144,128]{2,1,0:T(8,128)} %bitcast.24), calls=%async_computation | async-start | bytes 4718592 | tf_op jit(solution)/shard_map/all_to_all | solution.py:657
  37.5 0.6 reduce_sum.18
  38.8 0.6 fusion.7
  40.7 0.7 fusion.1.diag_ref
  42.0 0.6 pad_maximum_fusion.3.scale_ref
  42.6 25.8 %all-to-all-done.parts_ref = f32[32,144,128]{2,1,0:T(8,128)} async-done(((f32[32,144,128]{2,1,0:T(8,128)}), f32[32,144,128]{2,1,0:T(8,128)}, u32[]{:S(2)}, u32[]{:S(2)}) %all-to-all-start) | async-done | bytes 2359328 | tf_op jit(solution)/shard_map/all_to_all | solution.py:657
  68.4 3.7 %damp_and_spread.1 = (bf16[32,144,128]{2,1,0:T(8,128)(2,1)}, f32[8,128]{1,0:T(8,128)}) custom-call(f32[2]{0:T(128)} %pad_maximum_fusion.3.scale_ref, f32[32,144,128]{2,1,0:T(8,128)} %all-to-all-done.parts_ref, f32[144,128]{1,0:T(8,128)} %fusion.1.diag_ref), custom_call_target="tpu_custom_call" | custom-call | flops 3300000000 | bytes 1048576 | tf_op jit(solution)/shard_map/damp_and_spread/pallas_call | solution.py:542
  72.1 6.5 %all-to-all-start.1 = ((bf16[32,144,128]{2,1,0:T(8,128)(2,1)}), bf16[32,144,128]{2,1,0:T(8,128)(2,1)S(1)}, u32[]{:S(2)}, u32[]{:S(2)}) async-start(bf16[32,144,128]{2,1,0:T(8,128)(2,1)} %get-tuple-element.21), calls=%async_computation.1 | async-start | bytes 2359296 | tf_op jit(solution)/shard_map/all_to_all | solution.py:669
  78.7 1.0 copy-done.5
  79.7 1.0 copy-done.7
  80.7 1.0 copy-done.9
  81.6 1.0 copy-done.11
  82.6 4.4 %cross.1 = f32[32,24,768]{2,1,0:T(8,128)S(1)} custom-call(s32[1]{0:T(128)} %bitcast.4.core_ref, s32[1]{0:T(128)} %bitcast.7.grp_ref, f32[6]{0:T(128)S(1)} %stack.36.keep_ref, f32[8,128]{1,0:T(8,128)S(1)} %copy-done.12, bf16[256,1408]{1,0:T(8,128)(2,1)S(1)} %get-tuple-element.19.refs_0_, bf16[256,1408]{1,0:T(8,128)(2,1)S(1)} %collective-permute-done.refs_1_, ...), custom_call_target="tpu_custom_call" | custom-call | flops 32999999488 | bytes 1048576 | tf_op jit(solution)/shard_map/cross/pallas_call | solution.py:130
  87.0 1.4 copy-done.1
  88.5 9.3 %all-to-all-done.1 = bf16[32,144,128]{2,1,0:T(8,128)(2,1)S(1)} async-done(((bf16[32,144,128]{2,1,0:T(8,128)(2,1)}), bf16[32,144,128]{2,1,0:T(8,128)(2,1)S(1)}, u32[]{:S(2)}, u32[]{:S(2)}) %all-to-all-start.1) | async-done | bytes 1179680 | tf_op jit(solution)/shard_map/all_to_all | solution.py:669
  98.2 5.5 %all-to-all-start.2 = ((f32[32,24,768]{2,1,0:T(8,128)}), f32[32,24,768]{2,1,0:T(8,128)}, u32[]{:S(2)}, u32[]{:S(2)}) async-start(f32[32,24,768]{2,1,0:T(8,128)} %copy-done.1), calls=%async_computation.2 | async-start | bytes 4718592 | tf_op jit(solution)/shard_map/all_to_all | solution.py:678
  103.8 1.0 copy-done.2
  104.8 1.3 copy-done.3
  106.1 40.3 %cholesky.1 = (bf16[1408,14336]{1,0:T(8,128)(2,1)}, f32[256,256]{1,0:T(8,128)S(1)}, f32[128,128]{1,0:T(8,128)S(1)}, f32[8,128]{1,0:T(8,128)S(1)}) custom-call(s32[1]{0:T(128)} %bitcast.4.core_ref, bf16[4608,128]{1,0:T(8,128)(2,1)S(1)} %bitcast.26, bf16[4608,128]{1,0:T(8,128)(2,1)S(1)} %copy-done.3), custom_call_target="tpu_custom_call" | custom-call | flops 42900000768 | bytes 1048576 | tf_op jit(solution)/shard_map/cholesky/pallas_call | solution.py:367
  146.5 1.8 sum_parts.1.one_ref
  148.2 1.5 collective-permute-start.11
  149.8 10.6 %cholesky_tail.1.low_ref.low_hbm = bf16[1408,14336]{1,0:T(8,128)(2,1)} custom-call(f32[256,256]{1,0:T(8,128)S(1)} %get-tuple-element.28.tail_s_ref, f32[128,128]{1,0:T(8,128)S(1)} %get-tuple-element.29.tail_inv_ref, bf16[1408,14336]{1,0:T(8,128)(2,1)} %get-tuple-element.30.in_hbm), custom_call_target="tpu_custom_call", output_to_operand_aliasing={{}: (2, {})} | custom-call | flops 9900000256 | bytes 1048576 | tf_op jit(solution)/shard_map/cholesky_tail/pallas_call | solution.py:396
  160.4 5.5 %solve_and_route.1 = (f32[24,768]{1,0:T(8,128)S(1)}, f32[24,768]{1,0:T(8,128)S(1)}) custom-call(s32[2,32]{1,0:T(2,128)S(1)} %pad_add_fusion.owner_ref, f32[1]{0:T(128)} %bitcast.total_ref, f32[24,768]{1,0:T(8,128)S(1)} %sum_parts.1.one_ref, f32[24,768]{1,0:T(8,128)S(1)} %collective-permute-done.11.two_ref, bf16[1408,14336]{1,0:T(8,128)(2,1)} %cholesky_tail.1.low_ref.low_hbm), custom_call_target="tpu_custom_call" | custom-call | flops 9900000256 | bytes 1048576 | tf_op jit(solution)/shard_map/solve_and_route/pallas_call | solution.py:507
  165.9 4.6 %collective-permute-start.12 = (f32[24,768]{1,0:T(8,128)S(1)}, f32[24,768]{1,0:T(8,128)S(1)}, u32[]{:S(2)}, u32[]{:S(2)}) collective-permute-start(f32[24,768]{1,0:T(8,128)S(1)} %get-tuple-element.31), channel_id=1, source_target_pairs={{0,64},{1,65},{2,66},{3,67},{4,68},{5,69},{6,70},{7,71},{8,72},{9,... | collective-permute-start | bytes 221192 | tf_op jit(solution)/shard_map/ppermute | solution.py:689
  170.4 1.3 collective-permute-start.13
  172.4 1.5 collective-permute-done.13
  174.3 1.0 reshape.153
  175.3 9.8 %all-to-all-start.3 = ((f32[32,1,1078]{2,1,0:T(1,128)}), f32[32,1,1078]{2,1,0:T(1,128)S(1)}, u32[]{:S(2)}, u32[]{:S(2)}) async-start(f32[32,1,1078]{2,1,0:T(1,128)} %reshape.153), calls=%async_computation.3 | async-start | bytes 294912 | tf_op jit(solution)/shard_map/all_to_all | solution.py:696
  185.1 2.6 %rows.1.after_ref = f32[24,1408]{1,0:T(8,128)S(1)} custom-call(s32[1]{0:T(128)} %bitcast.10.at_ref, s32[1]{0:T(128)} %bitcast.4.core_ref, bf16[1408,14336]{1,0:T(8,128)(2,1)} %cholesky_tail.1.low_ref.low_hbm), custom_call_target="tpu_custom_call" | custom-call | flops 3300000000 | bytes 1048576 | tf_op jit(solution)/shard_map/rows/pallas_call | solution.py:588
  187.6 7.5 %all-to-all-done.3 = f32[32,1,1078]{2,1,0:T(1,128)S(1)} async-done(((f32[32,1,1078]{2,1,0:T(1,128)}), f32[32,1,1078]{2,1,0:T(1,128)S(1)}, u32[]{:S(2)}, u32[]{:S(2)}) %all-to-all-start.3) | async-done | bytes 138016 | tf_op jit(solution)/shard_map/all_to_all | solution.py:696
  195.1 0.5 broadcast.163
  195.7 1.0 reduce.7
  197.6 1.5 collective-permute-start.14
  199.1 4.2 %solve.1 = f32[24,1408]{1,0:T(8,128)S(1)} custom-call(f32[24,1408]{1,0:T(8,128)S(1)} %pad.4.rhs_ref, bf16[1408,14336]{1,0:T(8,128)(2,1)} %cholesky_tail.1.low_ref.low_hbm, f32[24,1408]{1,0:T(8,128)S(1)} %rows.1.after_ref), custom_call_target="tpu_custom_call" | custom-call | flops 7699999744 | bytes 1048576 | tf_op jit(solution)/shard_map/solve/pallas_call | solution.py:469
  203.3 1.3 collective-permute-start.15
  204.8 0.8 copy.15
  205.6 4.6 %collective-permute-done.15 = f32[22,1408]{1,0:T(8,128)S(1)} collective-permute-done((f32[22,1408]{1,0:T(8,128)S(1)}, f32[22,1408]{1,0:T(8,128)S(1)}, u32[]{:S(2)}, u32[]{:S(2)}) %collective-permute-start.15) | collective-permute-done | bytes 123936 | tf_op jit(solution)/shard_map/ppermute | solution.py:705
  210.2 0.7 select_bitcast_fusion
  (74 shorter events, 4.5 us)
Async XLA Ops:
  0.6 5.3 %copy-start.13 = (s32[128]{0:T(128)S(1)}, s32[128]{0:T(128)}, u32[]{:S(2)}) copy-start(s32[128]{0:T(128)} %param.7) | copy-start | bytes 1540
  2.9 11.5 %collective-permute-start.2 = (bf16[128,1408]{1,0:T(8,128)(2,1)}, bf16[128,1408]{1,0:T(8,128)(2,1)S(1)}, u32[]{:S(2)}, u32[]{:S(2)}) collective-permute-start(bf16[128,1408]{1,0:T(8,128)(2,1)} %get-tuple-element.44), channel_id=1, source_target_pairs={{0,96},{1,97},{2,98},{3,99},{4,100},{5,101},{6,102},{7,103},{8,104... | collective-permute-start | bytes 1081352 | tf_op jit(solution)/shard_map/ppermute | solution.py:633
  5.7 9.9 %collective-permute-start.1 = (bf16[128,1408]{1,0:T(8,128)(2,1)S(1)}, bf16[128,1408]{1,0:T(8,128)(2,1)S(1)}, u32[]{:S(2)}, u32[]{:S(2)}) collective-permute-start(bf16[128,1408]{1,0:T(8,128)(2,1)S(1)} %get-tuple-element.45), channel_id=1, source_target_pairs={{0,64},{1,65},{2,66},{3,67},{4,68},{5,69},{6,70},{7,71},{8,72},{9,... | collective-permute-start | bytes 1081352 | tf_op jit(solution)/shard_map/ppermute | solution.py:633
  6.0 12.1 %collective-permute-start = (bf16[256,1408]{1,0:T(8,128)(2,1)S(1)}, bf16[256,1408]{1,0:T(8,128)(2,1)S(1)}, u32[]{:S(2)}, u32[]{:S(2)}) collective-permute-start(bf16[256,1408]{1,0:T(8,128)(2,1)S(1)} %get-tuple-element.19.refs_0_), channel_id=1, source_target_pairs={{0,1},{1,0},{2,3},{3,2},{4,5},{5,4},{6,7},{7,6},{8,9},{9,8},{10,11... | collective-permute-start | bytes 2162696 | tf_op jit(solution)/shard_map/ppermute | solution.py:636
  14.4 7.1 %copy-start.4 = (bf16[128,1408]{1,0:T(8,128)(2,1)}, bf16[128,1408]{1,0:T(8,128)(2,1)S(1)}, u32[]{:S(2)}) copy-start(bf16[128,1408]{1,0:T(8,128)(2,1)S(1)} %collective-permute-done.2.refs_3_) | copy-start | bytes 1081348
  15.6 5.9 %copy-start.6 = (bf16[128,1408]{1,0:T(8,128)(2,1)}, bf16[128,1408]{1,0:T(8,128)(2,1)S(1)}, u32[]{:S(2)}) copy-start(bf16[128,1408]{1,0:T(8,128)(2,1)S(1)} %collective-permute-done.1.refs_2_) | copy-start | bytes 1081348
  15.6 2.4 %collective-permute-start.4 = (bf16[128,1408]{1,0:T(8,128)(2,1)S(1)}, bf16[128,1408]{1,0:T(8,128)(2,1)S(1)}, u32[]{:S(2)}, u32[]{:S(2)}) collective-permute-start(bf16[128,1408]{1,0:T(8,128)(2,1)S(1)} %collective-permute-done.2.refs_3_), channel_id=1, source_target_pairs={{0,1},{1,0},{2,3},{3,2},{4,5},{5,4},{6,7},{7,6},{8,9},{9,8},{10,11... | collective-permute-start | bytes 1081352 | tf_op jit(solution)/shard_map/ppermute | solution.py:636
  15.6 2.4 %collective-permute-start.3 = (bf16[128,1408]{1,0:T(8,128)(2,1)S(1)}, bf16[128,1408]{1,0:T(8,128)(2,1)S(1)}, u32[]{:S(2)}, u32[]{:S(2)}) collective-permute-start(bf16[128,1408]{1,0:T(8,128)(2,1)S(1)} %collective-permute-done.1.refs_2_), channel_id=1, source_target_pairs={{0,1},{1,0},{2,3},{3,2},{4,5},{5,4},{6,7},{7,6},{8,9},{9,8},{10,11... | collective-permute-start | bytes 1081352 | tf_op jit(solution)/shard_map/ppermute | solution.py:636
  16.2 11.7 %collective-permute-start.6 = (bf16[128,1408]{1,0:T(8,128)(2,1)S(1)}, bf16[128,1408]{1,0:T(8,128)(2,1)}, u32[]{:S(2)}, u32[]{:S(2)}) collective-permute-start(bf16[128,1408]{1,0:T(8,128)(2,1)S(1)} %get-tuple-element.42), channel_id=1, source_target_pairs={{0,96},{1,97},{2,98},{3,99},{4,100},{5,101},{6,102},{7,103},{8,104... | collective-permute-start | bytes 1081352 | tf_op jit(solution)/shard_map/ppermute | solution.py:633
  18.1 10.2 %collective-permute-start.5 = (bf16[128,1408]{1,0:T(8,128)(2,1)S(1)}, bf16[128,1408]{1,0:T(8,128)(2,1)}, u32[]{:S(2)}, u32[]{:S(2)}) collective-permute-start(bf16[128,1408]{1,0:T(8,128)(2,1)S(1)} %get-tuple-element.43), channel_id=1, source_target_pairs={{0,64},{1,65},{2,66},{3,67},{4,68},{5,69},{6,70},{7,71},{8,72},{9,... | collective-permute-start | bytes 1081352 | tf_op jit(solution)/shard_map/ppermute | solution.py:633
  18.1 3.5 %copy-start.8 = (bf16[128,1408]{1,0:T(8,128)(2,1)}, bf16[128,1408]{1,0:T(8,128)(2,1)S(1)}, u32[]{:S(2)}) copy-start(bf16[128,1408]{1,0:T(8,128)(2,1)S(1)} %collective-permute-done.4.refs_5_) | copy-start | bytes 1081348
  18.1 3.5 %copy-start.10 = (bf16[128,1408]{1,0:T(8,128)(2,1)}, bf16[128,1408]{1,0:T(8,128)(2,1)S(1)}, u32[]{:S(2)}) copy-start(bf16[128,1408]{1,0:T(8,128)(2,1)S(1)} %collective-permute-done.3.refs_4_) | copy-start | bytes 1081348
  21.5 1.4 copy-start
  28.3 10.5 %copy-start.14 = (f32[2]{0:T(128)S(1)}, f32[2]{0:T(128)}, u32[]{:S(2)}) copy-start(f32[2]{0:T(128)} %param.9) | copy-start | bytes 28
  28.3 40.1 %all-to-all-start = ((f32[32,144,128]{2,1,0:T(8,128)}), f32[32,144,128]{2,1,0:T(8,128)}, u32[]{:S(2)}, u32[]{:S(2)}) async-start(f32[32,144,128]{2,1,0:T(8,128)} %bitcast.24), calls=%async_computation | async-start | bytes 4718592 | tf_op jit(solution)/shard_map/all_to_all | solution.py:657
  37.4 41.2 %collective-permute-start.7 = (bf16[256,1408]{1,0:T(8,128)(2,1)S(1)}, bf16[256,1408]{1,0:T(8,128)(2,1)}, u32[]{:S(2)}, u32[]{:S(2)}) collective-permute-start(bf16[256,1408]{1,0:T(8,128)(2,1)S(1)} %get-tuple-element.40.refs_6_), channel_id=1, source_target_pairs={{0,1},{1,0},{2,3},{3,2},{4,5},{5,4},{6,7},{7,6},{8,9},{9,8},{10,11... | collective-permute-start | bytes 2162696 | tf_op jit(solution)/shard_map/ppermute | solution.py:636
  41.5 37.2 %collective-permute-start.8 = (bf16[128,1408]{1,0:T(8,128)(2,1)}, bf16[128,1408]{1,0:T(8,128)(2,1)}, u32[]{:S(2)}, u32[]{:S(2)}) collective-permute-start(bf16[128,1408]{1,0:T(8,128)(2,1)} %collective-permute-done.5.refs_8_), channel_id=1, source_target_pairs={{0,1},{1,0},{2,3},{3,2},{4,5},{5,4},{6,7},{7,6},{8,9},{9,8},{10,11... | collective-permute-start | bytes 1081352 | tf_op jit(solution)/shard_map/ppermute | solution.py:636
  42.0 36.7 %collective-permute-start.9 = (bf16[128,1408]{1,0:T(8,128)(2,1)}, bf16[128,1408]{1,0:T(8,128)(2,1)}, u32[]{:S(2)}, u32[]{:S(2)}) collective-permute-start(bf16[128,1408]{1,0:T(8,128)(2,1)} %collective-permute-done.6.refs_9_), channel_id=1, source_target_pairs={{0,1},{1,0},{2,3},{3,2},{4,5},{5,4},{6,7},{7,6},{8,9},{9,8},{10,11... | collective-permute-start | bytes 1081352 | tf_op jit(solution)/shard_map/ppermute | solution.py:636
  72.1 6.6 %copy-start.12 = (f32[8,128]{1,0:T(8,128)S(1)}, f32[8,128]{1,0:T(8,128)}, u32[]{:S(2)}) copy-start(f32[8,128]{1,0:T(8,128)} %get-tuple-element.22.after_ref) | copy-start | bytes 12292
  72.1 25.6 %all-to-all-start.1 = ((bf16[32,144,128]{2,1,0:T(8,128)(2,1)}), bf16[32,144,128]{2,1,0:T(8,128)(2,1)S(1)}, u32[]{:S(2)}, u32[]{:S(2)}) async-start(bf16[32,144,128]{2,1,0:T(8,128)(2,1)} %get-tuple-element.21), calls=%async_computation.1 | async-start | bytes 2359296 | tf_op jit(solution)/shard_map/all_to_all | solution.py:669
  78.7 1.0 copy-start.5
  79.7 1.0 copy-start.7
  80.7 1.0 copy-start.9
  81.6 1.0 copy-start.11
  82.6 15.1 %copy-start.15 = (s32[64]{0:T(128)S(1)}, s32[64]{0:T(128)}, u32[]{:S(2)}) copy-start(s32[64]{0:T(128)} %param.8) | copy-start | bytes 772
  87.0 1.4 copy-start.1
  97.7 6.0 %collective-permute-start.10 = (bf16[4608,128]{1,0:T(8,128)(2,1)S(1)}, bf16[4608,128]{1,0:T(8,128)(2,1)S(1)}, u32[]{:S(2)}, u32[]{:S(2)}) collective-permute-start(bf16[4608,128]{1,0:T(8,128)(2,1)S(1)} %bitcast.25), channel_id=1, source_target_pairs={{0,1},{1,0},{2,3},{3,2},{4,5},{5,4},{6,7},{7,6},{8,9},{9,8},{10,11... | collective-permute-start | bytes 3538952 | tf_op jit(solution)/shard_map/ppermute | solution.py:674
  98.2 48.2 %all-to-all-start.2 = ((f32[32,24,768]{2,1,0:T(8,128)}), f32[32,24,768]{2,1,0:T(8,128)}, u32[]{:S(2)}, u32[]{:S(2)}) async-start(f32[32,24,768]{2,1,0:T(8,128)} %copy-done.1), calls=%async_computation.2 | async-start | bytes 4718592 | tf_op jit(solution)/shard_map/all_to_all | solution.py:678
  103.8 1.0 copy-start.2
  104.8 1.3 copy-start.3
  148.2 12.2 %collective-permute-start.11 = (f32[24,768]{1,0:T(8,128)S(1)}, f32[24,768]{1,0:T(8,128)S(1)}, u32[]{:S(2)}, u32[]{:S(2)}) collective-permute-start(f32[24,768]{1,0:T(8,128)S(1)} %sum_parts.1.one_ref), channel_id=1, source_target_pairs={{64,0},{65,1},{66,2},{67,3},{68,4},{69,5},{70,6},{71,7},{72,8},{73... | collective-permute-start | bytes 221192 | tf_op jit(solution)/shard_map/ppermute | solution.py:685
  165.9 6.5 %collective-permute-start.12 = (f32[24,768]{1,0:T(8,128)S(1)}, f32[24,768]{1,0:T(8,128)S(1)}, u32[]{:S(2)}, u32[]{:S(2)}) collective-permute-start(f32[24,768]{1,0:T(8,128)S(1)} %get-tuple-element.31), channel_id=1, source_target_pairs={{0,64},{1,65},{2,66},{3,67},{4,68},{5,69},{6,70},{7,71},{8,72},{9,... | collective-permute-start | bytes 221192 | tf_op jit(solution)/shard_map/ppermute | solution.py:689
  170.4 3.4 %collective-permute-start.13 = (f32[24,768]{1,0:T(8,128)S(1)}, f32[24,768]{1,0:T(8,128)S(1)}, u32[]{:S(2)}, u32[]{:S(2)}) collective-permute-start(f32[24,768]{1,0:T(8,128)S(1)} %get-tuple-element.32), channel_id=1, source_target_pairs={{0,65},{1,64},{2,67},{3,66},{4,69},{5,68},{6,71},{7,70},{8,73},{9,... | collective-permute-start | bytes 221192 | tf_op jit(solution)/shard_map/ppermute | solution.py:690
  175.3 19.9 %all-to-all-start.3 = ((f32[32,1,1078]{2,1,0:T(1,128)}), f32[32,1,1078]{2,1,0:T(1,128)S(1)}, u32[]{:S(2)}, u32[]{:S(2)}) async-start(f32[32,1,1078]{2,1,0:T(1,128)} %reshape.153), calls=%async_computation.3 | async-start | bytes 294912 | tf_op jit(solution)/shard_map/all_to_all | solution.py:696
  197.6 7.1 %collective-permute-start.14 = (f32[22,1408]{1,0:T(8,128)S(1)}, f32[22,1408]{1,0:T(8,128)S(1)}, u32[]{:S(2)}, u32[]{:S(2)}) collective-permute-start(f32[22,1408]{1,0:T(8,128)S(1)} %slice_select_fusion), channel_id=1, source_target_pairs={{0,64},{64,0},{1,65},{65,1},{2,66},{66,2},{3,67},{67,3},{4,68},{68... | collective-permute-start | bytes 371720 | tf_op jit(solution)/shard_map/ppermute | solution.py:703
  203.3 6.9 %collective-permute-start.15 = (f32[22,1408]{1,0:T(8,128)S(1)}, f32[22,1408]{1,0:T(8,128)S(1)}, u32[]{:S(2)}, u32[]{:S(2)}) collective-permute-start(f32[22,1408]{1,0:T(8,128)S(1)} %bitcast.27), channel_id=1, source_target_pairs={{64,0},{65,1},{66,2},{67,3},{68,4},{69,5},{70,6},{71,7},{72,8},{73... | collective-permute-start | bytes 371720 | tf_op jit(solution)/shard_map/ppermute | solution.py:705

commit v10 on v9

--- a/solution.py
+++ b/solution.py
@@ -15,6 +15,7 @@
 WIDE = 14336
 STEP = 512
 REST = 4096
+MORE = 8192
 F32 = jnp.float32
 BF16 = jnp.bfloat16
 NT = (((1,), (1,)), ((), ()))
@@ -224,22 +225,6 @@
         size *= 2
 
 
-def keep_blocks(mine_ref, other_ref, low_hbm, sem, back):
-    n = low_hbm.shape[0]
-    copies = []
-    for half, ref in enumerate((mine_ref, other_ref)):
-        total = ref.shape[0]
-        for p in range(-(-total // n)):
-            rows = min(n, total - p * n)
-            at = n + 2 * STEP + (4 * half + p) * B
-            here, there = ref.at[p * n : p * n + rows], low_hbm.at[:rows, at : at + B]
-            k = len(copies)
-            copies.append(pltpu.make_async_copy(*((there, here) if back else (here, there)), sem.at[k]))
-    for copy in copies:
-        copy.start()
-    return copies
-
-
 def halves_of(x):
     return jnp.concatenate(split(x), 1)
 
@@ -291,11 +276,10 @@
 
 
 def chol_kernel(
-    cut, core_ref, mine_ref, other_ref, low_hbm, tail_s_ref, tail_inv_ref, done_ref,
-    low_ref, lo_ref, inv_ref, s_ref, w_ref, iv_ref, hl_ref, sem, keep_sem,
+    cut, core_ref, mine_ref, other_ref, low_hbm, done_ref,
+    low_ref, lo_ref, inv_ref, s_ref, w_ref, iv_ref, hl_ref, more_ref, sem, rest_sem,
 ):
     done_ref[...] = jnp.zeros_like(done_ref)
-    kept = keep_blocks(mine_ref, other_ref, low_hbm, keep_sem, False)
     n = low_ref.shape[0]
     nb = n // B
     first = core_ref[0] == 0
@@ -313,40 +297,44 @@
     last = pltpu.make_async_copy(hl_ref, low_hbm.at[:whole, n : n + 2 * STEP], sem.at[cut])
     last.start()
     rest = [
-        pltpu.make_async_copy(low_ref.at[cut * B :], low_hbm.at[cut * B : n, :n], keep_sem.at[8]),
-        pltpu.make_async_copy(lo_ref.at[cut * B :], low_hbm.at[cut * B : n, REST : REST + n], keep_sem.at[9]),
+        pltpu.make_async_copy(low_ref.at[cut * B :], low_hbm.at[cut * B : n, :n], rest_sem.at[0]),
+        pltpu.make_async_copy(lo_ref.at[cut * B :], low_hbm.at[cut * B : n, REST : REST + n], rest_sem.at[1]),
     ]
+    skip = cut * B - whole
+    more_ref[:skip, : 2 * B] = halves_of(inv_ref[whole : cut * B, :])
+    for i in range(cut, nb):
+        for j in range(cut, i + 1):
+            at = skip + (i - cut) * B
+            more_ref[at : at + B, (j - cut) * B : (j - cut + 1) * B] = block_of(mine_ref, other_ref, first, i, j).astype(BF16)
+    rest.append(pltpu.make_async_copy(more_ref, low_hbm.at[whole:n, MORE : MORE + more_ref.shape[1]], rest_sem.at[2]))
     for copy in rest:
         copy.start()
-    tail_inv_ref[...] = inv_ref[whole : cut * B, :]
-    for i in range(cut, nb):
-        for j in range(cut, i + 1):
-            at = (slice((i - cut) * B, (i - cut + 1) * B), slice((j - cut) * B, (j - cut + 1) * B))
-            tail_s_ref[at] = block_of(mine_ref, other_ref, first, i, j)
     for k in range(cut):
         row_copy(k, slice(k * B, (k + 1) * B)).wait()
-    for copy in [last, *rest, *kept]:
+    for copy in [last, *rest]:
         copy.wait()
 
 
 def chol_tail_kernel(
-    cut, n, tail_s_ref, tail_inv_ref, in_hbm, low_hbm,
-    low_ref, lo_ref, inv_ref, s_ref, w_ref, iv_ref, hl_ref, sem,
+    cut, n, in_hbm, low_hbm,
+    low_ref, lo_ref, inv_ref, s_ref, w_ref, iv_ref, hl_ref, more_ref, sem,
 ):
     whole = cut * B // STEP * STEP
     skip = cut * B - whole
     loads = [
         pltpu.make_async_copy(in_hbm.at[whole:n, :n], low_ref, sem.at[0]),
         pltpu.make_async_copy(in_hbm.at[cut * B : n, REST : REST + n], lo_ref.at[skip:], sem.at[1]),
+        pltpu.make_async_copy(in_hbm.at[whole:n, MORE : MORE + more_ref.shape[1]], more_ref, sem.at[2]),
     ]
     for copy in loads:
         copy.start()
     for copy in loads:
         copy.wait()
-    inv_ref[:skip, :] = tail_inv_ref[...]
+    inv_ref[:skip, :] = more_ref[:skip, :B].astype(F32) + more_ref[:skip, B : 2 * B].astype(F32)
 
     def block(i, j):
-        return tail_s_ref[(i - cut) * B : (i - cut + 1) * B, (j - cut) * B : (j - cut + 1) * B]
+        at = skip + (i - cut) * B
+        return more_ref[at : at + B, (j - cut) * B : (j - cut + 1) * B].astype(F32)
 
     factor_steps(cut, n // B, n // B, whole, block, low_ref, lo_ref, inv_ref, s_ref, w_ref, lambda k, rows: None)
     join_inverses(lambda rows, cols: low_ref[rows.start - whole : rows.stop - whole, cols], inv_ref, iv_ref, whole, n)
@@ -368,12 +356,10 @@
         functools.partial(chol_kernel, cut),
         out_shape=(
             jax.ShapeDtypeStruct((n, WIDE), BF16),
-            jax.ShapeDtypeStruct((left, left), F32),
-            jax.ShapeDtypeStruct((cut * B - whole, B), F32),
             TOKEN,
         ),
         in_specs=[SM, VM, VM],
-        out_specs=(HBM, VM, VM, VM),
+        out_specs=(HBM, VM),
         scratch_shapes=[
             pltpu.VMEM((n, n), BF16),
             pltpu.VMEM((n, n), BF16),
@@ -382,8 +368,9 @@
             pltpu.VMEM((2 * B, B), BF16),
             pltpu.VMEM((whole, STEP), F32),
             pltpu.VMEM((whole, 2 * STEP), BF16),
+            pltpu.VMEM((n - whole, max(2 * B, left)), BF16),
             pltpu.SemaphoreType.DMA((cut + 1,)),
-            pltpu.SemaphoreType.DMA((10,)),
+            pltpu.SemaphoreType.DMA((3,)),
         ],
         compiler_params=params(28),
         cost_estimate=cost(39),
@@ -391,14 +378,14 @@
     )(core, mine, other)
 
 
-def chol_tail(tail, low, n, cut):
+def chol_tail(low, n, cut):
     rows = n - cut * B // STEP * STEP
     return pl.pallas_call(
         functools.partial(chol_tail_kernel, cut, n),
         out_shape=jax.ShapeDtypeStruct(low.shape, BF16),
-        in_specs=[VM, VM, HBM],
+        in_specs=[HBM],
         out_specs=HBM,
-        input_output_aliases={2: 0},
+        input_output_aliases={0: 0},
         scratch_shapes=[
             pltpu.VMEM((rows, n), BF16),
             pltpu.VMEM((rows, n), BF16),
@@ -407,12 +394,13 @@
             pltpu.VMEM((2 * B, B), BF16),
             pltpu.VMEM((rows, STEP), F32),
             pltpu.VMEM((rows, 2 * STEP), BF16),
-            pltpu.SemaphoreType.DMA((2,)),
+            pltpu.VMEM((rows, max(2 * B, n - cut * B)), BF16),
+            pltpu.SemaphoreType.DMA((3,)),
         ],
         compiler_params=params(28),
         cost_estimate=cost(9),
         name="cholesky_tail",
-    )(*tail, low)
+    )(low)
 
 
 def solve_into(rhs, m, n, low_hbm, out_ref, low_ref, hl_ref, sem):
@@ -563,9 +551,7 @@
     )(parts, *after)
 
 
-def rows_kernel(at_ref, core_ref, low_hbm, out_ref, s_ref, mine_ref, other_ref, sem):
-    for copy in keep_blocks(mine_ref, other_ref, low_hbm, sem, True):
-        copy.wait()
+def rows_kernel(at_ref, core_ref, mine_ref, other_ref, out_ref, s_ref):
     m, n = out_ref.shape
     nb = n // B
     first = core_ref[0] == 0
@@ -584,22 +570,17 @@
     out_ref[...] = out
 
 
-def rows_of(at, core, low, n, m, rows):
+def rows_of(at, core, mine, other, n, m):
     return pl.pallas_call(
         rows_kernel,
         out_shape=jax.ShapeDtypeStruct((m, n), F32),
-        in_specs=[SM, SM, HBM],
+        in_specs=[SM, SM, VM, VM],
         out_specs=VM,
-        scratch_shapes=[
-            pltpu.VMEM((n + 8, n), F32),
-            pltpu.VMEM((rows, B), BF16),
-            pltpu.VMEM((rows, B), BF16),
-            pltpu.SemaphoreType.DMA((8,)),
-        ],
-        compiler_params=params(20),
+        scratch_shapes=[pltpu.VMEM((n + 8, n), F32)],
+        compiler_params=params(16),
         cost_estimate=cost(3),
         name="rows",
-    )(at, core, low)
+    )(at, core, mine, other)
 
 
 def per_device(attn_out, out_grad, image_counts, column_owner, damping):
@@ -673,7 +654,7 @@
     mine, part_w = lax.optimization_barrier((mine, part_w))
     theirs = lax.ppermute(mine, "dp", swap_core)
     cut = nb - 2
-    low, *tail, chol_done = chol(core_arr, mine, theirs, width, cut)
+    low, chol_done = chol(core_arr, mine, theirs, width, cut)
 
     got_w = lax.all_to_all(part_w, "dp", split_axis=0, concat_axis=0, tiled=True, axis_index_groups=same_core)
 
@@ -683,8 +664,8 @@
     order = jnp.stack([jnp.where(core == 0, order[:, 0], order[:, 1]), jnp.where(core == 0, order[:, 1], order[:, 0])])
     my_w = sum_parts(got_w, chol_done)
     their_w = lax.ppermute(my_w, "grp", [(1, 0)])
-    low = chol_tail(tail, low, width, cut)
-    my_rows = rows_of(at, core_arr, low, width, ROWS, mine.shape[0])
+    low = chol_tail(low, width, cut)
+    my_rows = rows_of(at, core_arr, mine, theirs, width, ROWS)
     same, cross_t = solve_and_route(order, total[None], my_w, their_w, low, width, block)
     same = lax.ppermute(same, both, [(d, n_dp + d) for d in range(n_dp)])
     cross_t = lax.ppermute(cross_t, both, [(d, n_dp + (d ^ 1)) for d in range(n_dp)])

time: 212 us -> 211 us (level)
  local copies, waits for them, and re-layouts: 15 us -> 12.7 us
    ppermute x2, waiting for transfers between devices: 8.63 us -> 3.77 us  [swap(): lax.ppermute(rows[half:], both, far)]
    ppermute x2, waiting for transfers between devices: 1.63 us -> 5.18 us  [swap(): lax.ppermute(rows[:half], both, near)]
    unnamed x35 -> x31, local copies, waits for them, and re-layouts: 11.1 us -> 8.85 us
  transfers between devices with their start and end apart: 20 -> 20, of which waited for: 10 -> 10; matrix products, arithmetic and copies ran while one was open for 2% -> 3% of each run, Pallas kernels for 33% -> 33%
where the time goes in v10:
time: 211 us; the launch traced here: 210 us
  Pallas kernels  77.3 us (37%)
  waiting for transfers between devices  58.2 us (28%)
  starting transfers between devices  48.8 us (23%)
  local copies, waits for them, and re-layouts  12.7 us (6%)
  between operations  6.96 us (3%)
  other arithmetic  6.08 us (3%)
    pallas_call x1, Pallas kernels, chol(): pl.pallas_call(functools.partial(chol_kernel, cut), out_shape=(jax.ShapeD...  41.6 us
    all_to_all x1, waiting for transfers between devices, per_device(): lax.all_to_all(part.reshape(chips, per_chip * SLAB, B), 'dp', split_axis=...  25.6 us
    pallas_call x1, Pallas kernels, chol_tail(): pl.pallas_call(functools.partial(chol_tail_kernel, cut, n), out_shape=jax...  10.6 us
    all_to_all x1, starting transfers between devices, per_device(): lax.all_to_all(part.reshape(chips, per_chip * SLAB, B), 'dp', split_axis=...  9.99 us
    all_to_all x1, starting transfers between devices, per_device(): lax.all_to_all(pair, 'dp', split_axis=0, concat_axis=0, tiled=True, axis_...  9.76 us
    all_to_all x1, waiting for transfers between devices, per_device(): lax.all_to_all(spread, 'dp', split_axis=0, concat_axis=0, tiled=True, axi...  9.27 us
    unnamed x31, local copies, waits for them, and re-layouts  8.85 us
    all_to_all x1, waiting for transfers between devices, per_device(): lax.all_to_all(pair, 'dp', split_axis=0, concat_axis=0, tiled=True, axis_...  8.01 us
  transfers between devices with their start and end apart: 20, of which 10 were waited for; matrix products, arithmetic and copies ran while one was open for 3% of the time, Pallas kernels for 33%

profile of v10, /device:TPU:0, one launch (start us, length us, event | category | flops | bytes accessed | tf_op | source)
XLA Modules:
  0.0 210.1 jit_solution(13788879928471417561)
XLA Ops:
  0.6 1.5 broadcast_select_fusion
  2.1 0.8 fusion.5
  2.9 1.6 collective-permute-start.1
  4.5 2.1 collective-permute-start.2
  6.6 0.7 fusion.6
  11.2 1.9 collective-permute-done.1.refs_2_
  13.1 2.5 %collective-permute-done.2.refs_3_ = bf16[128,1408]{1,0:T(8,128)(2,1)S(1)} collective-permute-done((bf16[128,1408]{1,0:T(8,128)(2,1)S(1)}, bf16[128,1408]{1,0:T(8,128)(2,1)S(1)}, u32[]{:S(2)}, u32[]{:S(2)}) %collective-permute-start.2) | collective-permute-done | bytes 360480 | tf_op jit(solution)/shard_map/ppermute | solution.py:614
  16.2 2.2 %collective-permute-start.6 = (bf16[128,1408]{1,0:T(8,128)(2,1)S(1)}, bf16[128,1408]{1,0:T(8,128)(2,1)}, u32[]{:S(2)}, u32[]{:S(2)}) collective-permute-start(bf16[128,1408]{1,0:T(8,128)(2,1)S(1)} %get-tuple-element.38), channel_id=1, source_target_pairs={{0,96},{1,97},{2,98},{3,99},{4,100},{5,101},{6,102},{7,103},{8,104... | collective-permute-start | bytes 1081352 | tf_op jit(solution)/shard_map/ppermute | solution.py:614
  18.4 3.4 %gram.1 = (f32[4608,128]{1,0:T(8,128)S(1)}, f32[8,1408]{1,0:T(8,128)S(1)}) custom-call(s32[1]{0:T(128)} %bitcast.4.core_ref, f32[6]{0:T(128)S(1)} %stack.36.keep_ref, bf16[256,1408]{1,0:T(8,128)(2,1)S(1)} %get-tuple-element.17.refs_0_, bf16[256,1408]{1,0:T(8,128)(2,1)S(1)} %collective-permute-done.refs_1_, ...), custom_call_target="tpu_custom_call" | custom-call | flops 4400000000 | bytes 1048576 | tf_op jit(solution)/shard_map/gram/pallas_call | solution.py:98
  21.9 1.4 copy-done
  23.3 3.3 %collective-permute-done.5.refs_8_ = bf16[128,1408]{1,0:T(8,128)(2,1)} collective-permute-done((bf16[128,1408]{1,0:T(8,128)(2,1)S(1)}, bf16[128,1408]{1,0:T(8,128)(2,1)}, u32[]{:S(2)}, u32[]{:S(2)}) %collective-permute-start.5) | collective-permute-done | bytes 360480 | tf_op jit(solution)/shard_map/ppermute | solution.py:614
  26.6 1.3 collective-permute-done.6.refs_9_
  28.0 10.0 %all-to-all-start = ((f32[32,144,128]{2,1,0:T(8,128)}), f32[32,144,128]{2,1,0:T(8,128)}, u32[]{:S(2)}, u32[]{:S(2)}) async-start(f32[32,144,128]{2,1,0:T(8,128)} %bitcast.24), calls=%async_computation | async-start | bytes 4718592 | tf_op jit(solution)/shard_map/all_to_all | solution.py:638
  38.0 0.6 reduce_sum.18
  39.3 0.6 fusion.7
  41.3 0.7 fusion.1.diag_ref
  42.5 0.7 pad_maximum_fusion.3.scale_ref
  43.2 25.6 %all-to-all-done.parts_ref = f32[32,144,128]{2,1,0:T(8,128)} async-done(((f32[32,144,128]{2,1,0:T(8,128)}), f32[32,144,128]{2,1,0:T(8,128)}, u32[]{:S(2)}, u32[]{:S(2)}) %all-to-all-start) | async-done | bytes 2359328 | tf_op jit(solution)/shard_map/all_to_all | solution.py:638
  68.8 3.7 %damp_and_spread.1 = (bf16[32,144,128]{2,1,0:T(8,128)(2,1)}, f32[8,128]{1,0:T(8,128)}) custom-call(f32[2]{0:T(128)} %pad_maximum_fusion.3.scale_ref, f32[32,144,128]{2,1,0:T(8,128)} %all-to-all-done.parts_ref, f32[144,128]{1,0:T(8,128)} %fusion.1.diag_ref), custom_call_target="tpu_custom_call" | custom-call | flops 3300000000 | bytes 1048576 | tf_op jit(solution)/shard_map/damp_and_spread/pallas_call | solution.py:530
  72.5 6.3 %all-to-all-start.1 = ((bf16[32,144,128]{2,1,0:T(8,128)(2,1)}), bf16[32,144,128]{2,1,0:T(8,128)(2,1)S(1)}, u32[]{:S(2)}, u32[]{:S(2)}) async-start(bf16[32,144,128]{2,1,0:T(8,128)(2,1)} %get-tuple-element.19), calls=%async_computation.1 | async-start | bytes 2359296 | tf_op jit(solution)/shard_map/all_to_all | solution.py:650
  78.9 1.0 copy-done.3
  79.8 1.0 copy-done.5
  80.8 1.0 copy-done.7
  81.8 1.0 copy-done.9
  82.8 4.4 %cross.1 = f32[32,24,768]{2,1,0:T(8,128)S(1)} custom-call(s32[1]{0:T(128)} %bitcast.4.core_ref, s32[1]{0:T(128)} %bitcast.7.grp_ref, f32[6]{0:T(128)S(1)} %stack.36.keep_ref, f32[8,128]{1,0:T(8,128)S(1)} %copy-done.10, bf16[256,1408]{1,0:T(8,128)(2,1)S(1)} %get-tuple-element.17.refs_0_, bf16[256,1408]{1,0:T(8,128)(2,1)S(1)} %collective-permute-done.refs_1_, ...), custom_call_target="tpu_custom_call" | custom-call | flops 32999999488 | bytes 1048576 | tf_op jit(solution)/shard_map/cross/pallas_call | solution.py:131
  87.2 1.4 copy-done.1
  88.6 9.3 %all-to-all-done.1 = bf16[32,144,128]{2,1,0:T(8,128)(2,1)S(1)} async-done(((bf16[32,144,128]{2,1,0:T(8,128)(2,1)}), bf16[32,144,128]{2,1,0:T(8,128)(2,1)S(1)}, u32[]{:S(2)}, u32[]{:S(2)}) %all-to-all-start.1) | async-done | bytes 1179680 | tf_op jit(solution)/shard_map/all_to_all | solution.py:650
  98.4 5.5 %all-to-all-start.2 = ((f32[32,24,768]{2,1,0:T(8,128)}), f32[32,24,768]{2,1,0:T(8,128)}, u32[]{:S(2)}, u32[]{:S(2)}) async-start(f32[32,24,768]{2,1,0:T(8,128)} %copy-done.1), calls=%async_computation.2 | async-start | bytes 4718592 | tf_op jit(solution)/shard_map/all_to_all | solution.py:659
  103.9 41.6 %cholesky.1 = (bf16[1408,14336]{1,0:T(8,128)(2,1)}, f32[8,128]{1,0:T(8,128)S(1)}) custom-call(s32[1]{0:T(128)} %bitcast.4.core_ref, bf16[4608,128]{1,0:T(8,128)(2,1)S(1)} %bitcast.26, bf16[4608,128]{1,0:T(8,128)(2,1)} %collective-permute-done.10.other_ref), custom_call_target="tpu_custom_call" | custom-call | flops 42900000768 | bytes 1048576 | tf_op jit(solution)/shard_map/cholesky/pallas_call | solution.py:355
  145.6 1.8 sum_parts.1.one_ref
  147.4 1.5 collective-permute-start.11
  148.9 10.6 %cholesky_tail.1.low_ref = bf16[1408,14336]{1,0:T(8,128)(2,1)} custom-call(bf16[1408,14336]{1,0:T(8,128)(2,1)} %get-tuple-element.26.in_hbm), custom_call_target="tpu_custom_call", output_to_operand_aliasing={{}: (0, {})} | custom-call | flops 9900000256 | bytes 1048576 | tf_op jit(solution)/shard_map/cholesky_tail/pallas_call | solution.py:383
  159.6 5.5 %solve_and_route.1 = (f32[24,768]{1,0:T(8,128)S(1)}, f32[24,768]{1,0:T(8,128)S(1)}) custom-call(s32[2,32]{1,0:T(2,128)S(1)} %pad_add_fusion.owner_ref, f32[1]{0:T(128)} %bitcast.total_ref, f32[24,768]{1,0:T(8,128)S(1)} %sum_parts.1.one_ref, f32[24,768]{1,0:T(8,128)S(1)} %collective-permute-done.11.two_ref, bf16[1408,14336]{1,0:T(8,128)(2,1)} %cholesky_tail.1.low_ref), custom_call_target="tpu_custom_call" | custom-call | flops 9900000256 | bytes 1048576 | tf_op jit(solution)/shard_map/solve_and_route/pallas_call | solution.py:495
  165.0 4.6 %collective-permute-start.12 = (f32[24,768]{1,0:T(8,128)S(1)}, f32[24,768]{1,0:T(8,128)S(1)}, u32[]{:S(2)}, u32[]{:S(2)}) collective-permute-start(f32[24,768]{1,0:T(8,128)S(1)} %get-tuple-element.27), channel_id=1, source_target_pairs={{0,64},{1,65},{2,66},{3,67},{4,68},{5,69},{6,70},{7,71},{8,72},{9,... | collective-permute-start | bytes 221192 | tf_op jit(solution)/shard_map/ppermute | solution.py:670
  169.6 1.3 collective-permute-start.13
  171.5 1.5 collective-permute-done.13
  173.4 1.0 reshape.153
  174.4 9.8 %all-to-all-start.3 = ((f32[32,1,1078]{2,1,0:T(1,128)}), f32[32,1,1078]{2,1,0:T(1,128)S(1)}, u32[]{:S(2)}, u32[]{:S(2)}) async-start(f32[32,1,1078]{2,1,0:T(1,128)} %reshape.153), calls=%async_computation.3 | async-start | bytes 294912 | tf_op jit(solution)/shard_map/all_to_all | solution.py:677
  184.2 2.1 rows.1.after_ref
  186.3 8.0 %all-to-all-done.3 = f32[32,1,1078]{2,1,0:T(1,128)S(1)} async-done(((f32[32,1,1078]{2,1,0:T(1,128)}), f32[32,1,1078]{2,1,0:T(1,128)S(1)}, u32[]{:S(2)}, u32[]{:S(2)}) %all-to-all-start.3) | async-done | bytes 138016 | tf_op jit(solution)/shard_map/all_to_all | solution.py:677
  194.3 0.5 broadcast.163
  194.8 1.0 reduce.7
  196.4 1.5 collective-permute-start.14
  198.2 4.2 %solve.1 = f32[24,1408]{1,0:T(8,128)S(1)} custom-call(f32[24,1408]{1,0:T(8,128)S(1)} %pad.4.rhs_ref, bf16[1408,14336]{1,0:T(8,128)(2,1)} %cholesky_tail.1.low_ref, f32[24,1408]{1,0:T(8,128)S(1)} %rows.1.after_ref), custom_call_target="tpu_custom_call" | custom-call | flops 7699999744 | bytes 1048576 | tf_op jit(solution)/shard_map/solve/pallas_call | solution.py:457
  202.5 1.3 collective-permute-start.15
  203.9 0.8 copy.15
  204.7 4.6 %collective-permute-done.15 = f32[22,1408]{1,0:T(8,128)S(1)} collective-permute-done((f32[22,1408]{1,0:T(8,128)S(1)}, f32[22,1408]{1,0:T(8,128)S(1)}, u32[]{:S(2)}, u32[]{:S(2)}) %collective-permute-start.15) | collective-permute-done | bytes 123936 | tf_op jit(solution)/shard_map/ppermute | solution.py:686
  209.4 0.7 select_bitcast_fusion
  (70 shorter events, 4.0 us)
Async XLA Ops:
  0.6 6.0 %copy-start.11 = (s32[128]{0:T(128)S(1)}, s32[128]{0:T(128)}, u32[]{:S(2)}) copy-start(s32[128]{0:T(128)} %param.7) | copy-start | bytes 1540
  2.9 10.2 %collective-permute-start.1 = (bf16[128,1408]{1,0:T(8,128)(2,1)}, bf16[128,1408]{1,0:T(8,128)(2,1)S(1)}, u32[]{:S(2)}, u32[]{:S(2)}) collective-permute-start(bf16[128,1408]{1,0:T(8,128)(2,1)} %get-tuple-element.41), channel_id=1, source_target_pairs={{0,64},{1,65},{2,66},{3,67},{4,68},{5,69},{6,70},{7,71},{8,72},{9,... | collective-permute-start | bytes 1081352 | tf_op jit(solution)/shard_map/ppermute | solution.py:614
  4.5 11.1 %collective-permute-start.2 = (bf16[128,1408]{1,0:T(8,128)(2,1)S(1)}, bf16[128,1408]{1,0:T(8,128)(2,1)S(1)}, u32[]{:S(2)}, u32[]{:S(2)}) collective-permute-start(bf16[128,1408]{1,0:T(8,128)(2,1)S(1)} %get-tuple-element.40), channel_id=1, source_target_pairs={{0,96},{1,97},{2,98},{3,99},{4,100},{5,101},{6,102},{7,103},{8,104... | collective-permute-start | bytes 1081352 | tf_op jit(solution)/shard_map/ppermute | solution.py:614
  6.6 11.8 %collective-permute-start = (bf16[256,1408]{1,0:T(8,128)(2,1)S(1)}, bf16[256,1408]{1,0:T(8,128)(2,1)S(1)}, u32[]{:S(2)}, u32[]{:S(2)}) collective-permute-start(bf16[256,1408]{1,0:T(8,128)(2,1)S(1)} %get-tuple-element.17.refs_0_), channel_id=1, source_target_pairs={{0,1},{1,0},{2,3},{3,2},{4,5},{5,4},{6,7},{7,6},{8,9},{9,8},{10,11... | collective-permute-start | bytes 2162696 | tf_op jit(solution)/shard_map/ppermute | solution.py:617
  13.1 8.7 %copy-start.2 = (bf16[128,1408]{1,0:T(8,128)(2,1)}, bf16[128,1408]{1,0:T(8,128)(2,1)S(1)}, u32[]{:S(2)}) copy-start(bf16[128,1408]{1,0:T(8,128)(2,1)S(1)} %collective-permute-done.1.refs_2_) | copy-start | bytes 1081348
  15.6 6.3 %copy-start.4 = (bf16[128,1408]{1,0:T(8,128)(2,1)}, bf16[128,1408]{1,0:T(8,128)(2,1)S(1)}, u32[]{:S(2)}) copy-start(bf16[128,1408]{1,0:T(8,128)(2,1)S(1)} %collective-permute-done.2.refs_3_) | copy-start | bytes 1081348
  15.6 2.8 %collective-permute-start.3 = (bf16[128,1408]{1,0:T(8,128)(2,1)S(1)}, bf16[128,1408]{1,0:T(8,128)(2,1)S(1)}, u32[]{:S(2)}, u32[]{:S(2)}) collective-permute-start(bf16[128,1408]{1,0:T(8,128)(2,1)S(1)} %collective-permute-done.1.refs_2_), channel_id=1, source_target_pairs={{0,1},{1,0},{2,3},{3,2},{4,5},{5,4},{6,7},{7,6},{8,9},{9,8},{10,11... | collective-permute-start | bytes 1081352 | tf_op jit(solution)/shard_map/ppermute | solution.py:617
  15.6 2.8 %collective-permute-start.4 = (bf16[128,1408]{1,0:T(8,128)(2,1)S(1)}, bf16[128,1408]{1,0:T(8,128)(2,1)S(1)}, u32[]{:S(2)}, u32[]{:S(2)}) collective-permute-start(bf16[128,1408]{1,0:T(8,128)(2,1)S(1)} %collective-permute-done.2.refs_3_), channel_id=1, source_target_pairs={{0,1},{1,0},{2,3},{3,2},{4,5},{5,4},{6,7},{7,6},{8,9},{9,8},{10,11... | collective-permute-start | bytes 1081352 | tf_op jit(solution)/shard_map/ppermute | solution.py:617
  16.1 10.5 %collective-permute-start.5 = (bf16[128,1408]{1,0:T(8,128)(2,1)S(1)}, bf16[128,1408]{1,0:T(8,128)(2,1)}, u32[]{:S(2)}, u32[]{:S(2)}) collective-permute-start(bf16[128,1408]{1,0:T(8,128)(2,1)S(1)} %get-tuple-element.39), channel_id=1, source_target_pairs={{0,64},{1,65},{2,66},{3,67},{4,68},{5,69},{6,70},{7,71},{8,72},{9,... | collective-permute-start | bytes 1081352 | tf_op jit(solution)/shard_map/ppermute | solution.py:614
  16.2 11.7 %collective-permute-start.6 = (bf16[128,1408]{1,0:T(8,128)(2,1)S(1)}, bf16[128,1408]{1,0:T(8,128)(2,1)}, u32[]{:S(2)}, u32[]{:S(2)}) collective-permute-start(bf16[128,1408]{1,0:T(8,128)(2,1)S(1)} %get-tuple-element.38), channel_id=1, source_target_pairs={{0,96},{1,97},{2,98},{3,99},{4,100},{5,101},{6,102},{7,103},{8,104... | collective-permute-start | bytes 1081352 | tf_op jit(solution)/shard_map/ppermute | solution.py:614
  18.4 3.5 %copy-start.6 = (bf16[128,1408]{1,0:T(8,128)(2,1)}, bf16[128,1408]{1,0:T(8,128)(2,1)S(1)}, u32[]{:S(2)}) copy-start(bf16[128,1408]{1,0:T(8,128)(2,1)S(1)} %collective-permute-done.3.refs_4_) | copy-start | bytes 1081348
  18.4 3.4 %copy-start.8 = (bf16[128,1408]{1,0:T(8,128)(2,1)}, bf16[128,1408]{1,0:T(8,128)(2,1)S(1)}, u32[]{:S(2)}) copy-start(bf16[128,1408]{1,0:T(8,128)(2,1)S(1)} %collective-permute-done.4.refs_5_) | copy-start | bytes 1081348
  21.9 1.4 copy-start
  27.9 11.4 %copy-start.12 = (f32[2]{0:T(128)S(1)}, f32[2]{0:T(128)}, u32[]{:S(2)}) copy-start(f32[2]{0:T(128)} %param.9) | copy-start | bytes 28
  28.0 40.8 %all-to-all-start = ((f32[32,144,128]{2,1,0:T(8,128)}), f32[32,144,128]{2,1,0:T(8,128)}, u32[]{:S(2)}, u32[]{:S(2)}) async-start(f32[32,144,128]{2,1,0:T(8,128)} %bitcast.24), calls=%async_computation | async-start | bytes 4718592 | tf_op jit(solution)/shard_map/all_to_all | solution.py:638
  38.0 40.9 %collective-permute-start.7 = (bf16[256,1408]{1,0:T(8,128)(2,1)S(1)}, bf16[256,1408]{1,0:T(8,128)(2,1)}, u32[]{:S(2)}, u32[]{:S(2)}) collective-permute-start(bf16[256,1408]{1,0:T(8,128)(2,1)S(1)} %get-tuple-element.36.refs_6_), channel_id=1, source_target_pairs={{0,1},{1,0},{2,3},{3,2},{4,5},{5,4},{6,7},{7,6},{8,9},{9,8},{10,11... | collective-permute-start | bytes 2162696 | tf_op jit(solution)/shard_map/ppermute | solution.py:617
  42.0 36.8 %collective-permute-start.8 = (bf16[128,1408]{1,0:T(8,128)(2,1)}, bf16[128,1408]{1,0:T(8,128)(2,1)}, u32[]{:S(2)}, u32[]{:S(2)}) collective-permute-start(bf16[128,1408]{1,0:T(8,128)(2,1)} %collective-permute-done.5.refs_8_), channel_id=1, source_target_pairs={{0,1},{1,0},{2,3},{3,2},{4,5},{5,4},{6,7},{7,6},{8,9},{9,8},{10,11... | collective-permute-start | bytes 1081352 | tf_op jit(solution)/shard_map/ppermute | solution.py:617
  42.5 36.3 %collective-permute-start.9 = (bf16[128,1408]{1,0:T(8,128)(2,1)}, bf16[128,1408]{1,0:T(8,128)(2,1)}, u32[]{:S(2)}, u32[]{:S(2)}) collective-permute-start(bf16[128,1408]{1,0:T(8,128)(2,1)} %collective-permute-done.6.refs_9_), channel_id=1, source_target_pairs={{0,1},{1,0},{2,3},{3,2},{4,5},{5,4},{6,7},{7,6},{8,9},{9,8},{10,11... | collective-permute-start | bytes 1081352 | tf_op jit(solution)/shard_map/ppermute | solution.py:617
  72.5 6.4 %copy-start.10 = (f32[8,128]{1,0:T(8,128)S(1)}, f32[8,128]{1,0:T(8,128)}, u32[]{:S(2)}) copy-start(f32[8,128]{1,0:T(8,128)} %get-tuple-element.20.after_ref) | copy-start | bytes 12292
  72.5 25.4 %all-to-all-start.1 = ((bf16[32,144,128]{2,1,0:T(8,128)(2,1)}), bf16[32,144,128]{2,1,0:T(8,128)(2,1)S(1)}, u32[]{:S(2)}, u32[]{:S(2)}) async-start(bf16[32,144,128]{2,1,0:T(8,128)(2,1)} %get-tuple-element.19), calls=%async_computation.1 | async-start | bytes 2359296 | tf_op jit(solution)/shard_map/all_to_all | solution.py:650
  78.8 1.0 copy-start.3
  79.8 1.0 copy-start.5
  80.8 1.0 copy-start.7
  81.8 1.0 copy-start.9
  82.8 15.1 %copy-start.13 = (s32[64]{0:T(128)S(1)}, s32[64]{0:T(128)}, u32[]{:S(2)}) copy-start(s32[64]{0:T(128)} %param.8) | copy-start | bytes 772
  87.2 1.4 copy-start.1
  97.9 6.0 %collective-permute-start.10 = (bf16[4608,128]{1,0:T(8,128)(2,1)S(1)}, bf16[4608,128]{1,0:T(8,128)(2,1)}, u32[]{:S(2)}, u32[]{:S(2)}) collective-permute-start(bf16[4608,128]{1,0:T(8,128)(2,1)S(1)} %bitcast.25), channel_id=1, source_target_pairs={{0,1},{1,0},{2,3},{3,2},{4,5},{5,4},{6,7},{7,6},{8,9},{9,8},{10,11... | collective-permute-start | bytes 3538952 | tf_op jit(solution)/shard_map/ppermute | solution.py:655
  98.4 47.2 %all-to-all-start.2 = ((f32[32,24,768]{2,1,0:T(8,128)}), f32[32,24,768]{2,1,0:T(8,128)}, u32[]{:S(2)}, u32[]{:S(2)}) async-start(f32[32,24,768]{2,1,0:T(8,128)} %copy-done.1), calls=%async_computation.2 | async-start | bytes 4718592 | tf_op jit(solution)/shard_map/all_to_all | solution.py:659
  147.4 12.2 %collective-permute-start.11 = (f32[24,768]{1,0:T(8,128)S(1)}, f32[24,768]{1,0:T(8,128)S(1)}, u32[]{:S(2)}, u32[]{:S(2)}) collective-permute-start(f32[24,768]{1,0:T(8,128)S(1)} %sum_parts.1.one_ref), channel_id=1, source_target_pairs={{64,0},{65,1},{66,2},{67,3},{68,4},{69,5},{70,6},{71,7},{72,8},{73... | collective-permute-start | bytes 221192 | tf_op jit(solution)/shard_map/ppermute | solution.py:666
  165.0 6.5 %collective-permute-start.12 = (f32[24,768]{1,0:T(8,128)S(1)}, f32[24,768]{1,0:T(8,128)S(1)}, u32[]{:S(2)}, u32[]{:S(2)}) collective-permute-start(f32[24,768]{1,0:T(8,128)S(1)} %get-tuple-element.27), channel_id=1, source_target_pairs={{0,64},{1,65},{2,66},{3,67},{4,68},{5,69},{6,70},{7,71},{8,72},{9,... | collective-permute-start | bytes 221192 | tf_op jit(solution)/shard_map/ppermute | solution.py:670
  169.6 3.4 %collective-permute-start.13 = (f32[24,768]{1,0:T(8,128)S(1)}, f32[24,768]{1,0:T(8,128)S(1)}, u32[]{:S(2)}, u32[]{:S(2)}) collective-permute-start(f32[24,768]{1,0:T(8,128)S(1)} %get-tuple-element.28), channel_id=1, source_target_pairs={{0,65},{1,64},{2,67},{3,66},{4,69},{5,68},{6,71},{7,70},{8,73},{9,... | collective-permute-start | bytes 221192 | tf_op jit(solution)/shard_map/ppermute | solution.py:671
  174.4 19.9 %all-to-all-start.3 = ((f32[32,1,1078]{2,1,0:T(1,128)}), f32[32,1,1078]{2,1,0:T(1,128)S(1)}, u32[]{:S(2)}, u32[]{:S(2)}) async-start(f32[32,1,1078]{2,1,0:T(1,128)} %reshape.153), calls=%async_computation.3 | async-start | bytes 294912 | tf_op jit(solution)/shard_map/all_to_all | solution.py:677
  196.4 7.4 %collective-permute-start.14 = (f32[22,1408]{1,0:T(8,128)S(1)}, f32[22,1408]{1,0:T(8,128)S(1)}, u32[]{:S(2)}, u32[]{:S(2)}) collective-permute-start(f32[22,1408]{1,0:T(8,128)S(1)} %slice_select_fusion), channel_id=1, source_target_pairs={{0,64},{64,0},{1,65},{65,1},{2,66},{66,2},{3,67},{67,3},{4,68},{68... | collective-permute-start | bytes 371720 | tf_op jit(solution)/shard_map/ppermute | solution.py:684
  202.5 6.9 %collective-permute-start.15 = (f32[22,1408]{1,0:T(8,128)S(1)}, f32[22,1408]{1,0:T(8,128)S(1)}, u32[]{:S(2)}, u32[]{:S(2)}) collective-permute-start(f32[22,1408]{1,0:T(8,128)S(1)} %bitcast.28), channel_id=1, source_target_pairs={{64,0},{65,1},{66,2},{67,3},{68,4},{69,5},{70,6},{71,7},{72,8},{73... | collective-permute-start | bytes 371720 | tf_op jit(solution)/shard_map/ppermute | solution.py:686

commit v11 on v10

--- a/solution.py
+++ b/solution.py
@@ -448,25 +448,29 @@
     return [pltpu.VMEM((n, n), BF16), pltpu.VMEM((n, 2 * STEP), BF16), pltpu.SemaphoreType.DMA((2 * -(-n // STEP) - 1,))]
 
 
-def solve_kernel(rhs_ref, low_ref, after_ref, out_ref, *scratch):
+def solve_kernel(grp_ref, rhs_ref, low_ref, after_ref, out_ref, *scratch):
     m, n = rhs_ref.shape
-    solve_into(lambda cols: rhs_ref[:, cols], m, n, low_ref, out_ref, *scratch)
-
-
-def solve(rhs, low, after):
+    pl.when(grp_ref[0] == 1)(lambda: solve_into(lambda cols: rhs_ref[:, cols], m, n, low_ref, out_ref, *scratch))
+
+
+def solve(grp, rhs, low, after):
     return pl.pallas_call(
         solve_kernel,
         out_shape=jax.ShapeDtypeStruct(rhs.shape, F32),
-        in_specs=[VM, HBM, ANY],
+        in_specs=[SM, VM, HBM, ANY],
         out_specs=VM,
         scratch_shapes=solve_scratch(rhs.shape[1]),
         compiler_params=params(16),
         cost_estimate=cost(7),
         name="solve",
-    )(rhs, low, after)
-
-
-def route_kernel(block, owner_ref, total_ref, one_ref, two_ref, low_ref, same_ref, cross_ref, t_ref, r_ref, *scratch):
+    )(grp, rhs, low, after)
+
+
+def route_kernel(block, grp_ref, *refs):
+    pl.when(grp_ref[0] == 0)(lambda: route(block, *refs))
+
+
+def route(block, owner_ref, total_ref, one_ref, two_ref, low_ref, same_ref, cross_ref, t_ref, r_ref, *scratch):
     m, wide = one_ref.shape
     n = t_ref.shape[1] - B
     right = jnp.concatenate([one_ref[...], two_ref[:, 2 * wide - n :]], 1) / total_ref[0]
@@ -488,20 +492,20 @@
         out_ref[...] = r_ref[:, : out_ref.shape[1]]
 
 
-def solve_and_route(owner, total, one, two, low, n, block):
+def solve_and_route(grp, owner, total, one, two, low, n, block):
     m = one.shape[0]
     wide = -(-owner.shape[1] * block // B) * B
     out = jax.ShapeDtypeStruct((m, wide), F32)
     return pl.pallas_call(
         functools.partial(route_kernel, block),
         out_shape=(out, out),
-        in_specs=[SM, SM, VM, VM, HBM],
+        in_specs=[SM, SM, SM, VM, VM, HBM],
         out_specs=(VM, VM),
         scratch_shapes=[pltpu.VMEM((m, n + B), F32), pltpu.VMEM((m, wide + B), F32)] + solve_scratch(n),
         compiler_params=params(16),
         cost_estimate=cost(9),
         name="solve_and_route",
-    )(owner, total, one, two, low)
+    )(grp, owner, total, one, two, low)
 
 
 def sum_kernel(parts_ref, *refs):
@@ -599,6 +603,7 @@
     swap_core = [(d, d ^ 1) for d in range(n_dp)]
     swap_grp = [(0, 1), (1, 0)]
     core_arr = core.astype(jnp.int32)[None]
+    grp_arr = grp_index.astype(jnp.int32)[None]
     is_a = grp_index == 0
 
     def keep_of(grp, dp):
@@ -650,7 +655,7 @@
     mine = lax.all_to_all(spread, "dp", split_axis=0, concat_axis=0, tiled=True, axis_index_groups=same_core)
     mine = mine.reshape(chips * per_chip * SLAB, B)
     wide = (nb + 2) // 2 * B
-    part_w = cross(core_arr, grp_index.astype(jnp.int32)[None], keeps, damp_done, mine_rows, other_rows, chips, wide)
+    part_w = cross(core_arr, grp_arr, keeps, damp_done, mine_rows, other_rows, chips, wide)
     mine, part_w = lax.optimization_barrier((mine, part_w))
     theirs = lax.ppermute(mine, "dp", swap_core)
     cut = nb - 2
@@ -666,7 +671,7 @@
     their_w = lax.ppermute(my_w, "grp", [(1, 0)])
     low = chol_tail(low, width, cut)
     my_rows = rows_of(at, core_arr, mine, theirs, width, ROWS)
-    same, cross_t = solve_and_route(order, total[None], my_w, their_w, low, width, block)
+    same, cross_t = solve_and_route(grp_arr, order, total[None], my_w, their_w, low, width, block)
     same = lax.ppermute(same, both, [(d, n_dp + d) for d in range(n_dp)])
     cross_t = lax.ppermute(cross_t, both, [(d, n_dp + (d ^ 1)) for d in range(n_dp)])
     is_first = core == 0
@@ -678,7 +683,7 @@
     squares = jnp.sum(columns[:, :, 2 * ROWS], axis=0) / total
     columns = columns[:, :, : 2 * ROWS].transpose(1, 0, 2).reshape(block, n_dp * ROWS)[:, :width]
     columns = jnp.pad(columns, ((0, ROWS - block), (0, 0)))
-    left = solve(columns, low, my_rows)[:block]
+    left = solve(grp_arr, columns, low, my_rows)[:block]
     here = (dp_index * block + jnp.arange(block))[:, None] == jnp.arange(width)[None, :]
     my_rows = jnp.where(here, squares[:, None], my_rows[:block])
     their_rows = lax.ppermute(my_rows, "grp", swap_grp)

time: 211 us -> 206 us (0.976)
  Pallas kernels: 77.3 us -> 73.2 us
  starting transfers between devices: 48.8 us -> 45.2 us
  waiting for transfers between devices: 58.2 us -> 60.7 us
    pallas_call x1, Pallas kernels: 4.24 us -> 0.05 us  [solve(): pl.pallas_call(solve_kernel, out_shape=jax.ShapeDtypeStruct(rhs.shape, F3...]
    ppermute x1, starting transfers between devices: 4.55 us -> 1.29 us  [per_device(): same = lax.ppermute(same, both, [(d, n_dp + d) for d in range(n_dp)])]
  transfers between devices with their start and end apart: 20 -> 20, of which waited for: 10 -> 11; matrix products, arithmetic and copies ran while one was open for 3% -> 3% of each run, Pallas kernels for 33% -> 32%
where the time goes in v11:
time: 206 us; the launch traced here: 205 us
  Pallas kernels  73.2 us (36%)
  waiting for transfers between devices  60.7 us (29%)
  starting transfers between devices  45.2 us (22%)
  local copies, waits for them, and re-layouts  12.7 us (6%)
  between operations  6.95 us (3%)
  other arithmetic  6.02 us (3%)
    pallas_call x1, Pallas kernels, chol(): pl.pallas_call(functools.partial(chol_kernel, cut), out_shape=(jax.ShapeD...  41.6 us
    all_to_all x1, waiting for transfers between devices, per_device(): lax.all_to_all(part.reshape(chips, per_chip * SLAB, B), 'dp', split_axis=...  25.6 us
    pallas_call x1, Pallas kernels, chol_tail(): pl.pallas_call(functools.partial(chol_tail_kernel, cut, n), out_shape=jax...  10.6 us
    all_to_all x1, starting transfers between devices, per_device(): lax.all_to_all(part.reshape(chips, per_chip * SLAB, B), 'dp', split_axis=...  9.99 us
    all_to_all x1, starting transfers between devices, per_device(): lax.all_to_all(pair, 'dp', split_axis=0, concat_axis=0, tiled=True, axis_...  9.47 us
    all_to_all x1, waiting for transfers between devices, per_device(): lax.all_to_all(spread, 'dp', split_axis=0, concat_axis=0, tiled=True, axi...  9.27 us
    unnamed x31, local copies, waits for them, and re-layouts  8.85 us
    all_to_all x1, waiting for transfers between devices, per_device(): lax.all_to_all(pair, 'dp', split_axis=0, concat_axis=0, tiled=True, axis_...  8.01 us
  transfers between devices with their start and end apart: 20, of which 11 were waited for; matrix products, arithmetic and copies ran while one was open for 3% of the time, Pallas kernels for 32%

profile of v11, /device:TPU:0, one launch (start us, length us, event | category | flops | bytes accessed | tf_op | source)
XLA Modules:
  0.0 204.8 jit_solution(10870847003646668805)
XLA Ops:
  0.6 1.5 broadcast_select_fusion
  2.1 0.8 fusion.5
  2.9 1.6 collective-permute-start.1
  4.5 2.1 %collective-permute-start.2 = (bf16[128,1408]{1,0:T(8,128)(2,1)S(1)}, bf16[128,1408]{1,0:T(8,128)(2,1)S(1)}, u32[]{:S(2)}, u32[]{:S(2)}) collective-permute-start(bf16[128,1408]{1,0:T(8,128)(2,1)S(1)} %get-tuple-element.40), channel_id=1, source_target_pairs={{0,96},{1,97},{2,98},{3,99},{4,100},{5,101},{6,102},{7,103},{8,104... | collective-permute-start | bytes 1081352 | tf_op jit(solution)/shard_map/ppermute | solution.py:619
  6.6 0.7 fusion.6
  11.2 1.9 collective-permute-done.1.refs_2_
  13.1 2.5 %collective-permute-done.2.refs_3_ = bf16[128,1408]{1,0:T(8,128)(2,1)S(1)} collective-permute-done((bf16[128,1408]{1,0:T(8,128)(2,1)S(1)}, bf16[128,1408]{1,0:T(8,128)(2,1)S(1)}, u32[]{:S(2)}, u32[]{:S(2)}) %collective-permute-start.2) | collective-permute-done | bytes 360480 | tf_op jit(solution)/shard_map/ppermute | solution.py:619
  16.2 2.2 %collective-permute-start.6 = (bf16[128,1408]{1,0:T(8,128)(2,1)S(1)}, bf16[128,1408]{1,0:T(8,128)(2,1)}, u32[]{:S(2)}, u32[]{:S(2)}) collective-permute-start(bf16[128,1408]{1,0:T(8,128)(2,1)S(1)} %get-tuple-element.38), channel_id=1, source_target_pairs={{0,96},{1,97},{2,98},{3,99},{4,100},{5,101},{6,102},{7,103},{8,104... | collective-permute-start | bytes 1081352 | tf_op jit(solution)/shard_map/ppermute | solution.py:619
  18.4 3.4 %gram.1 = (f32[4608,128]{1,0:T(8,128)S(1)}, f32[8,1408]{1,0:T(8,128)S(1)}) custom-call(s32[1]{0:T(128)} %bitcast.5.core_ref, f32[6]{0:T(128)S(1)} %stack.36.keep_ref, bf16[256,1408]{1,0:T(8,128)(2,1)S(1)} %get-tuple-element.17.refs_0_, bf16[256,1408]{1,0:T(8,128)(2,1)S(1)} %collective-permute-done.refs_1_, ...), custom_call_target="tpu_custom_call" | custom-call | flops 4400000000 | bytes 1048576 | tf_op jit(solution)/shard_map/gram/pallas_call | solution.py:98
  21.9 1.4 copy-done
  23.3 3.3 %collective-permute-done.5.refs_8_ = bf16[128,1408]{1,0:T(8,128)(2,1)} collective-permute-done((bf16[128,1408]{1,0:T(8,128)(2,1)S(1)}, bf16[128,1408]{1,0:T(8,128)(2,1)}, u32[]{:S(2)}, u32[]{:S(2)}) %collective-permute-start.5) | collective-permute-done | bytes 360480 | tf_op jit(solution)/shard_map/ppermute | solution.py:619
  26.6 1.3 collective-permute-done.6.refs_9_
  28.0 10.0 %all-to-all-start = ((f32[32,144,128]{2,1,0:T(8,128)}), f32[32,144,128]{2,1,0:T(8,128)}, u32[]{:S(2)}, u32[]{:S(2)}) async-start(f32[32,144,128]{2,1,0:T(8,128)} %bitcast.24), calls=%async_computation | async-start | bytes 4718592 | tf_op jit(solution)/shard_map/all_to_all | solution.py:643
  38.0 0.6 reduce_sum.18
  39.3 0.6 fusion.7
  41.3 0.7 fusion.1.diag_ref
  42.5 0.6 pad_maximum_fusion.3.scale_ref
  43.2 25.6 %all-to-all-done.parts_ref = f32[32,144,128]{2,1,0:T(8,128)} async-done(((f32[32,144,128]{2,1,0:T(8,128)}), f32[32,144,128]{2,1,0:T(8,128)}, u32[]{:S(2)}, u32[]{:S(2)}) %all-to-all-start) | async-done | bytes 2359328 | tf_op jit(solution)/shard_map/all_to_all | solution.py:643
  68.8 3.7 %damp_and_spread.1 = (bf16[32,144,128]{2,1,0:T(8,128)(2,1)}, f32[8,128]{1,0:T(8,128)}) custom-call(f32[2]{0:T(128)} %pad_maximum_fusion.3.scale_ref, f32[32,144,128]{2,1,0:T(8,128)} %all-to-all-done.parts_ref, f32[144,128]{1,0:T(8,128)} %fusion.1.diag_ref), custom_call_target="tpu_custom_call" | custom-call | flops 3300000000 | bytes 1048576 | tf_op jit(solution)/shard_map/damp_and_spread/pallas_call | solution.py:534
  72.5 6.3 %all-to-all-start.1 = ((bf16[32,144,128]{2,1,0:T(8,128)(2,1)}), bf16[32,144,128]{2,1,0:T(8,128)(2,1)S(1)}, u32[]{:S(2)}, u32[]{:S(2)}) async-start(bf16[32,144,128]{2,1,0:T(8,128)(2,1)} %get-tuple-element.19), calls=%async_computation.1 | async-start | bytes 2359296 | tf_op jit(solution)/shard_map/all_to_all | solution.py:655
  78.9 1.0 copy-done.3
  79.8 1.0 copy-done.5
  80.8 1.0 copy-done.7
  81.8 1.0 copy-done.9
  82.8 4.4 %cross.1 = f32[32,24,768]{2,1,0:T(8,128)S(1)} custom-call(s32[1]{0:T(128)} %bitcast.5.core_ref, s32[1]{0:T(128)} %bitcast.grp_ref, f32[6]{0:T(128)S(1)} %stack.36.keep_ref, f32[8,128]{1,0:T(8,128)S(1)} %copy-done.10, bf16[256,1408]{1,0:T(8,128)(2,1)S(1)} %get-tuple-element.17.refs_0_, bf16[256,1408]{1,0:T(8,128)(2,1)S(1)} %collective-permute-done.refs_1_, ...), custom_call_target="tpu_custom_call" | custom-call | flops 32999999488 | bytes 1048576 | tf_op jit(solution)/shard_map/cross/pallas_call | solution.py:131
  87.2 1.4 copy-done.1
  88.6 9.3 %all-to-all-done.1 = bf16[32,144,128]{2,1,0:T(8,128)(2,1)S(1)} async-done(((bf16[32,144,128]{2,1,0:T(8,128)(2,1)}), bf16[32,144,128]{2,1,0:T(8,128)(2,1)S(1)}, u32[]{:S(2)}, u32[]{:S(2)}) %all-to-all-start.1) | async-done | bytes 1179680 | tf_op jit(solution)/shard_map/all_to_all | solution.py:655
  98.4 5.5 %all-to-all-start.2 = ((f32[32,24,768]{2,1,0:T(8,128)}), f32[32,24,768]{2,1,0:T(8,128)}, u32[]{:S(2)}, u32[]{:S(2)}) async-start(f32[32,24,768]{2,1,0:T(8,128)} %copy-done.1), calls=%async_computation.2 | async-start | bytes 4718592 | tf_op jit(solution)/shard_map/all_to_all | solution.py:664
  103.9 41.6 %cholesky.1 = (bf16[1408,14336]{1,0:T(8,128)(2,1)}, f32[8,128]{1,0:T(8,128)S(1)}) custom-call(s32[1]{0:T(128)} %bitcast.5.core_ref, bf16[4608,128]{1,0:T(8,128)(2,1)S(1)} %bitcast.26, bf16[4608,128]{1,0:T(8,128)(2,1)} %collective-permute-done.10.other_ref), custom_call_target="tpu_custom_call" | custom-call | flops 42900000768 | bytes 1048576 | tf_op jit(solution)/shard_map/cholesky/pallas_call | solution.py:355
  145.6 1.8 sum_parts.1.refs_2_
  147.4 1.5 collective-permute-start.11
  148.9 10.6 %cholesky_tail.1.refs_4_.low_ref = bf16[1408,14336]{1,0:T(8,128)(2,1)} custom-call(bf16[1408,14336]{1,0:T(8,128)(2,1)} %get-tuple-element.26.in_hbm), custom_call_target="tpu_custom_call", output_to_operand_aliasing={{}: (0, {})} | custom-call | flops 9900000256 | bytes 1048576 | tf_op jit(solution)/shard_map/cholesky_tail/pallas_call | solution.py:383
  159.6 5.5 %solve_and_route.1 = (f32[24,768]{1,0:T(8,128)S(1)}, f32[24,768]{1,0:T(8,128)S(1)}) custom-call(s32[1]{0:T(128)} %bitcast.grp_ref, s32[2,32]{1,0:T(2,128)S(1)} %pad_add_fusion.refs_0_, f32[1]{0:T(128)} %bitcast.1.refs_1_, f32[24,768]{1,0:T(8,128)S(1)} %sum_parts.1.refs_2_, f32[24,768]{1,0:T(8,128)S(1)} %collective-permute-done.11.refs_3_, ...), custom_call_target="tpu_custom_call" | custom-call | flops 9900000256 | bytes 1048576 | tf_op jit(solution)/shard_map/solve_and_route/pallas_call | solution.py:499
  165.0 1.3 collective-permute-start.12
  166.3 1.3 collective-permute-start.13
  168.0 0.8 collective-permute-done.12
  168.8 1.3 collective-permute-done.13
  170.5 1.0 reshape.153
  171.5 9.5 %all-to-all-start.3 = ((f32[32,1,1078]{2,1,0:T(1,128)}), f32[32,1,1078]{2,1,0:T(1,128)S(1)}, u32[]{:S(2)}, u32[]{:S(2)}) async-start(f32[32,1,1078]{2,1,0:T(1,128)} %reshape.153), calls=%async_computation.3 | async-start | bytes 294912 | tf_op jit(solution)/shard_map/all_to_all | solution.py:682
  181.0 2.1 %rows.1.after_ref = f32[24,1408]{1,0:T(8,128)S(1)} custom-call(s32[1]{0:T(128)} %bitcast.10.at_ref, s32[1]{0:T(128)} %bitcast.5.core_ref, bf16[4608,128]{1,0:T(8,128)(2,1)S(1)} %bitcast.27, bf16[4608,128]{1,0:T(8,128)(2,1)} %collective-permute-done.10.other_ref), custom_call_target="tpu_custom_call" | custom-call | flops 3300000000 | bytes 1048576 | tf_op jit(solution)/shard_map/rows/pallas_call | solution.py:578
  183.1 8.0 %all-to-all-done.3 = f32[32,1,1078]{2,1,0:T(1,128)S(1)} async-done(((f32[32,1,1078]{2,1,0:T(1,128)}), f32[32,1,1078]{2,1,0:T(1,128)S(1)}, u32[]{:S(2)}, u32[]{:S(2)}) %all-to-all-start.3) | async-done | bytes 138016 | tf_op jit(solution)/shard_map/all_to_all | solution.py:682
  191.6 1.0 reduce.7
  193.2 1.5 collective-permute-start.14
  195.1 1.3 collective-permute-start.15
  196.4 1.9 collective-permute-done.14
  198.4 0.8 copy.15
  199.2 4.9 %collective-permute-done.15 = f32[22,1408]{1,0:T(8,128)S(1)} collective-permute-done((f32[22,1408]{1,0:T(8,128)S(1)}, f32[22,1408]{1,0:T(8,128)S(1)}, u32[]{:S(2)}, u32[]{:S(2)}) %collective-permute-start.15) | collective-permute-done | bytes 123936 | tf_op jit(solution)/shard_map/ppermute | solution.py:691
  204.2 0.7 select_bitcast_fusion
  (70 shorter events, 4.2 us)
Async XLA Ops:
  0.6 6.0 %copy-start.11 = (s32[128]{0:T(128)S(1)}, s32[128]{0:T(128)}, u32[]{:S(2)}) copy-start(s32[128]{0:T(128)} %param.7) | copy-start | bytes 1540
  2.9 10.2 %collective-permute-start.1 = (bf16[128,1408]{1,0:T(8,128)(2,1)}, bf16[128,1408]{1,0:T(8,128)(2,1)S(1)}, u32[]{:S(2)}, u32[]{:S(2)}) collective-permute-start(bf16[128,1408]{1,0:T(8,128)(2,1)} %get-tuple-element.41), channel_id=1, source_target_pairs={{0,64},{1,65},{2,66},{3,67},{4,68},{5,69},{6,70},{7,71},{8,72},{9,... | collective-permute-start | bytes 1081352 | tf_op jit(solution)/shard_map/ppermute | solution.py:619
  4.5 11.1 %collective-permute-start.2 = (bf16[128,1408]{1,0:T(8,128)(2,1)S(1)}, bf16[128,1408]{1,0:T(8,128)(2,1)S(1)}, u32[]{:S(2)}, u32[]{:S(2)}) collective-permute-start(bf16[128,1408]{1,0:T(8,128)(2,1)S(1)} %get-tuple-element.40), channel_id=1, source_target_pairs={{0,96},{1,97},{2,98},{3,99},{4,100},{5,101},{6,102},{7,103},{8,104... | collective-permute-start | bytes 1081352 | tf_op jit(solution)/shard_map/ppermute | solution.py:619
  6.6 11.8 %collective-permute-start = (bf16[256,1408]{1,0:T(8,128)(2,1)S(1)}, bf16[256,1408]{1,0:T(8,128)(2,1)S(1)}, u32[]{:S(2)}, u32[]{:S(2)}) collective-permute-start(bf16[256,1408]{1,0:T(8,128)(2,1)S(1)} %get-tuple-element.17.refs_0_), channel_id=1, source_target_pairs={{0,1},{1,0},{2,3},{3,2},{4,5},{5,4},{6,7},{7,6},{8,9},{9,8},{10,11... | collective-permute-start | bytes 2162696 | tf_op jit(solution)/shard_map/ppermute | solution.py:622
  13.1 8.7 %copy-start.2 = (bf16[128,1408]{1,0:T(8,128)(2,1)}, bf16[128,1408]{1,0:T(8,128)(2,1)S(1)}, u32[]{:S(2)}) copy-start(bf16[128,1408]{1,0:T(8,128)(2,1)S(1)} %collective-permute-done.1.refs_2_) | copy-start | bytes 1081348
  15.6 6.3 %copy-start.4 = (bf16[128,1408]{1,0:T(8,128)(2,1)}, bf16[128,1408]{1,0:T(8,128)(2,1)S(1)}, u32[]{:S(2)}) copy-start(bf16[128,1408]{1,0:T(8,128)(2,1)S(1)} %collective-permute-done.2.refs_3_) | copy-start | bytes 1081348
  15.6 2.8 %collective-permute-start.3 = (bf16[128,1408]{1,0:T(8,128)(2,1)S(1)}, bf16[128,1408]{1,0:T(8,128)(2,1)S(1)}, u32[]{:S(2)}, u32[]{:S(2)}) collective-permute-start(bf16[128,1408]{1,0:T(8,128)(2,1)S(1)} %collective-permute-done.1.refs_2_), channel_id=1, source_target_pairs={{0,1},{1,0},{2,3},{3,2},{4,5},{5,4},{6,7},{7,6},{8,9},{9,8},{10,11... | collective-permute-start | bytes 1081352 | tf_op jit(solution)/shard_map/ppermute | solution.py:622
  15.6 2.8 %collective-permute-start.4 = (bf16[128,1408]{1,0:T(8,128)(2,1)S(1)}, bf16[128,1408]{1,0:T(8,128)(2,1)S(1)}, u32[]{:S(2)}, u32[]{:S(2)}) collective-permute-start(bf16[128,1408]{1,0:T(8,128)(2,1)S(1)} %collective-permute-done.2.refs_3_), channel_id=1, source_target_pairs={{0,1},{1,0},{2,3},{3,2},{4,5},{5,4},{6,7},{7,6},{8,9},{9,8},{10,11... | collective-permute-start | bytes 1081352 | tf_op jit(solution)/shard_map/ppermute | solution.py:622
  16.1 10.5 %collective-permute-start.5 = (bf16[128,1408]{1,0:T(8,128)(2,1)S(1)}, bf16[128,1408]{1,0:T(8,128)(2,1)}, u32[]{:S(2)}, u32[]{:S(2)}) collective-permute-start(bf16[128,1408]{1,0:T(8,128)(2,1)S(1)} %get-tuple-element.39), channel_id=1, source_target_pairs={{0,64},{1,65},{2,66},{3,67},{4,68},{5,69},{6,70},{7,71},{8,72},{9,... | collective-permute-start | bytes 1081352 | tf_op jit(solution)/shard_map/ppermute | solution.py:619
  16.2 11.7 %collective-permute-start.6 = (bf16[128,1408]{1,0:T(8,128)(2,1)S(1)}, bf16[128,1408]{1,0:T(8,128)(2,1)}, u32[]{:S(2)}, u32[]{:S(2)}) collective-permute-start(bf16[128,1408]{1,0:T(8,128)(2,1)S(1)} %get-tuple-element.38), channel_id=1, source_target_pairs={{0,96},{1,97},{2,98},{3,99},{4,100},{5,101},{6,102},{7,103},{8,104... | collective-permute-start | bytes 1081352 | tf_op jit(solution)/shard_map/ppermute | solution.py:619
  18.4 3.5 %copy-start.6 = (bf16[128,1408]{1,0:T(8,128)(2,1)}, bf16[128,1408]{1,0:T(8,128)(2,1)S(1)}, u32[]{:S(2)}) copy-start(bf16[128,1408]{1,0:T(8,128)(2,1)S(1)} %collective-permute-done.3.refs_4_) | copy-start | bytes 1081348
  18.4 3.4 %copy-start.8 = (bf16[128,1408]{1,0:T(8,128)(2,1)}, bf16[128,1408]{1,0:T(8,128)(2,1)S(1)}, u32[]{:S(2)}) copy-start(bf16[128,1408]{1,0:T(8,128)(2,1)S(1)} %collective-permute-done.4.refs_5_) | copy-start | bytes 1081348
  21.9 1.4 copy-start
  27.9 11.4 %copy-start.12 = (f32[2]{0:T(128)S(1)}, f32[2]{0:T(128)}, u32[]{:S(2)}) copy-start(f32[2]{0:T(128)} %param.9) | copy-start | bytes 28
  28.0 40.8 %all-to-all-start = ((f32[32,144,128]{2,1,0:T(8,128)}), f32[32,144,128]{2,1,0:T(8,128)}, u32[]{:S(2)}, u32[]{:S(2)}) async-start(f32[32,144,128]{2,1,0:T(8,128)} %bitcast.24), calls=%async_computation | async-start | bytes 4718592 | tf_op jit(solution)/shard_map/all_to_all | solution.py:643
  38.0 40.9 %collective-permute-start.7 = (bf16[256,1408]{1,0:T(8,128)(2,1)S(1)}, bf16[256,1408]{1,0:T(8,128)(2,1)}, u32[]{:S(2)}, u32[]{:S(2)}) collective-permute-start(bf16[256,1408]{1,0:T(8,128)(2,1)S(1)} %get-tuple-element.36.refs_6_), channel_id=1, source_target_pairs={{0,1},{1,0},{2,3},{3,2},{4,5},{5,4},{6,7},{7,6},{8,9},{9,8},{10,11... | collective-permute-start | bytes 2162696 | tf_op jit(solution)/shard_map/ppermute | solution.py:622
  42.0 36.8 %collective-permute-start.8 = (bf16[128,1408]{1,0:T(8,128)(2,1)}, bf16[128,1408]{1,0:T(8,128)(2,1)}, u32[]{:S(2)}, u32[]{:S(2)}) collective-permute-start(bf16[128,1408]{1,0:T(8,128)(2,1)} %collective-permute-done.5.refs_8_), channel_id=1, source_target_pairs={{0,1},{1,0},{2,3},{3,2},{4,5},{5,4},{6,7},{7,6},{8,9},{9,8},{10,11... | collective-permute-start | bytes 1081352 | tf_op jit(solution)/shard_map/ppermute | solution.py:622
  42.5 36.3 %collective-permute-start.9 = (bf16[128,1408]{1,0:T(8,128)(2,1)}, bf16[128,1408]{1,0:T(8,128)(2,1)}, u32[]{:S(2)}, u32[]{:S(2)}) collective-permute-start(bf16[128,1408]{1,0:T(8,128)(2,1)} %collective-permute-done.6.refs_9_), channel_id=1, source_target_pairs={{0,1},{1,0},{2,3},{3,2},{4,5},{5,4},{6,7},{7,6},{8,9},{9,8},{10,11... | collective-permute-start | bytes 1081352 | tf_op jit(solution)/shard_map/ppermute | solution.py:622
  72.5 6.4 %copy-start.10 = (f32[8,128]{1,0:T(8,128)S(1)}, f32[8,128]{1,0:T(8,128)}, u32[]{:S(2)}) copy-start(f32[8,128]{1,0:T(8,128)} %get-tuple-element.20.after_ref) | copy-start | bytes 12292
  72.5 25.4 %all-to-all-start.1 = ((bf16[32,144,128]{2,1,0:T(8,128)(2,1)}), bf16[32,144,128]{2,1,0:T(8,128)(2,1)S(1)}, u32[]{:S(2)}, u32[]{:S(2)}) async-start(bf16[32,144,128]{2,1,0:T(8,128)(2,1)} %get-tuple-element.19), calls=%async_computation.1 | async-start | bytes 2359296 | tf_op jit(solution)/shard_map/all_to_all | solution.py:655
  78.8 1.0 copy-start.3
  79.8 1.0 copy-start.5
  80.8 1.0 copy-start.7
  81.8 1.0 copy-start.9
  82.8 15.1 %copy-start.13 = (s32[64]{0:T(128)S(1)}, s32[64]{0:T(128)}, u32[]{:S(2)}) copy-start(s32[64]{0:T(128)} %param.8) | copy-start | bytes 772
  87.2 1.4 copy-start.1
  97.9 6.0 %collective-permute-start.10 = (bf16[4608,128]{1,0:T(8,128)(2,1)S(1)}, bf16[4608,128]{1,0:T(8,128)(2,1)}, u32[]{:S(2)}, u32[]{:S(2)}) collective-permute-start(bf16[4608,128]{1,0:T(8,128)(2,1)S(1)} %bitcast.25), channel_id=1, source_target_pairs={{0,1},{1,0},{2,3},{3,2},{4,5},{5,4},{6,7},{7,6},{8,9},{9,8},{10,11... | collective-permute-start | bytes 3538952 | tf_op jit(solution)/shard_map/ppermute | solution.py:660
  98.4 47.2 %all-to-all-start.2 = ((f32[32,24,768]{2,1,0:T(8,128)}), f32[32,24,768]{2,1,0:T(8,128)}, u32[]{:S(2)}, u32[]{:S(2)}) async-start(f32[32,24,768]{2,1,0:T(8,128)} %copy-done.1), calls=%async_computation.2 | async-start | bytes 4718592 | tf_op jit(solution)/shard_map/all_to_all | solution.py:664
  147.4 12.2 %collective-permute-start.11 = (f32[24,768]{1,0:T(8,128)S(1)}, f32[24,768]{1,0:T(8,128)S(1)}, u32[]{:S(2)}, u32[]{:S(2)}) collective-permute-start(f32[24,768]{1,0:T(8,128)S(1)} %sum_parts.1.refs_2_), channel_id=1, source_target_pairs={{64,0},{65,1},{66,2},{67,3},{68,4},{69,5},{70,6},{71,7},{72,8},{73... | collective-permute-start | bytes 221192 | tf_op jit(solution)/shard_map/ppermute | solution.py:671
  165.0 3.8 %collective-permute-start.12 = (f32[24,768]{1,0:T(8,128)S(1)}, f32[24,768]{1,0:T(8,128)S(1)}, u32[]{:S(2)}, u32[]{:S(2)}) collective-permute-start(f32[24,768]{1,0:T(8,128)S(1)} %get-tuple-element.27), channel_id=1, source_target_pairs={{0,64},{1,65},{2,66},{3,67},{4,68},{5,69},{6,70},{7,71},{8,72},{9,... | collective-permute-start | bytes 221192 | tf_op jit(solution)/shard_map/ppermute | solution.py:675
  166.3 3.8 %collective-permute-start.13 = (f32[24,768]{1,0:T(8,128)S(1)}, f32[24,768]{1,0:T(8,128)S(1)}, u32[]{:S(2)}, u32[]{:S(2)}) collective-permute-start(f32[24,768]{1,0:T(8,128)S(1)} %get-tuple-element.28), channel_id=1, source_target_pairs={{0,65},{1,64},{2,67},{3,66},{4,69},{5,68},{6,71},{7,70},{8,73},{9,... | collective-permute-start | bytes 221192 | tf_op jit(solution)/shard_map/ppermute | solution.py:676
  171.5 19.6 %all-to-all-start.3 = ((f32[32,1,1078]{2,1,0:T(1,128)}), f32[32,1,1078]{2,1,0:T(1,128)S(1)}, u32[]{:S(2)}, u32[]{:S(2)}) async-start(f32[32,1,1078]{2,1,0:T(1,128)} %reshape.153), calls=%async_computation.3 | async-start | bytes 294912 | tf_op jit(solution)/shard_map/all_to_all | solution.py:682
  193.2 5.1 %collective-permute-start.14 = (f32[22,1408]{1,0:T(8,128)S(1)}, f32[22,1408]{1,0:T(8,128)S(1)}, u32[]{:S(2)}, u32[]{:S(2)}) collective-permute-start(f32[22,1408]{1,0:T(8,128)S(1)} %slice_select_fusion), channel_id=1, source_target_pairs={{0,64},{64,0},{1,65},{65,1},{2,66},{66,2},{3,67},{67,3},{4,68},{68... | collective-permute-start | bytes 371720 | tf_op jit(solution)/shard_map/ppermute | solution.py:689
  195.1 9.0 %collective-permute-start.15 = (f32[22,1408]{1,0:T(8,128)S(1)}, f32[22,1408]{1,0:T(8,128)S(1)}, u32[]{:S(2)}, u32[]{:S(2)}) collective-permute-start(f32[22,1408]{1,0:T(8,128)S(1)} %bitcast.28), channel_id=1, source_target_pairs={{64,0},{65,1},{66,2},{67,3},{68,4},{69,5},{70,6},{71,7},{72,8},{73... | collective-permute-start | bytes 371720 | tf_op jit(solution)/shard_map/ppermute | solution.py:691

commit v12 on v11

--- a/solution.py
+++ b/solution.py
@@ -509,17 +509,29 @@
 
 
 def sum_kernel(parts_ref, *refs):
-    out_ref = refs[-1]
-    acc = parts_ref[0]
-    for k in range(1, parts_ref.shape[0]):
-        acc = acc + parts_ref[k]
-    out_ref[...] = acc
-
-
-def damp_kernel(scale_ref, parts_ref, diag_ref, out_ref, done_ref, sum_ref, sem):
-    acc = parts_ref[0]
-    for k in range(1, parts_ref.shape[0]):
-        acc = acc + parts_ref[k]
+    out_ref, buf_ref, sem = refs[-3:]
+    out_ref[...] = summed(parts_ref, buf_ref, sem)
+
+
+def summed(parts_hbm, buf_ref, sem):
+    count = parts_hbm.shape[0]
+    step = count // sem.shape[0]
+    copies = [
+        pltpu.make_async_copy(parts_hbm.at[k : k + step], buf_ref.at[k : k + step], sem.at[k // step])
+        for k in range(0, count, step)
+    ]
+    for copy in copies:
+        copy.start()
+    acc = None
+    for k in range(count):
+        if k % step == 0:
+            copies[k // step].wait()
+        acc = buf_ref[k] if acc is None else acc + buf_ref[k]
+    return acc
+
+
+def damp_kernel(scale_ref, parts_ref, diag_ref, out_ref, done_ref, sum_ref, buf_ref, sem, buf_sem):
+    acc = summed(parts_ref, buf_ref, buf_sem)
     sum_ref[...] = (acc / scale_ref[0] + scale_ref[1] * diag_ref[...]).astype(BF16)
     copies = [pltpu.make_async_copy(sum_ref, out_ref.at[k], sem.at[k]) for k in range(out_ref.shape[0])]
     for copy in copies:
@@ -534,9 +546,14 @@
     return pl.pallas_call(
         damp_kernel,
         out_shape=(jax.ShapeDtypeStruct(parts.shape, BF16), TOKEN),
-        in_specs=[SM, VM, VM],
+        in_specs=[SM, HBM, VM],
         out_specs=(HBM, VM),
-        scratch_shapes=[pltpu.VMEM(parts.shape[1:], BF16), pltpu.SemaphoreType.DMA((chips,))],
+        scratch_shapes=[
+            pltpu.VMEM(parts.shape[1:], BF16),
+            pltpu.VMEM(parts.shape, F32),
+            pltpu.SemaphoreType.DMA((chips,)),
+            pltpu.SemaphoreType.DMA((4,)),
+        ],
         compiler_params=params(60),
         cost_estimate=cost(3),
         name="damp_and_spread",
@@ -547,8 +564,9 @@
     return pl.pallas_call(
         sum_kernel,
         out_shape=jax.ShapeDtypeStruct(parts.shape[1:], F32),
-        in_specs=[VM] + [ANY] * len(after),
+        in_specs=[HBM] + [ANY] * len(after),
         out_specs=VM,
+        scratch_shapes=[pltpu.VMEM(parts.shape, F32), pltpu.SemaphoreType.DMA((4,))],
         compiler_params=params(16),
         cost_estimate=cost(3),
         name="sum_parts",

time: 206 us -> 207 us (level)
  no operation moved by 1% of the time
where the time goes in v12:
time: 207 us; the launch traced here: 205 us
  Pallas kernels  73.8 us (36%)
  waiting for transfers between devices  60.7 us (29%)
  starting transfers between devices  45.3 us (22%)
  local copies, waits for them, and re-layouts  12.7 us (6%)
  between operations  6.96 us (3%)
  other arithmetic  6.02 us (3%)
    pallas_call x1, Pallas kernels, chol(): pl.pallas_call(functools.partial(chol_kernel, cut), out_shape=(jax.ShapeD...  41.6 us
    all_to_all x1, waiting for transfers between devices, per_device(): lax.all_to_all(part.reshape(chips, per_chip * SLAB, B), 'dp', split_axis=...  25.6 us
    pallas_call x1, Pallas kernels, chol_tail(): pl.pallas_call(functools.partial(chol_tail_kernel, cut, n), out_shape=jax...  10.6 us
    all_to_all x1, starting transfers between devices, per_device(): lax.all_to_all(part.reshape(chips, per_chip * SLAB, B), 'dp', split_axis=...  9.99 us
    all_to_all x1, starting transfers between devices, per_device(): lax.all_to_all(pair, 'dp', split_axis=0, concat_axis=0, tiled=True, axis_...  9.48 us
    all_to_all x1, waiting for transfers between devices, per_device(): lax.all_to_all(spread, 'dp', split_axis=0, concat_axis=0, tiled=True, axi...  9.27 us
    unnamed x31, local copies, waits for them, and re-layouts  8.85 us
    all_to_all x1, waiting for transfers between devices, per_device(): lax.all_to_all(pair, 'dp', split_axis=0, concat_axis=0, tiled=True, axis_...  8.01 us
  transfers between devices with their start and end apart: 20, of which 11 were waited for; matrix products, arithmetic and copies ran while one was open for 3% of the time, Pallas kernels for 32%

profile of v12, /device:TPU:0, one launch (start us, length us, event | category | flops | bytes accessed | tf_op | source)
XLA Modules:
  0.0 205.5 jit_solution(1106878046655830562)
XLA Ops:
  0.6 1.5 broadcast_select_fusion
  2.1 0.8 fusion.5
  2.9 1.6 collective-permute-start.1
  4.5 2.1 %collective-permute-start.2 = (bf16[128,1408]{1,0:T(8,128)(2,1)S(1)}, bf16[128,1408]{1,0:T(8,128)(2,1)S(1)}, u32[]{:S(2)}, u32[]{:S(2)}) collective-permute-start(bf16[128,1408]{1,0:T(8,128)(2,1)S(1)} %get-tuple-element.40), channel_id=1, source_target_pairs={{0,96},{1,97},{2,98},{3,99},{4,100},{5,101},{6,102},{7,103},{8,104... | collective-permute-start | bytes 1081352 | tf_op jit(solution)/shard_map/ppermute | solution.py:637
  6.6 0.7 fusion.6
  11.2 1.9 collective-permute-done.1.refs_2_
  13.1 2.5 %collective-permute-done.2.refs_3_ = bf16[128,1408]{1,0:T(8,128)(2,1)S(1)} collective-permute-done((bf16[128,1408]{1,0:T(8,128)(2,1)S(1)}, bf16[128,1408]{1,0:T(8,128)(2,1)S(1)}, u32[]{:S(2)}, u32[]{:S(2)}) %collective-permute-start.2) | collective-permute-done | bytes 360480 | tf_op jit(solution)/shard_map/ppermute | solution.py:637
  16.2 2.2 %collective-permute-start.6 = (bf16[128,1408]{1,0:T(8,128)(2,1)S(1)}, bf16[128,1408]{1,0:T(8,128)(2,1)}, u32[]{:S(2)}, u32[]{:S(2)}) collective-permute-start(bf16[128,1408]{1,0:T(8,128)(2,1)S(1)} %get-tuple-element.38), channel_id=1, source_target_pairs={{0,96},{1,97},{2,98},{3,99},{4,100},{5,101},{6,102},{7,103},{8,104... | collective-permute-start | bytes 1081352 | tf_op jit(solution)/shard_map/ppermute | solution.py:637
  18.4 3.4 %gram.1 = (f32[4608,128]{1,0:T(8,128)S(1)}, f32[8,1408]{1,0:T(8,128)S(1)}) custom-call(s32[1]{0:T(128)} %bitcast.5.core_ref, f32[6]{0:T(128)S(1)} %stack.36.keep_ref, bf16[256,1408]{1,0:T(8,128)(2,1)S(1)} %get-tuple-element.17.refs_0_, bf16[256,1408]{1,0:T(8,128)(2,1)S(1)} %collective-permute-done.refs_1_, ...), custom_call_target="tpu_custom_call" | custom-call | flops 4400000000 | bytes 1048576 | tf_op jit(solution)/shard_map/gram/pallas_call | solution.py:98
  21.9 1.4 copy-done
  23.3 3.3 %collective-permute-done.5.refs_8_ = bf16[128,1408]{1,0:T(8,128)(2,1)} collective-permute-done((bf16[128,1408]{1,0:T(8,128)(2,1)S(1)}, bf16[128,1408]{1,0:T(8,128)(2,1)}, u32[]{:S(2)}, u32[]{:S(2)}) %collective-permute-start.5) | collective-permute-done | bytes 360480 | tf_op jit(solution)/shard_map/ppermute | solution.py:637
  26.6 1.3 collective-permute-done.6.refs_9_
  28.0 10.0 %all-to-all-start = ((f32[32,144,128]{2,1,0:T(8,128)}), f32[32,144,128]{2,1,0:T(8,128)}, u32[]{:S(2)}, u32[]{:S(2)}) async-start(f32[32,144,128]{2,1,0:T(8,128)} %bitcast.24), calls=%async_computation | async-start | bytes 4718592 | tf_op jit(solution)/shard_map/all_to_all | solution.py:661
  38.0 0.6 reduce_sum.18
  39.3 0.6 fusion.7
  41.3 0.7 fusion.1.diag_ref
  42.5 0.6 pad_maximum_fusion.3.scale_ref
  43.2 25.6 %all-to-all-done.parts_ref = f32[32,144,128]{2,1,0:T(8,128)} async-done(((f32[32,144,128]{2,1,0:T(8,128)}), f32[32,144,128]{2,1,0:T(8,128)}, u32[]{:S(2)}, u32[]{:S(2)}) %all-to-all-start) | async-done | bytes 2359328 | tf_op jit(solution)/shard_map/all_to_all | solution.py:661
  68.8 4.5 %damp_and_spread.1 = (bf16[32,144,128]{2,1,0:T(8,128)(2,1)}, f32[8,128]{1,0:T(8,128)}) custom-call(f32[2]{0:T(128)} %pad_maximum_fusion.3.scale_ref, f32[32,144,128]{2,1,0:T(8,128)} %all-to-all-done.parts_ref, f32[144,128]{1,0:T(8,128)} %fusion.1.diag_ref), custom_call_target="tpu_custom_call" | custom-call | flops 3300000000 | bytes 1048576 | tf_op jit(solution)/shard_map/damp_and_spread/pallas_call | solution.py:546
  73.2 6.3 %all-to-all-start.1 = ((bf16[32,144,128]{2,1,0:T(8,128)(2,1)}), bf16[32,144,128]{2,1,0:T(8,128)(2,1)S(1)}, u32[]{:S(2)}, u32[]{:S(2)}) async-start(bf16[32,144,128]{2,1,0:T(8,128)(2,1)} %get-tuple-element.19), calls=%async_computation.1 | async-start | bytes 2359296 | tf_op jit(solution)/shard_map/all_to_all | solution.py:673
  79.6 1.0 copy-done.3
  80.6 1.0 copy-done.5
  81.6 1.0 copy-done.7
  82.6 1.0 copy-done.9
  83.5 4.4 %cross.1 = f32[32,24,768]{2,1,0:T(8,128)S(1)} custom-call(s32[1]{0:T(128)} %bitcast.5.core_ref, s32[1]{0:T(128)} %bitcast.grp_ref, f32[6]{0:T(128)S(1)} %stack.36.keep_ref, f32[8,128]{1,0:T(8,128)S(1)} %copy-done.10, bf16[256,1408]{1,0:T(8,128)(2,1)S(1)} %get-tuple-element.17.refs_0_, bf16[256,1408]{1,0:T(8,128)(2,1)S(1)} %collective-permute-done.refs_1_, ...), custom_call_target="tpu_custom_call" | custom-call | flops 32999999488 | bytes 1048576 | tf_op jit(solution)/shard_map/cross/pallas_call | solution.py:131
  88.0 1.4 copy-done.1
  89.4 9.3 %all-to-all-done.1 = bf16[32,144,128]{2,1,0:T(8,128)(2,1)S(1)} async-done(((bf16[32,144,128]{2,1,0:T(8,128)(2,1)}), bf16[32,144,128]{2,1,0:T(8,128)(2,1)S(1)}, u32[]{:S(2)}, u32[]{:S(2)}) %all-to-all-start.1) | async-done | bytes 1179680 | tf_op jit(solution)/shard_map/all_to_all | solution.py:673
  99.2 5.5 %all-to-all-start.2 = ((f32[32,24,768]{2,1,0:T(8,128)}), f32[32,24,768]{2,1,0:T(8,128)}, u32[]{:S(2)}, u32[]{:S(2)}) async-start(f32[32,24,768]{2,1,0:T(8,128)} %copy-done.1), calls=%async_computation.2 | async-start | bytes 4718592 | tf_op jit(solution)/shard_map/all_to_all | solution.py:682
  104.7 41.6 %cholesky.1 = (bf16[1408,14336]{1,0:T(8,128)(2,1)}, f32[8,128]{1,0:T(8,128)S(1)}) custom-call(s32[1]{0:T(128)} %bitcast.5.core_ref, bf16[4608,128]{1,0:T(8,128)(2,1)S(1)} %bitcast.26, bf16[4608,128]{1,0:T(8,128)(2,1)} %collective-permute-done.10.other_ref), custom_call_target="tpu_custom_call" | custom-call | flops 42900000768 | bytes 1048576 | tf_op jit(solution)/shard_map/cholesky/pallas_call | solution.py:355
  146.3 1.7 sum_parts.1.refs_2_
  148.0 1.5 collective-permute-start.11
  149.5 10.6 %cholesky_tail.1.refs_4_.low_ref = bf16[1408,14336]{1,0:T(8,128)(2,1)} custom-call(bf16[1408,14336]{1,0:T(8,128)(2,1)} %get-tuple-element.26.in_hbm), custom_call_target="tpu_custom_call", output_to_operand_aliasing={{}: (0, {})} | custom-call | flops 9900000256 | bytes 1048576 | tf_op jit(solution)/shard_map/cholesky_tail/pallas_call | solution.py:383
  160.2 5.5 %solve_and_route.1 = (f32[24,768]{1,0:T(8,128)S(1)}, f32[24,768]{1,0:T(8,128)S(1)}) custom-call(s32[1]{0:T(128)} %bitcast.grp_ref, s32[2,32]{1,0:T(2,128)S(1)} %pad_add_fusion.refs_0_, f32[1]{0:T(128)} %bitcast.1.refs_1_, f32[24,768]{1,0:T(8,128)S(1)} %sum_parts.1.refs_2_, f32[24,768]{1,0:T(8,128)S(1)} %collective-permute-done.11.refs_3_, ...), custom_call_target="tpu_custom_call" | custom-call | flops 9900000256 | bytes 1048576 | tf_op jit(solution)/shard_map/solve_and_route/pallas_call | solution.py:499
  165.7 1.3 collective-permute-start.12
  167.0 1.3 collective-permute-start.13
  168.6 0.8 collective-permute-done.12
  169.4 1.3 collective-permute-done.13
  171.1 1.0 reshape.153
  172.1 9.5 %all-to-all-start.3 = ((f32[32,1,1078]{2,1,0:T(1,128)}), f32[32,1,1078]{2,1,0:T(1,128)S(1)}, u32[]{:S(2)}, u32[]{:S(2)}) async-start(f32[32,1,1078]{2,1,0:T(1,128)} %reshape.153), calls=%async_computation.3 | async-start | bytes 294912 | tf_op jit(solution)/shard_map/all_to_all | solution.py:700
  181.6 2.1 %rows.1.after_ref = f32[24,1408]{1,0:T(8,128)S(1)} custom-call(s32[1]{0:T(128)} %bitcast.10.at_ref, s32[1]{0:T(128)} %bitcast.5.core_ref, bf16[4608,128]{1,0:T(8,128)(2,1)S(1)} %bitcast.27, bf16[4608,128]{1,0:T(8,128)(2,1)} %collective-permute-done.10.other_ref), custom_call_target="tpu_custom_call" | custom-call | flops 3300000000 | bytes 1048576 | tf_op jit(solution)/shard_map/rows/pallas_call | solution.py:596
  183.7 8.0 %all-to-all-done.3 = f32[32,1,1078]{2,1,0:T(1,128)S(1)} async-done(((f32[32,1,1078]{2,1,0:T(1,128)}), f32[32,1,1078]{2,1,0:T(1,128)S(1)}, u32[]{:S(2)}, u32[]{:S(2)}) %all-to-all-start.3) | async-done | bytes 138016 | tf_op jit(solution)/shard_map/all_to_all | solution.py:700
  192.2 1.0 reduce.7
  193.9 1.5 collective-permute-start.14
  195.8 1.3 collective-permute-start.15
  197.1 1.9 collective-permute-done.14
  199.1 0.8 copy.15
  199.9 4.9 %collective-permute-done.15 = f32[22,1408]{1,0:T(8,128)S(1)} collective-permute-done((f32[22,1408]{1,0:T(8,128)S(1)}, f32[22,1408]{1,0:T(8,128)S(1)}, u32[]{:S(2)}, u32[]{:S(2)}) %collective-permute-start.15) | collective-permute-done | bytes 123936 | tf_op jit(solution)/shard_map/ppermute | solution.py:709
  204.8 0.7 select_bitcast_fusion
  (70 shorter events, 4.2 us)
Async XLA Ops:
  0.6 6.0 %copy-start.11 = (s32[128]{0:T(128)S(1)}, s32[128]{0:T(128)}, u32[]{:S(2)}) copy-start(s32[128]{0:T(128)} %param.7) | copy-start | bytes 1540
  2.9 10.2 %collective-permute-start.1 = (bf16[128,1408]{1,0:T(8,128)(2,1)}, bf16[128,1408]{1,0:T(8,128)(2,1)S(1)}, u32[]{:S(2)}, u32[]{:S(2)}) collective-permute-start(bf16[128,1408]{1,0:T(8,128)(2,1)} %get-tuple-element.41), channel_id=1, source_target_pairs={{0,64},{1,65},{2,66},{3,67},{4,68},{5,69},{6,70},{7,71},{8,72},{9,... | collective-permute-start | bytes 1081352 | tf_op jit(solution)/shard_map/ppermute | solution.py:637
  4.5 11.1 %collective-permute-start.2 = (bf16[128,1408]{1,0:T(8,128)(2,1)S(1)}, bf16[128,1408]{1,0:T(8,128)(2,1)S(1)}, u32[]{:S(2)}, u32[]{:S(2)}) collective-permute-start(bf16[128,1408]{1,0:T(8,128)(2,1)S(1)} %get-tuple-element.40), channel_id=1, source_target_pairs={{0,96},{1,97},{2,98},{3,99},{4,100},{5,101},{6,102},{7,103},{8,104... | collective-permute-start | bytes 1081352 | tf_op jit(solution)/shard_map/ppermute | solution.py:637
  6.6 11.8 %collective-permute-start = (bf16[256,1408]{1,0:T(8,128)(2,1)S(1)}, bf16[256,1408]{1,0:T(8,128)(2,1)S(1)}, u32[]{:S(2)}, u32[]{:S(2)}) collective-permute-start(bf16[256,1408]{1,0:T(8,128)(2,1)S(1)} %get-tuple-element.17.refs_0_), channel_id=1, source_target_pairs={{0,1},{1,0},{2,3},{3,2},{4,5},{5,4},{6,7},{7,6},{8,9},{9,8},{10,11... | collective-permute-start | bytes 2162696 | tf_op jit(solution)/shard_map/ppermute | solution.py:640
  13.1 8.7 %copy-start.2 = (bf16[128,1408]{1,0:T(8,128)(2,1)}, bf16[128,1408]{1,0:T(8,128)(2,1)S(1)}, u32[]{:S(2)}) copy-start(bf16[128,1408]{1,0:T(8,128)(2,1)S(1)} %collective-permute-done.1.refs_2_) | copy-start | bytes 1081348
  15.6 6.3 %copy-start.4 = (bf16[128,1408]{1,0:T(8,128)(2,1)}, bf16[128,1408]{1,0:T(8,128)(2,1)S(1)}, u32[]{:S(2)}) copy-start(bf16[128,1408]{1,0:T(8,128)(2,1)S(1)} %collective-permute-done.2.refs_3_) | copy-start | bytes 1081348
  15.6 2.8 %collective-permute-start.3 = (bf16[128,1408]{1,0:T(8,128)(2,1)S(1)}, bf16[128,1408]{1,0:T(8,128)(2,1)S(1)}, u32[]{:S(2)}, u32[]{:S(2)}) collective-permute-start(bf16[128,1408]{1,0:T(8,128)(2,1)S(1)} %collective-permute-done.1.refs_2_), channel_id=1, source_target_pairs={{0,1},{1,0},{2,3},{3,2},{4,5},{5,4},{6,7},{7,6},{8,9},{9,8},{10,11... | collective-permute-start | bytes 1081352 | tf_op jit(solution)/shard_map/ppermute | solution.py:640
  15.6 2.8 %collective-permute-start.4 = (bf16[128,1408]{1,0:T(8,128)(2,1)S(1)}, bf16[128,1408]{1,0:T(8,128)(2,1)S(1)}, u32[]{:S(2)}, u32[]{:S(2)}) collective-permute-start(bf16[128,1408]{1,0:T(8,128)(2,1)S(1)} %collective-permute-done.2.refs_3_), channel_id=1, source_target_pairs={{0,1},{1,0},{2,3},{3,2},{4,5},{5,4},{6,7},{7,6},{8,9},{9,8},{10,11... | collective-permute-start | bytes 1081352 | tf_op jit(solution)/shard_map/ppermute | solution.py:640
  16.1 10.5 %collective-permute-start.5 = (bf16[128,1408]{1,0:T(8,128)(2,1)S(1)}, bf16[128,1408]{1,0:T(8,128)(2,1)}, u32[]{:S(2)}, u32[]{:S(2)}) collective-permute-start(bf16[128,1408]{1,0:T(8,128)(2,1)S(1)} %get-tuple-element.39), channel_id=1, source_target_pairs={{0,64},{1,65},{2,66},{3,67},{4,68},{5,69},{6,70},{7,71},{8,72},{9,... | collective-permute-start | bytes 1081352 | tf_op jit(solution)/shard_map/ppermute | solution.py:637
  16.2 11.7 %collective-permute-start.6 = (bf16[128,1408]{1,0:T(8,128)(2,1)S(1)}, bf16[128,1408]{1,0:T(8,128)(2,1)}, u32[]{:S(2)}, u32[]{:S(2)}) collective-permute-start(bf16[128,1408]{1,0:T(8,128)(2,1)S(1)} %get-tuple-element.38), channel_id=1, source_target_pairs={{0,96},{1,97},{2,98},{3,99},{4,100},{5,101},{6,102},{7,103},{8,104... | collective-permute-start | bytes 1081352 | tf_op jit(solution)/shard_map/ppermute | solution.py:637
  18.4 3.5 %copy-start.6 = (bf16[128,1408]{1,0:T(8,128)(2,1)}, bf16[128,1408]{1,0:T(8,128)(2,1)S(1)}, u32[]{:S(2)}) copy-start(bf16[128,1408]{1,0:T(8,128)(2,1)S(1)} %collective-permute-done.3.refs_4_) | copy-start | bytes 1081348
  18.4 3.4 %copy-start.8 = (bf16[128,1408]{1,0:T(8,128)(2,1)}, bf16[128,1408]{1,0:T(8,128)(2,1)S(1)}, u32[]{:S(2)}) copy-start(bf16[128,1408]{1,0:T(8,128)(2,1)S(1)} %collective-permute-done.4.refs_5_) | copy-start | bytes 1081348
  21.9 1.4 copy-start
  27.9 11.4 %copy-start.12 = (f32[2]{0:T(128)S(1)}, f32[2]{0:T(128)}, u32[]{:S(2)}) copy-start(f32[2]{0:T(128)} %param.9) | copy-start | bytes 28
  28.0 40.8 %all-to-all-start = ((f32[32,144,128]{2,1,0:T(8,128)}), f32[32,144,128]{2,1,0:T(8,128)}, u32[]{:S(2)}, u32[]{:S(2)}) async-start(f32[32,144,128]{2,1,0:T(8,128)} %bitcast.24), calls=%async_computation | async-start | bytes 4718592 | tf_op jit(solution)/shard_map/all_to_all | solution.py:661
  38.0 41.6 %collective-permute-start.7 = (bf16[256,1408]{1,0:T(8,128)(2,1)S(1)}, bf16[256,1408]{1,0:T(8,128)(2,1)}, u32[]{:S(2)}, u32[]{:S(2)}) collective-permute-start(bf16[256,1408]{1,0:T(8,128)(2,1)S(1)} %get-tuple-element.36.refs_6_), channel_id=1, source_target_pairs={{0,1},{1,0},{2,3},{3,2},{4,5},{5,4},{6,7},{7,6},{8,9},{9,8},{10,11... | collective-permute-start | bytes 2162696 | tf_op jit(solution)/shard_map/ppermute | solution.py:640
  42.0 37.5 %collective-permute-start.8 = (bf16[128,1408]{1,0:T(8,128)(2,1)}, bf16[128,1408]{1,0:T(8,128)(2,1)}, u32[]{:S(2)}, u32[]{:S(2)}) collective-permute-start(bf16[128,1408]{1,0:T(8,128)(2,1)} %collective-permute-done.5.refs_8_), channel_id=1, source_target_pairs={{0,1},{1,0},{2,3},{3,2},{4,5},{5,4},{6,7},{7,6},{8,9},{9,8},{10,11... | collective-permute-start | bytes 1081352 | tf_op jit(solution)/shard_map/ppermute | solution.py:640
  42.5 37.1 %collective-permute-start.9 = (bf16[128,1408]{1,0:T(8,128)(2,1)}, bf16[128,1408]{1,0:T(8,128)(2,1)}, u32[]{:S(2)}, u32[]{:S(2)}) collective-permute-start(bf16[128,1408]{1,0:T(8,128)(2,1)} %collective-permute-done.6.refs_9_), channel_id=1, source_target_pairs={{0,1},{1,0},{2,3},{3,2},{4,5},{5,4},{6,7},{7,6},{8,9},{9,8},{10,11... | collective-permute-start | bytes 1081352 | tf_op jit(solution)/shard_map/ppermute | solution.py:640
  73.2 6.4 %copy-start.10 = (f32[8,128]{1,0:T(8,128)S(1)}, f32[8,128]{1,0:T(8,128)}, u32[]{:S(2)}) copy-start(f32[8,128]{1,0:T(8,128)} %get-tuple-element.20.after_ref) | copy-start | bytes 12292
  73.2 25.4 %all-to-all-start.1 = ((bf16[32,144,128]{2,1,0:T(8,128)(2,1)}), bf16[32,144,128]{2,1,0:T(8,128)(2,1)S(1)}, u32[]{:S(2)}, u32[]{:S(2)}) async-start(bf16[32,144,128]{2,1,0:T(8,128)(2,1)} %get-tuple-element.19), calls=%async_computation.1 | async-start | bytes 2359296 | tf_op jit(solution)/shard_map/all_to_all | solution.py:673
  79.6 1.0 copy-start.3
  80.6 1.0 copy-start.5
  81.6 1.0 copy-start.7
  82.6 1.0 copy-start.9
  83.5 15.1 %copy-start.13 = (s32[64]{0:T(128)S(1)}, s32[64]{0:T(128)}, u32[]{:S(2)}) copy-start(s32[64]{0:T(128)} %param.8) | copy-start | bytes 772
  87.9 1.4 copy-start.1
  98.7 6.0 %collective-permute-start.10 = (bf16[4608,128]{1,0:T(8,128)(2,1)S(1)}, bf16[4608,128]{1,0:T(8,128)(2,1)}, u32[]{:S(2)}, u32[]{:S(2)}) collective-permute-start(bf16[4608,128]{1,0:T(8,128)(2,1)S(1)} %bitcast.25), channel_id=1, source_target_pairs={{0,1},{1,0},{2,3},{3,2},{4,5},{5,4},{6,7},{7,6},{8,9},{9,8},{10,11... | collective-permute-start | bytes 3538952 | tf_op jit(solution)/shard_map/ppermute | solution.py:678
  99.2 47.2 %all-to-all-start.2 = ((f32[32,24,768]{2,1,0:T(8,128)}), f32[32,24,768]{2,1,0:T(8,128)}, u32[]{:S(2)}, u32[]{:S(2)}) async-start(f32[32,24,768]{2,1,0:T(8,128)} %copy-done.1), calls=%async_computation.2 | async-start | bytes 4718592 | tf_op jit(solution)/shard_map/all_to_all | solution.py:682
  148.0 12.2 %collective-permute-start.11 = (f32[24,768]{1,0:T(8,128)S(1)}, f32[24,768]{1,0:T(8,128)S(1)}, u32[]{:S(2)}, u32[]{:S(2)}) collective-permute-start(f32[24,768]{1,0:T(8,128)S(1)} %sum_parts.1.refs_2_), channel_id=1, source_target_pairs={{64,0},{65,1},{66,2},{67,3},{68,4},{69,5},{70,6},{71,7},{72,8},{73... | collective-permute-start | bytes 221192 | tf_op jit(solution)/shard_map/ppermute | solution.py:689
  165.7 3.8 %collective-permute-start.12 = (f32[24,768]{1,0:T(8,128)S(1)}, f32[24,768]{1,0:T(8,128)S(1)}, u32[]{:S(2)}, u32[]{:S(2)}) collective-permute-start(f32[24,768]{1,0:T(8,128)S(1)} %get-tuple-element.27), channel_id=1, source_target_pairs={{0,64},{1,65},{2,66},{3,67},{4,68},{5,69},{6,70},{7,71},{8,72},{9,... | collective-permute-start | bytes 221192 | tf_op jit(solution)/shard_map/ppermute | solution.py:693
  167.0 3.8 %collective-permute-start.13 = (f32[24,768]{1,0:T(8,128)S(1)}, f32[24,768]{1,0:T(8,128)S(1)}, u32[]{:S(2)}, u32[]{:S(2)}) collective-permute-start(f32[24,768]{1,0:T(8,128)S(1)} %get-tuple-element.28), channel_id=1, source_target_pairs={{0,65},{1,64},{2,67},{3,66},{4,69},{5,68},{6,71},{7,70},{8,73},{9,... | collective-permute-start | bytes 221192 | tf_op jit(solution)/shard_map/ppermute | solution.py:694
  172.1 19.6 %all-to-all-start.3 = ((f32[32,1,1078]{2,1,0:T(1,128)}), f32[32,1,1078]{2,1,0:T(1,128)S(1)}, u32[]{:S(2)}, u32[]{:S(2)}) async-start(f32[32,1,1078]{2,1,0:T(1,128)} %reshape.153), calls=%async_computation.3 | async-start | bytes 294912 | tf_op jit(solution)/shard_map/all_to_all | solution.py:700
  193.9 5.1 %collective-permute-start.14 = (f32[22,1408]{1,0:T(8,128)S(1)}, f32[22,1408]{1,0:T(8,128)S(1)}, u32[]{:S(2)}, u32[]{:S(2)}) collective-permute-start(f32[22,1408]{1,0:T(8,128)S(1)} %slice_select_fusion), channel_id=1, source_target_pairs={{0,64},{64,0},{1,65},{65,1},{2,66},{66,2},{3,67},{67,3},{4,68},{68... | collective-permute-start | bytes 371720 | tf_op jit(solution)/shard_map/ppermute | solution.py:707
  195.8 9.0 %collective-permute-start.15 = (f32[22,1408]{1,0:T(8,128)S(1)}, f32[22,1408]{1,0:T(8,128)S(1)}, u32[]{:S(2)}, u32[]{:S(2)}) collective-permute-start(f32[22,1408]{1,0:T(8,128)S(1)} %bitcast.28), channel_id=1, source_target_pairs={{64,0},{65,1},{66,2},{67,3},{68,4},{69,5},{70,6},{71,7},{72,8},{73... | collective-permute-start | bytes 371720 | tf_op jit(solution)/shard_map/ppermute | solution.py:709
